TPU v7x, 32 devices: a whole 2x2x4 slice. The times are simulated.
32 devices in a mesh: dp: 32 (over z, y, x, core), tensor: 1.
Axes of the slice: x: 2, y: 2, z: 4, core: 2. Of those that a mesh axis runs over, the one named last changes fastest.
Arguments:
- user_feats: bfloat16 [4096, 1024], P(('dp', 'tensor')), may hold values from -240 to 240
- item_feats: bfloat16 [4096, 1024], P(('dp', 'tensor')), may hold values from -6 to 6
- user_w_in: bfloat16 [1024, 8192], P(None, 'tensor'), may hold values from -0.1875 to 0.1875
- user_w_out: bfloat16 [8192, 1024], P('tensor'), may hold values from -0.0625 to 0.0625
- item_w_in: bfloat16 [1024, 8192], P(None, 'tensor'), may hold values from -0.1875 to 0.1875
- item_w_out: bfloat16 [8192, 1024], P('tensor'), may hold values from -0.0625 to 0.0625
- teacher: float32 [4096, 2048], P(('dp', 'tensor')), may hold values from -250 to 250
- cand_blocks: int32 [32, 16], P(('dp', 'tensor')), may hold values from 0 to 31, all different within a row
- cand_count: int32 [32], P(('dp', 'tensor')), may hold values from 10 to 16
- owner_map: int32 [32], replicated, may hold values from 0 to 31, each once
Outputs:
- divergence: float32 [4096], P(('dp', 'tensor'))
- user_grad: float32 [4096, 1024], P(('dp', 'tensor'))
- item_grad: float32 [4096, 1024], P(('dp', 'tensor'))
Inputs may be any that keep to these rules, and one draw needn't show every extreme that they name: `cand_blocks`: the 16 ids of one row are distinct. `owner_map`: every dp index appears exactly once.
All inputs are finite; a program needn't handle non-finite values.
Results may differ from a plain program's by a relative error of at most 0.017.
The roundings to bfloat16 on the way count: a program that leaves them out, or rounds other values in their place, can miss the bound.
Values may be sent and summed in bfloat16 or wider, within the bound.
No kernel may reach another device: no remote copies, remote signals or barrier semaphores. Data moves between devices by JAX's collectives and lax.ppermute only.
A program may use at most 128 MiB of HBM per device.

v0:
```python
import math

import jax
import jax.numpy as jnp
from jax import lax
from jax.sharding import PartitionSpec as P


def masked_softmax(logits, usable):
    highest = jnp.max(jnp.where(usable, logits, -jnp.inf), axis=(1, 2), keepdims=True)
    shifted = jnp.where(usable, logits - highest, -jnp.inf)
    exponent = jnp.exp(shifted)
    denominator = jnp.sum(exponent, axis=(1, 2), keepdims=True)
    log_prob = jnp.where(usable, shifted - jnp.log(denominator), 0.0)
    return (exponent / denominator, log_prob)


def shards(
    user_feats,
    item_feats,
    user_w_in,
    user_w_out,
    item_w_in,
    item_w_out,
    teacher,
    cand_blocks,
    cand_count,
    owner_map,
):
    block_rows = user_feats.shape[0]
    width = user_feats.shape[1]
    slots = cand_blocks.shape[1]
    dp_count = lax.axis_size("dp")
    gathered_user, gathered_item = (
        lax.all_gather(user_feats, "tensor", axis=0, tiled=True),
        lax.all_gather(item_feats, "tensor", axis=0, tiled=True),
    )
    user_hidden = jax.nn.relu(
        jnp.dot(gathered_user, user_w_in, preferred_element_type=jnp.float32)
    ).astype(jnp.bfloat16)
    item_hidden = jax.nn.relu(
        jnp.dot(gathered_item, item_w_in, preferred_element_type=jnp.float32)
    ).astype(jnp.bfloat16)
    user_out = jnp.dot(user_hidden, user_w_out, preferred_element_type=jnp.float32)
    item_out = jnp.dot(item_hidden, item_w_out, preferred_element_type=jnp.float32)
    stacked = jnp.stack(
        (user_out.reshape(-1, block_rows, width), item_out.reshape(-1, block_rows, width)), axis=1
    )
    owned_rows = lax.psum_scatter(
        stacked.reshape(2 * block_rows * lax.axis_size("tensor"), width),
        "tensor",
        scatter_dimension=0,
        tiled=True,
    )
    user_emb = owned_rows[:block_rows].astype(jnp.bfloat16)
    item_emb = owned_rows[block_rows:].astype(jnp.bfloat16)
    item_table = lax.all_gather(item_emb, "dp", axis=0, tiled=True).reshape(
        dp_count, block_rows, width
    )
    owners = jnp.arange(dp_count, dtype=jnp.int32)
    onehot = cand_blocks[0][:, None] == owners[None, :]
    positions = jnp.sum(jnp.where(onehot, owner_map[None, :], 0), axis=1)
    picked = jnp.take(item_table, positions, axis=0)
    logit_scale = 3.0 / math.sqrt(width)
    loss_weight = block_rows * slots / 4.0
    student = logit_scale * jnp.einsum(
        "ud,kjd->ukj", user_emb, picked, preferred_element_type=jnp.float32
    )
    live_slots = jnp.arange(slots) < cand_count[0]
    usable = live_slots[None, :, None]
    teacher_rows = teacher.reshape(block_rows, slots, block_rows)
    teacher_prob, log_teacher = masked_softmax(teacher_rows, usable)
    student_prob, log_student = masked_softmax(student, usable)
    divergence = jnp.sum(
        jnp.where(usable, teacher_prob * (log_teacher - log_student), 0.0), axis=(1, 2)
    )
    logit_grads = (loss_weight * logit_scale * (student_prob - teacher_prob)).astype(jnp.bfloat16)
    user_grad = jnp.einsum("ukj,kjd->ud", logit_grads, picked, preferred_element_type=jnp.float32)
    contrib = jnp.einsum(
        "ukj,ud->kjd", logit_grads, user_emb, preferred_element_type=jnp.float32
    ).astype(jnp.bfloat16)
    selector = ((positions[None, :] == owners[:, None]) & live_slots[None, :]).astype(jnp.bfloat16)
    outgoing = jnp.dot(
        selector, contrib.reshape(slots, block_rows * width), preferred_element_type=jnp.float32
    )
    item_grad = lax.psum_scatter(
        outgoing.reshape(dp_count * block_rows, width).astype(jnp.bfloat16),
        "dp",
        scatter_dimension=0,
        tiled=True,
    ).astype(jnp.float32)
    return (divergence, user_grad, item_grad)


def solution(mesh):
    placed = (
        P(("dp", "tensor"), None),
        P(("dp", "tensor"), None),
        P(None, "tensor"),
        P("tensor", None),
        P(None, "tensor"),
        P("tensor", None),
        P(("dp", "tensor"), None),
        P(("dp", "tensor"), None),
        P(("dp", "tensor")),
        P(),
    )
    return jax.shard_map(
        shards,
        mesh=mesh,
        in_specs=placed,
        out_specs=(P(("dp", "tensor")), P(("dp", "tensor"), None), P(("dp", "tensor"), None)),
        check_vma=False,
    )
```

profile of v0, /device:TPU:0, one launch (start us, length us, event | category | flops | bytes accessed | tf_op | source)
XLA Modules:
  0.0 288.8 jit_solution(5523863814550337027)
XLA Ops:
  7.2 0.0 copy-start
  7.2 0.0 copy-start.2
  7.2 0.0 copy-start.4
  7.2 0.0 copy-start.5
  7.2 0.0 all-gather.2.cloned.1.call-start
  7.3 0.9 copy-done
  8.1 15.8 %convolution_convert_fusion.2 = bf16[128,1024]{1,0:T(8,128)(2,1)} fusion(bf16[8192,1024]{1,0:T(8,128)(2,1)} %param.15, bf16[128,1024]{1,0:T(8,128)(2,1)S(1)} %copy-done, bf16[1024,8192]{1,0:T(8,128)(2,1)} %param.14), kind=kOutput, calls=%fused_computation.12 | convolution fusion | flops 4297195520 | bytes 34078720 | tf_op jit(solution)/shard_map/dot_general | solution.py:45
  23.9 0.0 copy-start.3
  23.9 0.0 all-gather.2.cloned.1.call-update
  23.9 0.2 reduce-scatter.2.cloned.1.call-start
  24.8 0.0 copy-done.2
  24.8 0.3 copy.15
  25.2 0.0 copy-done.4
  25.2 0.0 copy-done.5
  25.2 0.2 select_reduce_fusion.3
  25.4 0.1 broadcast_bitcast_fusion
  25.5 0.2 select_reduce_fusion.2
  25.6 0.3 exponential_reduce_fusion
  26.0 0.0 copy-done.3
  26.0 15.4 %fusion.6 = bf16[128,1024,1]{1,0,2:T(8,128)(2,1)S(1)} fusion(bf16[8192,1024]{1,0:T(8,128)(2,1)} %param.13, bf16[128,1024]{1,0:T(8,128)(2,1)S(1)} %copy-done.3, bf16[1024,8192]{1,0:T(8,128)(2,1)} %param.12), kind=kOutput, calls=%fused_computation.14 | convolution fusion | flops 4297195520 | bytes 34078720 | tf_op jit(solution)/shard_map/dot_general | solution.py:44
  41.3 62.9 %all-gather.2.cloned.1.call-done = bf16[4096,1024]{1,0:T(8,128)(2,1)} async-done(((bf16[128,1024]{1,0:T(8,128)(2,1)}), bf16[4096,1024]{1,0:T(8,128)(2,1)}) %all-gather.2.cloned.1.call-update) | async-done | bytes 8388624 | tf_op jit(solution)/shard_map/all_gather | solution.py:57
  104.2 6.1 %gather_fusion = bf16[16,128,1024]{2,1,0:T(8,128)(2,1)} fusion(bf16[32,128,1024]{2,1,0:T(8,128)(2,1)} %bitcast.32, s32[1024]{0:T(1024)S(1)} %pad_clamp_fusion), kind=kCustom, calls=%fused_computation | custom fusion | bytes 8388672 | tf_op jit(solution)/shard_map/jit(_take)/gather | solution.py:63
  110.3 3.5 %select_reduce_fusion.1 = (f32[128]{0:T(128)S(1)}, f32[128,16,128]{0,2,1:T(8,128)S(1)}) fusion(pred[16]{0:T(512)(128)(4,1)S(1)} %get-tuple-element.6, bf16[128,1024,1]{1,0,2:T(8,128)(2,1)S(1)} %fusion.6, bf16[16,128,1024]{2,1,0:T(8,128)(2,1)} %gather_fusion, pred[16]{0:T(512)(128)(4,1)S(1)} %get-tuple-element.5), kind=kOutput, calls=%fused_computation.18 | convolution fusion | flops 539754368 | bytes 5505568 | tf_op jit(solution)/shard_map/ud,kjd->ukj/dot_general | solution.py:66
  113.8 0.4 exponential_reduce_fusion.1
  114.3 1.3 convolution_convert_fusion.1
  115.6 2.3 copy.18
  117.9 5.8 %convolution_convert_fusion = bf16[32,131072]{1,0:T(8,128)(2,1)} fusion(bf16[16,131072]{1,0:T(8,128)(2,1)S(1)} %bitcast.28, s32[16]{0:T(128)S(1)} %select_reduce_fusion.3, pred[16]{0:T(512)(128)(4,1)S(1)} %get-tuple-element.6), kind=kOutput, calls=%fused_computation.1 | convolution fusion | flops 138413056 | bytes 12582992 | tf_op jit(solution)/shard_map/dot_general | solution.py:83
  123.7 8.9 %convert_element_type.35 = bf16[4096,1024]{1,0:T(8,128)(2,1)} reshape(bf16[32,131072]{1,0:T(8,128)(2,1)} %convolution_convert_fusion) | data formatting | bytes 16777216 | tf_op jit(solution)/shard_map/convert_element_type | solution.py:87
  132.6 0.0 reduce-scatter.2.cloned.1.call-update
  132.6 1.1 select_reduce_fusion
  133.7 0.0 copy-start.1
  133.7 4.5 %fusion.5 = f32[128,1024]{1,0:T(8,128)} fusion(bf16[16,128,1024]{2,1,0:T(8,128)(2,1)} %gather_fusion, pred[16]{0:T(512)(128)(4,1)S(1)} %get-tuple-element.5, f32[128,16,128]{0,2,1:T(8,128)S(1)} %get-tuple-element.4, f32[128,16,128]{0,2,1:T(8,128)S(1)} %bitcast.30, f32[128]{0:T(128)S(1)} %exponential_reduce_fusion.1, f32[128]{0:T(128)S(1)} %get-tuple-element.3, ...), kind=kOutput, calls=%fused_computation.11 | convolution fusion | flops 541327360 | bytes 6817824 | tf_op jit(solution)/shard_map/ukj,kjd->ud/dot_general | solution.py:78
  138.2 142.0 %reduce-scatter.2.cloned.1.call-done = bf16[128,1024]{1,0:T(8,128)(2,1)} async-done(((bf16[4096,1024]{1,0:T(8,128)(2,1)}), bf16[128,1024]{1,0:T(8,128)(2,1)}) %reduce-scatter.2.cloned.1.call-update) | async-done | bytes 262160 | tf_op jit(solution)/shard_map/reduce_scatter | solution.py:86
  280.2 1.8 convert_element_type.36
  282.0 0.0 copy-done.1
  (5 shorter events, 0.0 us)
Async XLA Ops:
  7.2 1.0 copy-start
  7.2 17.6 %copy-start.2 = (f32[128,2048]{1,0:T(8,128)S(1)}, f32[128,2048]{1,0:T(8,128)}, u32[]{:S(2)}) copy-start(f32[128,2048]{1,0:T(8,128)} %param.16) | copy-start | bytes 3145732
  7.2 18.0 %copy-start.4 = (s32[32]{0:T(128)S(1)}, s32[32]{0:T(128)}, u32[]{:S(2)}) copy-start(s32[32]{0:T(128)} %param.19) | copy-start | bytes 388
  7.2 18.0 %copy-start.5 = (s32[1,16]{1,0:T(1,128)S(1)}, s32[1,16]{1,0:T(1,128)}, u32[]{:S(2)}) copy-start(s32[1,16]{1,0:T(1,128)} %param.17) | copy-start | bytes 196
  7.2 97.0 %all-gather.2.cloned.1.call-start = ((), (), s32[]{:S(2)}) async-start(), calls=%async_computation.1 | async-start | bytes 8650752 | tf_op jit(solution)/shard_map/all_gather | solution.py:57
  23.9 2.0 copy-start.3
  23.9 256.2 %reduce-scatter.2.cloned.1.call-start = ((), (), s32[]{:S(2)}) async-start(), calls=%async_computation.2 | async-start | bytes 8650752 | tf_op jit(solution)/shard_map/reduce_scatter | solution.py:86
  133.7 148.2 %copy-start.1 = (bf16[128,1024]{1,0:T(8,128)(2,1)S(1)}, bf16[128,1024]{1,0:T(8,128)(2,1)}, u32[]{:S(2)}) copy-start(bf16[128,1024]{1,0:T(8,128)(2,1)} %param.11) | copy-start | bytes 786436
Sparse Core Ops, SparseCore 0:
  24.1 80.1 all-gather.1
  132.7 147.3 reduce-scatter.1
where the time goes:
time: 289 us
  waiting for transfers between devices  205 us (71%)
  matrix products  46.2 us (16%)
  local copies, waits for them, and re-layouts  18.6 us (6%)
  between operations  14.8 us (5%)
  other arithmetic  4.01 us (1%)
    reduce_scatter x1, waiting for transfers between devices, shards(): lax.psum_scatter(outgoing.reshape(dp_count * block_rows, width).astype(jn...  142 us
    all_gather x1, waiting for transfers between devices, shards(): lax.all_gather(item_emb, 'dp', axis=0, tiled=True)  62.9 us
    dot_general x1, matrix products, shards(): jnp.dot(item_hidden, item_w_out, preferred_element_type=jnp.float32)  15.8 us
    dot_general x1, matrix products, shards(): jnp.dot(user_hidden, user_w_out, preferred_element_type=jnp.float32)  15.4 us
    convert_element_type x1, local copies, waits for them, and re-layouts, shards(): outgoing.reshape(dp_count * block_rows, width).astype(jnp.bfloat16)  8.9 us
    gather x1, local copies, waits for them, and re-layouts, shards(): picked = jnp.take(item_table, positions, axis=0)  6.12 us
  transfers between devices with their start and end apart: 2, of which 2 were waited for; matrix products, arithmetic and copies ran while one was open for 8% of the time, Pallas kernels for 0%

commit v1 on v0

v1 whole, which is shorter than its diff:
```python
import functools
import math

import jax
import jax.numpy as jnp
from jax import lax
from jax.experimental import pallas as pl
from jax.experimental.pallas import tpu as pltpu
from jax.sharding import PartitionSpec as P

CORES = 2
DEAD = -1e30
LIVE = -1e29
MIB = 1 << 20
ANY = pl.BlockSpec(memory_space=pl.ANY)
VMEM = pl.BlockSpec(memory_space=pltpu.VMEM)
SMEM = pl.BlockSpec(memory_space=pltpu.SMEM)


def struct(shape, dtype):
    return jax.ShapeDtypeStruct(shape, dtype)


def params(mib):
    return pltpu.CompilerParams(vmem_limit_bytes=mib * MIB)


def cost(flops, moved):
    return pl.CostEstimate(flops=int(flops), bytes_accessed=int(moved), transcendentals=0)


def tower_body(chunks, feats, w_in, w_out, out, held_in, held_out, total, sem_in, sem_out):
    step = w_in.shape[1] // chunks

    def copies(i):
        part = pl.ds(pl.multiple_of(i * step, step), step)
        return (
            pltpu.make_async_copy(w_in.at[:, part], held_in.at[:, part], sem_in.at[i]),
            pltpu.make_async_copy(w_out.at[part], held_out.at[part], sem_out.at[i]),
        )

    for i in range(chunks):
        for copy in copies(i):
            copy.start()
    total[...] = jnp.zeros_like(total)

    def one(i, carry):
        first, second = copies(i)
        part = pl.ds(pl.multiple_of(i * step, step), step)
        first.wait()
        hidden = jnp.dot(feats[...], held_in[:, part], preferred_element_type=jnp.float32)
        hidden = jnp.maximum(hidden, 0.0).astype(jnp.bfloat16)
        second.wait()
        total[...] += jnp.dot(hidden, held_out[part], preferred_element_type=jnp.float32)
        return carry

    lax.fori_loop(0, chunks, one, 0)
    out[...] = total[...].astype(out.dtype)


def tower(feats, w_in, w_out, dtype):
    rows, width = feats.shape
    hidden = w_in.shape[1]
    chunks = max(1, hidden // 512)
    return pl.pallas_call(
        functools.partial(tower_body, chunks),
        in_specs=[VMEM, ANY, ANY],
        out_specs=VMEM,
        out_shape=struct((rows, width), dtype),
        scratch_shapes=[
            pltpu.VMEM(w_in.shape, w_in.dtype),
            pltpu.VMEM(w_out.shape, w_out.dtype),
            pltpu.VMEM((rows, width), jnp.float32),
            pltpu.SemaphoreType.DMA((chunks,)),
            pltpu.SemaphoreType.DMA((chunks,)),
        ],
        compiler_params=params(52),
        cost_estimate=cost(4 * rows * width * hidden, 4 * width * hidden),
    )(feats, w_in, w_out)


def embed(feats, w_in, w_out):
    if lax.axis_size("tensor") == 1:
        return tower(feats, w_in, w_out, jnp.bfloat16)
    feats = lax.all_gather(feats, "tensor", axis=0, tiled=True)
    partial = tower(feats, w_in, w_out, jnp.float32)
    return lax.psum_scatter(partial, "tensor", scatter_dimension=0, tiled=True).astype(jnp.bfloat16)


def teacher_body(cols, planes, me, cands, count, owner, teacher, *refs):
    places = CORES * cols
    outs, dense, sems = refs[:places], refs[places], refs[places + 1]
    rows = teacher.shape[0]
    slots = cands.shape[1]
    live = count[0]
    logits = teacher[...]
    usable = lax.broadcasted_iota(jnp.int32, logits.shape, 1) < live * rows
    shifted = logits - jnp.max(jnp.where(usable, logits, -jnp.inf), axis=1, keepdims=True)
    norm = jnp.sum(jnp.where(usable, jnp.exp(shifted), 0.0), axis=1, keepdims=True)
    log_p = shifted - jnp.log(norm)
    dense[...] = jnp.full(dense.shape, DEAD, jnp.float32)
    for k in range(slots):

        @pl.when(k < live)
        def _():
            apart = owner[cands[0, k]] ^ me[0]
            plane = apart // (CORES * cols)
            inside = apart % (CORES * cols)
            place = (inside % CORES) * cols + inside // CORES
            dense[place, plane] = log_p[:, k * rows : (k + 1) * rows].T

    copies = [pltpu.make_async_copy(dense.at[i], outs[i], sems.at[i]) for i in range(places)]
    for copy in copies:
        copy.start()
    for copy in copies:
        copy.wait()


def spread_teacher(cols, planes, me, cands, count, owner, teacher):
    rows = teacher.shape[0]
    places = CORES * cols
    return pl.pallas_call(
        functools.partial(teacher_body, cols, planes),
        in_specs=[SMEM, SMEM, SMEM, SMEM, VMEM],
        out_specs=[ANY] * places,
        out_shape=[struct((planes, rows, rows), jnp.float32)] * places,
        scratch_shapes=[
            pltpu.VMEM((places, planes, rows, rows), jnp.float32),
            pltpu.SemaphoreType.DMA((places,)),
        ],
        compiler_params=params(24),
        cost_estimate=cost(teacher.size, 8 * teacher.size),
    )(me, cands, count, owner, teacher)


def score_body(places, planes, scale, *refs):
    items, users, logs = refs[:planes], refs[planes : planes + places], refs[planes + places : planes + 2 * places]
    weights, stats, all_items, all_users, all_logs, item_sems, user_sems, log_sems = refs[planes + 2 * places :]
    rows = users[0].shape[0]
    load_items = [
        pltpu.make_async_copy(items[i], all_items.at[pl.ds(i * rows, rows)], item_sems.at[i]) for i in range(planes)
    ]
    load_users = [
        pltpu.make_async_copy(users[i], all_users.at[pl.ds(i * rows, rows)], user_sems.at[i]) for i in range(places)
    ]
    load_logs = [pltpu.make_async_copy(logs[i], all_logs.at[i], log_sems.at[i]) for i in range(places)]
    for copy in load_items:
        copy.start()
    for one, other in zip(load_users, load_logs):
        one.start()
        other.start()
    for copy in load_items:
        copy.wait()
    for first in range(0, places, 2):
        for i in (first, first + 1):
            load_users[i].wait()
            load_logs[i].wait()
        pair = pl.ds(first * rows, 2 * rows)
        both = scale * lax.dot_general(
            all_items[...], all_users[pair], (((1,), (1,)), ((), ())), preferred_element_type=jnp.float32
        )
        for j in (0, 1):
            score = both[:, j * rows : (j + 1) * rows]
            log_p = all_logs[first + j].reshape(planes * rows, rows)
            live = log_p > LIVE
            top = jnp.max(jnp.where(live, score, DEAD), axis=0, keepdims=True)
            shifted = score - top
            weight = jnp.where(live, jnp.exp(shifted), 0.0)
            prob = jnp.exp(log_p)
            weights[:, (first + j) * rows : (first + j + 1) * rows] = weight
            stats[0, first + j : first + j + 1, :] = top
            stats[1, first + j : first + j + 1, :] = jnp.sum(weight, axis=0, keepdims=True)
            stats[2, first + j : first + j + 1, :] = jnp.sum(
                jnp.where(live, prob * (log_p - shifted), 0.0), axis=0, keepdims=True
            )
            stats[3, first + j : first + j + 1, :] = jnp.sum(prob, axis=0, keepdims=True)


def scores(scale, items, users, logs):
    planes, places = len(items), len(users)
    rows, width = users[0].shape
    return pl.pallas_call(
        functools.partial(score_body, places, planes, scale),
        in_specs=[ANY] * (planes + 2 * places),
        out_specs=[VMEM, VMEM],
        out_shape=[
            struct((planes * rows, places * rows), jnp.float32),
            struct((4, places, rows), jnp.float32),
        ],
        scratch_shapes=[
            pltpu.VMEM((planes * rows, width), jnp.bfloat16),
            pltpu.VMEM((places * rows, width), jnp.bfloat16),
            pltpu.VMEM((places, planes, rows, rows), jnp.float32),
            pltpu.SemaphoreType.DMA((planes,)),
            pltpu.SemaphoreType.DMA((places,)),
            pltpu.SemaphoreType.DMA((places,)),
        ],
        compiler_params=params(32),
        cost_estimate=cost(2 * planes * places * rows * rows * width, 8 * planes * places * rows * rows),
    )(*items, *users, *logs)


def item_body(places, planes, factor, *refs):
    stats, users, logs = refs[:places], refs[places : 2 * places], refs[2 * places : 3 * places]
    weights, grads, divergence = refs[3 * places : 3 * places + 3]
    parts = refs[3 * places + 3 : 3 * places + 3 + planes]
    all_users, all_logs, user_sems, log_sems = refs[3 * places + 3 + planes :]
    rows = users[0].shape[0]
    load_users = [
        pltpu.make_async_copy(users[i], all_users.at[pl.ds(i * rows, rows)], user_sems.at[i]) for i in range(places)
    ]
    load_logs = [pltpu.make_async_copy(logs[i], all_logs.at[i], log_sems.at[i]) for i in range(places)]
    for copy in load_logs + load_users:
        copy.start()
    for i in range(places):
        tops = [stats[j][0, i ^ j : (i ^ j) + 1, :] for j in range(places)]
        sums = [stats[j][1, i ^ j : (i ^ j) + 1, :] for j in range(places)]
        top = functools.reduce(jnp.maximum, tops)
        norm = functools.reduce(jnp.add, [s * jnp.exp(t - top) for s, t in zip(sums, tops)])
        ratio = jnp.exp(tops[0] - top) / norm
        if i == 0:
            lse = top + jnp.log(norm)
            terms = [stats[j][2, j : j + 1, :] + stats[j][3, j : j + 1, :] * (lse - tops[j]) for j in range(places)]
            divergence[...] = functools.reduce(jnp.add, terms)
        load_logs[i].wait()
        prob = jnp.exp(all_logs[i].reshape(planes * rows, rows))
        lanes = slice(i * rows, (i + 1) * rows)
        grads[:, lanes] = (factor * (weights[:, lanes] * ratio - prob)).astype(jnp.bfloat16)
    for copy in load_users:
        copy.wait()
    for i in range(planes - 1, -1, -1):
        part = jnp.dot(grads[i * rows : (i + 1) * rows], all_users[...], preferred_element_type=jnp.float32)
        parts[i][...] = part.astype(parts[i].dtype)


def item_parts(factor, stats, users, logs, weights):
    places, planes = len(users), logs[0].shape[0]
    rows, width = users[0].shape
    return pl.pallas_call(
        functools.partial(item_body, places, planes, factor),
        in_specs=[VMEM] * places + [ANY] * (2 * places) + [VMEM],
        out_specs=[VMEM] * (2 + planes),
        out_shape=[struct(weights.shape, jnp.bfloat16), struct((1, rows), jnp.float32)]
        + [struct((rows, width), jnp.bfloat16 if i else jnp.float32) for i in range(planes)],
        scratch_shapes=[
            pltpu.VMEM((places * rows, width), jnp.bfloat16),
            pltpu.VMEM((places, planes, rows, rows), jnp.float32),
            pltpu.SemaphoreType.DMA((places,)),
            pltpu.SemaphoreType.DMA((places,)),
        ],
        compiler_params=params(32),
        cost_estimate=cost(2 * planes * places * rows * rows * width, 8 * planes * places * rows * rows),
    )(*stats, *users, *logs, weights)


def user_body(cols, planes, *refs):
    grads, items = refs[0], refs[1 : 1 + planes]
    own, other, all_items, sems = refs[1 + planes :]
    rows = items[0].shape[0]
    loads = [pltpu.make_async_copy(items[i], all_items.at[pl.ds(i * rows, rows)], sems.at[i]) for i in range(planes)]
    for copy in loads:
        copy.start()
    for copy in loads:
        copy.wait()
    half = cols * rows
    for i, out in enumerate((own, other)):
        out[...] = lax.dot_general(
            grads[:, i * half : (i + 1) * half],
            all_items[...],
            (((0,), (0,)), ((), ())),
            preferred_element_type=jnp.float32,
        ).astype(out.dtype)


def user_parts(cols, grads, items):
    planes = len(items)
    rows, width = items[0].shape
    return pl.pallas_call(
        functools.partial(user_body, cols, planes),
        in_specs=[VMEM] + [ANY] * planes,
        out_specs=[VMEM, VMEM],
        out_shape=[struct((cols * rows, width), jnp.float32), struct((cols * rows, width), jnp.bfloat16)],
        scratch_shapes=[pltpu.VMEM((planes * rows, width), jnp.bfloat16), pltpu.SemaphoreType.DMA((planes,))],
        compiler_params=params(32),
        cost_estimate=cost(2 * grads.size * width, 4 * grads.size),
    )(grads, *items)


def shards(
    user_feats, item_feats, user_w_in, user_w_out, item_w_in, item_w_out, teacher, cand_blocks, cand_count, owner_map
):
    rows, width = user_feats.shape
    slots = cand_blocks.shape[1]
    count = lax.axis_size("dp")
    cols = 1 << ((count // CORES).bit_length() - 1) // 2
    planes = count // (CORES * cols)
    assert cols * planes * CORES == count and count & (count - 1) == 0
    scale = 3.0 / math.sqrt(width)
    factor = rows * slots / 4.0 * scale
    me = lax.axis_index("dp")

    def swap(array, apart):
        return lax.ppermute(array, "dp", [(i, i ^ apart) for i in range(count)])

    def plane_apart(place):
        return (place % cols) * CORES + place // cols

    logs = spread_teacher(cols, planes, me.reshape(1).astype(jnp.int32), cand_blocks, cand_count, owner_map, teacher)
    item_feats, *logs = lax.optimization_barrier((item_feats, *logs))
    crossed = [swap(logs[cols + c], 1) for c in range(cols)]
    own_logs = [swap(logs[c], c * CORES) if c else logs[c] for c in range(cols)]
    other_logs = [swap(crossed[c], c * CORES) if c else crossed[c] for c in range(cols)]
    logs = own_logs + other_logs

    item_emb = embed(item_feats, item_w_in, item_w_out)
    user_feats, item_emb = lax.optimization_barrier((user_feats, item_emb))
    items = [item_emb] + [swap(item_emb, z * cols * CORES) for z in range(1, planes)]
    user_emb = embed(user_feats, user_w_in, user_w_out)
    users = [user_emb] + [swap(user_emb, c * CORES) for c in range(1, cols)]
    users = users + [swap(block, 1) for block in users]

    weights, stats = scores(scale, items, users, logs)
    all_stats = [stats] + [swap(stats, plane_apart(j)) for j in range(1, CORES * cols)]
    grads, divergence, *parts = item_parts(factor, all_stats, users, logs, weights)
    sent = [swap(parts[z], z * cols * CORES) for z in range(1, planes)]
    own, other = user_parts(cols, grads, items)
    half = (own + swap(other, 1).astype(jnp.float32)).reshape(cols, rows, width)
    arrived = [swap(half[c].astype(jnp.bfloat16), c * CORES) for c in range(1, cols)]

    def add(first, rest):
        return functools.reduce(jnp.add, [part.astype(jnp.float32) for part in rest], first)

    return (divergence.reshape(rows), add(half[0], arrived), add(parts[0], sent))


def solution(mesh):
    both = ("dp", "tensor")
    placed = (
        P(both, None),
        P(both, None),
        P(None, "tensor"),
        P("tensor", None),
        P(None, "tensor"),
        P("tensor", None),
        P(both, None),
        P(both, None),
        P(both),
        P(),
    )
    return jax.shard_map(
        shards,
        mesh=mesh,
        in_specs=placed,
        out_specs=(P(both), P(both, None), P(both, None)),
        check_vma=False,
    )
```

time: 289 us -> 126 us (0.44)
  waiting for transfers between devices: 205 us -> 47.7 us
  matrix products: 46.2 us -> 0 us
  Pallas kernels: 0 us -> 34.5 us
  starting transfers between devices: 0.26 us -> 34.2 us
  local copies, waits for them, and re-layouts: 18.6 us -> 3.53 us
  between operations: 14.8 us -> 1.41 us
    reduce_scatter x1 -> x0, waiting for transfers between devices: 142 us -> none  [shards(): lax.psum_scatter(outgoing.reshape(dp_count * block_rows, width).astype(jn...]
    all_gather x1 -> x0, waiting for transfers between devices: 62.9 us -> none  [shards(): lax.all_gather(item_emb, 'dp', axis=0, tiled=True)]
    ppermute x0 -> x34, waiting for transfers between devices: none -> 47.7 us  [swap(): return lax.ppermute(array, 'dp', [(i, i ^ apart) for i in range(count)])]
    dot_general x6 -> x0, matrix products: 46.2 us -> none  [the longest x1 15.8 us: shards(): jnp.dot(item_hidden, item_w_out, preferred_element_type=jnp.float32)]
    pallas_call x0 -> x6, Pallas kernels: none -> 34.5 us  [the longest x2 23.4 us: tower(): pl.pallas_call(functools.partial(tower_body, chunks), in_specs=[VMEM, ANY...]
    ppermute x0 -> x34, starting transfers between devices: none -> 34.2 us  [swap(): return lax.ppermute(array, 'dp', [(i, i ^ apart) for i in range(count)])]
    convert_element_type x1 -> x0, local copies, waits for them, and re-layouts: 8.9 us -> none  [shards(): outgoing.reshape(dp_count * block_rows, width).astype(jnp.bfloat16)]
    gather x1 -> x0, local copies, waits for them, and re-layouts: 6.12 us -> none  [shards(): picked = jnp.take(item_table, positions, axis=0)]
  transfers between devices with their start and end apart: 2 -> 34, of which waited for: 2 -> 15; matrix products, arithmetic and copies ran while one was open for 8% -> 1% of each run, Pallas kernels for 0% -> 0%
where the time goes in v1:
time: 126 us; the launch traced here: 124 us
  waiting for transfers between devices  47.7 us (38%)
  Pallas kernels  34.5 us (27%)
  starting transfers between devices  34.2 us (27%)
  local copies, waits for them, and re-layouts  3.53 us (3%)
  other arithmetic  2.41 us (2%)
  between operations  1.41 us (1%)
    ppermute x34, waiting for transfers between devices, swap(): return lax.ppermute(array, 'dp', [(i, i ^ apart) for i in range(count)])  47.7 us
    ppermute x34, starting transfers between devices, swap(): return lax.ppermute(array, 'dp', [(i, i ^ apart) for i in range(count)])  34.2 us
    pallas_call x2, Pallas kernels, tower(): pl.pallas_call(functools.partial(tower_body, chunks), in_specs=[VMEM, ANY...  23.4 us
    pallas_call x1, Pallas kernels, scores(): pl.pallas_call(functools.partial(score_body, places, planes, scale), in_s...  4.7 us
    unnamed x10, local copies, waits for them, and re-layouts  3.48 us
    pallas_call x1, Pallas kernels, item_parts(): pl.pallas_call(functools.partial(item_body, places, planes, factor), in_s...  2.54 us
    pallas_call x1, Pallas kernels, spread_teacher(): pl.pallas_call(functools.partial(teacher_body, cols, planes), in_specs=[S...  2.53 us
  transfers between devices with their start and end apart: 34, of which 15 were waited for; matrix products, arithmetic and copies ran while one was open for 1% of the time, Pallas kernels for 0%

profile of v1, /device:TPU:0, one launch (start us, length us, event | category | flops | bytes accessed | tf_op | source)
XLA Modules:
  0.0 123.8 jit_solution(14959281728995828473)
XLA Ops:
  1.3 1.2 copy-done
  2.5 0.7 copy-done.3
  3.2 0.7 copy-done.4
  3.8 2.5 %shard_map.121 = (f32[4,128,128]{2,1,0:T(8,128)S(1)}, f32[4,128,128]{2,1,0:T(8,128)S(1)}, f32[4,128,128]{2,1,0:T(8,128)S(1)}, f32[4,128,128]{2,1,0:T(8,128)S(1)}...) custom-call(s32[1]{0:T(128)} %bitcast.me, ...), custom_call_target="tpu_custom_call" | custom-call | flops 262144 | bytes 2097152 | tf_op jit(solution)/shard_map/pallas_call | solution.py:122
  6.4 0.0 copy-start.1
  6.4 0.9 copy-done.1
  7.3 11.7 %shard_map.122.refs_0_.refs_1_ = bf16[128,1024]{1,0:T(8,128)(2,1)S(1)} custom-call(bf16[128,1024]{1,0:T(8,128)(2,1)S(1)} %copy-done.1, bf16[1024,8192]{1,0:T(8,128)(2,1)} %w_in.2, bf16[8192,1024]{1,0:T(8,128)(2,1)} %w_out.2), custom_call_target="tpu_custom_call" | custom-call | flops 4294967296 | bytes 33554432 | tf_op jit(solution)/shard_map/pallas_call | solution.py:65
  19.0 11.7 %shard_map.123.refs_4_.refs_8_ = bf16[128,1024]{1,0:T(8,128)(2,1)S(1)} custom-call(bf16[128,1024]{1,0:T(8,128)(2,1)S(1)} %copy-done.2, bf16[1024,8192]{1,0:T(8,128)(2,1)} %w_in.3, bf16[8192,1024]{1,0:T(8,128)(2,1)} %w_out.3), custom_call_target="tpu_custom_call" | custom-call | flops 4294967296 | bytes 33554432 | tf_op jit(solution)/shard_map/pallas_call | solution.py:65
  30.7 0.7 collective-permute-start.6
  31.4 3.2 %collective-permute-start.5 = (bf16[128,1024]{1,0:T(8,128)(2,1)S(1)}, bf16[128,1024]{1,0:T(8,128)(2,1)S(1)}, u32[]{:S(2)}, u32[]{:S(2)}) collective-permute-start(bf16[128,1024]{1,0:T(8,128)(2,1)S(1)} %shard_map.123.refs_4_.refs_8_), channel_id=1, source_target_pairs={{0,6},{1,7},{2,4},{3,5},{4,2},{5,3},{6,0},{7,1},{8,14},{9,15},{10,... | collective-permute-start | bytes 786440 | tf_op jit(solution)/shard_map/ppermute | solution.py:303
  34.6 0.3 collective-permute-start.4
  35.0 0.6 collective-permute-start.3
  35.6 3.9 %collective-permute-start.2 = (bf16[128,1024]{1,0:T(8,128)(2,1)S(1)}, bf16[128,1024]{1,0:T(8,128)(2,1)S(1)}, u32[]{:S(2)}, u32[]{:S(2)}) collective-permute-start(bf16[128,1024]{1,0:T(8,128)(2,1)S(1)} %shard_map.122.refs_0_.refs_1_), channel_id=1, source_target_pairs={{0,24},{1,25},{2,26},{3,27},{4,28},{5,29},{6,30},{7,31},{8,16},{9,... | collective-permute-start | bytes 786440 | tf_op jit(solution)/shard_map/ppermute | solution.py:303
  39.5 0.0 collective-permute-start.1
  39.5 2.3 %collective-permute-done.5.refs_7_.refs_11_ = bf16[128,1024]{1,0:T(8,128)(2,1)S(1)} collective-permute-done((bf16[128,1024]{1,0:T(8,128)(2,1)S(1)}, bf16[128,1024]{1,0:T(8,128)(2,1)S(1)}, u32[]{:S(2)}, u32[]{:S(2)}) %collective-permute-start.5) | collective-permute-done | bytes 262176 | tf_op jit(solution)/shard_map/ppermute | solution.py:303
  41.8 2.0 %collective-permute-start = (bf16[128,1024]{1,0:T(8,128)(2,1)S(1)}, bf16[128,1024]{1,0:T(8,128)(2,1)S(1)}, u32[]{:S(2)}, u32[]{:S(2)}) collective-permute-start(bf16[128,1024]{1,0:T(8,128)(2,1)S(1)} %shard_map.122.refs_0_.refs_1_), channel_id=1, source_target_pairs={{0,8},{1,9},{2,10},{3,11},{4,12},{5,13},{6,14},{7,15},{8,0},{9,1},... | collective-permute-start | bytes 786440 | tf_op jit(solution)/shard_map/ppermute | solution.py:303
  43.8 3.3 %collective-permute-done.4.refs_6_.refs_10_ = bf16[128,1024]{1,0:T(8,128)(2,1)S(1)} collective-permute-done((bf16[128,1024]{1,0:T(8,128)(2,1)S(1)}, bf16[128,1024]{1,0:T(8,128)(2,1)S(1)}, u32[]{:S(2)}, u32[]{:S(2)}) %collective-permute-start.4) | collective-permute-done | bytes 262176 | tf_op jit(solution)/shard_map/ppermute | solution.py:303
  47.2 1.5 %collective-permute-start.10 = (f32[4,128,128]{2,1,0:T(8,128)S(1)}, f32[4,128,128]{2,1,0:T(8,128)S(1)}, u32[]{:S(2)}, u32[]{:S(2)}) collective-permute-start(f32[4,128,128]{2,1,0:T(8,128)S(1)} %get-tuple-element.44), channel_id=1, source_target_pairs={{0,2},{1,3},{2,0},{3,1},{4,6},{5,7},{6,4},{7,5},{8,10},{9,11},{10,... | collective-permute-start | bytes 786440 | tf_op jit(solution)/shard_map/ppermute | solution.py:303
  48.7 1.2 collective-permute-start.11
  49.9 0.8 collective-permute-start.12
  50.7 10.9 %collective-permute-done.1.refs_2_.refs_3_ = bf16[128,1024]{1,0:T(8,128)(2,1)S(1)} collective-permute-done((bf16[128,1024]{1,0:T(8,128)(2,1)S(1)}, bf16[128,1024]{1,0:T(8,128)(2,1)S(1)}, u32[]{:S(2)}, u32[]{:S(2)}) %collective-permute-start.1) | collective-permute-done | bytes 262176 | tf_op jit(solution)/shard_map/ppermute | solution.py:303
  61.5 0.0 collective-permute-done.refs_1_.refs_2_
  61.5 0.5 collective-permute-start.14
  62.1 0.1 collective-permute-start.16
  62.1 0.1 collective-permute-done.11.refs_14_.refs_18_
  62.3 0.3 collective-permute-start.18
  62.6 0.2 collective-permute-start.9
  62.8 0.3 collective-permute-done.13.refs_16_.refs_20_
  63.1 0.1 collective-permute-start.8
  63.2 0.2 collective-permute-done.14
  63.5 0.1 collective-permute-start.7
  63.6 0.2 collective-permute-done.16
  63.8 1.6 %collective-permute-start.15 = (f32[4,128,128]{2,1,0:T(8,128)S(1)}, f32[4,128,128]{2,1,0:T(8,128)S(1)}, u32[]{:S(2)}, u32[]{:S(2)}) collective-permute-start(f32[4,128,128]{2,1,0:T(8,128)S(1)} %collective-permute-done.14), channel_id=1, source_target_pairs={{0,2},{1,3},{2,0},{3,1},{4,6},{5,7},{6,4},{7,5},{8,10},{9,11},{10,... | collective-permute-start | bytes 786440 | tf_op jit(solution)/shard_map/ppermute | solution.py:303
  65.4 1.6 %collective-permute-start.17 = (f32[4,128,128]{2,1,0:T(8,128)S(1)}, f32[4,128,128]{2,1,0:T(8,128)S(1)}, u32[]{:S(2)}, u32[]{:S(2)}) collective-permute-start(f32[4,128,128]{2,1,0:T(8,128)S(1)} %collective-permute-done.16), channel_id=1, source_target_pairs={{0,4},{1,5},{2,6},{3,7},{4,0},{5,1},{6,2},{7,3},{8,12},{9,13},{10,... | collective-permute-start | bytes 786440 | tf_op jit(solution)/shard_map/ppermute | solution.py:303
  67.1 0.3 collective-permute-start.19
  67.3 5.6 %collective-permute-done.15.refs_17_.refs_21_ = f32[4,128,128]{2,1,0:T(8,128)S(1)} collective-permute-done((f32[4,128,128]{2,1,0:T(8,128)S(1)}, f32[4,128,128]{2,1,0:T(8,128)S(1)}, u32[]{:S(2)}, u32[]{:S(2)}) %collective-permute-start.15) | collective-permute-done | bytes 262176 | tf_op jit(solution)/shard_map/ppermute | solution.py:303
  73.0 6.1 %collective-permute-done.17.refs_18_.refs_22_ = f32[4,128,128]{2,1,0:T(8,128)S(1)} collective-permute-done((f32[4,128,128]{2,1,0:T(8,128)S(1)}, f32[4,128,128]{2,1,0:T(8,128)S(1)}, u32[]{:S(2)}, u32[]{:S(2)}) %collective-permute-start.17) | collective-permute-done | bytes 262176 | tf_op jit(solution)/shard_map/ppermute | solution.py:303
  79.1 4.7 %shard_map.124 = (f32[512,1024]{1,0:T(8,128)S(1)}, f32[4,8,128]{2,1,0:T(8,128)S(1)}) custom-call(bf16[128,1024]{1,0:T(8,128)(2,1)S(1)} %shard_map.122.refs_0_.refs_1_, bf16[128,1024]{1,0:T(8,128)(2,1)S(1)} %collective-permute-done.refs_1_.refs_2_, bf16[128,1024]{1,0:T(8,128)(2,1)S(1)} %collective-permute-done.1.refs_2_.refs_3_, ...), custom_call_target="tpu_custom_call" | custom-call | flops 1073741824 | bytes 4194304 | tf_op jit(solution)/shard_map/pallas_call | solution.py:182
  83.8 0.2 collective-permute-start.26
  84.0 2.4 %collective-permute-start.25 = (f32[4,8,128]{2,1,0:T(8,128)S(1)}, f32[4,8,128]{2,1,0:T(8,128)S(1)}, u32[]{:S(2)}, u32[]{:S(2)}) collective-permute-start(f32[4,8,128]{2,1,0:T(8,128)S(1)} %get-tuple-element.51.refs_0_), channel_id=1, source_target_pairs={{0,5},{1,4},{2,7},{3,6},{4,1},{5,0},{6,3},{7,2},{8,13},{9,12},{10,... | collective-permute-start | bytes 49160 | tf_op jit(solution)/shard_map/ppermute | solution.py:303
  86.4 0.3 collective-permute-start.24
  86.7 0.5 collective-permute-start.23
  87.2 1.7 %collective-permute-start.22 = (f32[4,8,128]{2,1,0:T(8,128)S(1)}, f32[4,8,128]{2,1,0:T(8,128)S(1)}, u32[]{:S(2)}, u32[]{:S(2)}) collective-permute-start(f32[4,8,128]{2,1,0:T(8,128)S(1)} %get-tuple-element.51.refs_0_), channel_id=1, source_target_pairs={{0,6},{1,7},{2,4},{3,5},{4,2},{5,3},{6,0},{7,1},{8,14},{9,15},{10,... | collective-permute-start | bytes 49160 | tf_op jit(solution)/shard_map/ppermute | solution.py:303
  88.9 1.1 collective-permute-start.21
  90.0 0.7 collective-permute-start.20
  90.7 1.1 collective-permute-done.22.refs_3_
  91.9 0.8 collective-permute-done.21.refs_2_
  92.7 1.1 collective-permute-done.20.refs_1_
  93.8 2.5 %shard_map.125 = (bf16[512,1024]{1,0:T(8,128)(2,1)S(1)}, f32[1,128]{1,0:T(1,128)}, f32[128,1024]{1,0:T(8,128)S(1)}, bf16[128,1024]{1,0:T(8,128)(2,1)S(1)}, bf16[...) custom-call(f32[4,8,128]{2,1,0:T(8,128)S(1)} %get-tuple-element.51.refs_0_, ...), custom_call_target="tpu_custom_call" | custom-call | flops 1073741824 | bytes 4194304 | tf_op jit(solution)/shard_map/pallas_call | solution.py:239
  96.3 1.4 %shard_map.126 = (f32[512,1024]{1,0:T(8,128)S(1)}, bf16[512,1024]{1,0:T(8,128)(2,1)S(1)}) custom-call(bf16[512,1024]{1,0:T(8,128)(2,1)S(1)} %get-tuple-element.54.refs_0_, bf16[128,1024]{1,0:T(8,128)(2,1)S(1)} %shard_map.122.refs_0_.refs_1_, bf16[128,1024]{1,0:T(8,128)(2,1)S(1)} %collective-permute-done.refs_1_.refs_2_, ...), custom_call_target="tpu_custom_call" | custom-call | flops 1073741824 | bytes 2097152 | tf_op jit(solution)/shard_map/pallas_call | solution.py:278
  97.7 0.1 collective-permute-start.27
  97.8 2.0 %collective-permute-start.31 = (bf16[128,1024]{1,0:T(8,128)(2,1)S(1)}, bf16[128,1024]{1,0:T(8,128)(2,1)S(1)}, u32[]{:S(2)}, u32[]{:S(2)}) collective-permute-start(bf16[128,1024]{1,0:T(8,128)(2,1)S(1)} %get-tuple-element.58), channel_id=1, source_target_pairs={{0,8},{1,9},{2,10},{3,11},{4,12},{5,13},{6,14},{7,15},{8,0},{9,1},... | collective-permute-start | bytes 786440 | tf_op jit(solution)/shard_map/ppermute | solution.py:303
  99.8 1.1 collective-permute-start.32
  100.9 1.4 %collective-permute-start.33 = (bf16[128,1024]{1,0:T(8,128)(2,1)S(1)}, bf16[128,1024]{1,0:T(8,128)(2,1)S(1)}, u32[]{:S(2)}, u32[]{:S(2)}) collective-permute-start(bf16[128,1024]{1,0:T(8,128)(2,1)S(1)} %get-tuple-element.60), channel_id=1, source_target_pairs={{0,24},{1,25},{2,26},{3,27},{4,28},{5,29},{6,30},{7,31},{8,16},{9,... | collective-permute-start | bytes 786440 | tf_op jit(solution)/shard_map/ppermute | solution.py:303
  102.3 0.5 fusion.2
  102.8 0.1 fusion.3
  102.9 1.2 collective-permute-start.28
  104.1 1.5 %collective-permute-start.30 = (bf16[128,1024]{1,0:T(8,128)(2,1)S(1)}, bf16[128,1024]{1,0:T(8,128)(2,1)S(1)}, u32[]{:S(2)}, u32[]{:S(2)}) collective-permute-start(bf16[128,1024]{1,0:T(8,128)(2,1)S(1)} %get-tuple-element.64), channel_id=1, source_target_pairs={{0,6},{1,7},{2,4},{3,5},{4,2},{5,3},{6,0},{7,1},{8,14},{9,15},{10,... | collective-permute-start | bytes 786440 | tf_op jit(solution)/shard_map/ppermute | solution.py:303
  105.5 6.3 %collective-permute-done.31 = bf16[128,1024]{1,0:T(8,128)(2,1)S(1)} collective-permute-done((bf16[128,1024]{1,0:T(8,128)(2,1)S(1)}, bf16[128,1024]{1,0:T(8,128)(2,1)S(1)}, u32[]{:S(2)}, u32[]{:S(2)}) %collective-permute-start.31) | collective-permute-done | bytes 262176 | tf_op jit(solution)/shard_map/ppermute | solution.py:303
  111.8 1.0 collective-permute-start.29
  112.9 8.3 %collective-permute-done.32 = bf16[128,1024]{1,0:T(8,128)(2,1)S(1)} collective-permute-done((bf16[128,1024]{1,0:T(8,128)(2,1)S(1)}, bf16[128,1024]{1,0:T(8,128)(2,1)S(1)}, u32[]{:S(2)}, u32[]{:S(2)}) %collective-permute-start.32) | collective-permute-done | bytes 262176 | tf_op jit(solution)/shard_map/ppermute | solution.py:303
  121.2 0.9 convert_add_fusion.1
  122.1 0.7 collective-permute-done.29
  122.9 0.9 fusion.1
  (24 shorter events, 0.1 us)
Async XLA Ops:
  1.3 1.2 copy-start
  2.5 0.7 copy-start.3
  3.2 0.7 copy-start.4
  6.4 1.0 copy-start.1
  7.3 11.7 %copy-start.2 = (bf16[128,1024]{1,0:T(8,128)(2,1)S(1)}, bf16[128,1024]{1,0:T(8,128)(2,1)}, u32[]{:S(2)}) copy-start(bf16[128,1024]{1,0:T(8,128)(2,1)} %feats.1) | copy-start | bytes 786436
  30.7 8.8 %collective-permute-start.6 = (bf16[128,1024]{1,0:T(8,128)(2,1)S(1)}, bf16[128,1024]{1,0:T(8,128)(2,1)S(1)}, u32[]{:S(2)}, u32[]{:S(2)}) collective-permute-start(bf16[128,1024]{1,0:T(8,128)(2,1)S(1)} %shard_map.123.refs_4_.refs_8_), channel_id=1, source_target_pairs={{0,1},{1,0},{2,3},{3,2},{4,5},{5,4},{6,7},{7,6},{8,9},{9,8},{10,11... | collective-permute-start | bytes 786440 | tf_op jit(solution)/shard_map/ppermute | solution.py:303
  31.4 10.4 %collective-permute-start.5 = (bf16[128,1024]{1,0:T(8,128)(2,1)S(1)}, bf16[128,1024]{1,0:T(8,128)(2,1)S(1)}, u32[]{:S(2)}, u32[]{:S(2)}) collective-permute-start(bf16[128,1024]{1,0:T(8,128)(2,1)S(1)} %shard_map.123.refs_4_.refs_8_), channel_id=1, source_target_pairs={{0,6},{1,7},{2,4},{3,5},{4,2},{5,3},{6,0},{7,1},{8,14},{9,15},{10,... | collective-permute-start | bytes 786440 | tf_op jit(solution)/shard_map/ppermute | solution.py:303
  34.6 12.5 %collective-permute-start.4 = (bf16[128,1024]{1,0:T(8,128)(2,1)S(1)}, bf16[128,1024]{1,0:T(8,128)(2,1)S(1)}, u32[]{:S(2)}, u32[]{:S(2)}) collective-permute-start(bf16[128,1024]{1,0:T(8,128)(2,1)S(1)} %shard_map.123.refs_4_.refs_8_), channel_id=1, source_target_pairs={{0,4},{1,5},{2,6},{3,7},{4,0},{5,1},{6,2},{7,3},{8,12},{9,13},{10,... | collective-permute-start | bytes 786440 | tf_op jit(solution)/shard_map/ppermute | solution.py:303
  35.0 13.7 %collective-permute-start.3 = (bf16[128,1024]{1,0:T(8,128)(2,1)S(1)}, bf16[128,1024]{1,0:T(8,128)(2,1)S(1)}, u32[]{:S(2)}, u32[]{:S(2)}) collective-permute-start(bf16[128,1024]{1,0:T(8,128)(2,1)S(1)} %shard_map.123.refs_4_.refs_8_), channel_id=1, source_target_pairs={{0,2},{1,3},{2,0},{3,1},{4,6},{5,7},{6,4},{7,5},{8,10},{9,11},{10,... | collective-permute-start | bytes 786440 | tf_op jit(solution)/shard_map/ppermute | solution.py:303
  35.6 14.3 %collective-permute-start.2 = (bf16[128,1024]{1,0:T(8,128)(2,1)S(1)}, bf16[128,1024]{1,0:T(8,128)(2,1)S(1)}, u32[]{:S(2)}, u32[]{:S(2)}) collective-permute-start(bf16[128,1024]{1,0:T(8,128)(2,1)S(1)} %shard_map.122.refs_0_.refs_1_), channel_id=1, source_target_pairs={{0,24},{1,25},{2,26},{3,27},{4,28},{5,29},{6,30},{7,31},{8,16},{9,... | collective-permute-start | bytes 786440 | tf_op jit(solution)/shard_map/ppermute | solution.py:303
  39.5 22.1 %collective-permute-start.1 = (bf16[128,1024]{1,0:T(8,128)(2,1)S(1)}, bf16[128,1024]{1,0:T(8,128)(2,1)S(1)}, u32[]{:S(2)}, u32[]{:S(2)}) collective-permute-start(bf16[128,1024]{1,0:T(8,128)(2,1)S(1)} %shard_map.122.refs_0_.refs_1_), channel_id=1, source_target_pairs={{0,16},{1,17},{2,18},{3,19},{4,20},{5,21},{6,22},{7,23},{8,24},{9,... | collective-permute-start | bytes 786440 | tf_op jit(solution)/shard_map/ppermute | solution.py:303
  41.8 19.7 %collective-permute-start = (bf16[128,1024]{1,0:T(8,128)(2,1)S(1)}, bf16[128,1024]{1,0:T(8,128)(2,1)S(1)}, u32[]{:S(2)}, u32[]{:S(2)}) collective-permute-start(bf16[128,1024]{1,0:T(8,128)(2,1)S(1)} %shard_map.122.refs_0_.refs_1_), channel_id=1, source_target_pairs={{0,8},{1,9},{2,10},{3,11},{4,12},{5,13},{6,14},{7,15},{8,0},{9,1},... | collective-permute-start | bytes 786440 | tf_op jit(solution)/shard_map/ppermute | solution.py:303
  47.2 14.9 %collective-permute-start.10 = (f32[4,128,128]{2,1,0:T(8,128)S(1)}, f32[4,128,128]{2,1,0:T(8,128)S(1)}, u32[]{:S(2)}, u32[]{:S(2)}) collective-permute-start(f32[4,128,128]{2,1,0:T(8,128)S(1)} %get-tuple-element.44), channel_id=1, source_target_pairs={{0,2},{1,3},{2,0},{3,1},{4,6},{5,7},{6,4},{7,5},{8,10},{9,11},{10,... | collective-permute-start | bytes 786440 | tf_op jit(solution)/shard_map/ppermute | solution.py:303
  48.7 13.6 %collective-permute-start.11 = (f32[4,128,128]{2,1,0:T(8,128)S(1)}, f32[4,128,128]{2,1,0:T(8,128)S(1)}, u32[]{:S(2)}, u32[]{:S(2)}) collective-permute-start(f32[4,128,128]{2,1,0:T(8,128)S(1)} %get-tuple-element.45), channel_id=1, source_target_pairs={{0,4},{1,5},{2,6},{3,7},{4,0},{5,1},{6,2},{7,3},{8,12},{9,13},{10,... | collective-permute-start | bytes 786440 | tf_op jit(solution)/shard_map/ppermute | solution.py:303
  49.9 12.7 %collective-permute-start.12 = (f32[4,128,128]{2,1,0:T(8,128)S(1)}, f32[4,128,128]{2,1,0:T(8,128)S(1)}, u32[]{:S(2)}, u32[]{:S(2)}) collective-permute-start(f32[4,128,128]{2,1,0:T(8,128)S(1)} %get-tuple-element.46), channel_id=1, source_target_pairs={{0,6},{1,7},{2,4},{3,5},{4,2},{5,3},{6,0},{7,1},{8,14},{9,15},{10,... | collective-permute-start | bytes 786440 | tf_op jit(solution)/shard_map/ppermute | solution.py:303
  61.5 1.5 %collective-permute-start.13 = (f32[4,128,128]{2,1,0:T(8,128)S(1)}, f32[4,128,128]{2,1,0:T(8,128)S(1)}, u32[]{:S(2)}, u32[]{:S(2)}) collective-permute-start(f32[4,128,128]{2,1,0:T(8,128)S(1)} %get-tuple-element.47), channel_id=1, source_target_pairs={{0,1},{1,0},{2,3},{3,2},{4,5},{5,4},{6,7},{7,6},{8,9},{9,8},{10,11... | collective-permute-start | bytes 786440 | tf_op jit(solution)/shard_map/ppermute | solution.py:303
  61.5 1.9 %collective-permute-start.14 = (f32[4,128,128]{2,1,0:T(8,128)S(1)}, f32[4,128,128]{2,1,0:T(8,128)S(1)}, u32[]{:S(2)}, u32[]{:S(2)}) collective-permute-start(f32[4,128,128]{2,1,0:T(8,128)S(1)} %get-tuple-element.48), channel_id=1, source_target_pairs={{0,1},{1,0},{2,3},{3,2},{4,5},{5,4},{6,7},{7,6},{8,9},{9,8},{10,11... | collective-permute-start | bytes 786440 | tf_op jit(solution)/shard_map/ppermute | solution.py:303
  62.1 1.8 %collective-permute-start.16 = (f32[4,128,128]{2,1,0:T(8,128)S(1)}, f32[4,128,128]{2,1,0:T(8,128)S(1)}, u32[]{:S(2)}, u32[]{:S(2)}) collective-permute-start(f32[4,128,128]{2,1,0:T(8,128)S(1)} %get-tuple-element.49), channel_id=1, source_target_pairs={{0,1},{1,0},{2,3},{3,2},{4,5},{5,4},{6,7},{7,6},{8,9},{9,8},{10,11... | collective-permute-start | bytes 786440 | tf_op jit(solution)/shard_map/ppermute | solution.py:303
  62.3 3.2 %collective-permute-start.18 = (f32[4,128,128]{2,1,0:T(8,128)S(1)}, f32[4,128,128]{2,1,0:T(8,128)S(1)}, u32[]{:S(2)}, u32[]{:S(2)}) collective-permute-start(f32[4,128,128]{2,1,0:T(8,128)S(1)} %get-tuple-element.50), channel_id=1, source_target_pairs={{0,1},{1,0},{2,3},{3,2},{4,5},{5,4},{6,7},{7,6},{8,9},{9,8},{10,11... | collective-permute-start | bytes 786440 | tf_op jit(solution)/shard_map/ppermute | solution.py:303
  62.6 4.5 %collective-permute-start.9 = (bf16[128,1024]{1,0:T(8,128)(2,1)S(1)}, bf16[128,1024]{1,0:T(8,128)(2,1)S(1)}, u32[]{:S(2)}, u32[]{:S(2)}) collective-permute-start(bf16[128,1024]{1,0:T(8,128)(2,1)S(1)} %collective-permute-done.5.refs_7_.refs_11_), channel_id=1, source_target_pairs={{0,1},{1,0},{2,3},{3,2},{4,5},{5,4},{6,7},{7,6},{8,9},{9,8},{10,11... | collective-permute-start | bytes 786440 | tf_op jit(solution)/shard_map/ppermute | solution.py:303
  63.1 4.2 %collective-permute-start.8 = (bf16[128,1024]{1,0:T(8,128)(2,1)S(1)}, bf16[128,1024]{1,0:T(8,128)(2,1)S(1)}, u32[]{:S(2)}, u32[]{:S(2)}) collective-permute-start(bf16[128,1024]{1,0:T(8,128)(2,1)S(1)} %collective-permute-done.4.refs_6_.refs_10_), channel_id=1, source_target_pairs={{0,1},{1,0},{2,3},{3,2},{4,5},{5,4},{6,7},{7,6},{8,9},{9,8},{10,11... | collective-permute-start | bytes 786440 | tf_op jit(solution)/shard_map/ppermute | solution.py:303
  63.5 3.9 %collective-permute-start.7 = (bf16[128,1024]{1,0:T(8,128)(2,1)S(1)}, bf16[128,1024]{1,0:T(8,128)(2,1)S(1)}, u32[]{:S(2)}, u32[]{:S(2)}) collective-permute-start(bf16[128,1024]{1,0:T(8,128)(2,1)S(1)} %collective-permute-done.3.refs_5_.refs_9_), channel_id=1, source_target_pairs={{0,1},{1,0},{2,3},{3,2},{4,5},{5,4},{6,7},{7,6},{8,9},{9,8},{10,11... | collective-permute-start | bytes 786440 | tf_op jit(solution)/shard_map/ppermute | solution.py:303
  63.8 9.2 %collective-permute-start.15 = (f32[4,128,128]{2,1,0:T(8,128)S(1)}, f32[4,128,128]{2,1,0:T(8,128)S(1)}, u32[]{:S(2)}, u32[]{:S(2)}) collective-permute-start(f32[4,128,128]{2,1,0:T(8,128)S(1)} %collective-permute-done.14), channel_id=1, source_target_pairs={{0,2},{1,3},{2,0},{3,1},{4,6},{5,7},{6,4},{7,5},{8,10},{9,11},{10,... | collective-permute-start | bytes 786440 | tf_op jit(solution)/shard_map/ppermute | solution.py:303
  65.4 13.7 %collective-permute-start.17 = (f32[4,128,128]{2,1,0:T(8,128)S(1)}, f32[4,128,128]{2,1,0:T(8,128)S(1)}, u32[]{:S(2)}, u32[]{:S(2)}) collective-permute-start(f32[4,128,128]{2,1,0:T(8,128)S(1)} %collective-permute-done.16), channel_id=1, source_target_pairs={{0,4},{1,5},{2,6},{3,7},{4,0},{5,1},{6,2},{7,3},{8,12},{9,13},{10,... | collective-permute-start | bytes 786440 | tf_op jit(solution)/shard_map/ppermute | solution.py:303
  67.1 12.1 %collective-permute-start.19 = (f32[4,128,128]{2,1,0:T(8,128)S(1)}, f32[4,128,128]{2,1,0:T(8,128)S(1)}, u32[]{:S(2)}, u32[]{:S(2)}) collective-permute-start(f32[4,128,128]{2,1,0:T(8,128)S(1)} %collective-permute-done.18), channel_id=1, source_target_pairs={{0,6},{1,7},{2,4},{3,5},{4,2},{5,3},{6,0},{7,1},{8,14},{9,15},{10,... | collective-permute-start | bytes 786440 | tf_op jit(solution)/shard_map/ppermute | solution.py:303
  83.8 5.1 %collective-permute-start.26 = (f32[4,8,128]{2,1,0:T(8,128)S(1)}, f32[4,8,128]{2,1,0:T(8,128)S(1)}, u32[]{:S(2)}, u32[]{:S(2)}) collective-permute-start(f32[4,8,128]{2,1,0:T(8,128)S(1)} %get-tuple-element.51.refs_0_), channel_id=1, source_target_pairs={{0,7},{1,6},{2,5},{3,4},{4,3},{5,2},{6,1},{7,0},{8,15},{9,14},{10,... | collective-permute-start | bytes 49160 | tf_op jit(solution)/shard_map/ppermute | solution.py:303
  84.0 6.0 %collective-permute-start.25 = (f32[4,8,128]{2,1,0:T(8,128)S(1)}, f32[4,8,128]{2,1,0:T(8,128)S(1)}, u32[]{:S(2)}, u32[]{:S(2)}) collective-permute-start(f32[4,8,128]{2,1,0:T(8,128)S(1)} %get-tuple-element.51.refs_0_), channel_id=1, source_target_pairs={{0,5},{1,4},{2,7},{3,6},{4,1},{5,0},{6,3},{7,2},{8,13},{9,12},{10,... | collective-permute-start | bytes 49160 | tf_op jit(solution)/shard_map/ppermute | solution.py:303
  86.4 4.3 %collective-permute-start.24 = (f32[4,8,128]{2,1,0:T(8,128)S(1)}, f32[4,8,128]{2,1,0:T(8,128)S(1)}, u32[]{:S(2)}, u32[]{:S(2)}) collective-permute-start(f32[4,8,128]{2,1,0:T(8,128)S(1)} %get-tuple-element.51.refs_0_), channel_id=1, source_target_pairs={{0,3},{1,2},{2,1},{3,0},{4,7},{5,6},{6,5},{7,4},{8,11},{9,10},{10,... | collective-permute-start | bytes 49160 | tf_op jit(solution)/shard_map/ppermute | solution.py:303
  86.7 4.0 %collective-permute-start.23 = (f32[4,8,128]{2,1,0:T(8,128)S(1)}, f32[4,8,128]{2,1,0:T(8,128)S(1)}, u32[]{:S(2)}, u32[]{:S(2)}) collective-permute-start(f32[4,8,128]{2,1,0:T(8,128)S(1)} %get-tuple-element.51.refs_0_), channel_id=1, source_target_pairs={{0,1},{1,0},{2,3},{3,2},{4,5},{5,4},{6,7},{7,6},{8,9},{9,8},{10,11... | collective-permute-start | bytes 49160 | tf_op jit(solution)/shard_map/ppermute | solution.py:303
  87.2 4.6 %collective-permute-start.22 = (f32[4,8,128]{2,1,0:T(8,128)S(1)}, f32[4,8,128]{2,1,0:T(8,128)S(1)}, u32[]{:S(2)}, u32[]{:S(2)}) collective-permute-start(f32[4,8,128]{2,1,0:T(8,128)S(1)} %get-tuple-element.51.refs_0_), channel_id=1, source_target_pairs={{0,6},{1,7},{2,4},{3,5},{4,2},{5,3},{6,0},{7,1},{8,14},{9,15},{10,... | collective-permute-start | bytes 49160 | tf_op jit(solution)/shard_map/ppermute | solution.py:303
  88.9 3.7 %collective-permute-start.21 = (f32[4,8,128]{2,1,0:T(8,128)S(1)}, f32[4,8,128]{2,1,0:T(8,128)S(1)}, u32[]{:S(2)}, u32[]{:S(2)}) collective-permute-start(f32[4,8,128]{2,1,0:T(8,128)S(1)} %get-tuple-element.51.refs_0_), channel_id=1, source_target_pairs={{0,4},{1,5},{2,6},{3,7},{4,0},{5,1},{6,2},{7,3},{8,12},{9,13},{10,... | collective-permute-start | bytes 49160 | tf_op jit(solution)/shard_map/ppermute | solution.py:303
  90.0 3.7 %collective-permute-start.20 = (f32[4,8,128]{2,1,0:T(8,128)S(1)}, f32[4,8,128]{2,1,0:T(8,128)S(1)}, u32[]{:S(2)}, u32[]{:S(2)}) collective-permute-start(f32[4,8,128]{2,1,0:T(8,128)S(1)} %get-tuple-element.51.refs_0_), channel_id=1, source_target_pairs={{0,2},{1,3},{2,0},{3,1},{4,6},{5,7},{6,4},{7,5},{8,10},{9,11},{10,... | collective-permute-start | bytes 49160 | tf_op jit(solution)/shard_map/ppermute | solution.py:303
  97.7 4.5 %collective-permute-start.27 = (bf16[512,1024]{1,0:T(8,128)(2,1)S(1)}, bf16[512,1024]{1,0:T(8,128)(2,1)S(1)}, u32[]{:S(2)}, u32[]{:S(2)}) collective-permute-start(bf16[512,1024]{1,0:T(8,128)(2,1)S(1)} %get-tuple-element.56), channel_id=1, source_target_pairs={{0,1},{1,0},{2,3},{3,2},{4,5},{5,4},{6,7},{7,6},{8,9},{9,8},{10,11... | collective-permute-start | bytes 3145736 | tf_op jit(solution)/shard_map/ppermute | solution.py:303
  97.8 14.0 %collective-permute-start.31 = (bf16[128,1024]{1,0:T(8,128)(2,1)S(1)}, bf16[128,1024]{1,0:T(8,128)(2,1)S(1)}, u32[]{:S(2)}, u32[]{:S(2)}) collective-permute-start(bf16[128,1024]{1,0:T(8,128)(2,1)S(1)} %get-tuple-element.58), channel_id=1, source_target_pairs={{0,8},{1,9},{2,10},{3,11},{4,12},{5,13},{6,14},{7,15},{8,0},{9,1},... | collective-permute-start | bytes 786440 | tf_op jit(solution)/shard_map/ppermute | solution.py:303
  99.8 21.3 %collective-permute-start.32 = (bf16[128,1024]{1,0:T(8,128)(2,1)S(1)}, bf16[128,1024]{1,0:T(8,128)(2,1)S(1)}, u32[]{:S(2)}, u32[]{:S(2)}) collective-permute-start(bf16[128,1024]{1,0:T(8,128)(2,1)S(1)} %get-tuple-element.59), channel_id=1, source_target_pairs={{0,16},{1,17},{2,18},{3,19},{4,20},{5,21},{6,22},{7,23},{8,24},{9,... | collective-permute-start | bytes 786440 | tf_op jit(solution)/shard_map/ppermute | solution.py:303
  100.9 20.3 %collective-permute-start.33 = (bf16[128,1024]{1,0:T(8,128)(2,1)S(1)}, bf16[128,1024]{1,0:T(8,128)(2,1)S(1)}, u32[]{:S(2)}, u32[]{:S(2)}) collective-permute-start(bf16[128,1024]{1,0:T(8,128)(2,1)S(1)} %get-tuple-element.60), channel_id=1, source_target_pairs={{0,24},{1,25},{2,26},{3,27},{4,28},{5,29},{6,30},{7,31},{8,16},{9,... | collective-permute-start | bytes 786440 | tf_op jit(solution)/shard_map/ppermute | solution.py:303
  102.9 19.2 %collective-permute-start.28 = (bf16[128,1024]{1,0:T(8,128)(2,1)S(1)}, bf16[128,1024]{1,0:T(8,128)(2,1)S(1)}, u32[]{:S(2)}, u32[]{:S(2)}) collective-permute-start(bf16[128,1024]{1,0:T(8,128)(2,1)S(1)} %get-tuple-element.63), channel_id=1, source_target_pairs={{0,2},{1,3},{2,0},{3,1},{4,6},{5,7},{6,4},{7,5},{8,10},{9,11},{10,... | collective-permute-start | bytes 786440 | tf_op jit(solution)/shard_map/ppermute | solution.py:303
  104.1 18.0 %collective-permute-start.30 = (bf16[128,1024]{1,0:T(8,128)(2,1)S(1)}, bf16[128,1024]{1,0:T(8,128)(2,1)S(1)}, u32[]{:S(2)}, u32[]{:S(2)}) collective-permute-start(bf16[128,1024]{1,0:T(8,128)(2,1)S(1)} %get-tuple-element.64), channel_id=1, source_target_pairs={{0,6},{1,7},{2,4},{3,5},{4,2},{5,3},{6,0},{7,1},{8,14},{9,15},{10,... | collective-permute-start | bytes 786440 | tf_op jit(solution)/shard_map/ppermute | solution.py:303
  111.8 11.0 %collective-permute-start.29 = (bf16[128,1024]{1,0:T(8,128)(2,1)S(1)}, bf16[128,1024]{1,0:T(8,128)(2,1)S(1)}, u32[]{:S(2)}, u32[]{:S(2)}) collective-permute-start(bf16[128,1024]{1,0:T(8,128)(2,1)S(1)} %get-tuple-element.65), channel_id=1, source_target_pairs={{0,4},{1,5},{2,6},{3,7},{4,0},{5,1},{6,2},{7,3},{8,12},{9,13},{10,... | collective-permute-start | bytes 786440 | tf_op jit(solution)/shard_map/ppermute | solution.py:303

commit v2 on v1

v2 whole, which is shorter than its diff:
```python
import functools
import math

import jax
import jax.numpy as jnp
from jax import lax
from jax.experimental import pallas as pl
from jax.experimental.pallas import tpu as pltpu
from jax.sharding import PartitionSpec as P

CORES = 2
DEAD = -1e30
LIVE = -1e29
MIB = 1 << 20
ANY = pl.BlockSpec(memory_space=pl.ANY)
VMEM = pl.BlockSpec(memory_space=pltpu.VMEM)
SMEM = pl.BlockSpec(memory_space=pltpu.SMEM)


def struct(shape, dtype):
    return jax.ShapeDtypeStruct(shape, dtype)


def params(mib):
    return pltpu.CompilerParams(vmem_limit_bytes=mib * MIB)


def cost(flops, moved):
    return pl.CostEstimate(flops=int(flops), bytes_accessed=int(moved), transcendentals=0)


def tower_body(chunks, feats, w_in, w_out, *refs):
    out, held_in, held_out, total, sem_in, sem_out = refs[-6:]
    step = w_in.shape[1] // chunks

    def copies(i):
        part = pl.ds(pl.multiple_of(i * step, step), step)
        return (
            pltpu.make_async_copy(w_in.at[:, part], held_in.at[:, part], sem_in.at[i]),
            pltpu.make_async_copy(w_out.at[part], held_out.at[part], sem_out.at[i]),
        )

    for i in range(chunks):
        for copy in copies(i):
            copy.start()
    total[...] = jnp.zeros_like(total)

    def one(i, carry):
        first, second = copies(i)
        part = pl.ds(pl.multiple_of(i * step, step), step)
        first.wait()
        hidden = jnp.dot(feats[...], held_in[:, part], preferred_element_type=jnp.float32)
        hidden = jnp.maximum(hidden, 0.0).astype(jnp.bfloat16)
        second.wait()
        total[...] += jnp.dot(hidden, held_out[part], preferred_element_type=jnp.float32)
        return carry

    lax.fori_loop(0, chunks, one, 0)
    out[...] = total[...].astype(out.dtype)


def tower(feats, w_in, w_out, dtype, after):
    rows, width = feats.shape
    hidden = w_in.shape[1]
    chunks = max(1, hidden // 512)
    return pl.pallas_call(
        functools.partial(tower_body, chunks),
        in_specs=[VMEM, ANY, ANY] + [ANY] * len(after),
        out_specs=VMEM,
        out_shape=struct((rows, width), dtype),
        scratch_shapes=[
            pltpu.VMEM(w_in.shape, w_in.dtype),
            pltpu.VMEM(w_out.shape, w_out.dtype),
            pltpu.VMEM((rows, width), jnp.float32),
            pltpu.SemaphoreType.DMA((chunks,)),
            pltpu.SemaphoreType.DMA((chunks,)),
        ],
        compiler_params=params(52),
        cost_estimate=cost(1, 1),
    )(feats, w_in, w_out, *after)


def embed(feats, w_in, w_out, after):
    if lax.axis_size("tensor") == 1:
        return tower(feats, w_in, w_out, jnp.bfloat16, after)
    feats = lax.all_gather(feats, "tensor", axis=0, tiled=True)
    partial = tower(feats, w_in, w_out, jnp.float32, after)
    return lax.psum_scatter(partial, "tensor", scatter_dimension=0, tiled=True).astype(jnp.bfloat16)


def teacher_body(cols, planes, me, cands, count, owner, teacher, *refs):
    outs, dense, sems = refs[:cols], refs[cols], refs[cols + 1]
    rows = teacher.shape[0]
    slots = cands.shape[1]
    live = count[0]
    logits = teacher[...]
    usable = lax.broadcasted_iota(jnp.int32, logits.shape, 1) < live * rows
    shifted = logits - jnp.max(jnp.where(usable, logits, -jnp.inf), axis=1, keepdims=True)
    norm = jnp.sum(jnp.where(usable, jnp.exp(shifted), 0.0), axis=1, keepdims=True)
    log_p = shifted - jnp.log(norm)
    dense[...] = jnp.full(dense.shape, DEAD, jnp.float32)
    for k in range(slots):

        @pl.when(k < live)
        def _():
            apart = owner[cands[0, k]] ^ me[0]
            inside = apart % (CORES * cols)
            place = (inside % CORES) * planes + apart // (CORES * cols)
            dense[inside // CORES, place] = log_p[:, k * rows : (k + 1) * rows].T

    copies = [pltpu.make_async_copy(dense.at[i], outs[i], sems.at[i]) for i in range(cols)]
    for copy in copies:
        copy.start()
    for copy in copies:
        copy.wait()


def spread_teacher(cols, planes, me, cands, count, owner, teacher):
    rows = teacher.shape[0]
    places = CORES * planes
    return pl.pallas_call(
        functools.partial(teacher_body, cols, planes),
        in_specs=[SMEM, SMEM, SMEM, SMEM, VMEM],
        out_specs=[ANY] * cols,
        out_shape=[struct((places, rows, rows), jnp.float32)] * cols,
        scratch_shapes=[
            pltpu.VMEM((cols, places, rows, rows), jnp.float32),
            pltpu.SemaphoreType.DMA((cols,)),
        ],
        compiler_params=params(24),
        cost_estimate=cost(teacher.size, 8 * teacher.size),
    )(me, cands, count, owner, teacher)


def loads_of(sources, target, sems):
    rows = sources[0].shape[0]
    return [
        pltpu.make_async_copy(source, target.at[pl.ds(i * rows, rows)], sems.at[i]) for i, source in enumerate(sources)
    ]


def score_body(cols, places, scale, *refs):
    users, items, logs = refs[:cols], refs[cols : cols + places], refs[cols + places : 2 * cols + places]
    weights, stats, all_users, all_items, all_logs, user_sems, item_sems, log_sems = refs[2 * cols + places :]
    rows = users[0].shape[0]
    load_users = loads_of(users, all_users, user_sems)
    load_items = loads_of(items, all_items, item_sems)
    load_logs = loads_of(logs, all_logs, log_sems)
    for copy in load_items + load_users + load_logs:
        copy.start()
    for copy in load_items:
        copy.wait()
    step = 2 if cols % 2 == 0 else 1
    for first in range(0, cols, step):
        for i in range(first, first + step):
            load_users[i].wait()
        both = scale * lax.dot_general(
            all_items[...],
            all_users[first * rows : (first + step) * rows],
            (((1,), (1,)), ((), ())),
            preferred_element_type=jnp.float32,
        )
        for j in range(step):
            i = first + j
            load_logs[i].wait()
            score = both[:, j * rows : (j + 1) * rows]
            log_p = all_logs[i * places : (i + 1) * places].reshape(places * rows, rows)
            live = log_p > LIVE
            top = jnp.max(jnp.where(live, score, DEAD), axis=0, keepdims=True)
            shifted = score - top
            weight = jnp.where(live, jnp.exp(shifted), 0.0)
            prob = jnp.exp(log_p)
            weights[:, i * rows : (i + 1) * rows] = weight
            stats[0, i : i + 1, :] = top
            stats[1, i : i + 1, :] = jnp.sum(weight, axis=0, keepdims=True)
            stats[2, i : i + 1, :] = jnp.sum(jnp.where(live, prob * (log_p - shifted), 0.0), axis=0, keepdims=True)
            stats[3, i : i + 1, :] = jnp.sum(prob, axis=0, keepdims=True)


def scores(scale, users, items, logs):
    cols, places = len(users), len(items)
    rows, width = users[0].shape
    return pl.pallas_call(
        functools.partial(score_body, cols, places, scale),
        in_specs=[ANY] * (2 * cols + places),
        out_specs=[VMEM, VMEM],
        out_shape=[
            struct((places * rows, cols * rows), jnp.float32),
            struct((4, cols, rows), jnp.float32),
        ],
        scratch_shapes=[
            pltpu.VMEM((cols * rows, width), jnp.bfloat16),
            pltpu.VMEM((places * rows, width), jnp.bfloat16),
            pltpu.VMEM((cols * places, rows, rows), jnp.float32),
            pltpu.SemaphoreType.DMA((cols,)),
            pltpu.SemaphoreType.DMA((places,)),
            pltpu.SemaphoreType.DMA((cols,)),
        ],
        compiler_params=params(32),
        cost_estimate=cost(2 * cols * places * rows * rows * width, 8 * cols * places * rows * rows),
    )(*users, *items, *logs)


def far_body(cols, places, factor, *refs):
    stats, users, logs = refs[:cols], refs[cols : 2 * cols], refs[2 * cols : 3 * cols]
    weights, grads, divergence, far = refs[3 * cols : 3 * cols + 4]
    all_users, all_logs, user_sems, log_sems = refs[3 * cols + 4 :]
    rows = users[0].shape[0]
    load_users = loads_of(users, all_users, user_sems)
    load_logs = loads_of(logs, all_logs, log_sems)
    for copy in load_logs + load_users:
        copy.start()
    for i in range(cols):
        tops = [stats[j][0, i ^ j : (i ^ j) + 1, :] for j in range(cols)]
        sums = [stats[j][1, i ^ j : (i ^ j) + 1, :] for j in range(cols)]
        top = functools.reduce(jnp.maximum, tops)
        norm = functools.reduce(jnp.add, [s * jnp.exp(t - top) for s, t in zip(sums, tops)])
        ratio = jnp.exp(tops[0] - top) / norm
        if i == 0:
            lse = top + jnp.log(norm)
            terms = [stats[j][2, j : j + 1, :] + stats[j][3, j : j + 1, :] * (lse - tops[j]) for j in range(cols)]
            divergence[...] = functools.reduce(jnp.add, terms)
        load_logs[i].wait()
        prob = jnp.exp(all_logs[i * places : (i + 1) * places].reshape(places * rows, rows))
        lanes = slice(i * rows, (i + 1) * rows)
        grads[:, lanes] = (factor * (weights[:, lanes] * ratio - prob)).astype(jnp.bfloat16)
    for copy in load_users:
        copy.wait()
    half = places * rows // CORES
    far[...] = jnp.dot(grads[half:], all_users[...], preferred_element_type=jnp.float32).astype(far.dtype)


def far_parts(factor, stats, users, logs, weights):
    cols, places = len(users), logs[0].shape[0]
    rows, width = users[0].shape
    return pl.pallas_call(
        functools.partial(far_body, cols, places, factor),
        in_specs=[VMEM] * cols + [ANY] * (2 * cols) + [VMEM],
        out_specs=[VMEM] * 3,
        out_shape=[
            struct(weights.shape, jnp.bfloat16),
            struct((1, rows), jnp.float32),
            struct((places * rows // CORES, width), jnp.bfloat16),
        ],
        scratch_shapes=[
            pltpu.VMEM((cols * rows, width), jnp.bfloat16),
            pltpu.VMEM((cols * places, rows, rows), jnp.float32),
            pltpu.SemaphoreType.DMA((cols,)),
            pltpu.SemaphoreType.DMA((cols,)),
        ],
        compiler_params=params(32),
        cost_estimate=cost(cols * places * rows * rows * width, 8 * cols * places * rows * rows),
    )(*stats, *users, *logs, weights)


def near_body(cols, places, *refs):
    grads, users, items = refs[0], refs[1 : 1 + cols], refs[1 + cols : 1 + cols + places]
    near = refs[1 + cols + places]
    parts = refs[2 + cols + places : 2 + 2 * cols + places]
    all_users, all_items, user_sems, item_sems = refs[2 + 2 * cols + places :]
    rows = users[0].shape[0]
    load_users = loads_of(users, all_users, user_sems)
    load_items = loads_of(items, all_items, item_sems)
    for copy in load_users + load_items:
        copy.start()
    for copy in load_users:
        copy.wait()
    half = places * rows // CORES
    near[...] = jnp.dot(grads[:half], all_users[...], preferred_element_type=jnp.float32)
    for copy in load_items:
        copy.wait()
    for i in range(cols):
        part = lax.dot_general(
            grads[:, i * rows : (i + 1) * rows],
            all_items[...],
            (((0,), (0,)), ((), ())),
            preferred_element_type=jnp.float32,
        )
        parts[i][...] = part.astype(parts[i].dtype)


def near_parts(grads, users, items):
    cols, places = len(users), len(items)
    rows, width = users[0].shape
    return pl.pallas_call(
        functools.partial(near_body, cols, places),
        in_specs=[VMEM] + [ANY] * (cols + places),
        out_specs=[VMEM] * (1 + cols),
        out_shape=[struct((places * rows // CORES, width), jnp.float32)]
        + [struct((rows, width), jnp.bfloat16 if i else jnp.float32) for i in range(cols)],
        scratch_shapes=[
            pltpu.VMEM((cols * rows, width), jnp.bfloat16),
            pltpu.VMEM((places * rows, width), jnp.bfloat16),
            pltpu.SemaphoreType.DMA((cols,)),
            pltpu.SemaphoreType.DMA((places,)),
        ],
        compiler_params=params(32),
        cost_estimate=cost(3 * cols * places * rows * rows * width, 8 * cols * places * rows * rows),
    )(grads, *users, *items)


def join_body(planes, near, far, *outs):
    rows = outs[0].shape[0]
    for i in range(planes - 1, -1, -1):
        part = slice(i * rows, (i + 1) * rows)
        outs[i][...] = (near[part] + far[part].astype(jnp.float32)).astype(outs[i].dtype)


def join(planes, near, far):
    rows, width = near.shape[0] // planes, near.shape[1]
    return pl.pallas_call(
        functools.partial(join_body, planes),
        in_specs=[VMEM, VMEM],
        out_specs=[VMEM] * planes,
        out_shape=[struct((rows, width), jnp.bfloat16 if i else jnp.float32) for i in range(planes)],
        compiler_params=params(24),
        cost_estimate=cost(near.size, 8 * near.size),
    )(near, far)


def shards(
    user_feats, item_feats, user_w_in, user_w_out, item_w_in, item_w_out, teacher, cand_blocks, cand_count, owner_map
):
    rows, width = user_feats.shape
    slots = cand_blocks.shape[1]
    count = lax.axis_size("dp")
    cols = 1 << ((count // CORES).bit_length() - 1) // 2
    planes = count // (CORES * cols)
    assert cols * planes * CORES == count and count & (count - 1) == 0
    scale = 3.0 / math.sqrt(width)
    factor = rows * slots / 4.0 * scale
    me = lax.axis_index("dp").reshape(1).astype(jnp.int32)

    def swap(array, apart):
        return lax.ppermute(array, "dp", [(i, i ^ apart) for i in range(count)])

    def over_columns(own):
        return [swap(own, c * CORES) for c in range(1, cols)]

    logs = spread_teacher(cols, planes, me, cand_blocks, cand_count, owner_map, teacher)
    first, *rest = logs
    logs = [first] + [swap(part, (c + 1) * CORES) for c, part in enumerate(rest)]

    item_emb = embed(item_feats, item_w_in, item_w_out, [first])
    wide = planes // 2
    crossed = [swap(item_emb, z * cols * CORES) for z in range(wide, planes if planes > 1 else 0, max(wide, 1))]
    nearby = [swap(item_emb, z * cols * CORES) for z in range(1, wide)]
    user_emb = embed(user_feats, user_w_in, user_w_out, [item_emb])
    user_emb, item_emb, logs, crossed, nearby = lax.optimization_barrier((user_emb, item_emb, logs, crossed, nearby))
    users = [user_emb] + over_columns(user_emb)
    items = [item_emb] + nearby + crossed + [swap(block, z * cols * CORES) for block in crossed for z in range(1, wide)]
    items = items + [swap(block, 1) for block in items]

    weights, stats = scores(scale, users, items, logs)
    grads, divergence, far = far_parts(factor, [stats] + over_columns(stats), users, logs, weights)
    far = swap(far, 1)
    near, own, *others = near_parts(grads, users, items)
    arrived = [swap(part, (c + 1) * CORES) for c, part in enumerate(others)]
    parts = join(planes, near, far)
    sent = [swap(parts[z], z * cols * CORES) for z in range(planes - 1, 0, -1)]

    def add(start, parts):
        return functools.reduce(jnp.add, [part.astype(jnp.float32) for part in parts], start)

    return (divergence.reshape(rows), add(own, arrived), add(parts[0], sent))


def solution(mesh):
    both = ("dp", "tensor")
    placed = (
        P(both, None),
        P(both, None),
        P(None, "tensor"),
        P("tensor", None),
        P(None, "tensor"),
        P("tensor", None),
        P(both, None),
        P(both, None),
        P(both),
        P(),
    )
    return jax.shard_map(
        shards,
        mesh=mesh,
        in_specs=placed,
        out_specs=(P(both), P(both, None), P(both, None)),
        check_vma=False,
    )
```

time: 126 us -> 102 us (0.81); the launches traced: 124 us -> 102 us
  waiting for transfers between devices: 47.7 us -> 35.3 us
  starting transfers between devices: 34.2 us -> 25.2 us
    ppermute x34 -> x23, waiting for transfers between devices: 47.7 us -> 35.3 us  [swap(): return lax.ppermute(array, 'dp', [(i, i ^ apart) for i in range(count)])]
    ppermute x34 -> x23, starting transfers between devices: 34.2 us -> 25.2 us  [swap(): return lax.ppermute(array, 'dp', [(i, i ^ apart) for i in range(count)])]
    pallas_call x3 -> x4, Pallas kernels: 8.65 us -> 8.56 us  [the longest x1 4.55 us: scores(): pl.pallas_call(functools.partial(score_body, cols, places, scale), in_spe...]
  transfers between devices with their start and end apart: 34 -> 23, of which waited for: 15 -> 9; matrix products, arithmetic and copies ran while one was open for 1% -> 1% of each run, Pallas kernels for 0% -> 25%
where the time goes in v2:
time: 102 us
  waiting for transfers between devices  35.3 us (35%)
  Pallas kernels  34.6 us (34%)
  starting transfers between devices  25.2 us (25%)
  local copies, waits for them, and re-layouts  3.48 us (3%)
  other arithmetic  1.86 us (2%)
  between operations  1.42 us (1%)
    ppermute x23, waiting for transfers between devices, swap(): return lax.ppermute(array, 'dp', [(i, i ^ apart) for i in range(count)])  35.3 us
    ppermute x23, starting transfers between devices, swap(): return lax.ppermute(array, 'dp', [(i, i ^ apart) for i in range(count)])  25.2 us
    pallas_call x2, Pallas kernels, tower(): pl.pallas_call(functools.partial(tower_body, chunks), in_specs=[VMEM, ANY...  23.4 us
    pallas_call x1, Pallas kernels, scores(): pl.pallas_call(functools.partial(score_body, cols, places, scale), in_spe...  4.55 us
    unnamed x10, local copies, waits for them, and re-layouts  3.48 us
    pallas_call x1, Pallas kernels, spread_teacher(): pl.pallas_call(functools.partial(teacher_body, cols, planes), in_specs=[S...  2.68 us
    pallas_call x1, Pallas kernels, near_parts(): pl.pallas_call(functools.partial(near_body, cols, places), in_specs=[VMEM...  2.35 us
  transfers between devices with their start and end apart: 23, of which 9 were waited for; matrix products, arithmetic and copies ran while one was open for 1% of the time, Pallas kernels for 25%

profile of v2, /device:TPU:0, one launch (start us, length us, event | category | flops | bytes accessed | tf_op | source)
XLA Modules:
  0.0 101.8 jit_solution(14756942197971116305)
XLA Ops:
  1.3 0.0 copy-start
  1.3 1.2 %copy-done = f32[128,2048]{1,0:T(8,128)S(1)} copy-done((f32[128,2048]{1,0:T(8,128)S(1)}, f32[128,2048]{1,0:T(8,128)}, u32[]{:S(2)}) %copy-start) | copy-done | bytes 1048600
  2.5 0.0 copy-start.3
  2.5 0.7 copy-done.3
  3.2 0.0 copy-start.4
  3.2 0.7 copy-done.4
  3.8 2.7 %shard_map.121 = (f32[8,128,128]{2,1,0:T(8,128)S(1)}, f32[8,128,128]{2,1,0:T(8,128)S(1)}, f32[8,128,128]{2,1,0:T(8,128)S(1)}, f32[8,128,128]{2,1,0:T(8,128)S(1)}) custom-call(s32[1]{0:T(128)} %bitcast.me, s32[1,16]{1,0:T(1,128)S(1)} %copy-done.3, s32[1]{0:T(128)S(6)} %copy.13.count, s32[32]{0:T(128)S(1)} %copy-done.4, f32[128,2048]{1,0:T(8,128)S(1)} %copy-done), custom_call_target="tpu_custom_call" | custom-call | flops 262144 | bytes 2097152 | tf_op jit(solution)/shard_map/pallas_call | solution.py:121
  6.5 3.0 %collective-permute-start = (f32[8,128,128]{2,1,0:T(8,128)S(1)}, f32[8,128,128]{2,1,0:T(8,128)S(1)}, u32[]{:S(2)}, u32[]{:S(2)}) collective-permute-start(f32[8,128,128]{2,1,0:T(8,128)S(1)} %get-tuple-element.30), channel_id=1, source_target_pairs={{0,2},{1,3},{2,0},{3,1},{4,6},{5,7},{6,4},{7,5},{8,10},{9,11},{10,... | collective-permute-start | bytes 1572872 | tf_op jit(solution)/shard_map/ppermute | solution.py:335
  9.5 1.5 %collective-permute-start.1 = (f32[8,128,128]{2,1,0:T(8,128)S(1)}, f32[8,128,128]{2,1,0:T(8,128)S(1)}, u32[]{:S(2)}, u32[]{:S(2)}) collective-permute-start(f32[8,128,128]{2,1,0:T(8,128)S(1)} %get-tuple-element.31), channel_id=1, source_target_pairs={{0,4},{1,5},{2,6},{3,7},{4,0},{5,1},{6,2},{7,3},{8,12},{9,13},{10,... | collective-permute-start | bytes 1572872 | tf_op jit(solution)/shard_map/ppermute | solution.py:335
  11.0 0.0 collective-permute-start.2
  11.0 0.0 copy-start.1
  11.1 0.9 copy-done.1
  12.0 11.7 %shard_map.122.refs_0_.refs_4_.refs_5_ = bf16[128,1024]{1,0:T(8,128)(2,1)S(1)} custom-call(bf16[128,1024]{1,0:T(8,128)(2,1)S(1)} %copy-done.1, bf16[1024,8192]{1,0:T(8,128)(2,1)} %w_in.2, bf16[8192,1024]{1,0:T(8,128)(2,1)} %w_out.2, f32[8,128,128]{2,1,0:T(8,128)S(1)} %get-tuple-element.37.refs_0_.refs_12_.refs_8_), custom_call_target="tpu_custom_call" | custom-call | flops 1 | bytes 1 | tf_op jit(solution)/shard_map/pallas_call | solution.py:66
  23.7 2.1 %collective-permute-start.4 = (bf16[128,1024]{1,0:T(8,128)(2,1)S(1)}, bf16[128,1024]{1,0:T(8,128)(2,1)S(1)}, u32[]{:S(2)}, u32[]{:S(2)}) collective-permute-start(bf16[128,1024]{1,0:T(8,128)(2,1)S(1)} %shard_map.122.refs_0_.refs_4_.refs_5_), channel_id=1, source_target_pairs={{0,8},{1,9},{2,10},{3,11},{4,12},{5,13},{6,14},{7,15},{8,0},{9,1},... | collective-permute-start | bytes 786440 | tf_op jit(solution)/shard_map/ppermute | solution.py:335
  25.8 2.1 %collective-permute-start.3 = (bf16[128,1024]{1,0:T(8,128)(2,1)S(1)}, bf16[128,1024]{1,0:T(8,128)(2,1)S(1)}, u32[]{:S(2)}, u32[]{:S(2)}) collective-permute-start(bf16[128,1024]{1,0:T(8,128)(2,1)S(1)} %shard_map.122.refs_0_.refs_4_.refs_5_), channel_id=1, source_target_pairs={{0,16},{1,17},{2,18},{3,19},{4,20},{5,21},{6,22},{7,23},{8,24},{9,... | collective-permute-start | bytes 786440 | tf_op jit(solution)/shard_map/ppermute | solution.py:335
  27.9 0.0 copy-done.2
  27.9 11.7 %shard_map.123.refs_0_.refs_4_.refs_1_ = bf16[128,1024]{1,0:T(8,128)(2,1)S(1)} custom-call(bf16[128,1024]{1,0:T(8,128)(2,1)S(1)} %copy-done.2, bf16[1024,8192]{1,0:T(8,128)(2,1)} %w_in.3, bf16[8192,1024]{1,0:T(8,128)(2,1)} %w_out.3, bf16[128,1024]{1,0:T(8,128)(2,1)S(1)} %shard_map.122.refs_0_.refs_4_.refs_5_), custom_call_target="tpu_custom_call" | custom-call | flops 1 | bytes 1 | tf_op jit(solution)/shard_map/pallas_call | solution.py:66
  39.6 0.0 collective-permute-done.4.refs_5_.refs_6_
  39.6 0.0 collective-permute-done.3.refs_6_.refs_7_
  39.6 0.0 collective-permute-done.refs_13_.refs_9_
  39.6 0.0 collective-permute-done.1.refs_14_.refs_10_
  39.6 0.0 collective-permute-done.2.refs_15_.refs_11_
  39.6 0.1 collective-permute-start.9
  39.7 0.5 collective-permute-start.10
  40.2 0.9 collective-permute-start.8
  41.1 0.0 collective-permute-start.11
  41.1 2.4 %collective-permute-start.7 = (bf16[128,1024]{1,0:T(8,128)(2,1)S(1)}, bf16[128,1024]{1,0:T(8,128)(2,1)S(1)}, u32[]{:S(2)}, u32[]{:S(2)}) collective-permute-start(bf16[128,1024]{1,0:T(8,128)(2,1)S(1)} %shard_map.123.refs_0_.refs_4_.refs_1_), channel_id=1, source_target_pairs={{0,6},{1,7},{2,4},{3,5},{4,2},{5,3},{6,0},{7,1},{8,14},{9,15},{10,... | collective-permute-start | bytes 786440 | tf_op jit(solution)/shard_map/ppermute | solution.py:335
  43.5 0.0 collective-permute-done.9.refs_8_.refs_9_
  43.5 0.3 collective-permute-start.6
  43.8 0.0 collective-permute-done.10.refs_9_.refs_10_
  43.8 0.7 collective-permute-start.5
  44.6 3.9 %collective-permute-done.8.refs_7_.refs_8_ = bf16[128,1024]{1,0:T(8,128)(2,1)S(1)} collective-permute-done((bf16[128,1024]{1,0:T(8,128)(2,1)S(1)}, bf16[128,1024]{1,0:T(8,128)(2,1)S(1)}, u32[]{:S(2)}, u32[]{:S(2)}) %collective-permute-start.8) | collective-permute-done | bytes 262176 | tf_op jit(solution)/shard_map/ppermute | solution.py:335
  48.5 0.0 collective-permute-start.12
  48.5 0.0 collective-permute-done.11.refs_10_.refs_11_
  48.5 2.6 %collective-permute-done.7.refs_3_.refs_7_.refs_4_ = bf16[128,1024]{1,0:T(8,128)(2,1)S(1)} collective-permute-done((bf16[128,1024]{1,0:T(8,128)(2,1)S(1)}, bf16[128,1024]{1,0:T(8,128)(2,1)S(1)}, u32[]{:S(2)}, u32[]{:S(2)}) %collective-permute-start.7) | collective-permute-done | bytes 262176 | tf_op jit(solution)/shard_map/ppermute | solution.py:335
  51.1 5.2 %collective-permute-done.6.refs_2_.refs_6_.refs_3_ = bf16[128,1024]{1,0:T(8,128)(2,1)S(1)} collective-permute-done((bf16[128,1024]{1,0:T(8,128)(2,1)S(1)}, bf16[128,1024]{1,0:T(8,128)(2,1)S(1)}, u32[]{:S(2)}, u32[]{:S(2)}) %collective-permute-start.6) | collective-permute-done | bytes 262176 | tf_op jit(solution)/shard_map/ppermute | solution.py:335
  56.3 0.0 collective-permute-done.5.refs_1_.refs_5_.refs_2_
  56.3 0.0 collective-permute-done.12.refs_11_.refs_12_
  56.3 4.5 %shard_map.124 = (f32[1024,512]{1,0:T(8,128)S(1)}, f32[4,4,128]{2,1,0:T(4,128)S(1)}) custom-call(bf16[128,1024]{1,0:T(8,128)(2,1)S(1)} %shard_map.123.refs_0_.refs_4_.refs_1_, bf16[128,1024]{1,0:T(8,128)(2,1)S(1)} %collective-permute-done.5.refs_1_.refs_5_.refs_2_, bf16[128,1024]{1,0:T(8,128)(2,1)S(1)} %collective-permute-done.6.refs_2_.refs_6_.refs_3_, ...), custom_call_target="tpu_custom_call" | custom-call | flops 1073741824 | bytes 4194304 | tf_op jit(solution)/shard_map/pallas_call | solution.py:183
  60.9 1.8 %collective-permute-start.15 = (f32[4,4,128]{2,1,0:T(4,128)S(1)}, f32[4,4,128]{2,1,0:T(4,128)S(1)}, u32[]{:S(2)}, u32[]{:S(2)}) collective-permute-start(f32[4,4,128]{2,1,0:T(4,128)S(1)} %get-tuple-element.41.refs_0_), channel_id=1, source_target_pairs={{0,6},{1,7},{2,4},{3,5},{4,2},{5,3},{6,0},{7,1},{8,14},{9,15},{10,... | collective-permute-start | bytes 24584 | tf_op jit(solution)/shard_map/ppermute | solution.py:335
  62.7 1.3 %collective-permute-start.14 = (f32[4,4,128]{2,1,0:T(4,128)S(1)}, f32[4,4,128]{2,1,0:T(4,128)S(1)}, u32[]{:S(2)}, u32[]{:S(2)}) collective-permute-start(f32[4,4,128]{2,1,0:T(4,128)S(1)} %get-tuple-element.41.refs_0_), channel_id=1, source_target_pairs={{0,4},{1,5},{2,6},{3,7},{4,0},{5,1},{6,2},{7,3},{8,12},{9,13},{10,... | collective-permute-start | bytes 24584 | tf_op jit(solution)/shard_map/ppermute | solution.py:335
  64.0 0.5 collective-permute-start.13
  64.4 1.1 %collective-permute-done.15.refs_3_ = f32[4,4,128]{2,1,0:T(4,128)S(1)} collective-permute-done((f32[4,4,128]{2,1,0:T(4,128)S(1)}, f32[4,4,128]{2,1,0:T(4,128)S(1)}, u32[]{:S(2)}, u32[]{:S(2)}) %collective-permute-start.15) | collective-permute-done | bytes 8224 | tf_op jit(solution)/shard_map/ppermute | solution.py:335
  65.5 0.9 collective-permute-done.14.refs_2_
  66.3 1.3 %collective-permute-done.13.refs_1_ = f32[4,4,128]{2,1,0:T(4,128)S(1)} collective-permute-done((f32[4,4,128]{2,1,0:T(4,128)S(1)}, f32[4,4,128]{2,1,0:T(4,128)S(1)}, u32[]{:S(2)}, u32[]{:S(2)}) %collective-permute-start.13) | collective-permute-done | bytes 8224 | tf_op jit(solution)/shard_map/ppermute | solution.py:335
  67.6 1.5 %shard_map.125 = (bf16[1024,512]{1,0:T(8,128)(2,1)S(1)}, f32[1,128]{1,0:T(1,128)}, bf16[512,1024]{1,0:T(8,128)(2,1)S(1)}) custom-call(f32[4,4,128]{2,1,0:T(4,128)S(1)} %get-tuple-element.41.refs_0_, f32[4,4,128]{2,1,0:T(4,128)S(1)} %collective-permute-done.13.refs_1_, f32[4,4,128]{2,1,0:T(4,128)S(1)} %collective-permute-done.14.refs_2_, ...), custom_call_target="tpu_custom_call" | custom-call | flops 536870912 | bytes 4194304 | tf_op jit(solution)/shard_map/pallas_call | solution.py:236
  69.1 0.1 collective-permute-start.19
  69.2 2.4 %shard_map.126 = (f32[512,1024]{1,0:T(8,128)S(1)}, f32[128,1024]{1,0:T(8,128)S(1)}, bf16[128,1024]{1,0:T(8,128)(2,1)S(1)}, bf16[128,1024]{1,0:T(8,128)(2,1)S(1)}, bf16[128,1024]{1,0:T(8,128)(2,1)S(1)}) custom-call(bf16[1024,512]{1,0:T(8,128)(2,1)S(1)} %get-tuple-element.44.refs_0_, bf16[128,1024]{1,0:T(8,128)(2,1)S(1)} %shard_map.123.refs_0_.refs_4_.refs_1_, ...), custom_call_target="tpu_custom_call" | custom-call | flops 1610612736 | bytes 4194304 | tf_op jit(solution)/shard_map/pallas_call | solution.py:285
  71.6 0.5 collective-permute-start.16
  72.1 1.4 %collective-permute-start.17 = (bf16[128,1024]{1,0:T(8,128)(2,1)S(1)}, bf16[128,1024]{1,0:T(8,128)(2,1)S(1)}, u32[]{:S(2)}, u32[]{:S(2)}) collective-permute-start(bf16[128,1024]{1,0:T(8,128)(2,1)S(1)} %get-tuple-element.47), channel_id=1, source_target_pairs={{0,4},{1,5},{2,6},{3,7},{4,0},{5,1},{6,2},{7,3},{8,12},{9,13},{10,... | collective-permute-start | bytes 786440 | tf_op jit(solution)/shard_map/ppermute | solution.py:335
  73.5 1.6 %collective-permute-start.18 = (bf16[128,1024]{1,0:T(8,128)(2,1)S(1)}, bf16[128,1024]{1,0:T(8,128)(2,1)S(1)}, u32[]{:S(2)}, u32[]{:S(2)}) collective-permute-start(bf16[128,1024]{1,0:T(8,128)(2,1)S(1)} %get-tuple-element.48), channel_id=1, source_target_pairs={{0,6},{1,7},{2,4},{3,5},{4,2},{5,3},{6,0},{7,1},{8,14},{9,15},{10,... | collective-permute-start | bytes 786440 | tf_op jit(solution)/shard_map/ppermute | solution.py:335
  75.1 0.0 collective-permute-done.19.far
  75.1 0.2 shard_map.127
  75.3 1.5 %collective-permute-start.20 = (bf16[128,1024]{1,0:T(8,128)(2,1)S(1)}, bf16[128,1024]{1,0:T(8,128)(2,1)S(1)}, u32[]{:S(2)}, u32[]{:S(2)}) collective-permute-start(bf16[128,1024]{1,0:T(8,128)(2,1)S(1)} %get-tuple-element.52), channel_id=1, source_target_pairs={{0,24},{1,25},{2,26},{3,27},{4,28},{5,29},{6,30},{7,31},{8,16},{9,... | collective-permute-start | bytes 786440 | tf_op jit(solution)/shard_map/ppermute | solution.py:335
  76.8 1.4 %collective-permute-start.21 = (bf16[128,1024]{1,0:T(8,128)(2,1)S(1)}, bf16[128,1024]{1,0:T(8,128)(2,1)S(1)}, u32[]{:S(2)}, u32[]{:S(2)}) collective-permute-start(bf16[128,1024]{1,0:T(8,128)(2,1)S(1)} %get-tuple-element.53), channel_id=1, source_target_pairs={{0,16},{1,17},{2,18},{3,19},{4,20},{5,21},{6,22},{7,23},{8,24},{9,... | collective-permute-start | bytes 786440 | tf_op jit(solution)/shard_map/ppermute | solution.py:335
  78.2 2.5 %collective-permute-done.16 = bf16[128,1024]{1,0:T(8,128)(2,1)S(1)} collective-permute-done((bf16[128,1024]{1,0:T(8,128)(2,1)S(1)}, bf16[128,1024]{1,0:T(8,128)(2,1)S(1)}, u32[]{:S(2)}, u32[]{:S(2)}) %collective-permute-start.16) | collective-permute-done | bytes 262176 | tf_op jit(solution)/shard_map/ppermute | solution.py:335
  80.7 1.4 %collective-permute-start.22 = (bf16[128,1024]{1,0:T(8,128)(2,1)S(1)}, bf16[128,1024]{1,0:T(8,128)(2,1)S(1)}, u32[]{:S(2)}, u32[]{:S(2)}) collective-permute-start(bf16[128,1024]{1,0:T(8,128)(2,1)S(1)} %get-tuple-element.54), channel_id=1, source_target_pairs={{0,8},{1,9},{2,10},{3,11},{4,12},{5,13},{6,14},{7,15},{8,0},{9,1},... | collective-permute-start | bytes 786440 | tf_op jit(solution)/shard_map/ppermute | solution.py:335
  82.1 0.0 collective-permute-done.17
  82.1 4.0 %collective-permute-done.18 = bf16[128,1024]{1,0:T(8,128)(2,1)S(1)} collective-permute-done((bf16[128,1024]{1,0:T(8,128)(2,1)S(1)}, bf16[128,1024]{1,0:T(8,128)(2,1)S(1)}, u32[]{:S(2)}, u32[]{:S(2)}) %collective-permute-start.18) | collective-permute-done | bytes 262176 | tf_op jit(solution)/shard_map/ppermute | solution.py:335
  86.1 0.9 convert_add_fusion.1
  87.1 0.0 collective-permute-done.20
  87.1 13.8 %collective-permute-done.21 = bf16[128,1024]{1,0:T(8,128)(2,1)S(1)} collective-permute-done((bf16[128,1024]{1,0:T(8,128)(2,1)S(1)}, bf16[128,1024]{1,0:T(8,128)(2,1)S(1)}, u32[]{:S(2)}, u32[]{:S(2)}) %collective-permute-start.21) | collective-permute-done | bytes 262176 | tf_op jit(solution)/shard_map/ppermute | solution.py:335
  100.9 0.0 collective-permute-done.22
  100.9 0.9 convert_add_fusion
  (1 shorter events, 0.0 us)
Async XLA Ops:
  1.3 1.2 %copy-start = (f32[128,2048]{1,0:T(8,128)S(1)}, f32[128,2048]{1,0:T(8,128)}, u32[]{:S(2)}) copy-start(f32[128,2048]{1,0:T(8,128)} %teacher.1) | copy-start | bytes 3145732
  2.5 0.7 copy-start.3
  3.2 0.7 copy-start.4
  6.5 33.1 %collective-permute-start = (f32[8,128,128]{2,1,0:T(8,128)S(1)}, f32[8,128,128]{2,1,0:T(8,128)S(1)}, u32[]{:S(2)}, u32[]{:S(2)}) collective-permute-start(f32[8,128,128]{2,1,0:T(8,128)S(1)} %get-tuple-element.30), channel_id=1, source_target_pairs={{0,2},{1,3},{2,0},{3,1},{4,6},{5,7},{6,4},{7,5},{8,10},{9,11},{10,... | collective-permute-start | bytes 1572872 | tf_op jit(solution)/shard_map/ppermute | solution.py:335
  9.5 30.1 %collective-permute-start.1 = (f32[8,128,128]{2,1,0:T(8,128)S(1)}, f32[8,128,128]{2,1,0:T(8,128)S(1)}, u32[]{:S(2)}, u32[]{:S(2)}) collective-permute-start(f32[8,128,128]{2,1,0:T(8,128)S(1)} %get-tuple-element.31), channel_id=1, source_target_pairs={{0,4},{1,5},{2,6},{3,7},{4,0},{5,1},{6,2},{7,3},{8,12},{9,13},{10,... | collective-permute-start | bytes 1572872 | tf_op jit(solution)/shard_map/ppermute | solution.py:335
  11.0 28.6 %collective-permute-start.2 = (f32[8,128,128]{2,1,0:T(8,128)S(1)}, f32[8,128,128]{2,1,0:T(8,128)S(1)}, u32[]{:S(2)}, u32[]{:S(2)}) collective-permute-start(f32[8,128,128]{2,1,0:T(8,128)S(1)} %get-tuple-element.32), channel_id=1, source_target_pairs={{0,6},{1,7},{2,4},{3,5},{4,2},{5,3},{6,0},{7,1},{8,14},{9,15},{10,... | collective-permute-start | bytes 1572872 | tf_op jit(solution)/shard_map/ppermute | solution.py:335
  11.0 0.9 copy-start.1
  12.0 15.9 %copy-start.2 = (bf16[128,1024]{1,0:T(8,128)(2,1)S(1)}, bf16[128,1024]{1,0:T(8,128)(2,1)}, u32[]{:S(2)}) copy-start(bf16[128,1024]{1,0:T(8,128)(2,1)} %feats.3) | copy-start | bytes 786436
  23.7 15.9 %collective-permute-start.4 = (bf16[128,1024]{1,0:T(8,128)(2,1)S(1)}, bf16[128,1024]{1,0:T(8,128)(2,1)S(1)}, u32[]{:S(2)}, u32[]{:S(2)}) collective-permute-start(bf16[128,1024]{1,0:T(8,128)(2,1)S(1)} %shard_map.122.refs_0_.refs_4_.refs_5_), channel_id=1, source_target_pairs={{0,8},{1,9},{2,10},{3,11},{4,12},{5,13},{6,14},{7,15},{8,0},{9,1},... | collective-permute-start | bytes 786440 | tf_op jit(solution)/shard_map/ppermute | solution.py:335
  25.8 13.8 %collective-permute-start.3 = (bf16[128,1024]{1,0:T(8,128)(2,1)S(1)}, bf16[128,1024]{1,0:T(8,128)(2,1)S(1)}, u32[]{:S(2)}, u32[]{:S(2)}) collective-permute-start(bf16[128,1024]{1,0:T(8,128)(2,1)S(1)} %shard_map.122.refs_0_.refs_4_.refs_5_), channel_id=1, source_target_pairs={{0,16},{1,17},{2,18},{3,19},{4,20},{5,21},{6,22},{7,23},{8,24},{9,... | collective-permute-start | bytes 786440 | tf_op jit(solution)/shard_map/ppermute | solution.py:335
  39.6 3.9 %collective-permute-start.9 = (bf16[128,1024]{1,0:T(8,128)(2,1)S(1)}, bf16[128,1024]{1,0:T(8,128)(2,1)S(1)}, u32[]{:S(2)}, u32[]{:S(2)}) collective-permute-start(bf16[128,1024]{1,0:T(8,128)(2,1)S(1)} %shard_map.122.refs_0_.refs_4_.refs_5_), channel_id=1, source_target_pairs={{0,1},{1,0},{2,3},{3,2},{4,5},{5,4},{6,7},{7,6},{8,9},{9,8},{10,11... | collective-permute-start | bytes 786440 | tf_op jit(solution)/shard_map/ppermute | solution.py:335
  39.7 4.1 %collective-permute-start.10 = (bf16[128,1024]{1,0:T(8,128)(2,1)S(1)}, bf16[128,1024]{1,0:T(8,128)(2,1)S(1)}, u32[]{:S(2)}, u32[]{:S(2)}) collective-permute-start(bf16[128,1024]{1,0:T(8,128)(2,1)S(1)} %collective-permute-done.4.refs_5_.refs_6_), channel_id=1, source_target_pairs={{0,1},{1,0},{2,3},{3,2},{4,5},{5,4},{6,7},{7,6},{8,9},{9,8},{10,11... | collective-permute-start | bytes 786440 | tf_op jit(solution)/shard_map/ppermute | solution.py:335
  40.2 8.3 %collective-permute-start.8 = (bf16[128,1024]{1,0:T(8,128)(2,1)S(1)}, bf16[128,1024]{1,0:T(8,128)(2,1)S(1)}, u32[]{:S(2)}, u32[]{:S(2)}) collective-permute-start(bf16[128,1024]{1,0:T(8,128)(2,1)S(1)} %collective-permute-done.3.refs_6_.refs_7_), channel_id=1, source_target_pairs={{0,8},{1,9},{2,10},{3,11},{4,12},{5,13},{6,14},{7,15},{8,0},{9,1},... | collective-permute-start | bytes 786440 | tf_op jit(solution)/shard_map/ppermute | solution.py:335
  41.1 7.4 %collective-permute-start.11 = (bf16[128,1024]{1,0:T(8,128)(2,1)S(1)}, bf16[128,1024]{1,0:T(8,128)(2,1)S(1)}, u32[]{:S(2)}, u32[]{:S(2)}) collective-permute-start(bf16[128,1024]{1,0:T(8,128)(2,1)S(1)} %collective-permute-done.3.refs_6_.refs_7_), channel_id=1, source_target_pairs={{0,1},{1,0},{2,3},{3,2},{4,5},{5,4},{6,7},{7,6},{8,9},{9,8},{10,11... | collective-permute-start | bytes 786440 | tf_op jit(solution)/shard_map/ppermute | solution.py:335
  41.1 10.0 %collective-permute-start.7 = (bf16[128,1024]{1,0:T(8,128)(2,1)S(1)}, bf16[128,1024]{1,0:T(8,128)(2,1)S(1)}, u32[]{:S(2)}, u32[]{:S(2)}) collective-permute-start(bf16[128,1024]{1,0:T(8,128)(2,1)S(1)} %shard_map.123.refs_0_.refs_4_.refs_1_), channel_id=1, source_target_pairs={{0,6},{1,7},{2,4},{3,5},{4,2},{5,3},{6,0},{7,1},{8,14},{9,15},{10,... | collective-permute-start | bytes 786440 | tf_op jit(solution)/shard_map/ppermute | solution.py:335
  43.5 12.8 %collective-permute-start.6 = (bf16[128,1024]{1,0:T(8,128)(2,1)S(1)}, bf16[128,1024]{1,0:T(8,128)(2,1)S(1)}, u32[]{:S(2)}, u32[]{:S(2)}) collective-permute-start(bf16[128,1024]{1,0:T(8,128)(2,1)S(1)} %shard_map.123.refs_0_.refs_4_.refs_1_), channel_id=1, source_target_pairs={{0,4},{1,5},{2,6},{3,7},{4,0},{5,1},{6,2},{7,3},{8,12},{9,13},{10,... | collective-permute-start | bytes 786440 | tf_op jit(solution)/shard_map/ppermute | solution.py:335
  43.8 12.5 %collective-permute-start.5 = (bf16[128,1024]{1,0:T(8,128)(2,1)S(1)}, bf16[128,1024]{1,0:T(8,128)(2,1)S(1)}, u32[]{:S(2)}, u32[]{:S(2)}) collective-permute-start(bf16[128,1024]{1,0:T(8,128)(2,1)S(1)} %shard_map.123.refs_0_.refs_4_.refs_1_), channel_id=1, source_target_pairs={{0,2},{1,3},{2,0},{3,1},{4,6},{5,7},{6,4},{7,5},{8,10},{9,11},{10,... | collective-permute-start | bytes 786440 | tf_op jit(solution)/shard_map/ppermute | solution.py:335
  48.5 7.8 %collective-permute-start.12 = (bf16[128,1024]{1,0:T(8,128)(2,1)S(1)}, bf16[128,1024]{1,0:T(8,128)(2,1)S(1)}, u32[]{:S(2)}, u32[]{:S(2)}) collective-permute-start(bf16[128,1024]{1,0:T(8,128)(2,1)S(1)} %collective-permute-done.8.refs_7_.refs_8_), channel_id=1, source_target_pairs={{0,1},{1,0},{2,3},{3,2},{4,5},{5,4},{6,7},{7,6},{8,9},{9,8},{10,11... | collective-permute-start | bytes 786440 | tf_op jit(solution)/shard_map/ppermute | solution.py:335
  60.9 4.6 %collective-permute-start.15 = (f32[4,4,128]{2,1,0:T(4,128)S(1)}, f32[4,4,128]{2,1,0:T(4,128)S(1)}, u32[]{:S(2)}, u32[]{:S(2)}) collective-permute-start(f32[4,4,128]{2,1,0:T(4,128)S(1)} %get-tuple-element.41.refs_0_), channel_id=1, source_target_pairs={{0,6},{1,7},{2,4},{3,5},{4,2},{5,3},{6,0},{7,1},{8,14},{9,15},{10,... | collective-permute-start | bytes 24584 | tf_op jit(solution)/shard_map/ppermute | solution.py:335
  62.7 3.7 %collective-permute-start.14 = (f32[4,4,128]{2,1,0:T(4,128)S(1)}, f32[4,4,128]{2,1,0:T(4,128)S(1)}, u32[]{:S(2)}, u32[]{:S(2)}) collective-permute-start(f32[4,4,128]{2,1,0:T(4,128)S(1)} %get-tuple-element.41.refs_0_), channel_id=1, source_target_pairs={{0,4},{1,5},{2,6},{3,7},{4,0},{5,1},{6,2},{7,3},{8,12},{9,13},{10,... | collective-permute-start | bytes 24584 | tf_op jit(solution)/shard_map/ppermute | solution.py:335
  64.0 3.7 %collective-permute-start.13 = (f32[4,4,128]{2,1,0:T(4,128)S(1)}, f32[4,4,128]{2,1,0:T(4,128)S(1)}, u32[]{:S(2)}, u32[]{:S(2)}) collective-permute-start(f32[4,4,128]{2,1,0:T(4,128)S(1)} %get-tuple-element.41.refs_0_), channel_id=1, source_target_pairs={{0,2},{1,3},{2,0},{3,1},{4,6},{5,7},{6,4},{7,5},{8,10},{9,11},{10,... | collective-permute-start | bytes 24584 | tf_op jit(solution)/shard_map/ppermute | solution.py:335
  69.1 6.0 %collective-permute-start.19 = (bf16[512,1024]{1,0:T(8,128)(2,1)S(1)}, bf16[512,1024]{1,0:T(8,128)(2,1)S(1)}, u32[]{:S(2)}, u32[]{:S(2)}) collective-permute-start(bf16[512,1024]{1,0:T(8,128)(2,1)S(1)} %get-tuple-element.50), channel_id=1, source_target_pairs={{0,1},{1,0},{2,3},{3,2},{4,5},{5,4},{6,7},{7,6},{8,9},{9,8},{10,11... | collective-permute-start | bytes 3145736 | tf_op jit(solution)/shard_map/ppermute | solution.py:335
  71.6 9.2 %collective-permute-start.16 = (bf16[128,1024]{1,0:T(8,128)(2,1)S(1)}, bf16[128,1024]{1,0:T(8,128)(2,1)S(1)}, u32[]{:S(2)}, u32[]{:S(2)}) collective-permute-start(bf16[128,1024]{1,0:T(8,128)(2,1)S(1)} %get-tuple-element.46), channel_id=1, source_target_pairs={{0,2},{1,3},{2,0},{3,1},{4,6},{5,7},{6,4},{7,5},{8,10},{9,11},{10,... | collective-permute-start | bytes 786440 | tf_op jit(solution)/shard_map/ppermute | solution.py:335
  72.1 10.1 %collective-permute-start.17 = (bf16[128,1024]{1,0:T(8,128)(2,1)S(1)}, bf16[128,1024]{1,0:T(8,128)(2,1)S(1)}, u32[]{:S(2)}, u32[]{:S(2)}) collective-permute-start(bf16[128,1024]{1,0:T(8,128)(2,1)S(1)} %get-tuple-element.47), channel_id=1, source_target_pairs={{0,4},{1,5},{2,6},{3,7},{4,0},{5,1},{6,2},{7,3},{8,12},{9,13},{10,... | collective-permute-start | bytes 786440 | tf_op jit(solution)/shard_map/ppermute | solution.py:335
  73.5 12.6 %collective-permute-start.18 = (bf16[128,1024]{1,0:T(8,128)(2,1)S(1)}, bf16[128,1024]{1,0:T(8,128)(2,1)S(1)}, u32[]{:S(2)}, u32[]{:S(2)}) collective-permute-start(bf16[128,1024]{1,0:T(8,128)(2,1)S(1)} %get-tuple-element.48), channel_id=1, source_target_pairs={{0,6},{1,7},{2,4},{3,5},{4,2},{5,3},{6,0},{7,1},{8,14},{9,15},{10,... | collective-permute-start | bytes 786440 | tf_op jit(solution)/shard_map/ppermute | solution.py:335
  75.3 11.8 %collective-permute-start.20 = (bf16[128,1024]{1,0:T(8,128)(2,1)S(1)}, bf16[128,1024]{1,0:T(8,128)(2,1)S(1)}, u32[]{:S(2)}, u32[]{:S(2)}) collective-permute-start(bf16[128,1024]{1,0:T(8,128)(2,1)S(1)} %get-tuple-element.52), channel_id=1, source_target_pairs={{0,24},{1,25},{2,26},{3,27},{4,28},{5,29},{6,30},{7,31},{8,16},{9,... | collective-permute-start | bytes 786440 | tf_op jit(solution)/shard_map/ppermute | solution.py:335
  76.8 24.1 %collective-permute-start.21 = (bf16[128,1024]{1,0:T(8,128)(2,1)S(1)}, bf16[128,1024]{1,0:T(8,128)(2,1)S(1)}, u32[]{:S(2)}, u32[]{:S(2)}) collective-permute-start(bf16[128,1024]{1,0:T(8,128)(2,1)S(1)} %get-tuple-element.53), channel_id=1, source_target_pairs={{0,16},{1,17},{2,18},{3,19},{4,20},{5,21},{6,22},{7,23},{8,24},{9,... | collective-permute-start | bytes 786440 | tf_op jit(solution)/shard_map/ppermute | solution.py:335
  80.7 20.2 %collective-permute-start.22 = (bf16[128,1024]{1,0:T(8,128)(2,1)S(1)}, bf16[128,1024]{1,0:T(8,128)(2,1)S(1)}, u32[]{:S(2)}, u32[]{:S(2)}) collective-permute-start(bf16[128,1024]{1,0:T(8,128)(2,1)S(1)} %get-tuple-element.54), channel_id=1, source_target_pairs={{0,8},{1,9},{2,10},{3,11},{4,12},{5,13},{6,14},{7,15},{8,0},{9,1},... | collective-permute-start | bytes 786440 | tf_op jit(solution)/shard_map/ppermute | solution.py:335

commit v3 on v2

--- a/solution.py
+++ b/solution.py
@@ -253,23 +253,40 @@
     )(*stats, *users, *logs, weights)
 
 
-def near_body(cols, places, *refs):
-    grads, users, items = refs[0], refs[1 : 1 + cols], refs[1 + cols : 1 + cols + places]
-    near = refs[1 + cols + places]
-    parts = refs[2 + cols + places : 2 + 2 * cols + places]
-    all_users, all_items, user_sems, item_sems = refs[2 + 2 * cols + places :]
-    rows = users[0].shape[0]
-    load_users = loads_of(users, all_users, user_sems)
-    load_items = loads_of(items, all_items, item_sems)
-    for copy in load_users + load_items:
+def near_body(cols, grads, *refs):
+    users, (near, all_users, sems) = refs[:cols], refs[cols:]
+    loads = loads_of(users, all_users, sems)
+    for copy in loads:
         copy.start()
-    for copy in load_users:
+    for copy in loads:
         copy.wait()
-    half = places * rows // CORES
-    near[...] = jnp.dot(grads[:half], all_users[...], preferred_element_type=jnp.float32)
-    for copy in load_items:
+    near[...] = jnp.dot(grads[: near.shape[0]], all_users[...], preferred_element_type=jnp.float32)
+
+
+def near_part(grads, users):
+    cols, places = len(users), grads.shape[0]
+    rows, width = users[0].shape
+    return pl.pallas_call(
+        functools.partial(near_body, cols),
+        in_specs=[VMEM] + [ANY] * cols,
+        out_specs=VMEM,
+        out_shape=struct((places // CORES, width), jnp.float32),
+        scratch_shapes=[pltpu.VMEM((cols * rows, width), jnp.bfloat16), pltpu.SemaphoreType.DMA((cols,))],
+        compiler_params=params(32),
+        cost_estimate=cost(grads.size * width, 4 * grads.size),
+    )(grads, *users)
+
+
+def user_body(cols, places, grads, *refs):
+    items, refs = refs[:places], refs[-cols - 2 :]
+    parts, (all_items, sems) = refs[:cols], refs[cols:]
+    rows = items[0].shape[0]
+    loads = loads_of(items, all_items, sems)
+    for copy in loads:
+        copy.start()
+    for copy in loads:
         copy.wait()
-    for i in range(cols):
+    for i in range(cols - 1, -1, -1):
         part = lax.dot_general(
             grads[:, i * rows : (i + 1) * rows],
             all_items[...],
@@ -279,24 +296,18 @@
         parts[i][...] = part.astype(parts[i].dtype)
 
 
-def near_parts(grads, users, items):
-    cols, places = len(users), len(items)
-    rows, width = users[0].shape
-    return pl.pallas_call(
-        functools.partial(near_body, cols, places),
-        in_specs=[VMEM] + [ANY] * (cols + places),
-        out_specs=[VMEM] * (1 + cols),
-        out_shape=[struct((places * rows // CORES, width), jnp.float32)]
-        + [struct((rows, width), jnp.bfloat16 if i else jnp.float32) for i in range(cols)],
-        scratch_shapes=[
-            pltpu.VMEM((cols * rows, width), jnp.bfloat16),
-            pltpu.VMEM((places * rows, width), jnp.bfloat16),
-            pltpu.SemaphoreType.DMA((cols,)),
-            pltpu.SemaphoreType.DMA((places,)),
-        ],
+def user_parts(cols, grads, items, after):
+    places = len(items)
+    rows, width = items[0].shape
+    return pl.pallas_call(
+        functools.partial(user_body, cols, places),
+        in_specs=[VMEM] + [ANY] * (places + len(after)),
+        out_specs=[VMEM] * cols,
+        out_shape=[struct((rows, width), jnp.bfloat16 if i else jnp.float32) for i in range(cols)],
+        scratch_shapes=[pltpu.VMEM((places * rows, width), jnp.bfloat16), pltpu.SemaphoreType.DMA((places,))],
         compiler_params=params(32),
-        cost_estimate=cost(3 * cols * places * rows * rows * width, 8 * cols * places * rows * rows),
-    )(grads, *users, *items)
+        cost_estimate=cost(2 * grads.size * width, 4 * grads.size),
+    )(grads, *items, *after)
 
 
 def join_body(planes, near, far, *outs):
@@ -348,16 +359,19 @@
     user_emb = embed(user_feats, user_w_in, user_w_out, [item_emb])
     user_emb, item_emb, logs, crossed, nearby = lax.optimization_barrier((user_emb, item_emb, logs, crossed, nearby))
     users = [user_emb] + over_columns(user_emb)
-    items = [item_emb] + nearby + crossed + [swap(block, z * cols * CORES) for block in crossed for z in range(1, wide)]
+    derived = [swap(block, z * cols * CORES) for block in crossed for z in range(1, wide)]
+    if cols > 1:
+        users[1], item_emb, nearby, crossed = lax.optimization_barrier((users[1], item_emb, nearby, crossed))
+    items = [item_emb] + nearby + crossed + derived
     items = items + [swap(block, 1) for block in items]
 
     weights, stats = scores(scale, users, items, logs)
     grads, divergence, far = far_parts(factor, [stats] + over_columns(stats), users, logs, weights)
     far = swap(far, 1)
-    near, own, *others = near_parts(grads, users, items)
+    parts = join(planes, near_part(grads, users), far)
+    sent = [swap(parts[z], z * cols * CORES) for z in range(planes - 1, 0, -1)]
+    own, *others = user_parts(cols, grads, items, [parts[0]])
     arrived = [swap(part, (c + 1) * CORES) for c, part in enumerate(others)]
-    parts = join(planes, near, far)
-    sent = [swap(parts[z], z * cols * CORES) for z in range(planes - 1, 0, -1)]
 
     def add(start, parts):
         return functools.reduce(jnp.add, [part.astype(jnp.float32) for part in parts], start)

time: 102 us -> 98.7 us (0.968)
  waiting for transfers between devices: 35.3 us -> 33.4 us
  starting transfers between devices: 25.2 us -> 24 us
    ppermute x23, waiting for transfers between devices: 35.3 us -> 33.4 us  [swap(): return lax.ppermute(array, 'dp', [(i, i ^ apart) for i in range(count)])]
    ppermute x23, starting transfers between devices: 25.2 us -> 24 us  [swap(): return lax.ppermute(array, 'dp', [(i, i ^ apart) for i in range(count)])]
    pallas_call x1 -> x2, Pallas kernels: 2.35 us -> 2.35 us  [the longest x1 1.52 us: user_parts(): pl.pallas_call(functools.partial(user_body, cols, places), in_specs=[VMEM...]
  transfers between devices with their start and end apart: 23 -> 23, of which waited for: 9 -> 9; matrix products, arithmetic and copies ran while one was open for 1% -> 1% of each run, Pallas kernels for 25% -> 26%
where the time goes in v3:
time: 98.7 us; the launch traced here: 98.5 us
  Pallas kernels  34.2 us (35%)
  waiting for transfers between devices  33.4 us (34%)
  starting transfers between devices  24 us (24%)
  local copies, waits for them, and re-layouts  3.48 us (4%)
  other arithmetic  1.86 us (2%)
  between operations  1.43 us (1%)
    ppermute x23, waiting for transfers between devices, swap(): return lax.ppermute(array, 'dp', [(i, i ^ apart) for i in range(count)])  33.4 us
    ppermute x23, starting transfers between devices, swap(): return lax.ppermute(array, 'dp', [(i, i ^ apart) for i in range(count)])  24 us
    pallas_call x2, Pallas kernels, tower(): pl.pallas_call(functools.partial(tower_body, chunks), in_specs=[VMEM, ANY...  23.4 us
    pallas_call x1, Pallas kernels, scores(): pl.pallas_call(functools.partial(score_body, cols, places, scale), in_spe...  4.55 us
    unnamed x10, local copies, waits for them, and re-layouts  3.48 us
    pallas_call x1, Pallas kernels, spread_teacher(): pl.pallas_call(functools.partial(teacher_body, cols, planes), in_specs=[S...  2.3 us
  transfers between devices with their start and end apart: 23, of which 9 were waited for; matrix products, arithmetic and copies ran while one was open for 1% of the time, Pallas kernels for 26%

profile of v3, /device:TPU:0, one launch (start us, length us, event | category | flops | bytes accessed | tf_op | source)
XLA Modules:
  0.0 98.5 jit_solution(7387184160706215715)
XLA Ops:
  1.3 0.0 copy-start
  1.3 1.2 %copy-done = f32[128,2048]{1,0:T(8,128)S(1)} copy-done((f32[128,2048]{1,0:T(8,128)S(1)}, f32[128,2048]{1,0:T(8,128)}, u32[]{:S(2)}) %copy-start) | copy-done | bytes 1048600
  2.5 0.0 copy-start.3
  2.5 0.7 copy-done.3
  3.2 0.0 copy-start.4
  3.2 0.7 copy-done.4
  3.8 2.3 %shard_map.121 = (f32[8,128,128]{2,1,0:T(8,128)S(1)}, f32[8,128,128]{2,1,0:T(8,128)S(1)}, f32[8,128,128]{2,1,0:T(8,128)S(1)}, f32[8,128,128]{2,1,0:T(8,128)S(1)}) custom-call(s32[1]{0:T(128)} %bitcast.me, s32[1,16]{1,0:T(1,128)S(1)} %copy-done.3, s32[1]{0:T(128)S(6)} %copy.13.count, s32[32]{0:T(128)S(1)} %copy-done.4, f32[128,2048]{1,0:T(8,128)S(1)} %copy-done), custom_call_target="tpu_custom_call" | custom-call | flops 262144 | bytes 2097152 | tf_op jit(solution)/shard_map/pallas_call | solution.py:121
  6.1 2.9 %collective-permute-start = (f32[8,128,128]{2,1,0:T(8,128)S(1)}, f32[8,128,128]{2,1,0:T(8,128)S(1)}, u32[]{:S(2)}, u32[]{:S(2)}) collective-permute-start(f32[8,128,128]{2,1,0:T(8,128)S(1)} %get-tuple-element.33), channel_id=1, source_target_pairs={{0,2},{1,3},{2,0},{3,1},{4,6},{5,7},{6,4},{7,5},{8,10},{9,11},{10,... | collective-permute-start | bytes 1572872 | tf_op jit(solution)/shard_map/ppermute | solution.py:346
  9.0 1.6 %collective-permute-start.1 = (f32[8,128,128]{2,1,0:T(8,128)S(1)}, f32[8,128,128]{2,1,0:T(8,128)S(1)}, u32[]{:S(2)}, u32[]{:S(2)}) collective-permute-start(f32[8,128,128]{2,1,0:T(8,128)S(1)} %get-tuple-element.34), channel_id=1, source_target_pairs={{0,4},{1,5},{2,6},{3,7},{4,0},{5,1},{6,2},{7,3},{8,12},{9,13},{10,... | collective-permute-start | bytes 1572872 | tf_op jit(solution)/shard_map/ppermute | solution.py:346
  10.6 0.0 collective-permute-start.2
  10.7 0.9 copy-done.1
  11.6 11.7 %shard_map.122.refs_0_.refs_4_ = bf16[128,1024]{1,0:T(8,128)(2,1)S(1)} custom-call(bf16[128,1024]{1,0:T(8,128)(2,1)S(1)} %copy-done.1, bf16[1024,8192]{1,0:T(8,128)(2,1)} %w_in.2, bf16[8192,1024]{1,0:T(8,128)(2,1)} %w_out.2, f32[8,128,128]{2,1,0:T(8,128)S(1)} %get-tuple-element.44.refs_0_.refs_12_.refs_8_), custom_call_target="tpu_custom_call" | custom-call | flops 1 | bytes 1 | tf_op jit(solution)/shard_map/pallas_call | solution.py:66
  23.3 2.5 %collective-permute-start.4 = (bf16[128,1024]{1,0:T(8,128)(2,1)S(1)}, bf16[128,1024]{1,0:T(8,128)(2,1)S(1)}, u32[]{:S(2)}, u32[]{:S(2)}) collective-permute-start(bf16[128,1024]{1,0:T(8,128)(2,1)S(1)} %shard_map.122.refs_0_.refs_4_), channel_id=1, source_target_pairs={{0,8},{1,9},{2,10},{3,11},{4,12},{5,13},{6,14},{7,15},{8,0},{9,1},... | collective-permute-start | bytes 786440 | tf_op jit(solution)/shard_map/ppermute | solution.py:346
  25.8 2.7 %collective-permute-start.3 = (bf16[128,1024]{1,0:T(8,128)(2,1)S(1)}, bf16[128,1024]{1,0:T(8,128)(2,1)S(1)}, u32[]{:S(2)}, u32[]{:S(2)}) collective-permute-start(bf16[128,1024]{1,0:T(8,128)(2,1)S(1)} %shard_map.122.refs_0_.refs_4_), channel_id=1, source_target_pairs={{0,16},{1,17},{2,18},{3,19},{4,20},{5,21},{6,22},{7,23},{8,24},{9,... | collective-permute-start | bytes 786440 | tf_op jit(solution)/shard_map/ppermute | solution.py:346
  28.5 0.0 copy-done.2
  28.5 11.7 %shard_map.123.refs_0_.refs_4_ = bf16[128,1024]{1,0:T(8,128)(2,1)S(1)} custom-call(bf16[128,1024]{1,0:T(8,128)(2,1)S(1)} %copy-done.2, bf16[1024,8192]{1,0:T(8,128)(2,1)} %w_in.3, bf16[8192,1024]{1,0:T(8,128)(2,1)} %w_out.3, bf16[128,1024]{1,0:T(8,128)(2,1)S(1)} %shard_map.122.refs_0_.refs_4_), custom_call_target="tpu_custom_call" | custom-call | flops 1 | bytes 1 | tf_op jit(solution)/shard_map/pallas_call | solution.py:66
  40.2 0.0 collective-permute-done.4.refs_5_.refs_1_
  40.2 0.0 collective-permute-done.3.refs_6_.refs_2_
  40.2 0.0 collective-permute-done.refs_13_.refs_9_
  40.2 0.0 collective-permute-done.1.refs_14_.refs_10_
  40.2 0.0 collective-permute-done.2.refs_15_.refs_11_
  40.2 1.2 %collective-permute-start.5 = (bf16[128,1024]{1,0:T(8,128)(2,1)S(1)}, bf16[128,1024]{1,0:T(8,128)(2,1)S(1)}, u32[]{:S(2)}, u32[]{:S(2)}) collective-permute-start(bf16[128,1024]{1,0:T(8,128)(2,1)S(1)} %shard_map.123.refs_0_.refs_4_), channel_id=1, source_target_pairs={{0,2},{1,3},{2,0},{3,1},{4,6},{5,7},{6,4},{7,5},{8,10},{9,11},{10,... | collective-permute-start | bytes 786440 | tf_op jit(solution)/shard_map/ppermute | solution.py:346
  41.5 0.5 collective-permute-start.8
  42.0 1.7 %collective-permute-start.7 = (bf16[128,1024]{1,0:T(8,128)(2,1)S(1)}, bf16[128,1024]{1,0:T(8,128)(2,1)S(1)}, u32[]{:S(2)}, u32[]{:S(2)}) collective-permute-start(bf16[128,1024]{1,0:T(8,128)(2,1)S(1)} %shard_map.123.refs_0_.refs_4_), channel_id=1, source_target_pairs={{0,6},{1,7},{2,4},{3,5},{4,2},{5,3},{6,0},{7,1},{8,14},{9,15},{10,... | collective-permute-start | bytes 786440 | tf_op jit(solution)/shard_map/ppermute | solution.py:346
  43.6 0.5 collective-permute-start.6
  44.1 5.4 %collective-permute-done.5.refs_1_.refs_5_ = bf16[128,1024]{1,0:T(8,128)(2,1)S(1)} collective-permute-done((bf16[128,1024]{1,0:T(8,128)(2,1)S(1)}, bf16[128,1024]{1,0:T(8,128)(2,1)S(1)}, u32[]{:S(2)}, u32[]{:S(2)}) %collective-permute-start.5) | collective-permute-done | bytes 262176 | tf_op jit(solution)/shard_map/ppermute | solution.py:346
  49.5 0.0 collective-permute-start.9
  49.5 0.5 collective-permute-start.10
  50.1 0.0 collective-permute-done.8.refs_7_.refs_3_
  50.1 0.0 collective-permute-start.12
  50.1 3.0 %collective-permute-done.7.refs_3_.refs_7_ = bf16[128,1024]{1,0:T(8,128)(2,1)S(1)} collective-permute-done((bf16[128,1024]{1,0:T(8,128)(2,1)S(1)}, bf16[128,1024]{1,0:T(8,128)(2,1)S(1)}, u32[]{:S(2)}, u32[]{:S(2)}) %collective-permute-start.7) | collective-permute-done | bytes 262176 | tf_op jit(solution)/shard_map/ppermute | solution.py:346
  53.1 0.0 collective-permute-start.11
  53.1 1.8 %collective-permute-done.6.refs_2_.refs_6_ = bf16[128,1024]{1,0:T(8,128)(2,1)S(1)} collective-permute-done((bf16[128,1024]{1,0:T(8,128)(2,1)S(1)}, bf16[128,1024]{1,0:T(8,128)(2,1)S(1)}, u32[]{:S(2)}, u32[]{:S(2)}) %collective-permute-start.6) | collective-permute-done | bytes 262176 | tf_op jit(solution)/shard_map/ppermute | solution.py:346
  54.9 0.0 collective-permute-done.12.refs_11_.refs_7_
  54.9 0.0 collective-permute-done.9.refs_8_.refs_4_
  54.9 0.0 collective-permute-done.10.refs_9_.refs_5_
  54.9 0.0 collective-permute-done.11.refs_10_.refs_6_
  54.9 4.6 %shard_map.124 = (f32[1024,512]{1,0:T(8,128)S(1)}, f32[4,4,128]{2,1,0:T(4,128)S(1)}) custom-call(bf16[128,1024]{1,0:T(8,128)(2,1)S(1)} %shard_map.123.refs_0_.refs_4_, bf16[128,1024]{1,0:T(8,128)(2,1)S(1)} %collective-permute-done.5.refs_1_.refs_5_, bf16[128,1024]{1,0:T(8,128)(2,1)S(1)} %collective-permute-done.6.refs_2_.refs_6_, ...), custom_call_target="tpu_custom_call" | custom-call | flops 1073741824 | bytes 4194304 | tf_op jit(solution)/shard_map/pallas_call | solution.py:183
  59.4 1.5 %collective-permute-start.15 = (f32[4,4,128]{2,1,0:T(4,128)S(1)}, f32[4,4,128]{2,1,0:T(4,128)S(1)}, u32[]{:S(2)}, u32[]{:S(2)}) collective-permute-start(f32[4,4,128]{2,1,0:T(4,128)S(1)} %get-tuple-element.48.refs_0_), channel_id=1, source_target_pairs={{0,6},{1,7},{2,4},{3,5},{4,2},{5,3},{6,0},{7,1},{8,14},{9,15},{10,... | collective-permute-start | bytes 24584 | tf_op jit(solution)/shard_map/ppermute | solution.py:346
  60.9 1.7 %collective-permute-start.14 = (f32[4,4,128]{2,1,0:T(4,128)S(1)}, f32[4,4,128]{2,1,0:T(4,128)S(1)}, u32[]{:S(2)}, u32[]{:S(2)}) collective-permute-start(f32[4,4,128]{2,1,0:T(4,128)S(1)} %get-tuple-element.48.refs_0_), channel_id=1, source_target_pairs={{0,4},{1,5},{2,6},{3,7},{4,0},{5,1},{6,2},{7,3},{8,12},{9,13},{10,... | collective-permute-start | bytes 24584 | tf_op jit(solution)/shard_map/ppermute | solution.py:346
  62.6 0.4 collective-permute-start.13
  63.0 1.1 %collective-permute-done.15.refs_3_ = f32[4,4,128]{2,1,0:T(4,128)S(1)} collective-permute-done((f32[4,4,128]{2,1,0:T(4,128)S(1)}, f32[4,4,128]{2,1,0:T(4,128)S(1)}, u32[]{:S(2)}, u32[]{:S(2)}) %collective-permute-start.15) | collective-permute-done | bytes 8224 | tf_op jit(solution)/shard_map/ppermute | solution.py:346
  64.1 0.5 collective-permute-done.14.refs_2_
  64.6 1.7 %collective-permute-done.13.refs_1_ = f32[4,4,128]{2,1,0:T(4,128)S(1)} collective-permute-done((f32[4,4,128]{2,1,0:T(4,128)S(1)}, f32[4,4,128]{2,1,0:T(4,128)S(1)}, u32[]{:S(2)}, u32[]{:S(2)}) %collective-permute-start.13) | collective-permute-done | bytes 8224 | tf_op jit(solution)/shard_map/ppermute | solution.py:346
  66.3 1.5 %shard_map.125 = (bf16[1024,512]{1,0:T(8,128)(2,1)S(1)}, f32[1,128]{1,0:T(1,128)}, bf16[512,1024]{1,0:T(8,128)(2,1)S(1)}) custom-call(f32[4,4,128]{2,1,0:T(4,128)S(1)} %get-tuple-element.48.refs_0_, f32[4,4,128]{2,1,0:T(4,128)S(1)} %collective-permute-done.13.refs_1_, f32[4,4,128]{2,1,0:T(4,128)S(1)} %collective-permute-done.14.refs_2_, ...), custom_call_target="tpu_custom_call" | custom-call | flops 536870912 | bytes 4194304 | tf_op jit(solution)/shard_map/pallas_call | solution.py:236
  67.8 0.1 collective-permute-start.16
  67.9 0.8 shard_map.126.near
  68.7 1.8 %collective-permute-done.16.far = bf16[512,1024]{1,0:T(8,128)(2,1)S(1)} collective-permute-done((bf16[512,1024]{1,0:T(8,128)(2,1)S(1)}, bf16[512,1024]{1,0:T(8,128)(2,1)S(1)}, u32[]{:S(2)}, u32[]{:S(2)}) %collective-permute-start.16) | collective-permute-done | bytes 1048608 | tf_op jit(solution)/shard_map/ppermute | solution.py:346
  70.5 0.2 shard_map.127
  70.7 1.3 %collective-permute-start.20 = (bf16[128,1024]{1,0:T(8,128)(2,1)S(1)}, bf16[128,1024]{1,0:T(8,128)(2,1)S(1)}, u32[]{:S(2)}, u32[]{:S(2)}) collective-permute-start(bf16[128,1024]{1,0:T(8,128)(2,1)S(1)} %get-tuple-element.58), channel_id=1, source_target_pairs={{0,24},{1,25},{2,26},{3,27},{4,28},{5,29},{6,30},{7,31},{8,16},{9,... | collective-permute-start | bytes 786440 | tf_op jit(solution)/shard_map/ppermute | solution.py:346
  72.0 1.5 %collective-permute-start.21 = (bf16[128,1024]{1,0:T(8,128)(2,1)S(1)}, bf16[128,1024]{1,0:T(8,128)(2,1)S(1)}, u32[]{:S(2)}, u32[]{:S(2)}) collective-permute-start(bf16[128,1024]{1,0:T(8,128)(2,1)S(1)} %get-tuple-element.59), channel_id=1, source_target_pairs={{0,16},{1,17},{2,18},{3,19},{4,20},{5,21},{6,22},{7,23},{8,24},{9,... | collective-permute-start | bytes 786440 | tf_op jit(solution)/shard_map/ppermute | solution.py:346
  73.4 1.7 %collective-permute-start.22 = (bf16[128,1024]{1,0:T(8,128)(2,1)S(1)}, bf16[128,1024]{1,0:T(8,128)(2,1)S(1)}, u32[]{:S(2)}, u32[]{:S(2)}) collective-permute-start(bf16[128,1024]{1,0:T(8,128)(2,1)S(1)} %get-tuple-element.60), channel_id=1, source_target_pairs={{0,8},{1,9},{2,10},{3,11},{4,12},{5,13},{6,14},{7,15},{8,0},{9,1},... | collective-permute-start | bytes 786440 | tf_op jit(solution)/shard_map/ppermute | solution.py:346
  75.1 1.5 %shard_map.128 = (f32[128,1024]{1,0:T(8,128)S(1)}, bf16[128,1024]{1,0:T(8,128)(2,1)S(1)}, bf16[128,1024]{1,0:T(8,128)(2,1)S(1)}, bf16[128,1024]{1,0:T(8,128)(2,1)S(1)}) custom-call(bf16[1024,512]{1,0:T(8,128)(2,1)S(1)} %get-tuple-element.51.grads, bf16[128,1024]{1,0:T(8,128)(2,1)S(1)} %shard_map.122.refs_0_.refs_4_, ...), custom_call_target="tpu_custom_call" | custom-call | flops 1073741824 | bytes 2097152 | tf_op jit(solution)/shard_map/pallas_call | solution.py:302
  76.7 0.4 collective-permute-start.17
  77.1 0.8 collective-permute-start.18
  77.9 3.9 %collective-permute-done.20 = bf16[128,1024]{1,0:T(8,128)(2,1)S(1)} collective-permute-done((bf16[128,1024]{1,0:T(8,128)(2,1)S(1)}, bf16[128,1024]{1,0:T(8,128)(2,1)S(1)}, u32[]{:S(2)}, u32[]{:S(2)}) %collective-permute-start.20) | collective-permute-done | bytes 262176 | tf_op jit(solution)/shard_map/ppermute | solution.py:346
  81.8 0.6 collective-permute-start.19
  82.4 14.1 %collective-permute-done.21 = bf16[128,1024]{1,0:T(8,128)(2,1)S(1)} collective-permute-done((bf16[128,1024]{1,0:T(8,128)(2,1)S(1)}, bf16[128,1024]{1,0:T(8,128)(2,1)S(1)}, u32[]{:S(2)}, u32[]{:S(2)}) %collective-permute-start.21) | collective-permute-done | bytes 262176 | tf_op jit(solution)/shard_map/ppermute | solution.py:346
  96.6 0.0 collective-permute-done.22
  96.6 0.9 convert_add_fusion
  97.5 0.0 collective-permute-done.17
  97.5 0.0 collective-permute-done.18
  97.5 0.0 collective-permute-done.19
  97.5 0.9 convert_add_fusion.1
  (2 shorter events, 0.0 us)
Async XLA Ops:
  1.3 1.2 %copy-start = (f32[128,2048]{1,0:T(8,128)S(1)}, f32[128,2048]{1,0:T(8,128)}, u32[]{:S(2)}) copy-start(f32[128,2048]{1,0:T(8,128)} %teacher.1) | copy-start | bytes 3145732
  2.5 0.7 copy-start.3
  3.2 0.7 copy-start.4
  6.1 34.1 %collective-permute-start = (f32[8,128,128]{2,1,0:T(8,128)S(1)}, f32[8,128,128]{2,1,0:T(8,128)S(1)}, u32[]{:S(2)}, u32[]{:S(2)}) collective-permute-start(f32[8,128,128]{2,1,0:T(8,128)S(1)} %get-tuple-element.33), channel_id=1, source_target_pairs={{0,2},{1,3},{2,0},{3,1},{4,6},{5,7},{6,4},{7,5},{8,10},{9,11},{10,... | collective-permute-start | bytes 1572872 | tf_op jit(solution)/shard_map/ppermute | solution.py:346
  9.0 31.2 %collective-permute-start.1 = (f32[8,128,128]{2,1,0:T(8,128)S(1)}, f32[8,128,128]{2,1,0:T(8,128)S(1)}, u32[]{:S(2)}, u32[]{:S(2)}) collective-permute-start(f32[8,128,128]{2,1,0:T(8,128)S(1)} %get-tuple-element.34), channel_id=1, source_target_pairs={{0,4},{1,5},{2,6},{3,7},{4,0},{5,1},{6,2},{7,3},{8,12},{9,13},{10,... | collective-permute-start | bytes 1572872 | tf_op jit(solution)/shard_map/ppermute | solution.py:346
  10.6 29.6 %collective-permute-start.2 = (f32[8,128,128]{2,1,0:T(8,128)S(1)}, f32[8,128,128]{2,1,0:T(8,128)S(1)}, u32[]{:S(2)}, u32[]{:S(2)}) collective-permute-start(f32[8,128,128]{2,1,0:T(8,128)S(1)} %get-tuple-element.35), channel_id=1, source_target_pairs={{0,6},{1,7},{2,4},{3,5},{4,2},{5,3},{6,0},{7,1},{8,14},{9,15},{10,... | collective-permute-start | bytes 1572872 | tf_op jit(solution)/shard_map/ppermute | solution.py:346
  10.7 1.0 copy-start.1
  11.6 16.9 %copy-start.2 = (bf16[128,1024]{1,0:T(8,128)(2,1)S(1)}, bf16[128,1024]{1,0:T(8,128)(2,1)}, u32[]{:S(2)}) copy-start(bf16[128,1024]{1,0:T(8,128)(2,1)} %feats.3) | copy-start | bytes 786436
  23.3 16.9 %collective-permute-start.4 = (bf16[128,1024]{1,0:T(8,128)(2,1)S(1)}, bf16[128,1024]{1,0:T(8,128)(2,1)S(1)}, u32[]{:S(2)}, u32[]{:S(2)}) collective-permute-start(bf16[128,1024]{1,0:T(8,128)(2,1)S(1)} %shard_map.122.refs_0_.refs_4_), channel_id=1, source_target_pairs={{0,8},{1,9},{2,10},{3,11},{4,12},{5,13},{6,14},{7,15},{8,0},{9,1},... | collective-permute-start | bytes 786440 | tf_op jit(solution)/shard_map/ppermute | solution.py:346
  25.8 14.4 %collective-permute-start.3 = (bf16[128,1024]{1,0:T(8,128)(2,1)S(1)}, bf16[128,1024]{1,0:T(8,128)(2,1)S(1)}, u32[]{:S(2)}, u32[]{:S(2)}) collective-permute-start(bf16[128,1024]{1,0:T(8,128)(2,1)S(1)} %shard_map.122.refs_0_.refs_4_), channel_id=1, source_target_pairs={{0,16},{1,17},{2,18},{3,19},{4,20},{5,21},{6,22},{7,23},{8,24},{9,... | collective-permute-start | bytes 786440 | tf_op jit(solution)/shard_map/ppermute | solution.py:346
  40.2 9.3 %collective-permute-start.5 = (bf16[128,1024]{1,0:T(8,128)(2,1)S(1)}, bf16[128,1024]{1,0:T(8,128)(2,1)S(1)}, u32[]{:S(2)}, u32[]{:S(2)}) collective-permute-start(bf16[128,1024]{1,0:T(8,128)(2,1)S(1)} %shard_map.123.refs_0_.refs_4_), channel_id=1, source_target_pairs={{0,2},{1,3},{2,0},{3,1},{4,6},{5,7},{6,4},{7,5},{8,10},{9,11},{10,... | collective-permute-start | bytes 786440 | tf_op jit(solution)/shard_map/ppermute | solution.py:346
  41.5 8.6 %collective-permute-start.8 = (bf16[128,1024]{1,0:T(8,128)(2,1)S(1)}, bf16[128,1024]{1,0:T(8,128)(2,1)S(1)}, u32[]{:S(2)}, u32[]{:S(2)}) collective-permute-start(bf16[128,1024]{1,0:T(8,128)(2,1)S(1)} %collective-permute-done.3.refs_6_.refs_2_), channel_id=1, source_target_pairs={{0,8},{1,9},{2,10},{3,11},{4,12},{5,13},{6,14},{7,15},{8,0},{9,1},... | collective-permute-start | bytes 786440 | tf_op jit(solution)/shard_map/ppermute | solution.py:346
  42.0 11.1 %collective-permute-start.7 = (bf16[128,1024]{1,0:T(8,128)(2,1)S(1)}, bf16[128,1024]{1,0:T(8,128)(2,1)S(1)}, u32[]{:S(2)}, u32[]{:S(2)}) collective-permute-start(bf16[128,1024]{1,0:T(8,128)(2,1)S(1)} %shard_map.123.refs_0_.refs_4_), channel_id=1, source_target_pairs={{0,6},{1,7},{2,4},{3,5},{4,2},{5,3},{6,0},{7,1},{8,14},{9,15},{10,... | collective-permute-start | bytes 786440 | tf_op jit(solution)/shard_map/ppermute | solution.py:346
  43.6 11.2 %collective-permute-start.6 = (bf16[128,1024]{1,0:T(8,128)(2,1)S(1)}, bf16[128,1024]{1,0:T(8,128)(2,1)S(1)}, u32[]{:S(2)}, u32[]{:S(2)}) collective-permute-start(bf16[128,1024]{1,0:T(8,128)(2,1)S(1)} %shard_map.123.refs_0_.refs_4_), channel_id=1, source_target_pairs={{0,4},{1,5},{2,6},{3,7},{4,0},{5,1},{6,2},{7,3},{8,12},{9,13},{10,... | collective-permute-start | bytes 786440 | tf_op jit(solution)/shard_map/ppermute | solution.py:346
  49.5 5.3 %collective-permute-start.9 = (bf16[128,1024]{1,0:T(8,128)(2,1)S(1)}, bf16[128,1024]{1,0:T(8,128)(2,1)S(1)}, u32[]{:S(2)}, u32[]{:S(2)}) collective-permute-start(bf16[128,1024]{1,0:T(8,128)(2,1)S(1)} %shard_map.122.refs_0_.refs_4_), channel_id=1, source_target_pairs={{0,1},{1,0},{2,3},{3,2},{4,5},{5,4},{6,7},{7,6},{8,9},{9,8},{10,11... | collective-permute-start | bytes 786440 | tf_op jit(solution)/shard_map/ppermute | solution.py:346
  49.5 5.3 %collective-permute-start.10 = (bf16[128,1024]{1,0:T(8,128)(2,1)S(1)}, bf16[128,1024]{1,0:T(8,128)(2,1)S(1)}, u32[]{:S(2)}, u32[]{:S(2)}) collective-permute-start(bf16[128,1024]{1,0:T(8,128)(2,1)S(1)} %collective-permute-done.4.refs_5_.refs_1_), channel_id=1, source_target_pairs={{0,1},{1,0},{2,3},{3,2},{4,5},{5,4},{6,7},{7,6},{8,9},{9,8},{10,11... | collective-permute-start | bytes 786440 | tf_op jit(solution)/shard_map/ppermute | solution.py:346
  50.1 4.8 %collective-permute-start.12 = (bf16[128,1024]{1,0:T(8,128)(2,1)S(1)}, bf16[128,1024]{1,0:T(8,128)(2,1)S(1)}, u32[]{:S(2)}, u32[]{:S(2)}) collective-permute-start(bf16[128,1024]{1,0:T(8,128)(2,1)S(1)} %collective-permute-done.8.refs_7_.refs_3_), channel_id=1, source_target_pairs={{0,1},{1,0},{2,3},{3,2},{4,5},{5,4},{6,7},{7,6},{8,9},{9,8},{10,11... | collective-permute-start | bytes 786440 | tf_op jit(solution)/shard_map/ppermute | solution.py:346
  53.1 1.8 %collective-permute-start.11 = (bf16[128,1024]{1,0:T(8,128)(2,1)S(1)}, bf16[128,1024]{1,0:T(8,128)(2,1)S(1)}, u32[]{:S(2)}, u32[]{:S(2)}) collective-permute-start(bf16[128,1024]{1,0:T(8,128)(2,1)S(1)} %collective-permute-done.3.refs_6_.refs_2_), channel_id=1, source_target_pairs={{0,1},{1,0},{2,3},{3,2},{4,5},{5,4},{6,7},{7,6},{8,9},{9,8},{10,11... | collective-permute-start | bytes 786440 | tf_op jit(solution)/shard_map/ppermute | solution.py:346
  59.4 4.6 %collective-permute-start.15 = (f32[4,4,128]{2,1,0:T(4,128)S(1)}, f32[4,4,128]{2,1,0:T(4,128)S(1)}, u32[]{:S(2)}, u32[]{:S(2)}) collective-permute-start(f32[4,4,128]{2,1,0:T(4,128)S(1)} %get-tuple-element.48.refs_0_), channel_id=1, source_target_pairs={{0,6},{1,7},{2,4},{3,5},{4,2},{5,3},{6,0},{7,1},{8,14},{9,15},{10,... | collective-permute-start | bytes 24584 | tf_op jit(solution)/shard_map/ppermute | solution.py:346
  60.9 3.7 %collective-permute-start.14 = (f32[4,4,128]{2,1,0:T(4,128)S(1)}, f32[4,4,128]{2,1,0:T(4,128)S(1)}, u32[]{:S(2)}, u32[]{:S(2)}) collective-permute-start(f32[4,4,128]{2,1,0:T(4,128)S(1)} %get-tuple-element.48.refs_0_), channel_id=1, source_target_pairs={{0,4},{1,5},{2,6},{3,7},{4,0},{5,1},{6,2},{7,3},{8,12},{9,13},{10,... | collective-permute-start | bytes 24584 | tf_op jit(solution)/shard_map/ppermute | solution.py:346
  62.6 3.7 %collective-permute-start.13 = (f32[4,4,128]{2,1,0:T(4,128)S(1)}, f32[4,4,128]{2,1,0:T(4,128)S(1)}, u32[]{:S(2)}, u32[]{:S(2)}) collective-permute-start(f32[4,4,128]{2,1,0:T(4,128)S(1)} %get-tuple-element.48.refs_0_), channel_id=1, source_target_pairs={{0,2},{1,3},{2,0},{3,1},{4,6},{5,7},{6,4},{7,5},{8,10},{9,11},{10,... | collective-permute-start | bytes 24584 | tf_op jit(solution)/shard_map/ppermute | solution.py:346
  67.8 2.7 %collective-permute-start.16 = (bf16[512,1024]{1,0:T(8,128)(2,1)S(1)}, bf16[512,1024]{1,0:T(8,128)(2,1)S(1)}, u32[]{:S(2)}, u32[]{:S(2)}) collective-permute-start(bf16[512,1024]{1,0:T(8,128)(2,1)S(1)} %get-tuple-element.52), channel_id=1, source_target_pairs={{0,1},{1,0},{2,3},{3,2},{4,5},{5,4},{6,7},{7,6},{8,9},{9,8},{10,11... | collective-permute-start | bytes 3145736 | tf_op jit(solution)/shard_map/ppermute | solution.py:346
  70.7 11.2 %collective-permute-start.20 = (bf16[128,1024]{1,0:T(8,128)(2,1)S(1)}, bf16[128,1024]{1,0:T(8,128)(2,1)S(1)}, u32[]{:S(2)}, u32[]{:S(2)}) collective-permute-start(bf16[128,1024]{1,0:T(8,128)(2,1)S(1)} %get-tuple-element.58), channel_id=1, source_target_pairs={{0,24},{1,25},{2,26},{3,27},{4,28},{5,29},{6,30},{7,31},{8,16},{9,... | collective-permute-start | bytes 786440 | tf_op jit(solution)/shard_map/ppermute | solution.py:346
  72.0 24.6 %collective-permute-start.21 = (bf16[128,1024]{1,0:T(8,128)(2,1)S(1)}, bf16[128,1024]{1,0:T(8,128)(2,1)S(1)}, u32[]{:S(2)}, u32[]{:S(2)}) collective-permute-start(bf16[128,1024]{1,0:T(8,128)(2,1)S(1)} %get-tuple-element.59), channel_id=1, source_target_pairs={{0,16},{1,17},{2,18},{3,19},{4,20},{5,21},{6,22},{7,23},{8,24},{9,... | collective-permute-start | bytes 786440 | tf_op jit(solution)/shard_map/ppermute | solution.py:346
  73.4 23.2 %collective-permute-start.22 = (bf16[128,1024]{1,0:T(8,128)(2,1)S(1)}, bf16[128,1024]{1,0:T(8,128)(2,1)S(1)}, u32[]{:S(2)}, u32[]{:S(2)}) collective-permute-start(bf16[128,1024]{1,0:T(8,128)(2,1)S(1)} %get-tuple-element.60), channel_id=1, source_target_pairs={{0,8},{1,9},{2,10},{3,11},{4,12},{5,13},{6,14},{7,15},{8,0},{9,1},... | collective-permute-start | bytes 786440 | tf_op jit(solution)/shard_map/ppermute | solution.py:346
  76.7 20.9 %collective-permute-start.17 = (bf16[128,1024]{1,0:T(8,128)(2,1)S(1)}, bf16[128,1024]{1,0:T(8,128)(2,1)S(1)}, u32[]{:S(2)}, u32[]{:S(2)}) collective-permute-start(bf16[128,1024]{1,0:T(8,128)(2,1)S(1)} %get-tuple-element.55), channel_id=1, source_target_pairs={{0,2},{1,3},{2,0},{3,1},{4,6},{5,7},{6,4},{7,5},{8,10},{9,11},{10,... | collective-permute-start | bytes 786440 | tf_op jit(solution)/shard_map/ppermute | solution.py:346
  77.1 20.4 %collective-permute-start.18 = (bf16[128,1024]{1,0:T(8,128)(2,1)S(1)}, bf16[128,1024]{1,0:T(8,128)(2,1)S(1)}, u32[]{:S(2)}, u32[]{:S(2)}) collective-permute-start(bf16[128,1024]{1,0:T(8,128)(2,1)S(1)} %get-tuple-element.56), channel_id=1, source_target_pairs={{0,4},{1,5},{2,6},{3,7},{4,0},{5,1},{6,2},{7,3},{8,12},{9,13},{10,... | collective-permute-start | bytes 786440 | tf_op jit(solution)/shard_map/ppermute | solution.py:346
  81.8 15.7 %collective-permute-start.19 = (bf16[128,1024]{1,0:T(8,128)(2,1)S(1)}, bf16[128,1024]{1,0:T(8,128)(2,1)S(1)}, u32[]{:S(2)}, u32[]{:S(2)}) collective-permute-start(bf16[128,1024]{1,0:T(8,128)(2,1)S(1)} %get-tuple-element.57), channel_id=1, source_target_pairs={{0,6},{1,7},{2,4},{3,5},{4,2},{5,3},{6,0},{7,1},{8,14},{9,15},{10,... | collective-permute-start | bytes 786440 | tf_op jit(solution)/shard_map/ppermute | solution.py:346

commit v4 on v3

--- a/solution.py
+++ b/solution.py
@@ -323,7 +323,7 @@
         functools.partial(join_body, planes),
         in_specs=[VMEM, VMEM],
         out_specs=[VMEM] * planes,
-        out_shape=[struct((rows, width), jnp.bfloat16 if i else jnp.float32) for i in range(planes)],
+        out_shape=[struct((rows, width), jnp.bfloat16 if i % 2 else jnp.float32) for i in range(planes)],
         compiler_params=params(24),
         cost_estimate=cost(near.size, 8 * near.size),
     )(near, far)
@@ -369,7 +369,12 @@
     grads, divergence, far = far_parts(factor, [stats] + over_columns(stats), users, logs, weights)
     far = swap(far, 1)
     parts = join(planes, near_part(grads, users), far)
-    sent = [swap(parts[z], z * cols * CORES) for z in range(planes - 1, 0, -1)]
+    hop = cols * CORES
+    if planes == 4:
+        merged = (parts[2] + swap(parts[3], hop).astype(jnp.float32)).astype(jnp.bfloat16)
+        sent = [swap(merged, 2 * hop), swap(parts[1], hop)]
+    else:
+        sent = [swap(parts[z].astype(jnp.bfloat16), z * hop) for z in range(planes - 1, 0, -1)]
     own, *others = user_parts(cols, grads, items, [parts[0]])
     arrived = [swap(part, (c + 1) * CORES) for c, part in enumerate(others)]
 

time: 98.7 us -> 94.5 us (0.957)
  waiting for transfers between devices: 33.4 us -> 29.4 us
    ppermute x23, waiting for transfers between devices: 33.4 us -> 29.4 us  [swap(): return lax.ppermute(array, 'dp', [(i, i ^ apart) for i in range(count)])]
  transfers between devices with their start and end apart: 23 -> 23, of which waited for: 9 -> 11; matrix products, arithmetic and copies ran while one was open for 1% -> 1% of each run, Pallas kernels for 26% -> 27%
where the time goes in v4:
time: 94.5 us; the launch traced here: 94.3 us
  Pallas kernels  34.3 us (36%)
  waiting for transfers between devices  29.4 us (31%)
  starting transfers between devices  23.8 us (25%)
  local copies, waits for them, and re-layouts  3.48 us (4%)
  other arithmetic  1.86 us (2%)
  between operations  1.44 us (2%)
    ppermute x23, waiting for transfers between devices, swap(): return lax.ppermute(array, 'dp', [(i, i ^ apart) for i in range(count)])  29.4 us
    ppermute x23, starting transfers between devices, swap(): return lax.ppermute(array, 'dp', [(i, i ^ apart) for i in range(count)])  23.8 us
    pallas_call x2, Pallas kernels, tower(): pl.pallas_call(functools.partial(tower_body, chunks), in_specs=[VMEM, ANY...  23.4 us
    pallas_call x1, Pallas kernels, scores(): pl.pallas_call(functools.partial(score_body, cols, places, scale), in_spe...  4.56 us
    unnamed x10, local copies, waits for them, and re-layouts  3.48 us
    pallas_call x1, Pallas kernels, spread_teacher(): pl.pallas_call(functools.partial(teacher_body, cols, planes), in_specs=[S...  2.39 us
  transfers between devices with their start and end apart: 23, of which 11 were waited for; matrix products, arithmetic and copies ran while one was open for 1% of the time, Pallas kernels for 27%

profile of v4, /device:TPU:0, one launch (start us, length us, event | category | flops | bytes accessed | tf_op | source)
XLA Modules:
  0.0 94.3 jit_solution(18336334895488878311)
XLA Ops:
  1.3 0.0 copy-start
  1.3 1.2 %copy-done = f32[128,2048]{1,0:T(8,128)S(1)} copy-done((f32[128,2048]{1,0:T(8,128)S(1)}, f32[128,2048]{1,0:T(8,128)}, u32[]{:S(2)}) %copy-start) | copy-done | bytes 1048600
  2.5 0.0 copy-start.3
  2.5 0.7 copy-done.3
  3.2 0.7 copy-done.4
  3.8 2.4 %shard_map.121 = (f32[8,128,128]{2,1,0:T(8,128)S(1)}, f32[8,128,128]{2,1,0:T(8,128)S(1)}, f32[8,128,128]{2,1,0:T(8,128)S(1)}, f32[8,128,128]{2,1,0:T(8,128)S(1)}) custom-call(s32[1]{0:T(128)} %bitcast.me, s32[1,16]{1,0:T(1,128)S(1)} %copy-done.3, s32[1]{0:T(128)S(6)} %copy.13.count, s32[32]{0:T(128)S(1)} %copy-done.4, f32[128,2048]{1,0:T(8,128)S(1)} %copy-done), custom_call_target="tpu_custom_call" | custom-call | flops 262144 | bytes 2097152 | tf_op jit(solution)/shard_map/pallas_call | solution.py:121
  6.2 3.2 %collective-permute-start = (f32[8,128,128]{2,1,0:T(8,128)S(1)}, f32[8,128,128]{2,1,0:T(8,128)S(1)}, u32[]{:S(2)}, u32[]{:S(2)}) collective-permute-start(f32[8,128,128]{2,1,0:T(8,128)S(1)} %get-tuple-element.33), channel_id=1, source_target_pairs={{0,2},{1,3},{2,0},{3,1},{4,6},{5,7},{6,4},{7,5},{8,10},{9,11},{10,... | collective-permute-start | bytes 1572872 | tf_op jit(solution)/shard_map/ppermute | solution.py:346
  9.4 1.3 %collective-permute-start.1 = (f32[8,128,128]{2,1,0:T(8,128)S(1)}, f32[8,128,128]{2,1,0:T(8,128)S(1)}, u32[]{:S(2)}, u32[]{:S(2)}) collective-permute-start(f32[8,128,128]{2,1,0:T(8,128)S(1)} %get-tuple-element.34), channel_id=1, source_target_pairs={{0,4},{1,5},{2,6},{3,7},{4,0},{5,1},{6,2},{7,3},{8,12},{9,13},{10,... | collective-permute-start | bytes 1572872 | tf_op jit(solution)/shard_map/ppermute | solution.py:346
  10.7 0.2 collective-permute-start.2
  11.0 0.9 %copy-done.1 = bf16[128,1024]{1,0:T(8,128)(2,1)S(1)} copy-done((bf16[128,1024]{1,0:T(8,128)(2,1)S(1)}, bf16[128,1024]{1,0:T(8,128)(2,1)}, u32[]{:S(2)}) %copy-start.1) | copy-done | bytes 262168
  11.9 11.7 %shard_map.122.refs_0_.refs_4_ = bf16[128,1024]{1,0:T(8,128)(2,1)S(1)} custom-call(bf16[128,1024]{1,0:T(8,128)(2,1)S(1)} %copy-done.1, bf16[1024,8192]{1,0:T(8,128)(2,1)} %w_in.2, bf16[8192,1024]{1,0:T(8,128)(2,1)} %w_out.2, f32[8,128,128]{2,1,0:T(8,128)S(1)} %get-tuple-element.44.refs_0_.refs_12_.refs_8_), custom_call_target="tpu_custom_call" | custom-call | flops 1 | bytes 1 | tf_op jit(solution)/shard_map/pallas_call | solution.py:66
  23.6 2.1 %collective-permute-start.4 = (bf16[128,1024]{1,0:T(8,128)(2,1)S(1)}, bf16[128,1024]{1,0:T(8,128)(2,1)S(1)}, u32[]{:S(2)}, u32[]{:S(2)}) collective-permute-start(bf16[128,1024]{1,0:T(8,128)(2,1)S(1)} %shard_map.122.refs_0_.refs_4_), channel_id=1, source_target_pairs={{0,8},{1,9},{2,10},{3,11},{4,12},{5,13},{6,14},{7,15},{8,0},{9,1},... | collective-permute-start | bytes 786440 | tf_op jit(solution)/shard_map/ppermute | solution.py:346
  25.7 2.3 %collective-permute-start.3 = (bf16[128,1024]{1,0:T(8,128)(2,1)S(1)}, bf16[128,1024]{1,0:T(8,128)(2,1)S(1)}, u32[]{:S(2)}, u32[]{:S(2)}) collective-permute-start(bf16[128,1024]{1,0:T(8,128)(2,1)S(1)} %shard_map.122.refs_0_.refs_4_), channel_id=1, source_target_pairs={{0,16},{1,17},{2,18},{3,19},{4,20},{5,21},{6,22},{7,23},{8,24},{9,... | collective-permute-start | bytes 786440 | tf_op jit(solution)/shard_map/ppermute | solution.py:346
  28.0 0.0 copy-done.2
  28.0 11.7 %shard_map.123.refs_0_.refs_4_ = bf16[128,1024]{1,0:T(8,128)(2,1)S(1)} custom-call(bf16[128,1024]{1,0:T(8,128)(2,1)S(1)} %copy-done.2, bf16[1024,8192]{1,0:T(8,128)(2,1)} %w_in.3, bf16[8192,1024]{1,0:T(8,128)(2,1)} %w_out.3, bf16[128,1024]{1,0:T(8,128)(2,1)S(1)} %shard_map.122.refs_0_.refs_4_), custom_call_target="tpu_custom_call" | custom-call | flops 1 | bytes 1 | tf_op jit(solution)/shard_map/pallas_call | solution.py:66
  39.7 0.0 collective-permute-done.4.refs_5_.refs_1_
  39.7 0.0 collective-permute-done.3.refs_6_.refs_2_
  39.7 0.0 collective-permute-done.refs_13_.refs_9_
  39.7 0.0 collective-permute-done.1.refs_14_.refs_10_
  39.8 0.0 collective-permute-done.2.refs_15_.refs_11_
  39.8 2.0 %collective-permute-start.5 = (bf16[128,1024]{1,0:T(8,128)(2,1)S(1)}, bf16[128,1024]{1,0:T(8,128)(2,1)S(1)}, u32[]{:S(2)}, u32[]{:S(2)}) collective-permute-start(bf16[128,1024]{1,0:T(8,128)(2,1)S(1)} %shard_map.123.refs_0_.refs_4_), channel_id=1, source_target_pairs={{0,2},{1,3},{2,0},{3,1},{4,6},{5,7},{6,4},{7,5},{8,10},{9,11},{10,... | collective-permute-start | bytes 786440 | tf_op jit(solution)/shard_map/ppermute | solution.py:346
  41.8 0.1 collective-permute-start.8
  41.9 1.7 %collective-permute-start.7 = (bf16[128,1024]{1,0:T(8,128)(2,1)S(1)}, bf16[128,1024]{1,0:T(8,128)(2,1)S(1)}, u32[]{:S(2)}, u32[]{:S(2)}) collective-permute-start(bf16[128,1024]{1,0:T(8,128)(2,1)S(1)} %shard_map.123.refs_0_.refs_4_), channel_id=1, source_target_pairs={{0,6},{1,7},{2,4},{3,5},{4,2},{5,3},{6,0},{7,1},{8,14},{9,15},{10,... | collective-permute-start | bytes 786440 | tf_op jit(solution)/shard_map/ppermute | solution.py:346
  43.5 0.2 collective-permute-start.6
  43.7 5.4 %collective-permute-done.5.refs_1_.refs_5_ = bf16[128,1024]{1,0:T(8,128)(2,1)S(1)} collective-permute-done((bf16[128,1024]{1,0:T(8,128)(2,1)S(1)}, bf16[128,1024]{1,0:T(8,128)(2,1)S(1)}, u32[]{:S(2)}, u32[]{:S(2)}) %collective-permute-start.5) | collective-permute-done | bytes 262176 | tf_op jit(solution)/shard_map/ppermute | solution.py:346
  49.1 0.0 collective-permute-start.9
  49.1 0.5 collective-permute-start.10
  49.6 0.0 collective-permute-done.8.refs_7_.refs_3_
  49.6 0.0 collective-permute-start.12
  49.6 3.8 %collective-permute-done.7.refs_3_.refs_7_ = bf16[128,1024]{1,0:T(8,128)(2,1)S(1)} collective-permute-done((bf16[128,1024]{1,0:T(8,128)(2,1)S(1)}, bf16[128,1024]{1,0:T(8,128)(2,1)S(1)}, u32[]{:S(2)}, u32[]{:S(2)}) %collective-permute-start.7) | collective-permute-done | bytes 262176 | tf_op jit(solution)/shard_map/ppermute | solution.py:346
  53.4 0.0 collective-permute-start.11
  53.4 1.6 %collective-permute-done.6.refs_2_.refs_6_ = bf16[128,1024]{1,0:T(8,128)(2,1)S(1)} collective-permute-done((bf16[128,1024]{1,0:T(8,128)(2,1)S(1)}, bf16[128,1024]{1,0:T(8,128)(2,1)S(1)}, u32[]{:S(2)}, u32[]{:S(2)}) %collective-permute-start.6) | collective-permute-done | bytes 262176 | tf_op jit(solution)/shard_map/ppermute | solution.py:346
  55.0 0.0 collective-permute-done.12.refs_11_.refs_7_
  55.0 0.0 collective-permute-done.9.refs_8_.refs_4_
  55.0 0.0 collective-permute-done.10.refs_9_.refs_5_
  55.0 0.0 collective-permute-done.11.refs_10_.refs_6_
  55.0 4.6 %shard_map.124 = (f32[1024,512]{1,0:T(8,128)S(1)}, f32[4,4,128]{2,1,0:T(4,128)S(1)}) custom-call(bf16[128,1024]{1,0:T(8,128)(2,1)S(1)} %shard_map.123.refs_0_.refs_4_, bf16[128,1024]{1,0:T(8,128)(2,1)S(1)} %collective-permute-done.5.refs_1_.refs_5_, bf16[128,1024]{1,0:T(8,128)(2,1)S(1)} %collective-permute-done.6.refs_2_.refs_6_, ...), custom_call_target="tpu_custom_call" | custom-call | flops 1073741824 | bytes 4194304 | tf_op jit(solution)/shard_map/pallas_call | solution.py:183
  59.6 1.5 %collective-permute-start.15 = (f32[4,4,128]{2,1,0:T(4,128)S(1)}, f32[4,4,128]{2,1,0:T(4,128)S(1)}, u32[]{:S(2)}, u32[]{:S(2)}) collective-permute-start(f32[4,4,128]{2,1,0:T(4,128)S(1)} %get-tuple-element.48.refs_0_), channel_id=1, source_target_pairs={{0,6},{1,7},{2,4},{3,5},{4,2},{5,3},{6,0},{7,1},{8,14},{9,15},{10,... | collective-permute-start | bytes 24584 | tf_op jit(solution)/shard_map/ppermute | solution.py:346
  61.1 1.7 %collective-permute-start.14 = (f32[4,4,128]{2,1,0:T(4,128)S(1)}, f32[4,4,128]{2,1,0:T(4,128)S(1)}, u32[]{:S(2)}, u32[]{:S(2)}) collective-permute-start(f32[4,4,128]{2,1,0:T(4,128)S(1)} %get-tuple-element.48.refs_0_), channel_id=1, source_target_pairs={{0,4},{1,5},{2,6},{3,7},{4,0},{5,1},{6,2},{7,3},{8,12},{9,13},{10,... | collective-permute-start | bytes 24584 | tf_op jit(solution)/shard_map/ppermute | solution.py:346
  62.8 0.4 collective-permute-start.13
  63.1 1.1 %collective-permute-done.15.refs_3_ = f32[4,4,128]{2,1,0:T(4,128)S(1)} collective-permute-done((f32[4,4,128]{2,1,0:T(4,128)S(1)}, f32[4,4,128]{2,1,0:T(4,128)S(1)}, u32[]{:S(2)}, u32[]{:S(2)}) %collective-permute-start.15) | collective-permute-done | bytes 8224 | tf_op jit(solution)/shard_map/ppermute | solution.py:346
  64.2 0.5 collective-permute-done.14.refs_2_
  64.7 1.7 %collective-permute-done.13.refs_1_ = f32[4,4,128]{2,1,0:T(4,128)S(1)} collective-permute-done((f32[4,4,128]{2,1,0:T(4,128)S(1)}, f32[4,4,128]{2,1,0:T(4,128)S(1)}, u32[]{:S(2)}, u32[]{:S(2)}) %collective-permute-start.13) | collective-permute-done | bytes 8224 | tf_op jit(solution)/shard_map/ppermute | solution.py:346
  66.4 1.5 %shard_map.125 = (bf16[1024,512]{1,0:T(8,128)(2,1)S(1)}, f32[1,128]{1,0:T(1,128)}, bf16[512,1024]{1,0:T(8,128)(2,1)S(1)}) custom-call(f32[4,4,128]{2,1,0:T(4,128)S(1)} %get-tuple-element.48.refs_0_, f32[4,4,128]{2,1,0:T(4,128)S(1)} %collective-permute-done.13.refs_1_, f32[4,4,128]{2,1,0:T(4,128)S(1)} %collective-permute-done.14.refs_2_, ...), custom_call_target="tpu_custom_call" | custom-call | flops 536870912 | bytes 4194304 | tf_op jit(solution)/shard_map/pallas_call | solution.py:236
  67.9 0.1 collective-permute-start.16
  68.0 0.8 shard_map.126.near
  68.8 1.8 %collective-permute-done.16.far = bf16[512,1024]{1,0:T(8,128)(2,1)S(1)} collective-permute-done((bf16[512,1024]{1,0:T(8,128)(2,1)S(1)}, bf16[512,1024]{1,0:T(8,128)(2,1)S(1)}, u32[]{:S(2)}, u32[]{:S(2)}) %collective-permute-start.16) | collective-permute-done | bytes 1048608 | tf_op jit(solution)/shard_map/ppermute | solution.py:346
  70.7 0.2 shard_map.127
  70.8 1.5 %collective-permute-start.20 = (bf16[128,1024]{1,0:T(8,128)(2,1)S(1)}, bf16[128,1024]{1,0:T(8,128)(2,1)S(1)}, u32[]{:S(2)}, u32[]{:S(2)}) collective-permute-start(bf16[128,1024]{1,0:T(8,128)(2,1)S(1)} %get-tuple-element.59), channel_id=1, source_target_pairs={{0,8},{1,9},{2,10},{3,11},{4,12},{5,13},{6,14},{7,15},{8,0},{9,1},... | collective-permute-start | bytes 786440 | tf_op jit(solution)/shard_map/ppermute | solution.py:346
  72.3 1.5 %shard_map.128 = (f32[128,1024]{1,0:T(8,128)S(1)}, bf16[128,1024]{1,0:T(8,128)(2,1)S(1)}, bf16[128,1024]{1,0:T(8,128)(2,1)S(1)}, bf16[128,1024]{1,0:T(8,128)(2,1)S(1)}) custom-call(bf16[1024,512]{1,0:T(8,128)(2,1)S(1)} %get-tuple-element.51.grads, bf16[128,1024]{1,0:T(8,128)(2,1)S(1)} %shard_map.122.refs_0_.refs_4_, ...), custom_call_target="tpu_custom_call" | custom-call | flops 1073741824 | bytes 2097152 | tf_op jit(solution)/shard_map/pallas_call | solution.py:302
  73.9 0.5 collective-permute-start.17
  74.3 0.5 collective-permute-start.18
  74.8 2.6 %collective-permute-start.19 = (bf16[128,1024]{1,0:T(8,128)(2,1)S(1)}, bf16[128,1024]{1,0:T(8,128)(2,1)S(1)}, u32[]{:S(2)}, u32[]{:S(2)}) collective-permute-start(bf16[128,1024]{1,0:T(8,128)(2,1)S(1)} %get-tuple-element.57), channel_id=1, source_target_pairs={{0,6},{1,7},{2,4},{3,5},{4,2},{5,3},{6,0},{7,1},{8,14},{9,15},{10,... | collective-permute-start | bytes 786440 | tf_op jit(solution)/shard_map/ppermute | solution.py:346
  77.4 0.6 collective-permute-start.22
  78.0 1.4 %collective-permute-done.20 = bf16[128,1024]{1,0:T(8,128)(2,1)S(1)} collective-permute-done((bf16[128,1024]{1,0:T(8,128)(2,1)S(1)}, bf16[128,1024]{1,0:T(8,128)(2,1)S(1)}, u32[]{:S(2)}, u32[]{:S(2)}) %collective-permute-start.20) | collective-permute-done | bytes 262176 | tf_op jit(solution)/shard_map/ppermute | solution.py:346
  79.4 0.1 add_convert_fusion
  79.4 1.0 %collective-permute-start.21 = (bf16[128,1024]{1,0:T(8,128)(2,1)S(1)}, bf16[128,1024]{1,0:T(8,128)(2,1)S(1)}, u32[]{:S(2)}, u32[]{:S(2)}) collective-permute-start(bf16[128,1024]{1,0:T(8,128)(2,1)S(1)} %add_convert_fusion), channel_id=1, source_target_pairs={{0,16},{1,17},{2,18},{3,19},{4,20},{5,21},{6,22},{7,23},{8,24},{9,... | collective-permute-start | bytes 786440 | tf_op jit(solution)/shard_map/ppermute | solution.py:346
  80.4 2.7 %collective-permute-done.17 = bf16[128,1024]{1,0:T(8,128)(2,1)S(1)} collective-permute-done((bf16[128,1024]{1,0:T(8,128)(2,1)S(1)}, bf16[128,1024]{1,0:T(8,128)(2,1)S(1)}, u32[]{:S(2)}, u32[]{:S(2)}) %collective-permute-start.17) | collective-permute-done | bytes 262176 | tf_op jit(solution)/shard_map/ppermute | solution.py:346
  83.1 4.6 %collective-permute-done.18 = bf16[128,1024]{1,0:T(8,128)(2,1)S(1)} collective-permute-done((bf16[128,1024]{1,0:T(8,128)(2,1)S(1)}, bf16[128,1024]{1,0:T(8,128)(2,1)S(1)}, u32[]{:S(2)}, u32[]{:S(2)}) %collective-permute-start.18) | collective-permute-done | bytes 262176 | tf_op jit(solution)/shard_map/ppermute | solution.py:346
  87.7 0.0 collective-permute-done.19
  87.7 0.9 convert_add_fusion.1
  88.7 0.0 collective-permute-done.22
  88.7 4.8 %collective-permute-done.21 = bf16[128,1024]{1,0:T(8,128)(2,1)S(1)} collective-permute-done((bf16[128,1024]{1,0:T(8,128)(2,1)S(1)}, bf16[128,1024]{1,0:T(8,128)(2,1)S(1)}, u32[]{:S(2)}, u32[]{:S(2)}) %collective-permute-start.21) | collective-permute-done | bytes 262176 | tf_op jit(solution)/shard_map/ppermute | solution.py:346
  93.4 0.9 convert_add_fusion
  (3 shorter events, 0.0 us)
Async XLA Ops:
  1.3 1.2 %copy-start = (f32[128,2048]{1,0:T(8,128)S(1)}, f32[128,2048]{1,0:T(8,128)}, u32[]{:S(2)}) copy-start(f32[128,2048]{1,0:T(8,128)} %teacher.1) | copy-start | bytes 3145732
  2.5 0.7 copy-start.3
  3.2 0.7 copy-start.4
  6.2 33.5 %collective-permute-start = (f32[8,128,128]{2,1,0:T(8,128)S(1)}, f32[8,128,128]{2,1,0:T(8,128)S(1)}, u32[]{:S(2)}, u32[]{:S(2)}) collective-permute-start(f32[8,128,128]{2,1,0:T(8,128)S(1)} %get-tuple-element.33), channel_id=1, source_target_pairs={{0,2},{1,3},{2,0},{3,1},{4,6},{5,7},{6,4},{7,5},{8,10},{9,11},{10,... | collective-permute-start | bytes 1572872 | tf_op jit(solution)/shard_map/ppermute | solution.py:346
  9.4 30.3 %collective-permute-start.1 = (f32[8,128,128]{2,1,0:T(8,128)S(1)}, f32[8,128,128]{2,1,0:T(8,128)S(1)}, u32[]{:S(2)}, u32[]{:S(2)}) collective-permute-start(f32[8,128,128]{2,1,0:T(8,128)S(1)} %get-tuple-element.34), channel_id=1, source_target_pairs={{0,4},{1,5},{2,6},{3,7},{4,0},{5,1},{6,2},{7,3},{8,12},{9,13},{10,... | collective-permute-start | bytes 1572872 | tf_op jit(solution)/shard_map/ppermute | solution.py:346
  10.7 29.0 %collective-permute-start.2 = (f32[8,128,128]{2,1,0:T(8,128)S(1)}, f32[8,128,128]{2,1,0:T(8,128)S(1)}, u32[]{:S(2)}, u32[]{:S(2)}) collective-permute-start(f32[8,128,128]{2,1,0:T(8,128)S(1)} %get-tuple-element.35), channel_id=1, source_target_pairs={{0,6},{1,7},{2,4},{3,5},{4,2},{5,3},{6,0},{7,1},{8,14},{9,15},{10,... | collective-permute-start | bytes 1572872 | tf_op jit(solution)/shard_map/ppermute | solution.py:346
  11.0 0.9 %copy-start.1 = (bf16[128,1024]{1,0:T(8,128)(2,1)S(1)}, bf16[128,1024]{1,0:T(8,128)(2,1)}, u32[]{:S(2)}) copy-start(bf16[128,1024]{1,0:T(8,128)(2,1)} %feats.2) | copy-start | bytes 786436
  11.9 16.1 %copy-start.2 = (bf16[128,1024]{1,0:T(8,128)(2,1)S(1)}, bf16[128,1024]{1,0:T(8,128)(2,1)}, u32[]{:S(2)}) copy-start(bf16[128,1024]{1,0:T(8,128)(2,1)} %feats.3) | copy-start | bytes 786436
  23.6 16.1 %collective-permute-start.4 = (bf16[128,1024]{1,0:T(8,128)(2,1)S(1)}, bf16[128,1024]{1,0:T(8,128)(2,1)S(1)}, u32[]{:S(2)}, u32[]{:S(2)}) collective-permute-start(bf16[128,1024]{1,0:T(8,128)(2,1)S(1)} %shard_map.122.refs_0_.refs_4_), channel_id=1, source_target_pairs={{0,8},{1,9},{2,10},{3,11},{4,12},{5,13},{6,14},{7,15},{8,0},{9,1},... | collective-permute-start | bytes 786440 | tf_op jit(solution)/shard_map/ppermute | solution.py:346
  25.7 14.0 %collective-permute-start.3 = (bf16[128,1024]{1,0:T(8,128)(2,1)S(1)}, bf16[128,1024]{1,0:T(8,128)(2,1)S(1)}, u32[]{:S(2)}, u32[]{:S(2)}) collective-permute-start(bf16[128,1024]{1,0:T(8,128)(2,1)S(1)} %shard_map.122.refs_0_.refs_4_), channel_id=1, source_target_pairs={{0,16},{1,17},{2,18},{3,19},{4,20},{5,21},{6,22},{7,23},{8,24},{9,... | collective-permute-start | bytes 786440 | tf_op jit(solution)/shard_map/ppermute | solution.py:346
  39.8 9.3 %collective-permute-start.5 = (bf16[128,1024]{1,0:T(8,128)(2,1)S(1)}, bf16[128,1024]{1,0:T(8,128)(2,1)S(1)}, u32[]{:S(2)}, u32[]{:S(2)}) collective-permute-start(bf16[128,1024]{1,0:T(8,128)(2,1)S(1)} %shard_map.123.refs_0_.refs_4_), channel_id=1, source_target_pairs={{0,2},{1,3},{2,0},{3,1},{4,6},{5,7},{6,4},{7,5},{8,10},{9,11},{10,... | collective-permute-start | bytes 786440 | tf_op jit(solution)/shard_map/ppermute | solution.py:346
  41.8 7.8 %collective-permute-start.8 = (bf16[128,1024]{1,0:T(8,128)(2,1)S(1)}, bf16[128,1024]{1,0:T(8,128)(2,1)S(1)}, u32[]{:S(2)}, u32[]{:S(2)}) collective-permute-start(bf16[128,1024]{1,0:T(8,128)(2,1)S(1)} %collective-permute-done.3.refs_6_.refs_2_), channel_id=1, source_target_pairs={{0,8},{1,9},{2,10},{3,11},{4,12},{5,13},{6,14},{7,15},{8,0},{9,1},... | collective-permute-start | bytes 786440 | tf_op jit(solution)/shard_map/ppermute | solution.py:346
  41.9 11.5 %collective-permute-start.7 = (bf16[128,1024]{1,0:T(8,128)(2,1)S(1)}, bf16[128,1024]{1,0:T(8,128)(2,1)S(1)}, u32[]{:S(2)}, u32[]{:S(2)}) collective-permute-start(bf16[128,1024]{1,0:T(8,128)(2,1)S(1)} %shard_map.123.refs_0_.refs_4_), channel_id=1, source_target_pairs={{0,6},{1,7},{2,4},{3,5},{4,2},{5,3},{6,0},{7,1},{8,14},{9,15},{10,... | collective-permute-start | bytes 786440 | tf_op jit(solution)/shard_map/ppermute | solution.py:346
  43.5 11.5 %collective-permute-start.6 = (bf16[128,1024]{1,0:T(8,128)(2,1)S(1)}, bf16[128,1024]{1,0:T(8,128)(2,1)S(1)}, u32[]{:S(2)}, u32[]{:S(2)}) collective-permute-start(bf16[128,1024]{1,0:T(8,128)(2,1)S(1)} %shard_map.123.refs_0_.refs_4_), channel_id=1, source_target_pairs={{0,4},{1,5},{2,6},{3,7},{4,0},{5,1},{6,2},{7,3},{8,12},{9,13},{10,... | collective-permute-start | bytes 786440 | tf_op jit(solution)/shard_map/ppermute | solution.py:346
  49.1 5.9 %collective-permute-start.9 = (bf16[128,1024]{1,0:T(8,128)(2,1)S(1)}, bf16[128,1024]{1,0:T(8,128)(2,1)S(1)}, u32[]{:S(2)}, u32[]{:S(2)}) collective-permute-start(bf16[128,1024]{1,0:T(8,128)(2,1)S(1)} %shard_map.122.refs_0_.refs_4_), channel_id=1, source_target_pairs={{0,1},{1,0},{2,3},{3,2},{4,5},{5,4},{6,7},{7,6},{8,9},{9,8},{10,11... | collective-permute-start | bytes 786440 | tf_op jit(solution)/shard_map/ppermute | solution.py:346
  49.1 5.9 %collective-permute-start.10 = (bf16[128,1024]{1,0:T(8,128)(2,1)S(1)}, bf16[128,1024]{1,0:T(8,128)(2,1)S(1)}, u32[]{:S(2)}, u32[]{:S(2)}) collective-permute-start(bf16[128,1024]{1,0:T(8,128)(2,1)S(1)} %collective-permute-done.4.refs_5_.refs_1_), channel_id=1, source_target_pairs={{0,1},{1,0},{2,3},{3,2},{4,5},{5,4},{6,7},{7,6},{8,9},{9,8},{10,11... | collective-permute-start | bytes 786440 | tf_op jit(solution)/shard_map/ppermute | solution.py:346
  49.6 5.4 %collective-permute-start.12 = (bf16[128,1024]{1,0:T(8,128)(2,1)S(1)}, bf16[128,1024]{1,0:T(8,128)(2,1)S(1)}, u32[]{:S(2)}, u32[]{:S(2)}) collective-permute-start(bf16[128,1024]{1,0:T(8,128)(2,1)S(1)} %collective-permute-done.8.refs_7_.refs_3_), channel_id=1, source_target_pairs={{0,1},{1,0},{2,3},{3,2},{4,5},{5,4},{6,7},{7,6},{8,9},{9,8},{10,11... | collective-permute-start | bytes 786440 | tf_op jit(solution)/shard_map/ppermute | solution.py:346
  53.4 1.6 %collective-permute-start.11 = (bf16[128,1024]{1,0:T(8,128)(2,1)S(1)}, bf16[128,1024]{1,0:T(8,128)(2,1)S(1)}, u32[]{:S(2)}, u32[]{:S(2)}) collective-permute-start(bf16[128,1024]{1,0:T(8,128)(2,1)S(1)} %collective-permute-done.3.refs_6_.refs_2_), channel_id=1, source_target_pairs={{0,1},{1,0},{2,3},{3,2},{4,5},{5,4},{6,7},{7,6},{8,9},{9,8},{10,11... | collective-permute-start | bytes 786440 | tf_op jit(solution)/shard_map/ppermute | solution.py:346
  59.6 4.6 %collective-permute-start.15 = (f32[4,4,128]{2,1,0:T(4,128)S(1)}, f32[4,4,128]{2,1,0:T(4,128)S(1)}, u32[]{:S(2)}, u32[]{:S(2)}) collective-permute-start(f32[4,4,128]{2,1,0:T(4,128)S(1)} %get-tuple-element.48.refs_0_), channel_id=1, source_target_pairs={{0,6},{1,7},{2,4},{3,5},{4,2},{5,3},{6,0},{7,1},{8,14},{9,15},{10,... | collective-permute-start | bytes 24584 | tf_op jit(solution)/shard_map/ppermute | solution.py:346
  61.1 3.7 %collective-permute-start.14 = (f32[4,4,128]{2,1,0:T(4,128)S(1)}, f32[4,4,128]{2,1,0:T(4,128)S(1)}, u32[]{:S(2)}, u32[]{:S(2)}) collective-permute-start(f32[4,4,128]{2,1,0:T(4,128)S(1)} %get-tuple-element.48.refs_0_), channel_id=1, source_target_pairs={{0,4},{1,5},{2,6},{3,7},{4,0},{5,1},{6,2},{7,3},{8,12},{9,13},{10,... | collective-permute-start | bytes 24584 | tf_op jit(solution)/shard_map/ppermute | solution.py:346
  62.8 3.7 %collective-permute-start.13 = (f32[4,4,128]{2,1,0:T(4,128)S(1)}, f32[4,4,128]{2,1,0:T(4,128)S(1)}, u32[]{:S(2)}, u32[]{:S(2)}) collective-permute-start(f32[4,4,128]{2,1,0:T(4,128)S(1)} %get-tuple-element.48.refs_0_), channel_id=1, source_target_pairs={{0,2},{1,3},{2,0},{3,1},{4,6},{5,7},{6,4},{7,5},{8,10},{9,11},{10,... | collective-permute-start | bytes 24584 | tf_op jit(solution)/shard_map/ppermute | solution.py:346
  67.9 2.7 %collective-permute-start.16 = (bf16[512,1024]{1,0:T(8,128)(2,1)S(1)}, bf16[512,1024]{1,0:T(8,128)(2,1)S(1)}, u32[]{:S(2)}, u32[]{:S(2)}) collective-permute-start(bf16[512,1024]{1,0:T(8,128)(2,1)S(1)} %get-tuple-element.52), channel_id=1, source_target_pairs={{0,1},{1,0},{2,3},{3,2},{4,5},{5,4},{6,7},{7,6},{8,9},{9,8},{10,11... | collective-permute-start | bytes 3145736 | tf_op jit(solution)/shard_map/ppermute | solution.py:346
  70.8 8.6 %collective-permute-start.20 = (bf16[128,1024]{1,0:T(8,128)(2,1)S(1)}, bf16[128,1024]{1,0:T(8,128)(2,1)S(1)}, u32[]{:S(2)}, u32[]{:S(2)}) collective-permute-start(bf16[128,1024]{1,0:T(8,128)(2,1)S(1)} %get-tuple-element.59), channel_id=1, source_target_pairs={{0,8},{1,9},{2,10},{3,11},{4,12},{5,13},{6,14},{7,15},{8,0},{9,1},... | collective-permute-start | bytes 786440 | tf_op jit(solution)/shard_map/ppermute | solution.py:346
  73.9 9.3 %collective-permute-start.17 = (bf16[128,1024]{1,0:T(8,128)(2,1)S(1)}, bf16[128,1024]{1,0:T(8,128)(2,1)S(1)}, u32[]{:S(2)}, u32[]{:S(2)}) collective-permute-start(bf16[128,1024]{1,0:T(8,128)(2,1)S(1)} %get-tuple-element.55), channel_id=1, source_target_pairs={{0,2},{1,3},{2,0},{3,1},{4,6},{5,7},{6,4},{7,5},{8,10},{9,11},{10,... | collective-permute-start | bytes 786440 | tf_op jit(solution)/shard_map/ppermute | solution.py:346
  74.3 13.4 %collective-permute-start.18 = (bf16[128,1024]{1,0:T(8,128)(2,1)S(1)}, bf16[128,1024]{1,0:T(8,128)(2,1)S(1)}, u32[]{:S(2)}, u32[]{:S(2)}) collective-permute-start(bf16[128,1024]{1,0:T(8,128)(2,1)S(1)} %get-tuple-element.56), channel_id=1, source_target_pairs={{0,4},{1,5},{2,6},{3,7},{4,0},{5,1},{6,2},{7,3},{8,12},{9,13},{10,... | collective-permute-start | bytes 786440 | tf_op jit(solution)/shard_map/ppermute | solution.py:346
  74.8 12.9 %collective-permute-start.19 = (bf16[128,1024]{1,0:T(8,128)(2,1)S(1)}, bf16[128,1024]{1,0:T(8,128)(2,1)S(1)}, u32[]{:S(2)}, u32[]{:S(2)}) collective-permute-start(bf16[128,1024]{1,0:T(8,128)(2,1)S(1)} %get-tuple-element.57), channel_id=1, source_target_pairs={{0,6},{1,7},{2,4},{3,5},{4,2},{5,3},{6,0},{7,1},{8,14},{9,15},{10,... | collective-permute-start | bytes 786440 | tf_op jit(solution)/shard_map/ppermute | solution.py:346
  77.4 11.3 %collective-permute-start.22 = (bf16[128,1024]{1,0:T(8,128)(2,1)S(1)}, bf16[128,1024]{1,0:T(8,128)(2,1)S(1)}, u32[]{:S(2)}, u32[]{:S(2)}) collective-permute-start(bf16[128,1024]{1,0:T(8,128)(2,1)S(1)} %get-tuple-element.60), channel_id=1, source_target_pairs={{0,8},{1,9},{2,10},{3,11},{4,12},{5,13},{6,14},{7,15},{8,0},{9,1},... | collective-permute-start | bytes 786440 | tf_op jit(solution)/shard_map/ppermute | solution.py:346
  79.4 14.0 %collective-permute-start.21 = (bf16[128,1024]{1,0:T(8,128)(2,1)S(1)}, bf16[128,1024]{1,0:T(8,128)(2,1)S(1)}, u32[]{:S(2)}, u32[]{:S(2)}) collective-permute-start(bf16[128,1024]{1,0:T(8,128)(2,1)S(1)} %add_convert_fusion), channel_id=1, source_target_pairs={{0,16},{1,17},{2,18},{3,19},{4,20},{5,21},{6,22},{7,23},{8,24},{9,... | collective-permute-start | bytes 786440 | tf_op jit(solution)/shard_map/ppermute | solution.py:346

commit v5 on v4

--- a/solution.py
+++ b/solution.py
@@ -9,8 +9,8 @@
 from jax.sharding import PartitionSpec as P
 
 CORES = 2
-DEAD = -1e30
-LIVE = -1e29
+LOWEST = -1e30
+DEAD = -1.0
 MIB = 1 << 20
 ANY = pl.BlockSpec(memory_space=pl.ANY)
 VMEM = pl.BlockSpec(memory_space=pltpu.VMEM)
@@ -89,15 +89,18 @@
 
 
 def teacher_body(cols, planes, me, cands, count, owner, teacher, *refs):
-    outs, dense, sems = refs[:cols], refs[cols], refs[cols + 1]
+    outs, (entropy, dense, sems) = refs[:cols], refs[cols:]
     rows = teacher.shape[0]
     slots = cands.shape[1]
     live = count[0]
     logits = teacher[...]
     usable = lax.broadcasted_iota(jnp.int32, logits.shape, 1) < live * rows
     shifted = logits - jnp.max(jnp.where(usable, logits, -jnp.inf), axis=1, keepdims=True)
-    norm = jnp.sum(jnp.where(usable, jnp.exp(shifted), 0.0), axis=1, keepdims=True)
-    log_p = shifted - jnp.log(norm)
+    weight = jnp.where(usable, jnp.exp(shifted), 0.0)
+    norm = jnp.sum(weight, axis=1, keepdims=True)
+    prob = weight / norm
+    log_sum = jnp.sum(jnp.where(usable, prob * (shifted - jnp.log(norm)), 0.0), axis=1, keepdims=True)
+    entropy[...] = jnp.broadcast_to(log_sum, (rows, rows)).T[:1]
     dense[...] = jnp.full(dense.shape, DEAD, jnp.float32)
     for k in range(slots):
 
@@ -106,7 +109,7 @@
             apart = owner[cands[0, k]] ^ me[0]
             inside = apart % (CORES * cols)
             place = (inside % CORES) * planes + apart // (CORES * cols)
-            dense[inside // CORES, place] = log_p[:, k * rows : (k + 1) * rows].T
+            dense[inside // CORES, place] = prob[:, k * rows : (k + 1) * rows].T
 
     copies = [pltpu.make_async_copy(dense.at[i], outs[i], sems.at[i]) for i in range(cols)]
     for copy in copies:
@@ -121,8 +124,8 @@
     return pl.pallas_call(
         functools.partial(teacher_body, cols, planes),
         in_specs=[SMEM, SMEM, SMEM, SMEM, VMEM],
-        out_specs=[ANY] * cols,
-        out_shape=[struct((places, rows, rows), jnp.float32)] * cols,
+        out_specs=[ANY] * cols + [VMEM],
+        out_shape=[struct((places, rows, rows), jnp.float32)] * cols + [struct((1, rows), jnp.float32)],
         scratch_shapes=[
             pltpu.VMEM((cols, places, rows, rows), jnp.float32),
             pltpu.SemaphoreType.DMA((cols,)),
@@ -132,84 +135,62 @@
     )(me, cands, count, owner, teacher)
 
 
-def loads_of(sources, target, sems):
+def lay(sources, target):
     rows = sources[0].shape[0]
-    return [
-        pltpu.make_async_copy(source, target.at[pl.ds(i * rows, rows)], sems.at[i]) for i, source in enumerate(sources)
-    ]
+    for i, source in enumerate(sources):
+        target[i * rows : (i + 1) * rows] = source[...]
 
 
 def score_body(cols, places, scale, *refs):
-    users, items, logs = refs[:cols], refs[cols : cols + places], refs[cols + places : 2 * cols + places]
-    weights, stats, all_users, all_items, all_logs, user_sems, item_sems, log_sems = refs[2 * cols + places :]
+    users, items, probs = refs[:cols], refs[cols : cols + places], refs[cols + places : 2 * cols + places]
+    weights, stats, all_users, all_items = refs[2 * cols + places :]
     rows = users[0].shape[0]
-    load_users = loads_of(users, all_users, user_sems)
-    load_items = loads_of(items, all_items, item_sems)
-    load_logs = loads_of(logs, all_logs, log_sems)
-    for copy in load_items + load_users + load_logs:
-        copy.start()
-    for copy in load_items:
-        copy.wait()
-    step = 2 if cols % 2 == 0 else 1
-    for first in range(0, cols, step):
-        for i in range(first, first + step):
-            load_users[i].wait()
-        both = scale * lax.dot_general(
-            all_items[...],
-            all_users[first * rows : (first + step) * rows],
-            (((1,), (1,)), ((), ())),
-            preferred_element_type=jnp.float32,
+    lay(users, all_users)
+    step = 2 if places % 2 == 0 else 1
+    for first in range(0, places, step):
+        lay(items[first : first + step], all_items)
+        weights[first * rows : (first + step) * rows] = scale * lax.dot_general(
+            all_items[: step * rows], all_users[...], (((1,), (1,)), ((), ())), preferred_element_type=jnp.float32
         )
-        for j in range(step):
-            i = first + j
-            load_logs[i].wait()
-            score = both[:, j * rows : (j + 1) * rows]
-            log_p = all_logs[i * places : (i + 1) * places].reshape(places * rows, rows)
-            live = log_p > LIVE
-            top = jnp.max(jnp.where(live, score, DEAD), axis=0, keepdims=True)
-            shifted = score - top
-            weight = jnp.where(live, jnp.exp(shifted), 0.0)
-            prob = jnp.exp(log_p)
-            weights[:, i * rows : (i + 1) * rows] = weight
-            stats[0, i : i + 1, :] = top
-            stats[1, i : i + 1, :] = jnp.sum(weight, axis=0, keepdims=True)
-            stats[2, i : i + 1, :] = jnp.sum(jnp.where(live, prob * (log_p - shifted), 0.0), axis=0, keepdims=True)
-            stats[3, i : i + 1, :] = jnp.sum(prob, axis=0, keepdims=True)
-
-
-def scores(scale, users, items, logs):
+    for i in range(cols):
+        lanes = slice(i * rows, (i + 1) * rows)
+        score = weights[:, lanes]
+        prob = probs[i][...].reshape(places * rows, rows)
+        live = prob >= 0.0
+        prob = jnp.maximum(prob, 0.0)
+        top = jnp.max(jnp.where(live, score, LOWEST), axis=0, keepdims=True)
+        shifted = jnp.where(live, score - top, 0.0)
+        weight = jnp.where(live, jnp.exp(shifted), 0.0)
+        weights[:, lanes] = weight
+        stats[0, i : i + 1, :] = top
+        stats[1, i : i + 1, :] = jnp.sum(weight, axis=0, keepdims=True)
+        stats[2, i : i + 1, :] = jnp.sum(prob * shifted, axis=0, keepdims=True)
+        stats[3, i : i + 1, :] = jnp.sum(prob, axis=0, keepdims=True)
+
+
+def scores(scale, users, items, probs):
     cols, places = len(users), len(items)
     rows, width = users[0].shape
     return pl.pallas_call(
         functools.partial(score_body, cols, places, scale),
-        in_specs=[ANY] * (2 * cols + places),
+        in_specs=[VMEM] * (2 * cols + places),
         out_specs=[VMEM, VMEM],
         out_shape=[
             struct((places * rows, cols * rows), jnp.float32),
             struct((4, cols, rows), jnp.float32),
         ],
-        scratch_shapes=[
-            pltpu.VMEM((cols * rows, width), jnp.bfloat16),
-            pltpu.VMEM((places * rows, width), jnp.bfloat16),
-            pltpu.VMEM((cols * places, rows, rows), jnp.float32),
-            pltpu.SemaphoreType.DMA((cols,)),
-            pltpu.SemaphoreType.DMA((places,)),
-            pltpu.SemaphoreType.DMA((cols,)),
-        ],
+        scratch_shapes=[pltpu.VMEM((cols * rows, width), jnp.bfloat16), pltpu.VMEM((2 * rows, width), jnp.bfloat16)],
         compiler_params=params(32),
         cost_estimate=cost(2 * cols * places * rows * rows * width, 8 * cols * places * rows * rows),
-    )(*users, *items, *logs)
-
-
-def far_body(cols, places, factor, *refs):
-    stats, users, logs = refs[:cols], refs[cols : 2 * cols], refs[2 * cols : 3 * cols]
+    )(*users, *items, *probs)
+
+
+def far_body(cols, places, factor, entropy, *refs):
+    stats, users, probs = refs[:cols], refs[cols : 2 * cols], refs[2 * cols : 3 * cols]
     weights, grads, divergence, far = refs[3 * cols : 3 * cols + 4]
-    all_users, all_logs, user_sems, log_sems = refs[3 * cols + 4 :]
+    all_users = refs[3 * cols + 4]
     rows = users[0].shape[0]
-    load_users = loads_of(users, all_users, user_sems)
-    load_logs = loads_of(logs, all_logs, log_sems)
-    for copy in load_logs + load_users:
-        copy.start()
+    lay(users, all_users)
     for i in range(cols):
         tops = [stats[j][0, i ^ j : (i ^ j) + 1, :] for j in range(cols)]
         sums = [stats[j][1, i ^ j : (i ^ j) + 1, :] for j in range(cols)]
@@ -218,48 +199,36 @@
         ratio = jnp.exp(tops[0] - top) / norm
         if i == 0:
             lse = top + jnp.log(norm)
-            terms = [stats[j][2, j : j + 1, :] + stats[j][3, j : j + 1, :] * (lse - tops[j]) for j in range(cols)]
-            divergence[...] = functools.reduce(jnp.add, terms)
-        load_logs[i].wait()
-        prob = jnp.exp(all_logs[i * places : (i + 1) * places].reshape(places * rows, rows))
+            terms = [stats[j][3, j : j + 1, :] * (lse - tops[j]) - stats[j][2, j : j + 1, :] for j in range(cols)]
+            divergence[...] = functools.reduce(jnp.add, terms, entropy[...])
+        prob = jnp.maximum(probs[i][...].reshape(places * rows, rows), 0.0)
         lanes = slice(i * rows, (i + 1) * rows)
         grads[:, lanes] = (factor * (weights[:, lanes] * ratio - prob)).astype(jnp.bfloat16)
-    for copy in load_users:
-        copy.wait()
     half = places * rows // CORES
     far[...] = jnp.dot(grads[half:], all_users[...], preferred_element_type=jnp.float32).astype(far.dtype)
 
 
-def far_parts(factor, stats, users, logs, weights):
-    cols, places = len(users), logs[0].shape[0]
+def far_parts(factor, entropy, stats, users, probs, weights):
+    cols, places = len(users), probs[0].shape[0]
     rows, width = users[0].shape
     return pl.pallas_call(
         functools.partial(far_body, cols, places, factor),
-        in_specs=[VMEM] * cols + [ANY] * (2 * cols) + [VMEM],
+        in_specs=[VMEM] * (2 + 3 * cols),
         out_specs=[VMEM] * 3,
         out_shape=[
             struct(weights.shape, jnp.bfloat16),
             struct((1, rows), jnp.float32),
             struct((places * rows // CORES, width), jnp.bfloat16),
         ],
-        scratch_shapes=[
-            pltpu.VMEM((cols * rows, width), jnp.bfloat16),
-            pltpu.VMEM((cols * places, rows, rows), jnp.float32),
-            pltpu.SemaphoreType.DMA((cols,)),
-            pltpu.SemaphoreType.DMA((cols,)),
-        ],
+        scratch_shapes=[pltpu.VMEM((cols * rows, width), jnp.bfloat16)],
         compiler_params=params(32),
         cost_estimate=cost(cols * places * rows * rows * width, 8 * cols * places * rows * rows),
-    )(*stats, *users, *logs, weights)
+    )(entropy, *stats, *users, *probs, weights)
 
 
 def near_body(cols, grads, *refs):
-    users, (near, all_users, sems) = refs[:cols], refs[cols:]
-    loads = loads_of(users, all_users, sems)
-    for copy in loads:
-        copy.start()
-    for copy in loads:
-        copy.wait()
+    users, (near, all_users) = refs[:cols], refs[cols:]
+    lay(users, all_users)
     near[...] = jnp.dot(grads[: near.shape[0]], all_users[...], preferred_element_type=jnp.float32)
 
 
@@ -268,24 +237,20 @@
     rows, width = users[0].shape
     return pl.pallas_call(
         functools.partial(near_body, cols),
-        in_specs=[VMEM] + [ANY] * cols,
+        in_specs=[VMEM] * (1 + cols),
         out_specs=VMEM,
         out_shape=struct((places // CORES, width), jnp.float32),
-        scratch_shapes=[pltpu.VMEM((cols * rows, width), jnp.bfloat16), pltpu.SemaphoreType.DMA((cols,))],
+        scratch_shapes=[pltpu.VMEM((cols * rows, width), jnp.bfloat16)],
         compiler_params=params(32),
         cost_estimate=cost(grads.size * width, 4 * grads.size),
     )(grads, *users)
 
 
 def user_body(cols, places, grads, *refs):
-    items, refs = refs[:places], refs[-cols - 2 :]
-    parts, (all_items, sems) = refs[:cols], refs[cols:]
+    items, refs = refs[:places], refs[-cols - 1 :]
+    parts, all_items = refs[:cols], refs[cols]
     rows = items[0].shape[0]
-    loads = loads_of(items, all_items, sems)
-    for copy in loads:
-        copy.start()
-    for copy in loads:
-        copy.wait()
+    lay(items, all_items)
     for i in range(cols - 1, -1, -1):
         part = lax.dot_general(
             grads[:, i * rows : (i + 1) * rows],
@@ -301,10 +266,10 @@
     rows, width = items[0].shape
     return pl.pallas_call(
         functools.partial(user_body, cols, places),
-        in_specs=[VMEM] + [ANY] * (places + len(after)),
+        in_specs=[VMEM] * (1 + places) + [ANY] * len(after),
         out_specs=[VMEM] * cols,
         out_shape=[struct((rows, width), jnp.bfloat16 if i else jnp.float32) for i in range(cols)],
-        scratch_shapes=[pltpu.VMEM((places * rows, width), jnp.bfloat16), pltpu.SemaphoreType.DMA((places,))],
+        scratch_shapes=[pltpu.VMEM((places * rows, width), jnp.bfloat16)],
         compiler_params=params(32),
         cost_estimate=cost(2 * grads.size * width, 4 * grads.size),
     )(grads, *items, *after)
@@ -348,16 +313,16 @@
     def over_columns(own):
         return [swap(own, c * CORES) for c in range(1, cols)]
 
-    logs = spread_teacher(cols, planes, me, cand_blocks, cand_count, owner_map, teacher)
-    first, *rest = logs
-    logs = [first] + [swap(part, (c + 1) * CORES) for c, part in enumerate(rest)]
+    *probs, entropy = spread_teacher(cols, planes, me, cand_blocks, cand_count, owner_map, teacher)
+    first, *rest = probs
+    probs = [first] + [swap(part, (c + 1) * CORES) for c, part in enumerate(rest)]
 
     item_emb = embed(item_feats, item_w_in, item_w_out, [first])
     wide = planes // 2
     crossed = [swap(item_emb, z * cols * CORES) for z in range(wide, planes if planes > 1 else 0, max(wide, 1))]
     nearby = [swap(item_emb, z * cols * CORES) for z in range(1, wide)]
     user_emb = embed(user_feats, user_w_in, user_w_out, [item_emb])
-    user_emb, item_emb, logs, crossed, nearby = lax.optimization_barrier((user_emb, item_emb, logs, crossed, nearby))
+    user_emb, item_emb, probs, crossed, nearby = lax.optimization_barrier((user_emb, item_emb, probs, crossed, nearby))
     users = [user_emb] + over_columns(user_emb)
     derived = [swap(block, z * cols * CORES) for block in crossed for z in range(1, wide)]
     if cols > 1:
@@ -365,8 +330,8 @@
     items = [item_emb] + nearby + crossed + derived
     items = items + [swap(block, 1) for block in items]
 
-    weights, stats = scores(scale, users, items, logs)
-    grads, divergence, far = far_parts(factor, [stats] + over_columns(stats), users, logs, weights)
+    weights, stats = scores(scale, users, items, probs)
+    grads, divergence, far = far_parts(factor, entropy, [stats] + over_columns(stats), users, probs, weights)
     far = swap(far, 1)
     parts = join(planes, near_part(grads, users), far)
     hop = cols * CORES

time: 94.5 us -> 92.6 us (0.980)
  Pallas kernels: 34.3 us -> 32.7 us
    pallas_call x1, Pallas kernels: 4.56 us -> 2.74 us  [scores(): pl.pallas_call(functools.partial(score_body, cols, places, scale), in_spe...]
  transfers between devices with their start and end apart: 23 -> 23, of which waited for: 11 -> 12; matrix products, arithmetic and copies ran while one was open for 1% -> 1% of each run, Pallas kernels for 27% -> 28%
where the time goes in v5:
time: 92.6 us; the launch traced here: 92.2 us
  Pallas kernels  32.7 us (35%)
  waiting for transfers between devices  28.7 us (31%)
  starting transfers between devices  24.1 us (26%)
  local copies, waits for them, and re-layouts  3.48 us (4%)
  other arithmetic  1.89 us (2%)
  between operations  1.4 us (2%)
    ppermute x23, waiting for transfers between devices, swap(): return lax.ppermute(array, 'dp', [(i, i ^ apart) for i in range(count)])  28.7 us
    ppermute x23, starting transfers between devices, swap(): return lax.ppermute(array, 'dp', [(i, i ^ apart) for i in range(count)])  24.1 us
    pallas_call x2, Pallas kernels, tower(): pl.pallas_call(functools.partial(tower_body, chunks), in_specs=[VMEM, ANY...  23.3 us
    unnamed x10, local copies, waits for them, and re-layouts  3.48 us
    pallas_call x1, Pallas kernels, spread_teacher(): pl.pallas_call(functools.partial(teacher_body, cols, planes), in_specs=[S...  2.78 us
    pallas_call x1, Pallas kernels, scores(): pl.pallas_call(functools.partial(score_body, cols, places, scale), in_spe...  2.74 us
  transfers between devices with their start and end apart: 23, of which 12 were waited for; matrix products, arithmetic and copies ran while one was open for 1% of the time, Pallas kernels for 28%

profile of v5, /device:TPU:0, one launch (start us, length us, event | category | flops | bytes accessed | tf_op | source)
XLA Modules:
  0.0 92.2 jit_solution(4261310636351143032)
XLA Ops:
  1.3 0.0 copy-start
  1.3 1.2 %copy-done = f32[128,2048]{1,0:T(8,128)S(1)} copy-done((f32[128,2048]{1,0:T(8,128)S(1)}, f32[128,2048]{1,0:T(8,128)}, u32[]{:S(2)}) %copy-start) | copy-done | bytes 1048600
  2.5 0.0 copy-start.3
  2.5 0.7 copy-done.3
  3.2 0.7 copy-done.4
  3.8 2.8 %shard_map.121 = (f32[8,128,128]{2,1,0:T(8,128)S(1)}, f32[8,128,128]{2,1,0:T(8,128)S(1)}, f32[8,128,128]{2,1,0:T(8,128)S(1)}, f32[8,128,128]{2,1,0:T(8,128)S(1)}, f32[1,128]{1,0:T(1,128)S(1)}) custom-call(s32[1]{0:T(128)} %bitcast.me, s32[1,16]{1,0:T(1,128)S(1)} %copy-done.3, s32[1]{0:T(128)S(6)} %copy.13.count, s32[32]{0:T(128)S(1)} %copy-done.4, ...), custom_call_target="tpu_custom_call" | custom-call | flops 262144 | bytes 2097152 | tf_op jit(solution)/shard_map/pallas_call | solution.py:124
  6.6 2.5 %collective-permute-start = (f32[8,128,128]{2,1,0:T(8,128)S(1)}, f32[8,128,128]{2,1,0:T(8,128)S(1)}, u32[]{:S(2)}, u32[]{:S(2)}) collective-permute-start(f32[8,128,128]{2,1,0:T(8,128)S(1)} %get-tuple-element.35), channel_id=1, source_target_pairs={{0,2},{1,3},{2,0},{3,1},{4,6},{5,7},{6,4},{7,5},{8,10},{9,11},{10,... | collective-permute-start | bytes 1572872 | tf_op jit(solution)/shard_map/ppermute | solution.py:311
  9.1 1.5 %collective-permute-start.1 = (f32[8,128,128]{2,1,0:T(8,128)S(1)}, f32[8,128,128]{2,1,0:T(8,128)S(1)}, u32[]{:S(2)}, u32[]{:S(2)}) collective-permute-start(f32[8,128,128]{2,1,0:T(8,128)S(1)} %get-tuple-element.36), channel_id=1, source_target_pairs={{0,4},{1,5},{2,6},{3,7},{4,0},{5,1},{6,2},{7,3},{8,12},{9,13},{10,... | collective-permute-start | bytes 1572872 | tf_op jit(solution)/shard_map/ppermute | solution.py:311
  10.7 0.0 collective-permute-start.2
  10.7 0.9 %copy-done.1 = bf16[128,1024]{1,0:T(8,128)(2,1)S(1)} copy-done((bf16[128,1024]{1,0:T(8,128)(2,1)S(1)}, bf16[128,1024]{1,0:T(8,128)(2,1)}, u32[]{:S(2)}) %copy-start.1) | copy-done | bytes 262168
  11.6 11.7 %shard_map.122.refs_0_.refs_4_ = bf16[128,1024]{1,0:T(8,128)(2,1)S(1)} custom-call(bf16[128,1024]{1,0:T(8,128)(2,1)S(1)} %copy-done.1, bf16[1024,8192]{1,0:T(8,128)(2,1)} %w_in.2, bf16[8192,1024]{1,0:T(8,128)(2,1)} %w_out.2, f32[8,128,128]{2,1,0:T(8,128)S(1)} %get-tuple-element.46.refs_0_.refs_12_.refs_8_), custom_call_target="tpu_custom_call" | custom-call | flops 1 | bytes 1 | tf_op jit(solution)/shard_map/pallas_call | solution.py:66
  23.3 2.4 %collective-permute-start.4 = (bf16[128,1024]{1,0:T(8,128)(2,1)S(1)}, bf16[128,1024]{1,0:T(8,128)(2,1)S(1)}, u32[]{:S(2)}, u32[]{:S(2)}) collective-permute-start(bf16[128,1024]{1,0:T(8,128)(2,1)S(1)} %shard_map.122.refs_0_.refs_4_), channel_id=1, source_target_pairs={{0,8},{1,9},{2,10},{3,11},{4,12},{5,13},{6,14},{7,15},{8,0},{9,1},... | collective-permute-start | bytes 786440 | tf_op jit(solution)/shard_map/ppermute | solution.py:311
  25.7 2.4 %collective-permute-start.3 = (bf16[128,1024]{1,0:T(8,128)(2,1)S(1)}, bf16[128,1024]{1,0:T(8,128)(2,1)S(1)}, u32[]{:S(2)}, u32[]{:S(2)}) collective-permute-start(bf16[128,1024]{1,0:T(8,128)(2,1)S(1)} %shard_map.122.refs_0_.refs_4_), channel_id=1, source_target_pairs={{0,16},{1,17},{2,18},{3,19},{4,20},{5,21},{6,22},{7,23},{8,24},{9,... | collective-permute-start | bytes 786440 | tf_op jit(solution)/shard_map/ppermute | solution.py:311
  28.1 0.0 copy-done.2
  28.1 11.7 %shard_map.123.refs_0_.refs_4_ = bf16[128,1024]{1,0:T(8,128)(2,1)S(1)} custom-call(bf16[128,1024]{1,0:T(8,128)(2,1)S(1)} %copy-done.2, bf16[1024,8192]{1,0:T(8,128)(2,1)} %w_in.3, bf16[8192,1024]{1,0:T(8,128)(2,1)} %w_out.3, bf16[128,1024]{1,0:T(8,128)(2,1)S(1)} %shard_map.122.refs_0_.refs_4_), custom_call_target="tpu_custom_call" | custom-call | flops 1 | bytes 1 | tf_op jit(solution)/shard_map/pallas_call | solution.py:66
  39.8 0.0 collective-permute-done.4.refs_5_.refs_1_
  39.8 0.0 collective-permute-done.3.refs_6_.refs_2_
  39.8 0.0 collective-permute-done.refs_13_.refs_9_
  39.8 0.0 collective-permute-done.1.refs_14_.refs_10_
  39.8 0.0 collective-permute-done.2.refs_15_.refs_11_
  39.8 1.5 %collective-permute-start.5 = (bf16[128,1024]{1,0:T(8,128)(2,1)S(1)}, bf16[128,1024]{1,0:T(8,128)(2,1)S(1)}, u32[]{:S(2)}, u32[]{:S(2)}) collective-permute-start(bf16[128,1024]{1,0:T(8,128)(2,1)S(1)} %shard_map.123.refs_0_.refs_4_), channel_id=1, source_target_pairs={{0,2},{1,3},{2,0},{3,1},{4,6},{5,7},{6,4},{7,5},{8,10},{9,11},{10,... | collective-permute-start | bytes 786440 | tf_op jit(solution)/shard_map/ppermute | solution.py:311
  41.3 0.7 collective-permute-start.8
  42.0 1.6 %collective-permute-start.7 = (bf16[128,1024]{1,0:T(8,128)(2,1)S(1)}, bf16[128,1024]{1,0:T(8,128)(2,1)S(1)}, u32[]{:S(2)}, u32[]{:S(2)}) collective-permute-start(bf16[128,1024]{1,0:T(8,128)(2,1)S(1)} %shard_map.123.refs_0_.refs_4_), channel_id=1, source_target_pairs={{0,6},{1,7},{2,4},{3,5},{4,2},{5,3},{6,0},{7,1},{8,14},{9,15},{10,... | collective-permute-start | bytes 786440 | tf_op jit(solution)/shard_map/ppermute | solution.py:311
  43.5 0.6 collective-permute-start.6
  44.1 5.0 %collective-permute-done.5.refs_1_.refs_5_ = bf16[128,1024]{1,0:T(8,128)(2,1)S(1)} collective-permute-done((bf16[128,1024]{1,0:T(8,128)(2,1)S(1)}, bf16[128,1024]{1,0:T(8,128)(2,1)S(1)}, u32[]{:S(2)}, u32[]{:S(2)}) %collective-permute-start.5) | collective-permute-done | bytes 262176 | tf_op jit(solution)/shard_map/ppermute | solution.py:311
  49.1 0.0 collective-permute-start.9
  49.1 0.5 collective-permute-start.10
  49.6 0.0 collective-permute-done.8.refs_7_.refs_3_
  49.6 0.0 collective-permute-start.12
  49.6 3.9 %collective-permute-done.7.refs_3_.refs_7_ = bf16[128,1024]{1,0:T(8,128)(2,1)S(1)} collective-permute-done((bf16[128,1024]{1,0:T(8,128)(2,1)S(1)}, bf16[128,1024]{1,0:T(8,128)(2,1)S(1)}, u32[]{:S(2)}, u32[]{:S(2)}) %collective-permute-start.7) | collective-permute-done | bytes 262176 | tf_op jit(solution)/shard_map/ppermute | solution.py:311
  53.5 0.0 collective-permute-start.11
  53.5 1.4 %collective-permute-done.6.refs_2_.refs_6_ = bf16[128,1024]{1,0:T(8,128)(2,1)S(1)} collective-permute-done((bf16[128,1024]{1,0:T(8,128)(2,1)S(1)}, bf16[128,1024]{1,0:T(8,128)(2,1)S(1)}, u32[]{:S(2)}, u32[]{:S(2)}) %collective-permute-start.6) | collective-permute-done | bytes 262176 | tf_op jit(solution)/shard_map/ppermute | solution.py:311
  54.9 0.0 collective-permute-done.12.refs_11_.refs_7_
  55.0 0.0 collective-permute-done.9.refs_8_.refs_4_
  55.0 0.0 collective-permute-done.10.refs_9_.refs_5_
  55.0 0.1 collective-permute-done.11.refs_10_.refs_6_
  55.0 2.7 %shard_map.124 = (f32[1024,512]{1,0:T(8,128)S(1)}, f32[4,4,128]{2,1,0:T(4,128)S(1)}) custom-call(bf16[128,1024]{1,0:T(8,128)(2,1)S(1)} %shard_map.123.refs_0_.refs_4_, bf16[128,1024]{1,0:T(8,128)(2,1)S(1)} %collective-permute-done.5.refs_1_.refs_5_, bf16[128,1024]{1,0:T(8,128)(2,1)S(1)} %collective-permute-done.6.refs_2_.refs_6_, ...), custom_call_target="tpu_custom_call" | custom-call | flops 1073741824 | bytes 4194304 | tf_op jit(solution)/shard_map/pallas_call | solution.py:174
  57.8 1.7 %collective-permute-start.15 = (f32[4,4,128]{2,1,0:T(4,128)S(1)}, f32[4,4,128]{2,1,0:T(4,128)S(1)}, u32[]{:S(2)}, u32[]{:S(2)}) collective-permute-start(f32[4,4,128]{2,1,0:T(4,128)S(1)} %get-tuple-element.50.refs_0_), channel_id=1, source_target_pairs={{0,6},{1,7},{2,4},{3,5},{4,2},{5,3},{6,0},{7,1},{8,14},{9,15},{10,... | collective-permute-start | bytes 24584 | tf_op jit(solution)/shard_map/ppermute | solution.py:311
  59.5 1.1 %collective-permute-start.14 = (f32[4,4,128]{2,1,0:T(4,128)S(1)}, f32[4,4,128]{2,1,0:T(4,128)S(1)}, u32[]{:S(2)}, u32[]{:S(2)}) collective-permute-start(f32[4,4,128]{2,1,0:T(4,128)S(1)} %get-tuple-element.50.refs_0_), channel_id=1, source_target_pairs={{0,4},{1,5},{2,6},{3,7},{4,0},{5,1},{6,2},{7,3},{8,12},{9,13},{10,... | collective-permute-start | bytes 24584 | tf_op jit(solution)/shard_map/ppermute | solution.py:311
  60.7 0.7 collective-permute-start.13
  61.3 1.1 %collective-permute-done.15.refs_3_ = f32[4,4,128]{2,1,0:T(4,128)S(1)} collective-permute-done((f32[4,4,128]{2,1,0:T(4,128)S(1)}, f32[4,4,128]{2,1,0:T(4,128)S(1)}, u32[]{:S(2)}, u32[]{:S(2)}) %collective-permute-start.15) | collective-permute-done | bytes 8224 | tf_op jit(solution)/shard_map/ppermute | solution.py:311
  62.4 0.8 collective-permute-done.14.refs_2_
  63.2 1.1 %collective-permute-done.13.refs_1_ = f32[4,4,128]{2,1,0:T(4,128)S(1)} collective-permute-done((f32[4,4,128]{2,1,0:T(4,128)S(1)}, f32[4,4,128]{2,1,0:T(4,128)S(1)}, u32[]{:S(2)}, u32[]{:S(2)}) %collective-permute-start.13) | collective-permute-done | bytes 8224 | tf_op jit(solution)/shard_map/ppermute | solution.py:311
  64.3 1.6 %shard_map.125 = (bf16[1024,512]{1,0:T(8,128)(2,1)S(1)}, f32[1,128]{1,0:T(1,128)}, bf16[512,1024]{1,0:T(8,128)(2,1)S(1)}) custom-call(f32[1,128]{1,0:T(1,128)S(1)} %get-tuple-element.33.entropy, f32[4,4,128]{2,1,0:T(4,128)S(1)} %get-tuple-element.50.refs_0_, f32[4,4,128]{2,1,0:T(4,128)S(1)} %collective-permute-done.13.refs_1_, ...), custom_call_target="tpu_custom_call" | custom-call | flops 536870912 | bytes 4194304 | tf_op jit(solution)/shard_map/pallas_call | solution.py:214
  65.9 0.0 collective-permute-start.16
  65.9 0.7 shard_map.126.near
  66.6 1.9 %collective-permute-done.16.far = bf16[512,1024]{1,0:T(8,128)(2,1)S(1)} collective-permute-done((bf16[512,1024]{1,0:T(8,128)(2,1)S(1)}, bf16[512,1024]{1,0:T(8,128)(2,1)S(1)}, u32[]{:S(2)}, u32[]{:S(2)}) %collective-permute-start.16) | collective-permute-done | bytes 1048608 | tf_op jit(solution)/shard_map/ppermute | solution.py:311
  68.5 0.2 shard_map.127
  68.7 1.6 %collective-permute-start.20 = (bf16[128,1024]{1,0:T(8,128)(2,1)S(1)}, bf16[128,1024]{1,0:T(8,128)(2,1)S(1)}, u32[]{:S(2)}, u32[]{:S(2)}) collective-permute-start(bf16[128,1024]{1,0:T(8,128)(2,1)S(1)} %get-tuple-element.61), channel_id=1, source_target_pairs={{0,8},{1,9},{2,10},{3,11},{4,12},{5,13},{6,14},{7,15},{8,0},{9,1},... | collective-permute-start | bytes 786440 | tf_op jit(solution)/shard_map/ppermute | solution.py:311
  70.3 1.3 %shard_map.128 = (f32[128,1024]{1,0:T(8,128)S(1)}, bf16[128,1024]{1,0:T(8,128)(2,1)S(1)}, bf16[128,1024]{1,0:T(8,128)(2,1)S(1)}, bf16[128,1024]{1,0:T(8,128)(2,1)S(1)}) custom-call(bf16[1024,512]{1,0:T(8,128)(2,1)S(1)} %get-tuple-element.53.grads, bf16[128,1024]{1,0:T(8,128)(2,1)S(1)} %shard_map.122.refs_0_.refs_4_, ...), custom_call_target="tpu_custom_call" | custom-call | flops 1073741824 | bytes 2097152 | tf_op jit(solution)/shard_map/pallas_call | solution.py:267
  71.7 0.8 collective-permute-start.17
  72.5 0.4 collective-permute-start.18
  72.9 2.3 %collective-permute-start.19 = (bf16[128,1024]{1,0:T(8,128)(2,1)S(1)}, bf16[128,1024]{1,0:T(8,128)(2,1)S(1)}, u32[]{:S(2)}, u32[]{:S(2)}) collective-permute-start(bf16[128,1024]{1,0:T(8,128)(2,1)S(1)} %get-tuple-element.59), channel_id=1, source_target_pairs={{0,6},{1,7},{2,4},{3,5},{4,2},{5,3},{6,0},{7,1},{8,14},{9,15},{10,... | collective-permute-start | bytes 786440 | tf_op jit(solution)/shard_map/ppermute | solution.py:311
  75.2 0.5 collective-permute-start.22
  75.7 1.6 %collective-permute-done.20 = bf16[128,1024]{1,0:T(8,128)(2,1)S(1)} collective-permute-done((bf16[128,1024]{1,0:T(8,128)(2,1)S(1)}, bf16[128,1024]{1,0:T(8,128)(2,1)S(1)}, u32[]{:S(2)}, u32[]{:S(2)}) %collective-permute-start.20) | collective-permute-done | bytes 262176 | tf_op jit(solution)/shard_map/ppermute | solution.py:311
  77.3 0.1 add_convert_fusion
  77.4 1.2 %collective-permute-start.21 = (bf16[128,1024]{1,0:T(8,128)(2,1)S(1)}, bf16[128,1024]{1,0:T(8,128)(2,1)S(1)}, u32[]{:S(2)}, u32[]{:S(2)}) collective-permute-start(bf16[128,1024]{1,0:T(8,128)(2,1)S(1)} %add_convert_fusion), channel_id=1, source_target_pairs={{0,16},{1,17},{2,18},{3,19},{4,20},{5,21},{6,22},{7,23},{8,24},{9,... | collective-permute-start | bytes 786440 | tf_op jit(solution)/shard_map/ppermute | solution.py:311
  78.6 2.3 %collective-permute-done.17 = bf16[128,1024]{1,0:T(8,128)(2,1)S(1)} collective-permute-done((bf16[128,1024]{1,0:T(8,128)(2,1)S(1)}, bf16[128,1024]{1,0:T(8,128)(2,1)S(1)}, u32[]{:S(2)}, u32[]{:S(2)}) %collective-permute-start.17) | collective-permute-done | bytes 262176 | tf_op jit(solution)/shard_map/ppermute | solution.py:311
  80.9 4.9 %collective-permute-done.18 = bf16[128,1024]{1,0:T(8,128)(2,1)S(1)} collective-permute-done((bf16[128,1024]{1,0:T(8,128)(2,1)S(1)}, bf16[128,1024]{1,0:T(8,128)(2,1)S(1)}, u32[]{:S(2)}, u32[]{:S(2)}) %collective-permute-start.18) | collective-permute-done | bytes 262176 | tf_op jit(solution)/shard_map/ppermute | solution.py:311
  85.9 0.0 collective-permute-done.19
  85.9 0.9 %convert_add_fusion.1 = f32[128,1024]{1,0:T(8,128)} fusion(bf16[128,1024]{1,0:T(8,128)(2,1)S(1)} %collective-permute-done.19, bf16[128,1024]{1,0:T(8,128)(2,1)S(1)} %collective-permute-done.18, f32[128,1024]{1,0:T(8,128)S(1)} %get-tuple-element.56, bf16[128,1024]{1,0:T(8,128)(2,1)S(1)} %collective-permute-done.17), kind=kLoop, calls=%fused_computation.2 | loop fusion | flops 786432 | bytes 1835008 | tf_op jit(solution)/shard_map/add | solution.py:347
  86.8 0.0 collective-permute-done.22
  86.8 4.5 %collective-permute-done.21 = bf16[128,1024]{1,0:T(8,128)(2,1)S(1)} collective-permute-done((bf16[128,1024]{1,0:T(8,128)(2,1)S(1)}, bf16[128,1024]{1,0:T(8,128)(2,1)S(1)}, u32[]{:S(2)}, u32[]{:S(2)}) %collective-permute-start.21) | collective-permute-done | bytes 262176 | tf_op jit(solution)/shard_map/ppermute | solution.py:311
  91.3 0.9 convert_add_fusion
  (3 shorter events, 0.0 us)
Async XLA Ops:
  1.3 1.2 %copy-start = (f32[128,2048]{1,0:T(8,128)S(1)}, f32[128,2048]{1,0:T(8,128)}, u32[]{:S(2)}) copy-start(f32[128,2048]{1,0:T(8,128)} %teacher.1) | copy-start | bytes 3145732
  2.5 0.7 copy-start.3
  3.2 0.7 copy-start.4
  6.6 33.2 %collective-permute-start = (f32[8,128,128]{2,1,0:T(8,128)S(1)}, f32[8,128,128]{2,1,0:T(8,128)S(1)}, u32[]{:S(2)}, u32[]{:S(2)}) collective-permute-start(f32[8,128,128]{2,1,0:T(8,128)S(1)} %get-tuple-element.35), channel_id=1, source_target_pairs={{0,2},{1,3},{2,0},{3,1},{4,6},{5,7},{6,4},{7,5},{8,10},{9,11},{10,... | collective-permute-start | bytes 1572872 | tf_op jit(solution)/shard_map/ppermute | solution.py:311
  9.1 30.7 %collective-permute-start.1 = (f32[8,128,128]{2,1,0:T(8,128)S(1)}, f32[8,128,128]{2,1,0:T(8,128)S(1)}, u32[]{:S(2)}, u32[]{:S(2)}) collective-permute-start(f32[8,128,128]{2,1,0:T(8,128)S(1)} %get-tuple-element.36), channel_id=1, source_target_pairs={{0,4},{1,5},{2,6},{3,7},{4,0},{5,1},{6,2},{7,3},{8,12},{9,13},{10,... | collective-permute-start | bytes 1572872 | tf_op jit(solution)/shard_map/ppermute | solution.py:311
  10.7 29.1 %collective-permute-start.2 = (f32[8,128,128]{2,1,0:T(8,128)S(1)}, f32[8,128,128]{2,1,0:T(8,128)S(1)}, u32[]{:S(2)}, u32[]{:S(2)}) collective-permute-start(f32[8,128,128]{2,1,0:T(8,128)S(1)} %get-tuple-element.37), channel_id=1, source_target_pairs={{0,6},{1,7},{2,4},{3,5},{4,2},{5,3},{6,0},{7,1},{8,14},{9,15},{10,... | collective-permute-start | bytes 1572872 | tf_op jit(solution)/shard_map/ppermute | solution.py:311
  10.7 0.9 %copy-start.1 = (bf16[128,1024]{1,0:T(8,128)(2,1)S(1)}, bf16[128,1024]{1,0:T(8,128)(2,1)}, u32[]{:S(2)}) copy-start(bf16[128,1024]{1,0:T(8,128)(2,1)} %feats.2) | copy-start | bytes 786436
  11.6 16.5 %copy-start.2 = (bf16[128,1024]{1,0:T(8,128)(2,1)S(1)}, bf16[128,1024]{1,0:T(8,128)(2,1)}, u32[]{:S(2)}) copy-start(bf16[128,1024]{1,0:T(8,128)(2,1)} %feats.3) | copy-start | bytes 786436
  23.3 16.4 %collective-permute-start.4 = (bf16[128,1024]{1,0:T(8,128)(2,1)S(1)}, bf16[128,1024]{1,0:T(8,128)(2,1)S(1)}, u32[]{:S(2)}, u32[]{:S(2)}) collective-permute-start(bf16[128,1024]{1,0:T(8,128)(2,1)S(1)} %shard_map.122.refs_0_.refs_4_), channel_id=1, source_target_pairs={{0,8},{1,9},{2,10},{3,11},{4,12},{5,13},{6,14},{7,15},{8,0},{9,1},... | collective-permute-start | bytes 786440 | tf_op jit(solution)/shard_map/ppermute | solution.py:311
  25.7 14.1 %collective-permute-start.3 = (bf16[128,1024]{1,0:T(8,128)(2,1)S(1)}, bf16[128,1024]{1,0:T(8,128)(2,1)S(1)}, u32[]{:S(2)}, u32[]{:S(2)}) collective-permute-start(bf16[128,1024]{1,0:T(8,128)(2,1)S(1)} %shard_map.122.refs_0_.refs_4_), channel_id=1, source_target_pairs={{0,16},{1,17},{2,18},{3,19},{4,20},{5,21},{6,22},{7,23},{8,24},{9,... | collective-permute-start | bytes 786440 | tf_op jit(solution)/shard_map/ppermute | solution.py:311
  39.8 9.3 %collective-permute-start.5 = (bf16[128,1024]{1,0:T(8,128)(2,1)S(1)}, bf16[128,1024]{1,0:T(8,128)(2,1)S(1)}, u32[]{:S(2)}, u32[]{:S(2)}) collective-permute-start(bf16[128,1024]{1,0:T(8,128)(2,1)S(1)} %shard_map.123.refs_0_.refs_4_), channel_id=1, source_target_pairs={{0,2},{1,3},{2,0},{3,1},{4,6},{5,7},{6,4},{7,5},{8,10},{9,11},{10,... | collective-permute-start | bytes 786440 | tf_op jit(solution)/shard_map/ppermute | solution.py:311
  41.3 8.3 %collective-permute-start.8 = (bf16[128,1024]{1,0:T(8,128)(2,1)S(1)}, bf16[128,1024]{1,0:T(8,128)(2,1)S(1)}, u32[]{:S(2)}, u32[]{:S(2)}) collective-permute-start(bf16[128,1024]{1,0:T(8,128)(2,1)S(1)} %collective-permute-done.3.refs_6_.refs_2_), channel_id=1, source_target_pairs={{0,8},{1,9},{2,10},{3,11},{4,12},{5,13},{6,14},{7,15},{8,0},{9,1},... | collective-permute-start | bytes 786440 | tf_op jit(solution)/shard_map/ppermute | solution.py:311
  42.0 11.5 %collective-permute-start.7 = (bf16[128,1024]{1,0:T(8,128)(2,1)S(1)}, bf16[128,1024]{1,0:T(8,128)(2,1)S(1)}, u32[]{:S(2)}, u32[]{:S(2)}) collective-permute-start(bf16[128,1024]{1,0:T(8,128)(2,1)S(1)} %shard_map.123.refs_0_.refs_4_), channel_id=1, source_target_pairs={{0,6},{1,7},{2,4},{3,5},{4,2},{5,3},{6,0},{7,1},{8,14},{9,15},{10,... | collective-permute-start | bytes 786440 | tf_op jit(solution)/shard_map/ppermute | solution.py:311
  43.5 11.4 %collective-permute-start.6 = (bf16[128,1024]{1,0:T(8,128)(2,1)S(1)}, bf16[128,1024]{1,0:T(8,128)(2,1)S(1)}, u32[]{:S(2)}, u32[]{:S(2)}) collective-permute-start(bf16[128,1024]{1,0:T(8,128)(2,1)S(1)} %shard_map.123.refs_0_.refs_4_), channel_id=1, source_target_pairs={{0,4},{1,5},{2,6},{3,7},{4,0},{5,1},{6,2},{7,3},{8,12},{9,13},{10,... | collective-permute-start | bytes 786440 | tf_op jit(solution)/shard_map/ppermute | solution.py:311
  49.1 5.8 %collective-permute-start.9 = (bf16[128,1024]{1,0:T(8,128)(2,1)S(1)}, bf16[128,1024]{1,0:T(8,128)(2,1)S(1)}, u32[]{:S(2)}, u32[]{:S(2)}) collective-permute-start(bf16[128,1024]{1,0:T(8,128)(2,1)S(1)} %shard_map.122.refs_0_.refs_4_), channel_id=1, source_target_pairs={{0,1},{1,0},{2,3},{3,2},{4,5},{5,4},{6,7},{7,6},{8,9},{9,8},{10,11... | collective-permute-start | bytes 786440 | tf_op jit(solution)/shard_map/ppermute | solution.py:311
  49.1 5.8 %collective-permute-start.10 = (bf16[128,1024]{1,0:T(8,128)(2,1)S(1)}, bf16[128,1024]{1,0:T(8,128)(2,1)S(1)}, u32[]{:S(2)}, u32[]{:S(2)}) collective-permute-start(bf16[128,1024]{1,0:T(8,128)(2,1)S(1)} %collective-permute-done.4.refs_5_.refs_1_), channel_id=1, source_target_pairs={{0,1},{1,0},{2,3},{3,2},{4,5},{5,4},{6,7},{7,6},{8,9},{9,8},{10,11... | collective-permute-start | bytes 786440 | tf_op jit(solution)/shard_map/ppermute | solution.py:311
  49.6 5.3 %collective-permute-start.12 = (bf16[128,1024]{1,0:T(8,128)(2,1)S(1)}, bf16[128,1024]{1,0:T(8,128)(2,1)S(1)}, u32[]{:S(2)}, u32[]{:S(2)}) collective-permute-start(bf16[128,1024]{1,0:T(8,128)(2,1)S(1)} %collective-permute-done.8.refs_7_.refs_3_), channel_id=1, source_target_pairs={{0,1},{1,0},{2,3},{3,2},{4,5},{5,4},{6,7},{7,6},{8,9},{9,8},{10,11... | collective-permute-start | bytes 786440 | tf_op jit(solution)/shard_map/ppermute | solution.py:311
  53.5 1.5 %collective-permute-start.11 = (bf16[128,1024]{1,0:T(8,128)(2,1)S(1)}, bf16[128,1024]{1,0:T(8,128)(2,1)S(1)}, u32[]{:S(2)}, u32[]{:S(2)}) collective-permute-start(bf16[128,1024]{1,0:T(8,128)(2,1)S(1)} %collective-permute-done.3.refs_6_.refs_2_), channel_id=1, source_target_pairs={{0,1},{1,0},{2,3},{3,2},{4,5},{5,4},{6,7},{7,6},{8,9},{9,8},{10,11... | collective-permute-start | bytes 786440 | tf_op jit(solution)/shard_map/ppermute | solution.py:311
  57.8 4.6 %collective-permute-start.15 = (f32[4,4,128]{2,1,0:T(4,128)S(1)}, f32[4,4,128]{2,1,0:T(4,128)S(1)}, u32[]{:S(2)}, u32[]{:S(2)}) collective-permute-start(f32[4,4,128]{2,1,0:T(4,128)S(1)} %get-tuple-element.50.refs_0_), channel_id=1, source_target_pairs={{0,6},{1,7},{2,4},{3,5},{4,2},{5,3},{6,0},{7,1},{8,14},{9,15},{10,... | collective-permute-start | bytes 24584 | tf_op jit(solution)/shard_map/ppermute | solution.py:311
  59.5 3.7 %collective-permute-start.14 = (f32[4,4,128]{2,1,0:T(4,128)S(1)}, f32[4,4,128]{2,1,0:T(4,128)S(1)}, u32[]{:S(2)}, u32[]{:S(2)}) collective-permute-start(f32[4,4,128]{2,1,0:T(4,128)S(1)} %get-tuple-element.50.refs_0_), channel_id=1, source_target_pairs={{0,4},{1,5},{2,6},{3,7},{4,0},{5,1},{6,2},{7,3},{8,12},{9,13},{10,... | collective-permute-start | bytes 24584 | tf_op jit(solution)/shard_map/ppermute | solution.py:311
  60.7 3.7 %collective-permute-start.13 = (f32[4,4,128]{2,1,0:T(4,128)S(1)}, f32[4,4,128]{2,1,0:T(4,128)S(1)}, u32[]{:S(2)}, u32[]{:S(2)}) collective-permute-start(f32[4,4,128]{2,1,0:T(4,128)S(1)} %get-tuple-element.50.refs_0_), channel_id=1, source_target_pairs={{0,2},{1,3},{2,0},{3,1},{4,6},{5,7},{6,4},{7,5},{8,10},{9,11},{10,... | collective-permute-start | bytes 24584 | tf_op jit(solution)/shard_map/ppermute | solution.py:311
  65.9 2.7 %collective-permute-start.16 = (bf16[512,1024]{1,0:T(8,128)(2,1)S(1)}, bf16[512,1024]{1,0:T(8,128)(2,1)S(1)}, u32[]{:S(2)}, u32[]{:S(2)}) collective-permute-start(bf16[512,1024]{1,0:T(8,128)(2,1)S(1)} %get-tuple-element.54), channel_id=1, source_target_pairs={{0,1},{1,0},{2,3},{3,2},{4,5},{5,4},{6,7},{7,6},{8,9},{9,8},{10,11... | collective-permute-start | bytes 3145736 | tf_op jit(solution)/shard_map/ppermute | solution.py:311
  68.7 8.6 %collective-permute-start.20 = (bf16[128,1024]{1,0:T(8,128)(2,1)S(1)}, bf16[128,1024]{1,0:T(8,128)(2,1)S(1)}, u32[]{:S(2)}, u32[]{:S(2)}) collective-permute-start(bf16[128,1024]{1,0:T(8,128)(2,1)S(1)} %get-tuple-element.61), channel_id=1, source_target_pairs={{0,8},{1,9},{2,10},{3,11},{4,12},{5,13},{6,14},{7,15},{8,0},{9,1},... | collective-permute-start | bytes 786440 | tf_op jit(solution)/shard_map/ppermute | solution.py:311
  71.7 9.3 %collective-permute-start.17 = (bf16[128,1024]{1,0:T(8,128)(2,1)S(1)}, bf16[128,1024]{1,0:T(8,128)(2,1)S(1)}, u32[]{:S(2)}, u32[]{:S(2)}) collective-permute-start(bf16[128,1024]{1,0:T(8,128)(2,1)S(1)} %get-tuple-element.57), channel_id=1, source_target_pairs={{0,2},{1,3},{2,0},{3,1},{4,6},{5,7},{6,4},{7,5},{8,10},{9,11},{10,... | collective-permute-start | bytes 786440 | tf_op jit(solution)/shard_map/ppermute | solution.py:311
  72.5 13.4 %collective-permute-start.18 = (bf16[128,1024]{1,0:T(8,128)(2,1)S(1)}, bf16[128,1024]{1,0:T(8,128)(2,1)S(1)}, u32[]{:S(2)}, u32[]{:S(2)}) collective-permute-start(bf16[128,1024]{1,0:T(8,128)(2,1)S(1)} %get-tuple-element.58), channel_id=1, source_target_pairs={{0,4},{1,5},{2,6},{3,7},{4,0},{5,1},{6,2},{7,3},{8,12},{9,13},{10,... | collective-permute-start | bytes 786440 | tf_op jit(solution)/shard_map/ppermute | solution.py:311
  72.9 12.9 %collective-permute-start.19 = (bf16[128,1024]{1,0:T(8,128)(2,1)S(1)}, bf16[128,1024]{1,0:T(8,128)(2,1)S(1)}, u32[]{:S(2)}, u32[]{:S(2)}) collective-permute-start(bf16[128,1024]{1,0:T(8,128)(2,1)S(1)} %get-tuple-element.59), channel_id=1, source_target_pairs={{0,6},{1,7},{2,4},{3,5},{4,2},{5,3},{6,0},{7,1},{8,14},{9,15},{10,... | collective-permute-start | bytes 786440 | tf_op jit(solution)/shard_map/ppermute | solution.py:311
  75.2 11.6 %collective-permute-start.22 = (bf16[128,1024]{1,0:T(8,128)(2,1)S(1)}, bf16[128,1024]{1,0:T(8,128)(2,1)S(1)}, u32[]{:S(2)}, u32[]{:S(2)}) collective-permute-start(bf16[128,1024]{1,0:T(8,128)(2,1)S(1)} %get-tuple-element.62), channel_id=1, source_target_pairs={{0,8},{1,9},{2,10},{3,11},{4,12},{5,13},{6,14},{7,15},{8,0},{9,1},... | collective-permute-start | bytes 786440 | tf_op jit(solution)/shard_map/ppermute | solution.py:311
  77.4 13.9 %collective-permute-start.21 = (bf16[128,1024]{1,0:T(8,128)(2,1)S(1)}, bf16[128,1024]{1,0:T(8,128)(2,1)S(1)}, u32[]{:S(2)}, u32[]{:S(2)}) collective-permute-start(bf16[128,1024]{1,0:T(8,128)(2,1)S(1)} %add_convert_fusion), channel_id=1, source_target_pairs={{0,16},{1,17},{2,18},{3,19},{4,20},{5,21},{6,22},{7,23},{8,24},{9,... | collective-permute-start | bytes 786440 | tf_op jit(solution)/shard_map/ppermute | solution.py:311

commit v6 on v5

--- a/solution.py
+++ b/solution.py
@@ -29,8 +29,17 @@
     return pl.CostEstimate(flops=int(flops), bytes_accessed=int(moved), transcendentals=0)
 
 
-def tower_body(chunks, feats, w_in, w_out, *refs):
-    out, held_in, held_out, total, sem_in, sem_out = refs[-6:]
+def in_hbm(array):
+    return pltpu.with_memory_space_constraint(array, pltpu.HBM)
+
+
+def tower_body(chunks, held, feats, w_in, w_out, *refs):
+    out, held_in, held_out, total, sem_in, sem_out, *own = refs[-6 if held else -8 :]
+    if not held:
+        load = pltpu.make_async_copy(feats, *own)
+        load.start()
+        load.wait()
+        feats = own[0]
     step = w_in.shape[1] // chunks
 
     def copies(i):
@@ -59,13 +68,13 @@
     out[...] = total[...].astype(out.dtype)
 
 
-def tower(feats, w_in, w_out, dtype, after):
+def tower(feats, w_in, w_out, dtype, after, held):
     rows, width = feats.shape
     hidden = w_in.shape[1]
     chunks = max(1, hidden // 512)
     return pl.pallas_call(
-        functools.partial(tower_body, chunks),
-        in_specs=[VMEM, ANY, ANY] + [ANY] * len(after),
+        functools.partial(tower_body, chunks, held),
+        in_specs=[VMEM if held else ANY, ANY, ANY] + [ANY] * len(after),
         out_specs=VMEM,
         out_shape=struct((rows, width), dtype),
         scratch_shapes=[
@@ -74,22 +83,32 @@
             pltpu.VMEM((rows, width), jnp.float32),
             pltpu.SemaphoreType.DMA((chunks,)),
             pltpu.SemaphoreType.DMA((chunks,)),
-        ],
+        ]
+        + ([] if held else [pltpu.VMEM(feats.shape, feats.dtype), pltpu.SemaphoreType.DMA]),
         compiler_params=params(52),
         cost_estimate=cost(1, 1),
-    )(feats, w_in, w_out, *after)
-
-
-def embed(feats, w_in, w_out, after):
+    )(feats if held else in_hbm(feats), w_in, w_out, *after)
+
+
+def embed(feats, w_in, w_out, after, held):
     if lax.axis_size("tensor") == 1:
-        return tower(feats, w_in, w_out, jnp.bfloat16, after)
+        return tower(feats, w_in, w_out, jnp.bfloat16, after, held)
     feats = lax.all_gather(feats, "tensor", axis=0, tiled=True)
-    partial = tower(feats, w_in, w_out, jnp.float32, after)
+    partial = tower(feats, w_in, w_out, jnp.float32, after, held)
     return lax.psum_scatter(partial, "tensor", scatter_dimension=0, tiled=True).astype(jnp.bfloat16)
 
 
-def teacher_body(cols, planes, me, cands, count, owner, teacher, *refs):
-    outs, (entropy, dense, sems) = refs[:cols], refs[cols:]
+def teacher_body(cols, planes, me, cands_hbm, count, owner_hbm, teacher_hbm, *refs):
+    outs, (entropy, dense, sems, teacher, cands, owner, load_sems) = refs[:cols], refs[cols:]
+    loads = [
+        pltpu.make_async_copy(source, target, load_sems.at[i])
+        for i, (source, target) in enumerate([(teacher_hbm, teacher), (cands_hbm, cands), (owner_hbm, owner)])
+    ]
+    for copy in loads:
+        copy.start()
+    dense[...] = jnp.full(dense.shape, DEAD, jnp.float32)
+    for copy in loads:
+        copy.wait()
     rows = teacher.shape[0]
     slots = cands.shape[1]
     live = count[0]
@@ -101,7 +120,6 @@
     prob = weight / norm
     log_sum = jnp.sum(jnp.where(usable, prob * (shifted - jnp.log(norm)), 0.0), axis=1, keepdims=True)
     entropy[...] = jnp.broadcast_to(log_sum, (rows, rows)).T[:1]
-    dense[...] = jnp.full(dense.shape, DEAD, jnp.float32)
     for k in range(slots):
 
         @pl.when(k < live)
@@ -123,16 +141,20 @@
     places = CORES * planes
     return pl.pallas_call(
         functools.partial(teacher_body, cols, planes),
-        in_specs=[SMEM, SMEM, SMEM, SMEM, VMEM],
+        in_specs=[SMEM, ANY, SMEM, ANY, ANY],
         out_specs=[ANY] * cols + [VMEM],
         out_shape=[struct((places, rows, rows), jnp.float32)] * cols + [struct((1, rows), jnp.float32)],
         scratch_shapes=[
             pltpu.VMEM((cols, places, rows, rows), jnp.float32),
             pltpu.SemaphoreType.DMA((cols,)),
+            pltpu.VMEM(teacher.shape, teacher.dtype),
+            pltpu.SMEM(cands.shape, cands.dtype),
+            pltpu.SMEM(owner.shape, owner.dtype),
+            pltpu.SemaphoreType.DMA((3,)),
         ],
         compiler_params=params(24),
         cost_estimate=cost(teacher.size, 8 * teacher.size),
-    )(me, cands, count, owner, teacher)
+    )(me, in_hbm(cands), count, in_hbm(owner), in_hbm(teacher))
 
 
 def lay(sources, target):
@@ -317,11 +339,11 @@
     first, *rest = probs
     probs = [first] + [swap(part, (c + 1) * CORES) for c, part in enumerate(rest)]
 
-    item_emb = embed(item_feats, item_w_in, item_w_out, [first])
+    item_emb = embed(item_feats, item_w_in, item_w_out, [first], False)
     wide = planes // 2
     crossed = [swap(item_emb, z * cols * CORES) for z in range(wide, planes if planes > 1 else 0, max(wide, 1))]
     nearby = [swap(item_emb, z * cols * CORES) for z in range(1, wide)]
-    user_emb = embed(user_feats, user_w_in, user_w_out, [item_emb])
+    user_emb = embed(user_feats, user_w_in, user_w_out, [item_emb], True)
     user_emb, item_emb, probs, crossed, nearby = lax.optimization_barrier((user_emb, item_emb, probs, crossed, nearby))
     users = [user_emb] + over_columns(user_emb)
     derived = [swap(block, z * cols * CORES) for block in crossed for z in range(1, wide)]

time: 92.6 us -> 90.8 us (0.981)
  local copies, waits for them, and re-layouts: 3.48 us -> 0.01 us
  Pallas kernels: 32.7 us -> 34 us
    unnamed x10 -> x2, local copies, waits for them, and re-layouts: 3.48 us -> 0.01 us
    pallas_call x2, Pallas kernels: 23.3 us -> 24.3 us  [tower(): pl.pallas_call(functools.partial(tower_body, chunks, held), in_specs=[VME...]
  transfers between devices with their start and end apart: 23 -> 23, of which waited for: 12 -> 12; matrix products, arithmetic and copies ran while one was open for 1% -> 1% of each run, Pallas kernels for 28% -> 29%
where the time goes in v6:
time: 90.8 us
  Pallas kernels  34 us (37%)
  waiting for transfers between devices  29 us (32%)
  starting transfers between devices  24.6 us (27%)
  other arithmetic  1.89 us (2%)
  between operations  1.39 us (2%)
    ppermute x23, waiting for transfers between devices, swap(): return lax.ppermute(array, 'dp', [(i, i ^ apart) for i in range(count)])  29 us
    ppermute x23, starting transfers between devices, swap(): return lax.ppermute(array, 'dp', [(i, i ^ apart) for i in range(count)])  24.6 us
    pallas_call x2, Pallas kernels, tower(): pl.pallas_call(functools.partial(tower_body, chunks, held), in_specs=[VME...  24.3 us
    pallas_call x1, Pallas kernels, spread_teacher(): pl.pallas_call(functools.partial(teacher_body, cols, planes), in_specs=[S...  3.12 us
    pallas_call x1, Pallas kernels, scores(): pl.pallas_call(functools.partial(score_body, cols, places, scale), in_spe...  2.75 us
    add x2, other arithmetic, add(): functools.reduce(jnp.add, [part.astype(jnp.float32) for part in parts], s...  1.83 us
  transfers between devices with their start and end apart: 23, of which 12 were waited for; matrix products, arithmetic and copies ran while one was open for 1% of the time, Pallas kernels for 29%

profile of v6, /device:TPU:0, one launch (start us, length us, event | category | flops | bytes accessed | tf_op | source)
XLA Modules:
  0.0 90.8 jit_solution(3787188567302159035)
XLA Ops:
  1.3 3.1 %shard_map.121 = (f32[8,128,128]{2,1,0:T(8,128)S(1)}, f32[8,128,128]{2,1,0:T(8,128)S(1)}, f32[8,128,128]{2,1,0:T(8,128)S(1)}, f32[8,128,128]{2,1,0:T(8,128)S(1)}, f32[1,128]{1,0:T(1,128)S(1)}) custom-call(s32[1]{0:T(128)} %bitcast.me, s32[1,16]{1,0:T(1,128)} %cands_hbm.1, s32[1]{0:T(128)S(6)} %copy.13.count, s32[32]{0:T(128)} %owner_hbm.1, ...), custom_call_target="tpu_custom_call" | custom-call | flops 262144 | bytes 2097152 | tf_op jit(solution)/shard_map/pallas_call | solution.py:142
  4.4 3.3 %collective-permute-start = (f32[8,128,128]{2,1,0:T(8,128)S(1)}, f32[8,128,128]{2,1,0:T(8,128)S(1)}, u32[]{:S(2)}, u32[]{:S(2)}) collective-permute-start(f32[8,128,128]{2,1,0:T(8,128)S(1)} %get-tuple-element.35), channel_id=1, source_target_pairs={{0,2},{1,3},{2,0},{3,1},{4,6},{5,7},{6,4},{7,5},{8,10},{9,11},{10,... | collective-permute-start | bytes 1572872 | tf_op jit(solution)/shard_map/ppermute | solution.py:333
  7.7 1.1 %collective-permute-start.1 = (f32[8,128,128]{2,1,0:T(8,128)S(1)}, f32[8,128,128]{2,1,0:T(8,128)S(1)}, u32[]{:S(2)}, u32[]{:S(2)}) collective-permute-start(f32[8,128,128]{2,1,0:T(8,128)S(1)} %get-tuple-element.36), channel_id=1, source_target_pairs={{0,4},{1,5},{2,6},{3,7},{4,0},{5,1},{6,2},{7,3},{8,12},{9,13},{10,... | collective-permute-start | bytes 1572872 | tf_op jit(solution)/shard_map/ppermute | solution.py:333
  8.8 0.5 collective-permute-start.2
  9.4 0.0 copy-start
  9.4 12.7 %shard_map.122.refs_0_.refs_4_ = bf16[128,1024]{1,0:T(8,128)(2,1)S(1)} custom-call(bf16[128,1024]{1,0:T(8,128)(2,1)} %feats.2, bf16[1024,8192]{1,0:T(8,128)(2,1)} %w_in.2, bf16[8192,1024]{1,0:T(8,128)(2,1)} %w_out.2, f32[8,128,128]{2,1,0:T(8,128)S(1)} %get-tuple-element.46.refs_0_.refs_12_.refs_8_), custom_call_target="tpu_custom_call" | custom-call | flops 1 | bytes 1 | tf_op jit(solution)/shard_map/pallas_call | solution.py:75
  22.1 2.1 %collective-permute-start.4 = (bf16[128,1024]{1,0:T(8,128)(2,1)S(1)}, bf16[128,1024]{1,0:T(8,128)(2,1)S(1)}, u32[]{:S(2)}, u32[]{:S(2)}) collective-permute-start(bf16[128,1024]{1,0:T(8,128)(2,1)S(1)} %shard_map.122.refs_0_.refs_4_), channel_id=1, source_target_pairs={{0,8},{1,9},{2,10},{3,11},{4,12},{5,13},{6,14},{7,15},{8,0},{9,1},... | collective-permute-start | bytes 786440 | tf_op jit(solution)/shard_map/ppermute | solution.py:333
  24.2 2.6 %collective-permute-start.3 = (bf16[128,1024]{1,0:T(8,128)(2,1)S(1)}, bf16[128,1024]{1,0:T(8,128)(2,1)S(1)}, u32[]{:S(2)}, u32[]{:S(2)}) collective-permute-start(bf16[128,1024]{1,0:T(8,128)(2,1)S(1)} %shard_map.122.refs_0_.refs_4_), channel_id=1, source_target_pairs={{0,16},{1,17},{2,18},{3,19},{4,20},{5,21},{6,22},{7,23},{8,24},{9,... | collective-permute-start | bytes 786440 | tf_op jit(solution)/shard_map/ppermute | solution.py:333
  26.8 0.0 copy-done
  26.8 11.7 %shard_map.123.refs_0_.refs_4_ = bf16[128,1024]{1,0:T(8,128)(2,1)S(1)} custom-call(bf16[128,1024]{1,0:T(8,128)(2,1)S(1)} %copy-done, bf16[1024,8192]{1,0:T(8,128)(2,1)} %w_in.3, bf16[8192,1024]{1,0:T(8,128)(2,1)} %w_out.3, bf16[128,1024]{1,0:T(8,128)(2,1)S(1)} %shard_map.122.refs_0_.refs_4_), custom_call_target="tpu_custom_call" | custom-call | flops 1 | bytes 1 | tf_op jit(solution)/shard_map/pallas_call | solution.py:75
  38.5 0.0 collective-permute-done.4.refs_5_.refs_1_
  38.5 0.0 collective-permute-done.3.refs_6_.refs_2_
  38.5 0.0 collective-permute-done.refs_13_.refs_9_
  38.5 0.0 collective-permute-done.1.refs_14_.refs_10_
  38.5 0.0 collective-permute-done.2.refs_15_.refs_11_
  38.5 1.3 %collective-permute-start.5 = (bf16[128,1024]{1,0:T(8,128)(2,1)S(1)}, bf16[128,1024]{1,0:T(8,128)(2,1)S(1)}, u32[]{:S(2)}, u32[]{:S(2)}) collective-permute-start(bf16[128,1024]{1,0:T(8,128)(2,1)S(1)} %shard_map.123.refs_0_.refs_4_), channel_id=1, source_target_pairs={{0,2},{1,3},{2,0},{3,1},{4,6},{5,7},{6,4},{7,5},{8,10},{9,11},{10,... | collective-permute-start | bytes 786440 | tf_op jit(solution)/shard_map/ppermute | solution.py:333
  39.8 0.3 collective-permute-start.8
  40.1 1.8 %collective-permute-start.7 = (bf16[128,1024]{1,0:T(8,128)(2,1)S(1)}, bf16[128,1024]{1,0:T(8,128)(2,1)S(1)}, u32[]{:S(2)}, u32[]{:S(2)}) collective-permute-start(bf16[128,1024]{1,0:T(8,128)(2,1)S(1)} %shard_map.123.refs_0_.refs_4_), channel_id=1, source_target_pairs={{0,6},{1,7},{2,4},{3,5},{4,2},{5,3},{6,0},{7,1},{8,14},{9,15},{10,... | collective-permute-start | bytes 786440 | tf_op jit(solution)/shard_map/ppermute | solution.py:333
  41.9 0.5 collective-permute-start.6
  42.4 5.4 %collective-permute-done.5.refs_1_.refs_5_ = bf16[128,1024]{1,0:T(8,128)(2,1)S(1)} collective-permute-done((bf16[128,1024]{1,0:T(8,128)(2,1)S(1)}, bf16[128,1024]{1,0:T(8,128)(2,1)S(1)}, u32[]{:S(2)}, u32[]{:S(2)}) %collective-permute-start.5) | collective-permute-done | bytes 262176 | tf_op jit(solution)/shard_map/ppermute | solution.py:333
  47.8 0.0 collective-permute-start.9
  47.8 0.5 collective-permute-start.10
  48.4 0.0 collective-permute-done.8.refs_7_.refs_3_
  48.4 0.0 collective-permute-start.12
  48.4 3.4 %collective-permute-done.7.refs_3_.refs_7_ = bf16[128,1024]{1,0:T(8,128)(2,1)S(1)} collective-permute-done((bf16[128,1024]{1,0:T(8,128)(2,1)S(1)}, bf16[128,1024]{1,0:T(8,128)(2,1)S(1)}, u32[]{:S(2)}, u32[]{:S(2)}) %collective-permute-start.7) | collective-permute-done | bytes 262176 | tf_op jit(solution)/shard_map/ppermute | solution.py:333
  51.7 0.0 collective-permute-start.11
  51.7 1.4 %collective-permute-done.6.refs_2_.refs_6_ = bf16[128,1024]{1,0:T(8,128)(2,1)S(1)} collective-permute-done((bf16[128,1024]{1,0:T(8,128)(2,1)S(1)}, bf16[128,1024]{1,0:T(8,128)(2,1)S(1)}, u32[]{:S(2)}, u32[]{:S(2)}) %collective-permute-start.6) | collective-permute-done | bytes 262176 | tf_op jit(solution)/shard_map/ppermute | solution.py:333
  53.2 0.0 collective-permute-done.12.refs_11_.refs_7_
  53.2 0.0 collective-permute-done.9.refs_8_.refs_4_
  53.2 0.0 collective-permute-done.10.refs_9_.refs_5_
  53.2 0.1 collective-permute-done.11.refs_10_.refs_6_
  53.3 2.7 %shard_map.124 = (f32[1024,512]{1,0:T(8,128)S(1)}, f32[4,4,128]{2,1,0:T(4,128)S(1)}) custom-call(bf16[128,1024]{1,0:T(8,128)(2,1)S(1)} %shard_map.123.refs_0_.refs_4_, bf16[128,1024]{1,0:T(8,128)(2,1)S(1)} %collective-permute-done.5.refs_1_.refs_5_, bf16[128,1024]{1,0:T(8,128)(2,1)S(1)} %collective-permute-done.6.refs_2_.refs_6_, ...), custom_call_target="tpu_custom_call" | custom-call | flops 1073741824 | bytes 4194304 | tf_op jit(solution)/shard_map/pallas_call | solution.py:196
  56.0 1.5 %collective-permute-start.15 = (f32[4,4,128]{2,1,0:T(4,128)S(1)}, f32[4,4,128]{2,1,0:T(4,128)S(1)}, u32[]{:S(2)}, u32[]{:S(2)}) collective-permute-start(f32[4,4,128]{2,1,0:T(4,128)S(1)} %get-tuple-element.50.refs_0_), channel_id=1, source_target_pairs={{0,6},{1,7},{2,4},{3,5},{4,2},{5,3},{6,0},{7,1},{8,14},{9,15},{10,... | collective-permute-start | bytes 24584 | tf_op jit(solution)/shard_map/ppermute | solution.py:333
  57.5 1.7 %collective-permute-start.14 = (f32[4,4,128]{2,1,0:T(4,128)S(1)}, f32[4,4,128]{2,1,0:T(4,128)S(1)}, u32[]{:S(2)}, u32[]{:S(2)}) collective-permute-start(f32[4,4,128]{2,1,0:T(4,128)S(1)} %get-tuple-element.50.refs_0_), channel_id=1, source_target_pairs={{0,4},{1,5},{2,6},{3,7},{4,0},{5,1},{6,2},{7,3},{8,12},{9,13},{10,... | collective-permute-start | bytes 24584 | tf_op jit(solution)/shard_map/ppermute | solution.py:333
  59.2 0.4 collective-permute-start.13
  59.6 1.1 %collective-permute-done.15.refs_3_ = f32[4,4,128]{2,1,0:T(4,128)S(1)} collective-permute-done((f32[4,4,128]{2,1,0:T(4,128)S(1)}, f32[4,4,128]{2,1,0:T(4,128)S(1)}, u32[]{:S(2)}, u32[]{:S(2)}) %collective-permute-start.15) | collective-permute-done | bytes 8224 | tf_op jit(solution)/shard_map/ppermute | solution.py:333
  60.6 0.5 collective-permute-done.14.refs_2_
  61.2 1.7 %collective-permute-done.13.refs_1_ = f32[4,4,128]{2,1,0:T(4,128)S(1)} collective-permute-done((f32[4,4,128]{2,1,0:T(4,128)S(1)}, f32[4,4,128]{2,1,0:T(4,128)S(1)}, u32[]{:S(2)}, u32[]{:S(2)}) %collective-permute-start.13) | collective-permute-done | bytes 8224 | tf_op jit(solution)/shard_map/ppermute | solution.py:333
  62.9 1.6 %shard_map.125 = (bf16[1024,512]{1,0:T(8,128)(2,1)S(1)}, f32[1,128]{1,0:T(1,128)}, bf16[512,1024]{1,0:T(8,128)(2,1)S(1)}) custom-call(f32[1,128]{1,0:T(1,128)S(1)} %get-tuple-element.33.entropy, f32[4,4,128]{2,1,0:T(4,128)S(1)} %get-tuple-element.50.refs_0_, f32[4,4,128]{2,1,0:T(4,128)S(1)} %collective-permute-done.13.refs_1_, ...), custom_call_target="tpu_custom_call" | custom-call | flops 536870912 | bytes 4194304 | tf_op jit(solution)/shard_map/pallas_call | solution.py:236
  64.4 0.0 collective-permute-start.16
  64.4 0.7 shard_map.126.near
  65.2 1.9 %collective-permute-done.16.far = bf16[512,1024]{1,0:T(8,128)(2,1)S(1)} collective-permute-done((bf16[512,1024]{1,0:T(8,128)(2,1)S(1)}, bf16[512,1024]{1,0:T(8,128)(2,1)S(1)}, u32[]{:S(2)}, u32[]{:S(2)}) %collective-permute-start.16) | collective-permute-done | bytes 1048608 | tf_op jit(solution)/shard_map/ppermute | solution.py:333
  67.1 0.2 shard_map.127
  67.3 1.7 %collective-permute-start.20 = (bf16[128,1024]{1,0:T(8,128)(2,1)S(1)}, bf16[128,1024]{1,0:T(8,128)(2,1)S(1)}, u32[]{:S(2)}, u32[]{:S(2)}) collective-permute-start(bf16[128,1024]{1,0:T(8,128)(2,1)S(1)} %get-tuple-element.61), channel_id=1, source_target_pairs={{0,8},{1,9},{2,10},{3,11},{4,12},{5,13},{6,14},{7,15},{8,0},{9,1},... | collective-permute-start | bytes 786440 | tf_op jit(solution)/shard_map/ppermute | solution.py:333
  68.9 1.3 %shard_map.128 = (f32[128,1024]{1,0:T(8,128)S(1)}, bf16[128,1024]{1,0:T(8,128)(2,1)S(1)}, bf16[128,1024]{1,0:T(8,128)(2,1)S(1)}, bf16[128,1024]{1,0:T(8,128)(2,1)S(1)}) custom-call(bf16[1024,512]{1,0:T(8,128)(2,1)S(1)} %get-tuple-element.53.grads, bf16[128,1024]{1,0:T(8,128)(2,1)S(1)} %shard_map.122.refs_0_.refs_4_, ...), custom_call_target="tpu_custom_call" | custom-call | flops 1073741824 | bytes 2097152 | tf_op jit(solution)/shard_map/pallas_call | solution.py:289
  70.3 0.4 collective-permute-start.17
  70.7 0.5 collective-permute-start.18
  71.2 2.6 %collective-permute-start.19 = (bf16[128,1024]{1,0:T(8,128)(2,1)S(1)}, bf16[128,1024]{1,0:T(8,128)(2,1)S(1)}, u32[]{:S(2)}, u32[]{:S(2)}) collective-permute-start(bf16[128,1024]{1,0:T(8,128)(2,1)S(1)} %get-tuple-element.59), channel_id=1, source_target_pairs={{0,6},{1,7},{2,4},{3,5},{4,2},{5,3},{6,0},{7,1},{8,14},{9,15},{10,... | collective-permute-start | bytes 786440 | tf_op jit(solution)/shard_map/ppermute | solution.py:333
  73.8 0.4 collective-permute-start.22
  74.3 1.6 %collective-permute-done.20 = bf16[128,1024]{1,0:T(8,128)(2,1)S(1)} collective-permute-done((bf16[128,1024]{1,0:T(8,128)(2,1)S(1)}, bf16[128,1024]{1,0:T(8,128)(2,1)S(1)}, u32[]{:S(2)}, u32[]{:S(2)}) %collective-permute-start.20) | collective-permute-done | bytes 262176 | tf_op jit(solution)/shard_map/ppermute | solution.py:333
  75.8 0.1 add_convert_fusion
  75.9 1.2 %collective-permute-start.21 = (bf16[128,1024]{1,0:T(8,128)(2,1)S(1)}, bf16[128,1024]{1,0:T(8,128)(2,1)S(1)}, u32[]{:S(2)}, u32[]{:S(2)}) collective-permute-start(bf16[128,1024]{1,0:T(8,128)(2,1)S(1)} %add_convert_fusion), channel_id=1, source_target_pairs={{0,16},{1,17},{2,18},{3,19},{4,20},{5,21},{6,22},{7,23},{8,24},{9,... | collective-permute-start | bytes 786440 | tf_op jit(solution)/shard_map/ppermute | solution.py:333
  77.1 2.4 %collective-permute-done.17 = bf16[128,1024]{1,0:T(8,128)(2,1)S(1)} collective-permute-done((bf16[128,1024]{1,0:T(8,128)(2,1)S(1)}, bf16[128,1024]{1,0:T(8,128)(2,1)S(1)}, u32[]{:S(2)}, u32[]{:S(2)}) %collective-permute-start.17) | collective-permute-done | bytes 262176 | tf_op jit(solution)/shard_map/ppermute | solution.py:333
  79.5 4.6 %collective-permute-done.18 = bf16[128,1024]{1,0:T(8,128)(2,1)S(1)} collective-permute-done((bf16[128,1024]{1,0:T(8,128)(2,1)S(1)}, bf16[128,1024]{1,0:T(8,128)(2,1)S(1)}, u32[]{:S(2)}, u32[]{:S(2)}) %collective-permute-start.18) | collective-permute-done | bytes 262176 | tf_op jit(solution)/shard_map/ppermute | solution.py:333
  84.1 0.0 collective-permute-done.19
  84.1 0.9 %convert_add_fusion.1 = f32[128,1024]{1,0:T(8,128)} fusion(bf16[128,1024]{1,0:T(8,128)(2,1)S(1)} %collective-permute-done.19, bf16[128,1024]{1,0:T(8,128)(2,1)S(1)} %collective-permute-done.18, f32[128,1024]{1,0:T(8,128)S(1)} %get-tuple-element.56, bf16[128,1024]{1,0:T(8,128)(2,1)S(1)} %collective-permute-done.17), kind=kLoop, calls=%fused_computation.2 | loop fusion | flops 786432 | bytes 1835008 | tf_op jit(solution)/shard_map/add | solution.py:369
  85.1 0.0 collective-permute-done.22
  85.1 4.8 %collective-permute-done.21 = bf16[128,1024]{1,0:T(8,128)(2,1)S(1)} collective-permute-done((bf16[128,1024]{1,0:T(8,128)(2,1)S(1)}, bf16[128,1024]{1,0:T(8,128)(2,1)S(1)}, u32[]{:S(2)}, u32[]{:S(2)}) %collective-permute-start.21) | collective-permute-done | bytes 262176 | tf_op jit(solution)/shard_map/ppermute | solution.py:333
  89.9 0.9 convert_add_fusion
Async XLA Ops:
  4.4 34.1 %collective-permute-start = (f32[8,128,128]{2,1,0:T(8,128)S(1)}, f32[8,128,128]{2,1,0:T(8,128)S(1)}, u32[]{:S(2)}, u32[]{:S(2)}) collective-permute-start(f32[8,128,128]{2,1,0:T(8,128)S(1)} %get-tuple-element.35), channel_id=1, source_target_pairs={{0,2},{1,3},{2,0},{3,1},{4,6},{5,7},{6,4},{7,5},{8,10},{9,11},{10,... | collective-permute-start | bytes 1572872 | tf_op jit(solution)/shard_map/ppermute | solution.py:333
  7.7 30.8 %collective-permute-start.1 = (f32[8,128,128]{2,1,0:T(8,128)S(1)}, f32[8,128,128]{2,1,0:T(8,128)S(1)}, u32[]{:S(2)}, u32[]{:S(2)}) collective-permute-start(f32[8,128,128]{2,1,0:T(8,128)S(1)} %get-tuple-element.36), channel_id=1, source_target_pairs={{0,4},{1,5},{2,6},{3,7},{4,0},{5,1},{6,2},{7,3},{8,12},{9,13},{10,... | collective-permute-start | bytes 1572872 | tf_op jit(solution)/shard_map/ppermute | solution.py:333
  8.8 29.7 %collective-permute-start.2 = (f32[8,128,128]{2,1,0:T(8,128)S(1)}, f32[8,128,128]{2,1,0:T(8,128)S(1)}, u32[]{:S(2)}, u32[]{:S(2)}) collective-permute-start(f32[8,128,128]{2,1,0:T(8,128)S(1)} %get-tuple-element.37), channel_id=1, source_target_pairs={{0,6},{1,7},{2,4},{3,5},{4,2},{5,3},{6,0},{7,1},{8,14},{9,15},{10,... | collective-permute-start | bytes 1572872 | tf_op jit(solution)/shard_map/ppermute | solution.py:333
  9.4 17.4 %copy-start = (bf16[128,1024]{1,0:T(8,128)(2,1)S(1)}, bf16[128,1024]{1,0:T(8,128)(2,1)}, u32[]{:S(2)}) copy-start(bf16[128,1024]{1,0:T(8,128)(2,1)} %feats.3) | copy-start | bytes 786436
  22.1 16.4 %collective-permute-start.4 = (bf16[128,1024]{1,0:T(8,128)(2,1)S(1)}, bf16[128,1024]{1,0:T(8,128)(2,1)S(1)}, u32[]{:S(2)}, u32[]{:S(2)}) collective-permute-start(bf16[128,1024]{1,0:T(8,128)(2,1)S(1)} %shard_map.122.refs_0_.refs_4_), channel_id=1, source_target_pairs={{0,8},{1,9},{2,10},{3,11},{4,12},{5,13},{6,14},{7,15},{8,0},{9,1},... | collective-permute-start | bytes 786440 | tf_op jit(solution)/shard_map/ppermute | solution.py:333
  24.2 14.3 %collective-permute-start.3 = (bf16[128,1024]{1,0:T(8,128)(2,1)S(1)}, bf16[128,1024]{1,0:T(8,128)(2,1)S(1)}, u32[]{:S(2)}, u32[]{:S(2)}) collective-permute-start(bf16[128,1024]{1,0:T(8,128)(2,1)S(1)} %shard_map.122.refs_0_.refs_4_), channel_id=1, source_target_pairs={{0,16},{1,17},{2,18},{3,19},{4,20},{5,21},{6,22},{7,23},{8,24},{9,... | collective-permute-start | bytes 786440 | tf_op jit(solution)/shard_map/ppermute | solution.py:333
  38.5 9.3 %collective-permute-start.5 = (bf16[128,1024]{1,0:T(8,128)(2,1)S(1)}, bf16[128,1024]{1,0:T(8,128)(2,1)S(1)}, u32[]{:S(2)}, u32[]{:S(2)}) collective-permute-start(bf16[128,1024]{1,0:T(8,128)(2,1)S(1)} %shard_map.123.refs_0_.refs_4_), channel_id=1, source_target_pairs={{0,2},{1,3},{2,0},{3,1},{4,6},{5,7},{6,4},{7,5},{8,10},{9,11},{10,... | collective-permute-start | bytes 786440 | tf_op jit(solution)/shard_map/ppermute | solution.py:333
  39.8 8.5 %collective-permute-start.8 = (bf16[128,1024]{1,0:T(8,128)(2,1)S(1)}, bf16[128,1024]{1,0:T(8,128)(2,1)S(1)}, u32[]{:S(2)}, u32[]{:S(2)}) collective-permute-start(bf16[128,1024]{1,0:T(8,128)(2,1)S(1)} %collective-permute-done.3.refs_6_.refs_2_), channel_id=1, source_target_pairs={{0,8},{1,9},{2,10},{3,11},{4,12},{5,13},{6,14},{7,15},{8,0},{9,1},... | collective-permute-start | bytes 786440 | tf_op jit(solution)/shard_map/ppermute | solution.py:333
  40.1 11.6 %collective-permute-start.7 = (bf16[128,1024]{1,0:T(8,128)(2,1)S(1)}, bf16[128,1024]{1,0:T(8,128)(2,1)S(1)}, u32[]{:S(2)}, u32[]{:S(2)}) collective-permute-start(bf16[128,1024]{1,0:T(8,128)(2,1)S(1)} %shard_map.123.refs_0_.refs_4_), channel_id=1, source_target_pairs={{0,6},{1,7},{2,4},{3,5},{4,2},{5,3},{6,0},{7,1},{8,14},{9,15},{10,... | collective-permute-start | bytes 786440 | tf_op jit(solution)/shard_map/ppermute | solution.py:333
  41.9 11.3 %collective-permute-start.6 = (bf16[128,1024]{1,0:T(8,128)(2,1)S(1)}, bf16[128,1024]{1,0:T(8,128)(2,1)S(1)}, u32[]{:S(2)}, u32[]{:S(2)}) collective-permute-start(bf16[128,1024]{1,0:T(8,128)(2,1)S(1)} %shard_map.123.refs_0_.refs_4_), channel_id=1, source_target_pairs={{0,4},{1,5},{2,6},{3,7},{4,0},{5,1},{6,2},{7,3},{8,12},{9,13},{10,... | collective-permute-start | bytes 786440 | tf_op jit(solution)/shard_map/ppermute | solution.py:333
  47.8 5.4 %collective-permute-start.9 = (bf16[128,1024]{1,0:T(8,128)(2,1)S(1)}, bf16[128,1024]{1,0:T(8,128)(2,1)S(1)}, u32[]{:S(2)}, u32[]{:S(2)}) collective-permute-start(bf16[128,1024]{1,0:T(8,128)(2,1)S(1)} %shard_map.122.refs_0_.refs_4_), channel_id=1, source_target_pairs={{0,1},{1,0},{2,3},{3,2},{4,5},{5,4},{6,7},{7,6},{8,9},{9,8},{10,11... | collective-permute-start | bytes 786440 | tf_op jit(solution)/shard_map/ppermute | solution.py:333
  47.8 5.4 %collective-permute-start.10 = (bf16[128,1024]{1,0:T(8,128)(2,1)S(1)}, bf16[128,1024]{1,0:T(8,128)(2,1)S(1)}, u32[]{:S(2)}, u32[]{:S(2)}) collective-permute-start(bf16[128,1024]{1,0:T(8,128)(2,1)S(1)} %collective-permute-done.4.refs_5_.refs_1_), channel_id=1, source_target_pairs={{0,1},{1,0},{2,3},{3,2},{4,5},{5,4},{6,7},{7,6},{8,9},{9,8},{10,11... | collective-permute-start | bytes 786440 | tf_op jit(solution)/shard_map/ppermute | solution.py:333
  48.4 4.8 %collective-permute-start.12 = (bf16[128,1024]{1,0:T(8,128)(2,1)S(1)}, bf16[128,1024]{1,0:T(8,128)(2,1)S(1)}, u32[]{:S(2)}, u32[]{:S(2)}) collective-permute-start(bf16[128,1024]{1,0:T(8,128)(2,1)S(1)} %collective-permute-done.8.refs_7_.refs_3_), channel_id=1, source_target_pairs={{0,1},{1,0},{2,3},{3,2},{4,5},{5,4},{6,7},{7,6},{8,9},{9,8},{10,11... | collective-permute-start | bytes 786440 | tf_op jit(solution)/shard_map/ppermute | solution.py:333
  51.7 1.5 %collective-permute-start.11 = (bf16[128,1024]{1,0:T(8,128)(2,1)S(1)}, bf16[128,1024]{1,0:T(8,128)(2,1)S(1)}, u32[]{:S(2)}, u32[]{:S(2)}) collective-permute-start(bf16[128,1024]{1,0:T(8,128)(2,1)S(1)} %collective-permute-done.3.refs_6_.refs_2_), channel_id=1, source_target_pairs={{0,1},{1,0},{2,3},{3,2},{4,5},{5,4},{6,7},{7,6},{8,9},{9,8},{10,11... | collective-permute-start | bytes 786440 | tf_op jit(solution)/shard_map/ppermute | solution.py:333
  56.0 4.6 %collective-permute-start.15 = (f32[4,4,128]{2,1,0:T(4,128)S(1)}, f32[4,4,128]{2,1,0:T(4,128)S(1)}, u32[]{:S(2)}, u32[]{:S(2)}) collective-permute-start(f32[4,4,128]{2,1,0:T(4,128)S(1)} %get-tuple-element.50.refs_0_), channel_id=1, source_target_pairs={{0,6},{1,7},{2,4},{3,5},{4,2},{5,3},{6,0},{7,1},{8,14},{9,15},{10,... | collective-permute-start | bytes 24584 | tf_op jit(solution)/shard_map/ppermute | solution.py:333
  57.5 3.7 %collective-permute-start.14 = (f32[4,4,128]{2,1,0:T(4,128)S(1)}, f32[4,4,128]{2,1,0:T(4,128)S(1)}, u32[]{:S(2)}, u32[]{:S(2)}) collective-permute-start(f32[4,4,128]{2,1,0:T(4,128)S(1)} %get-tuple-element.50.refs_0_), channel_id=1, source_target_pairs={{0,4},{1,5},{2,6},{3,7},{4,0},{5,1},{6,2},{7,3},{8,12},{9,13},{10,... | collective-permute-start | bytes 24584 | tf_op jit(solution)/shard_map/ppermute | solution.py:333
  59.2 3.7 %collective-permute-start.13 = (f32[4,4,128]{2,1,0:T(4,128)S(1)}, f32[4,4,128]{2,1,0:T(4,128)S(1)}, u32[]{:S(2)}, u32[]{:S(2)}) collective-permute-start(f32[4,4,128]{2,1,0:T(4,128)S(1)} %get-tuple-element.50.refs_0_), channel_id=1, source_target_pairs={{0,2},{1,3},{2,0},{3,1},{4,6},{5,7},{6,4},{7,5},{8,10},{9,11},{10,... | collective-permute-start | bytes 24584 | tf_op jit(solution)/shard_map/ppermute | solution.py:333
  64.4 2.7 %collective-permute-start.16 = (bf16[512,1024]{1,0:T(8,128)(2,1)S(1)}, bf16[512,1024]{1,0:T(8,128)(2,1)S(1)}, u32[]{:S(2)}, u32[]{:S(2)}) collective-permute-start(bf16[512,1024]{1,0:T(8,128)(2,1)S(1)} %get-tuple-element.54), channel_id=1, source_target_pairs={{0,1},{1,0},{2,3},{3,2},{4,5},{5,4},{6,7},{7,6},{8,9},{9,8},{10,11... | collective-permute-start | bytes 3145736 | tf_op jit(solution)/shard_map/ppermute | solution.py:333
  67.3 8.6 %collective-permute-start.20 = (bf16[128,1024]{1,0:T(8,128)(2,1)S(1)}, bf16[128,1024]{1,0:T(8,128)(2,1)S(1)}, u32[]{:S(2)}, u32[]{:S(2)}) collective-permute-start(bf16[128,1024]{1,0:T(8,128)(2,1)S(1)} %get-tuple-element.61), channel_id=1, source_target_pairs={{0,8},{1,9},{2,10},{3,11},{4,12},{5,13},{6,14},{7,15},{8,0},{9,1},... | collective-permute-start | bytes 786440 | tf_op jit(solution)/shard_map/ppermute | solution.py:333
  70.3 9.3 %collective-permute-start.17 = (bf16[128,1024]{1,0:T(8,128)(2,1)S(1)}, bf16[128,1024]{1,0:T(8,128)(2,1)S(1)}, u32[]{:S(2)}, u32[]{:S(2)}) collective-permute-start(bf16[128,1024]{1,0:T(8,128)(2,1)S(1)} %get-tuple-element.57), channel_id=1, source_target_pairs={{0,2},{1,3},{2,0},{3,1},{4,6},{5,7},{6,4},{7,5},{8,10},{9,11},{10,... | collective-permute-start | bytes 786440 | tf_op jit(solution)/shard_map/ppermute | solution.py:333
  70.7 13.4 %collective-permute-start.18 = (bf16[128,1024]{1,0:T(8,128)(2,1)S(1)}, bf16[128,1024]{1,0:T(8,128)(2,1)S(1)}, u32[]{:S(2)}, u32[]{:S(2)}) collective-permute-start(bf16[128,1024]{1,0:T(8,128)(2,1)S(1)} %get-tuple-element.58), channel_id=1, source_target_pairs={{0,4},{1,5},{2,6},{3,7},{4,0},{5,1},{6,2},{7,3},{8,12},{9,13},{10,... | collective-permute-start | bytes 786440 | tf_op jit(solution)/shard_map/ppermute | solution.py:333
  71.2 12.9 %collective-permute-start.19 = (bf16[128,1024]{1,0:T(8,128)(2,1)S(1)}, bf16[128,1024]{1,0:T(8,128)(2,1)S(1)}, u32[]{:S(2)}, u32[]{:S(2)}) collective-permute-start(bf16[128,1024]{1,0:T(8,128)(2,1)S(1)} %get-tuple-element.59), channel_id=1, source_target_pairs={{0,6},{1,7},{2,4},{3,5},{4,2},{5,3},{6,0},{7,1},{8,14},{9,15},{10,... | collective-permute-start | bytes 786440 | tf_op jit(solution)/shard_map/ppermute | solution.py:333
  73.8 11.2 %collective-permute-start.22 = (bf16[128,1024]{1,0:T(8,128)(2,1)S(1)}, bf16[128,1024]{1,0:T(8,128)(2,1)S(1)}, u32[]{:S(2)}, u32[]{:S(2)}) collective-permute-start(bf16[128,1024]{1,0:T(8,128)(2,1)S(1)} %get-tuple-element.62), channel_id=1, source_target_pairs={{0,8},{1,9},{2,10},{3,11},{4,12},{5,13},{6,14},{7,15},{8,0},{9,1},... | collective-permute-start | bytes 786440 | tf_op jit(solution)/shard_map/ppermute | solution.py:333
  75.9 14.0 %collective-permute-start.21 = (bf16[128,1024]{1,0:T(8,128)(2,1)S(1)}, bf16[128,1024]{1,0:T(8,128)(2,1)S(1)}, u32[]{:S(2)}, u32[]{:S(2)}) collective-permute-start(bf16[128,1024]{1,0:T(8,128)(2,1)S(1)} %add_convert_fusion), channel_id=1, source_target_pairs={{0,16},{1,17},{2,18},{3,19},{4,20},{5,21},{6,22},{7,23},{8,24},{9,... | collective-permute-start | bytes 786440 | tf_op jit(solution)/shard_map/ppermute | solution.py:333

commit v7 on v6

--- a/solution.py
+++ b/solution.py
@@ -35,12 +35,8 @@
 
 def tower_body(chunks, held, feats, w_in, w_out, *refs):
     out, held_in, held_out, total, sem_in, sem_out, *own = refs[-6 if held else -8 :]
-    if not held:
-        load = pltpu.make_async_copy(feats, *own)
-        load.start()
-        load.wait()
-        feats = own[0]
     step = w_in.shape[1] // chunks
+    ahead = 0 if held else 1
 
     def copies(i):
         part = pl.ds(pl.multiple_of(i * step, step), step)
@@ -49,7 +45,14 @@
             pltpu.make_async_copy(w_out.at[part], held_out.at[part], sem_out.at[i]),
         )
 
-    for i in range(chunks):
+    if not held:
+        load = pltpu.make_async_copy(feats, *own)
+        load.start()
+        for copy in copies(0):
+            copy.start()
+        load.wait()
+        feats = own[0]
+    for i in range(ahead, chunks):
         for copy in copies(i):
             copy.start()
     total[...] = jnp.zeros_like(total)
@@ -64,7 +67,7 @@
         total[...] += jnp.dot(hidden, held_out[part], preferred_element_type=jnp.float32)
         return carry
 
-    lax.fori_loop(0, chunks, one, 0)
+    lax.fori_loop(0, chunks, one, 0, unroll=True)
     out[...] = total[...].astype(out.dtype)
 
 

time: 90.8 us -> 89.6 us (0.987)
    pallas_call x2, Pallas kernels: 24.3 us -> 23.1 us  [tower(): pl.pallas_call(functools.partial(tower_body, chunks, held), in_specs=[VME...]
  transfers between devices with their start and end apart: 23 -> 23, of which waited for: 12 -> 12; matrix products, arithmetic and copies ran while one was open for 1% -> 1% of each run, Pallas kernels for 29% -> 28%
where the time goes in v7:
time: 89.6 us; the launch traced here: 89.8 us
  Pallas kernels  33.2 us (37%)
  waiting for transfers between devices  28.5 us (32%)
  starting transfers between devices  24.8 us (28%)
  other arithmetic  1.89 us (2%)
  between operations  1.39 us (2%)
    ppermute x23, waiting for transfers between devices, swap(): return lax.ppermute(array, 'dp', [(i, i ^ apart) for i in range(count)])  28.5 us
    ppermute x23, starting transfers between devices, swap(): return lax.ppermute(array, 'dp', [(i, i ^ apart) for i in range(count)])  24.8 us
    pallas_call x2, Pallas kernels, tower(): pl.pallas_call(functools.partial(tower_body, chunks, held), in_specs=[VME...  23.1 us
    pallas_call x1, Pallas kernels, spread_teacher(): pl.pallas_call(functools.partial(teacher_body, cols, planes), in_specs=[S...  3.41 us
    pallas_call x1, Pallas kernels, scores(): pl.pallas_call(functools.partial(score_body, cols, places, scale), in_spe...  2.92 us
    add x2, other arithmetic, add(): functools.reduce(jnp.add, [part.astype(jnp.float32) for part in parts], s...  1.83 us
  transfers between devices with their start and end apart: 23, of which 12 were waited for; matrix products, arithmetic and copies ran while one was open for 1% of the time, Pallas kernels for 28%

profile of v7, /device:TPU:0, one launch (start us, length us, event | category | flops | bytes accessed | tf_op | source)
XLA Modules:
  0.0 89.8 jit_solution(7455944878734375678)
XLA Ops:
  1.3 3.4 %shard_map.121 = (f32[8,128,128]{2,1,0:T(8,128)S(1)}, f32[8,128,128]{2,1,0:T(8,128)S(1)}, f32[8,128,128]{2,1,0:T(8,128)S(1)}, f32[8,128,128]{2,1,0:T(8,128)S(1)}, f32[1,128]{1,0:T(1,128)S(1)}) custom-call(s32[1]{0:T(128)} %bitcast.me, s32[1,16]{1,0:T(1,128)} %cands_hbm.1, s32[1]{0:T(128)S(6)} %copy.13.count, s32[32]{0:T(128)} %owner_hbm.1, ...), custom_call_target="tpu_custom_call" | custom-call | flops 262144 | bytes 2097152 | tf_op jit(solution)/shard_map/pallas_call | solution.py:145
  4.7 2.6 %collective-permute-start = (f32[8,128,128]{2,1,0:T(8,128)S(1)}, f32[8,128,128]{2,1,0:T(8,128)S(1)}, u32[]{:S(2)}, u32[]{:S(2)}) collective-permute-start(f32[8,128,128]{2,1,0:T(8,128)S(1)} %get-tuple-element.35), channel_id=1, source_target_pairs={{0,2},{1,3},{2,0},{3,1},{4,6},{5,7},{6,4},{7,5},{8,10},{9,11},{10,... | collective-permute-start | bytes 1572872 | tf_op jit(solution)/shard_map/ppermute | solution.py:336
  7.3 2.0 %collective-permute-start.1 = (f32[8,128,128]{2,1,0:T(8,128)S(1)}, f32[8,128,128]{2,1,0:T(8,128)S(1)}, u32[]{:S(2)}, u32[]{:S(2)}) collective-permute-start(f32[8,128,128]{2,1,0:T(8,128)S(1)} %get-tuple-element.36), channel_id=1, source_target_pairs={{0,4},{1,5},{2,6},{3,7},{4,0},{5,1},{6,2},{7,3},{8,12},{9,13},{10,... | collective-permute-start | bytes 1572872 | tf_op jit(solution)/shard_map/ppermute | solution.py:336
  9.3 0.1 collective-permute-start.2
  9.4 0.0 copy-start
  9.4 11.8 %shard_map.122.refs_0_.refs_4_ = bf16[128,1024]{1,0:T(8,128)(2,1)S(1)} custom-call(bf16[128,1024]{1,0:T(8,128)(2,1)} %feats.2, bf16[1024,8192]{1,0:T(8,128)(2,1)} %w_in.2, bf16[8192,1024]{1,0:T(8,128)(2,1)} %w_out.2, f32[8,128,128]{2,1,0:T(8,128)S(1)} %get-tuple-element.46.refs_0_.refs_12_.refs_8_), custom_call_target="tpu_custom_call" | custom-call | flops 1 | bytes 1 | tf_op jit(solution)/shard_map/pallas_call | solution.py:78
  21.2 1.8 %collective-permute-start.4 = (bf16[128,1024]{1,0:T(8,128)(2,1)S(1)}, bf16[128,1024]{1,0:T(8,128)(2,1)S(1)}, u32[]{:S(2)}, u32[]{:S(2)}) collective-permute-start(bf16[128,1024]{1,0:T(8,128)(2,1)S(1)} %shard_map.122.refs_0_.refs_4_), channel_id=1, source_target_pairs={{0,8},{1,9},{2,10},{3,11},{4,12},{5,13},{6,14},{7,15},{8,0},{9,1},... | collective-permute-start | bytes 786440 | tf_op jit(solution)/shard_map/ppermute | solution.py:336
  23.0 2.5 %collective-permute-start.3 = (bf16[128,1024]{1,0:T(8,128)(2,1)S(1)}, bf16[128,1024]{1,0:T(8,128)(2,1)S(1)}, u32[]{:S(2)}, u32[]{:S(2)}) collective-permute-start(bf16[128,1024]{1,0:T(8,128)(2,1)S(1)} %shard_map.122.refs_0_.refs_4_), channel_id=1, source_target_pairs={{0,16},{1,17},{2,18},{3,19},{4,20},{5,21},{6,22},{7,23},{8,24},{9,... | collective-permute-start | bytes 786440 | tf_op jit(solution)/shard_map/ppermute | solution.py:336
  25.5 0.0 copy-done
  25.5 11.3 %shard_map.123.refs_0_.refs_4_ = bf16[128,1024]{1,0:T(8,128)(2,1)S(1)} custom-call(bf16[128,1024]{1,0:T(8,128)(2,1)S(1)} %copy-done, bf16[1024,8192]{1,0:T(8,128)(2,1)} %w_in.3, bf16[8192,1024]{1,0:T(8,128)(2,1)} %w_out.3, bf16[128,1024]{1,0:T(8,128)(2,1)S(1)} %shard_map.122.refs_0_.refs_4_), custom_call_target="tpu_custom_call" | custom-call | flops 1 | bytes 1 | tf_op jit(solution)/shard_map/pallas_call | solution.py:78
  36.8 0.0 collective-permute-done.4.refs_5_.refs_1_
  36.8 0.0 collective-permute-done.3.refs_6_.refs_2_
  36.8 0.0 collective-permute-done.refs_13_.refs_9_
  36.8 0.0 collective-permute-done.1.refs_14_.refs_10_
  36.8 0.0 collective-permute-done.2.refs_15_.refs_11_
  36.8 1.8 %collective-permute-start.5 = (bf16[128,1024]{1,0:T(8,128)(2,1)S(1)}, bf16[128,1024]{1,0:T(8,128)(2,1)S(1)}, u32[]{:S(2)}, u32[]{:S(2)}) collective-permute-start(bf16[128,1024]{1,0:T(8,128)(2,1)S(1)} %shard_map.123.refs_0_.refs_4_), channel_id=1, source_target_pairs={{0,2},{1,3},{2,0},{3,1},{4,6},{5,7},{6,4},{7,5},{8,10},{9,11},{10,... | collective-permute-start | bytes 786440 | tf_op jit(solution)/shard_map/ppermute | solution.py:336
  38.6 0.2 collective-permute-start.8
  38.8 2.0 %collective-permute-start.7 = (bf16[128,1024]{1,0:T(8,128)(2,1)S(1)}, bf16[128,1024]{1,0:T(8,128)(2,1)S(1)}, u32[]{:S(2)}, u32[]{:S(2)}) collective-permute-start(bf16[128,1024]{1,0:T(8,128)(2,1)S(1)} %shard_map.123.refs_0_.refs_4_), channel_id=1, source_target_pairs={{0,6},{1,7},{2,4},{3,5},{4,2},{5,3},{6,0},{7,1},{8,14},{9,15},{10,... | collective-permute-start | bytes 786440 | tf_op jit(solution)/shard_map/ppermute | solution.py:336
  40.8 0.5 collective-permute-start.6
  41.3 4.8 %collective-permute-done.5.refs_1_.refs_5_ = bf16[128,1024]{1,0:T(8,128)(2,1)S(1)} collective-permute-done((bf16[128,1024]{1,0:T(8,128)(2,1)S(1)}, bf16[128,1024]{1,0:T(8,128)(2,1)S(1)}, u32[]{:S(2)}, u32[]{:S(2)}) %collective-permute-start.5) | collective-permute-done | bytes 262176 | tf_op jit(solution)/shard_map/ppermute | solution.py:336
  46.1 0.0 collective-permute-start.9
  46.1 0.5 collective-permute-start.10
  46.6 0.0 collective-permute-done.8.refs_7_.refs_3_
  46.6 0.0 collective-permute-start.12
  46.6 4.1 %collective-permute-done.7.refs_3_.refs_7_ = bf16[128,1024]{1,0:T(8,128)(2,1)S(1)} collective-permute-done((bf16[128,1024]{1,0:T(8,128)(2,1)S(1)}, bf16[128,1024]{1,0:T(8,128)(2,1)S(1)}, u32[]{:S(2)}, u32[]{:S(2)}) %collective-permute-start.7) | collective-permute-done | bytes 262176 | tf_op jit(solution)/shard_map/ppermute | solution.py:336
  50.7 0.0 collective-permute-start.11
  50.7 1.4 %collective-permute-done.6.refs_2_.refs_6_ = bf16[128,1024]{1,0:T(8,128)(2,1)S(1)} collective-permute-done((bf16[128,1024]{1,0:T(8,128)(2,1)S(1)}, bf16[128,1024]{1,0:T(8,128)(2,1)S(1)}, u32[]{:S(2)}, u32[]{:S(2)}) %collective-permute-start.6) | collective-permute-done | bytes 262176 | tf_op jit(solution)/shard_map/ppermute | solution.py:336
  52.1 0.0 collective-permute-done.12.refs_11_.refs_7_
  52.2 0.0 collective-permute-done.9.refs_8_.refs_4_
  52.2 0.0 collective-permute-done.10.refs_9_.refs_5_
  52.2 0.1 collective-permute-done.11.refs_10_.refs_6_
  52.2 2.9 %shard_map.124 = (f32[1024,512]{1,0:T(8,128)S(1)}, f32[4,4,128]{2,1,0:T(4,128)S(1)}) custom-call(bf16[128,1024]{1,0:T(8,128)(2,1)S(1)} %shard_map.123.refs_0_.refs_4_, bf16[128,1024]{1,0:T(8,128)(2,1)S(1)} %collective-permute-done.5.refs_1_.refs_5_, bf16[128,1024]{1,0:T(8,128)(2,1)S(1)} %collective-permute-done.6.refs_2_.refs_6_, ...), custom_call_target="tpu_custom_call" | custom-call | flops 1073741824 | bytes 4194304 | tf_op jit(solution)/shard_map/pallas_call | solution.py:199
  55.2 1.4 %collective-permute-start.15 = (f32[4,4,128]{2,1,0:T(4,128)S(1)}, f32[4,4,128]{2,1,0:T(4,128)S(1)}, u32[]{:S(2)}, u32[]{:S(2)}) collective-permute-start(f32[4,4,128]{2,1,0:T(4,128)S(1)} %get-tuple-element.50.refs_0_), channel_id=1, source_target_pairs={{0,6},{1,7},{2,4},{3,5},{4,2},{5,3},{6,0},{7,1},{8,14},{9,15},{10,... | collective-permute-start | bytes 24584 | tf_op jit(solution)/shard_map/ppermute | solution.py:336
  56.6 1.6 %collective-permute-start.14 = (f32[4,4,128]{2,1,0:T(4,128)S(1)}, f32[4,4,128]{2,1,0:T(4,128)S(1)}, u32[]{:S(2)}, u32[]{:S(2)}) collective-permute-start(f32[4,4,128]{2,1,0:T(4,128)S(1)} %get-tuple-element.50.refs_0_), channel_id=1, source_target_pairs={{0,4},{1,5},{2,6},{3,7},{4,0},{5,1},{6,2},{7,3},{8,12},{9,13},{10,... | collective-permute-start | bytes 24584 | tf_op jit(solution)/shard_map/ppermute | solution.py:336
  58.2 0.5 collective-permute-start.13
  58.7 1.1 %collective-permute-done.15.refs_3_ = f32[4,4,128]{2,1,0:T(4,128)S(1)} collective-permute-done((f32[4,4,128]{2,1,0:T(4,128)S(1)}, f32[4,4,128]{2,1,0:T(4,128)S(1)}, u32[]{:S(2)}, u32[]{:S(2)}) %collective-permute-start.15) | collective-permute-done | bytes 8224 | tf_op jit(solution)/shard_map/ppermute | solution.py:336
  59.8 0.4 collective-permute-done.14.refs_2_
  60.2 1.6 %collective-permute-done.13.refs_1_ = f32[4,4,128]{2,1,0:T(4,128)S(1)} collective-permute-done((f32[4,4,128]{2,1,0:T(4,128)S(1)}, f32[4,4,128]{2,1,0:T(4,128)S(1)}, u32[]{:S(2)}, u32[]{:S(2)}) %collective-permute-start.13) | collective-permute-done | bytes 8224 | tf_op jit(solution)/shard_map/ppermute | solution.py:336
  61.8 1.6 %shard_map.125 = (bf16[1024,512]{1,0:T(8,128)(2,1)S(1)}, f32[1,128]{1,0:T(1,128)}, bf16[512,1024]{1,0:T(8,128)(2,1)S(1)}) custom-call(f32[1,128]{1,0:T(1,128)S(1)} %get-tuple-element.33.entropy, f32[4,4,128]{2,1,0:T(4,128)S(1)} %get-tuple-element.50.refs_0_, f32[4,4,128]{2,1,0:T(4,128)S(1)} %collective-permute-done.13.refs_1_, ...), custom_call_target="tpu_custom_call" | custom-call | flops 536870912 | bytes 4194304 | tf_op jit(solution)/shard_map/pallas_call | solution.py:239
  63.4 0.0 collective-permute-start.16
  63.4 0.7 shard_map.126.near
  64.1 1.9 %collective-permute-done.16.far = bf16[512,1024]{1,0:T(8,128)(2,1)S(1)} collective-permute-done((bf16[512,1024]{1,0:T(8,128)(2,1)S(1)}, bf16[512,1024]{1,0:T(8,128)(2,1)S(1)}, u32[]{:S(2)}, u32[]{:S(2)}) %collective-permute-start.16) | collective-permute-done | bytes 1048608 | tf_op jit(solution)/shard_map/ppermute | solution.py:336
  66.1 0.2 shard_map.127
  66.2 1.6 %collective-permute-start.20 = (bf16[128,1024]{1,0:T(8,128)(2,1)S(1)}, bf16[128,1024]{1,0:T(8,128)(2,1)S(1)}, u32[]{:S(2)}, u32[]{:S(2)}) collective-permute-start(bf16[128,1024]{1,0:T(8,128)(2,1)S(1)} %get-tuple-element.61), channel_id=1, source_target_pairs={{0,8},{1,9},{2,10},{3,11},{4,12},{5,13},{6,14},{7,15},{8,0},{9,1},... | collective-permute-start | bytes 786440 | tf_op jit(solution)/shard_map/ppermute | solution.py:336
  67.9 1.3 %shard_map.128 = (f32[128,1024]{1,0:T(8,128)S(1)}, bf16[128,1024]{1,0:T(8,128)(2,1)S(1)}, bf16[128,1024]{1,0:T(8,128)(2,1)S(1)}, bf16[128,1024]{1,0:T(8,128)(2,1)S(1)}) custom-call(bf16[1024,512]{1,0:T(8,128)(2,1)S(1)} %get-tuple-element.53.grads, bf16[128,1024]{1,0:T(8,128)(2,1)S(1)} %shard_map.122.refs_0_.refs_4_, ...), custom_call_target="tpu_custom_call" | custom-call | flops 1073741824 | bytes 2097152 | tf_op jit(solution)/shard_map/pallas_call | solution.py:292
  69.2 0.6 collective-permute-start.17
  69.8 0.3 collective-permute-start.18
  70.1 2.6 %collective-permute-start.19 = (bf16[128,1024]{1,0:T(8,128)(2,1)S(1)}, bf16[128,1024]{1,0:T(8,128)(2,1)S(1)}, u32[]{:S(2)}, u32[]{:S(2)}) collective-permute-start(bf16[128,1024]{1,0:T(8,128)(2,1)S(1)} %get-tuple-element.59), channel_id=1, source_target_pairs={{0,6},{1,7},{2,4},{3,5},{4,2},{5,3},{6,0},{7,1},{8,14},{9,15},{10,... | collective-permute-start | bytes 786440 | tf_op jit(solution)/shard_map/ppermute | solution.py:336
  72.8 0.5 collective-permute-start.22
  73.2 1.6 %collective-permute-done.20 = bf16[128,1024]{1,0:T(8,128)(2,1)S(1)} collective-permute-done((bf16[128,1024]{1,0:T(8,128)(2,1)S(1)}, bf16[128,1024]{1,0:T(8,128)(2,1)S(1)}, u32[]{:S(2)}, u32[]{:S(2)}) %collective-permute-start.20) | collective-permute-done | bytes 262176 | tf_op jit(solution)/shard_map/ppermute | solution.py:336
  74.8 0.1 add_convert_fusion
  74.9 1.7 %collective-permute-start.21 = (bf16[128,1024]{1,0:T(8,128)(2,1)S(1)}, bf16[128,1024]{1,0:T(8,128)(2,1)S(1)}, u32[]{:S(2)}, u32[]{:S(2)}) collective-permute-start(bf16[128,1024]{1,0:T(8,128)(2,1)S(1)} %add_convert_fusion), channel_id=1, source_target_pairs={{0,16},{1,17},{2,18},{3,19},{4,20},{5,21},{6,22},{7,23},{8,24},{9,... | collective-permute-start | bytes 786440 | tf_op jit(solution)/shard_map/ppermute | solution.py:336
  76.6 1.9 %collective-permute-done.17 = bf16[128,1024]{1,0:T(8,128)(2,1)S(1)} collective-permute-done((bf16[128,1024]{1,0:T(8,128)(2,1)S(1)}, bf16[128,1024]{1,0:T(8,128)(2,1)S(1)}, u32[]{:S(2)}, u32[]{:S(2)}) %collective-permute-start.17) | collective-permute-done | bytes 262176 | tf_op jit(solution)/shard_map/ppermute | solution.py:336
  78.5 4.8 %collective-permute-done.18 = bf16[128,1024]{1,0:T(8,128)(2,1)S(1)} collective-permute-done((bf16[128,1024]{1,0:T(8,128)(2,1)S(1)}, bf16[128,1024]{1,0:T(8,128)(2,1)S(1)}, u32[]{:S(2)}, u32[]{:S(2)}) %collective-permute-start.18) | collective-permute-done | bytes 262176 | tf_op jit(solution)/shard_map/ppermute | solution.py:336
  83.3 0.0 collective-permute-done.19
  83.3 0.9 %convert_add_fusion.1 = f32[128,1024]{1,0:T(8,128)} fusion(bf16[128,1024]{1,0:T(8,128)(2,1)S(1)} %collective-permute-done.19, bf16[128,1024]{1,0:T(8,128)(2,1)S(1)} %collective-permute-done.18, f32[128,1024]{1,0:T(8,128)S(1)} %get-tuple-element.56, bf16[128,1024]{1,0:T(8,128)(2,1)S(1)} %collective-permute-done.17), kind=kLoop, calls=%fused_computation.2 | loop fusion | flops 786432 | bytes 1835008 | tf_op jit(solution)/shard_map/add | solution.py:372
  84.2 0.0 collective-permute-done.22
  84.2 4.7 %collective-permute-done.21 = bf16[128,1024]{1,0:T(8,128)(2,1)S(1)} collective-permute-done((bf16[128,1024]{1,0:T(8,128)(2,1)S(1)}, bf16[128,1024]{1,0:T(8,128)(2,1)S(1)}, u32[]{:S(2)}, u32[]{:S(2)}) %collective-permute-start.21) | collective-permute-done | bytes 262176 | tf_op jit(solution)/shard_map/ppermute | solution.py:336
  88.9 0.9 convert_add_fusion
Async XLA Ops:
  4.7 32.1 %collective-permute-start = (f32[8,128,128]{2,1,0:T(8,128)S(1)}, f32[8,128,128]{2,1,0:T(8,128)S(1)}, u32[]{:S(2)}, u32[]{:S(2)}) collective-permute-start(f32[8,128,128]{2,1,0:T(8,128)S(1)} %get-tuple-element.35), channel_id=1, source_target_pairs={{0,2},{1,3},{2,0},{3,1},{4,6},{5,7},{6,4},{7,5},{8,10},{9,11},{10,... | collective-permute-start | bytes 1572872 | tf_op jit(solution)/shard_map/ppermute | solution.py:336
  7.3 29.5 %collective-permute-start.1 = (f32[8,128,128]{2,1,0:T(8,128)S(1)}, f32[8,128,128]{2,1,0:T(8,128)S(1)}, u32[]{:S(2)}, u32[]{:S(2)}) collective-permute-start(f32[8,128,128]{2,1,0:T(8,128)S(1)} %get-tuple-element.36), channel_id=1, source_target_pairs={{0,4},{1,5},{2,6},{3,7},{4,0},{5,1},{6,2},{7,3},{8,12},{9,13},{10,... | collective-permute-start | bytes 1572872 | tf_op jit(solution)/shard_map/ppermute | solution.py:336
  9.3 27.5 %collective-permute-start.2 = (f32[8,128,128]{2,1,0:T(8,128)S(1)}, f32[8,128,128]{2,1,0:T(8,128)S(1)}, u32[]{:S(2)}, u32[]{:S(2)}) collective-permute-start(f32[8,128,128]{2,1,0:T(8,128)S(1)} %get-tuple-element.37), channel_id=1, source_target_pairs={{0,6},{1,7},{2,4},{3,5},{4,2},{5,3},{6,0},{7,1},{8,14},{9,15},{10,... | collective-permute-start | bytes 1572872 | tf_op jit(solution)/shard_map/ppermute | solution.py:336
  9.4 16.1 %copy-start = (bf16[128,1024]{1,0:T(8,128)(2,1)S(1)}, bf16[128,1024]{1,0:T(8,128)(2,1)}, u32[]{:S(2)}) copy-start(bf16[128,1024]{1,0:T(8,128)(2,1)} %feats.3) | copy-start | bytes 786436
  21.2 15.6 %collective-permute-start.4 = (bf16[128,1024]{1,0:T(8,128)(2,1)S(1)}, bf16[128,1024]{1,0:T(8,128)(2,1)S(1)}, u32[]{:S(2)}, u32[]{:S(2)}) collective-permute-start(bf16[128,1024]{1,0:T(8,128)(2,1)S(1)} %shard_map.122.refs_0_.refs_4_), channel_id=1, source_target_pairs={{0,8},{1,9},{2,10},{3,11},{4,12},{5,13},{6,14},{7,15},{8,0},{9,1},... | collective-permute-start | bytes 786440 | tf_op jit(solution)/shard_map/ppermute | solution.py:336
  23.0 13.8 %collective-permute-start.3 = (bf16[128,1024]{1,0:T(8,128)(2,1)S(1)}, bf16[128,1024]{1,0:T(8,128)(2,1)S(1)}, u32[]{:S(2)}, u32[]{:S(2)}) collective-permute-start(bf16[128,1024]{1,0:T(8,128)(2,1)S(1)} %shard_map.122.refs_0_.refs_4_), channel_id=1, source_target_pairs={{0,16},{1,17},{2,18},{3,19},{4,20},{5,21},{6,22},{7,23},{8,24},{9,... | collective-permute-start | bytes 786440 | tf_op jit(solution)/shard_map/ppermute | solution.py:336
  36.8 9.3 %collective-permute-start.5 = (bf16[128,1024]{1,0:T(8,128)(2,1)S(1)}, bf16[128,1024]{1,0:T(8,128)(2,1)S(1)}, u32[]{:S(2)}, u32[]{:S(2)}) collective-permute-start(bf16[128,1024]{1,0:T(8,128)(2,1)S(1)} %shard_map.123.refs_0_.refs_4_), channel_id=1, source_target_pairs={{0,2},{1,3},{2,0},{3,1},{4,6},{5,7},{6,4},{7,5},{8,10},{9,11},{10,... | collective-permute-start | bytes 786440 | tf_op jit(solution)/shard_map/ppermute | solution.py:336
  38.6 8.1 %collective-permute-start.8 = (bf16[128,1024]{1,0:T(8,128)(2,1)S(1)}, bf16[128,1024]{1,0:T(8,128)(2,1)S(1)}, u32[]{:S(2)}, u32[]{:S(2)}) collective-permute-start(bf16[128,1024]{1,0:T(8,128)(2,1)S(1)} %collective-permute-done.3.refs_6_.refs_2_), channel_id=1, source_target_pairs={{0,8},{1,9},{2,10},{3,11},{4,12},{5,13},{6,14},{7,15},{8,0},{9,1},... | collective-permute-start | bytes 786440 | tf_op jit(solution)/shard_map/ppermute | solution.py:336
  38.8 11.9 %collective-permute-start.7 = (bf16[128,1024]{1,0:T(8,128)(2,1)S(1)}, bf16[128,1024]{1,0:T(8,128)(2,1)S(1)}, u32[]{:S(2)}, u32[]{:S(2)}) collective-permute-start(bf16[128,1024]{1,0:T(8,128)(2,1)S(1)} %shard_map.123.refs_0_.refs_4_), channel_id=1, source_target_pairs={{0,6},{1,7},{2,4},{3,5},{4,2},{5,3},{6,0},{7,1},{8,14},{9,15},{10,... | collective-permute-start | bytes 786440 | tf_op jit(solution)/shard_map/ppermute | solution.py:336
  40.8 11.3 %collective-permute-start.6 = (bf16[128,1024]{1,0:T(8,128)(2,1)S(1)}, bf16[128,1024]{1,0:T(8,128)(2,1)S(1)}, u32[]{:S(2)}, u32[]{:S(2)}) collective-permute-start(bf16[128,1024]{1,0:T(8,128)(2,1)S(1)} %shard_map.123.refs_0_.refs_4_), channel_id=1, source_target_pairs={{0,4},{1,5},{2,6},{3,7},{4,0},{5,1},{6,2},{7,3},{8,12},{9,13},{10,... | collective-permute-start | bytes 786440 | tf_op jit(solution)/shard_map/ppermute | solution.py:336
  46.1 6.0 %collective-permute-start.9 = (bf16[128,1024]{1,0:T(8,128)(2,1)S(1)}, bf16[128,1024]{1,0:T(8,128)(2,1)S(1)}, u32[]{:S(2)}, u32[]{:S(2)}) collective-permute-start(bf16[128,1024]{1,0:T(8,128)(2,1)S(1)} %shard_map.122.refs_0_.refs_4_), channel_id=1, source_target_pairs={{0,1},{1,0},{2,3},{3,2},{4,5},{5,4},{6,7},{7,6},{8,9},{9,8},{10,11... | collective-permute-start | bytes 786440 | tf_op jit(solution)/shard_map/ppermute | solution.py:336
  46.1 6.0 %collective-permute-start.10 = (bf16[128,1024]{1,0:T(8,128)(2,1)S(1)}, bf16[128,1024]{1,0:T(8,128)(2,1)S(1)}, u32[]{:S(2)}, u32[]{:S(2)}) collective-permute-start(bf16[128,1024]{1,0:T(8,128)(2,1)S(1)} %collective-permute-done.4.refs_5_.refs_1_), channel_id=1, source_target_pairs={{0,1},{1,0},{2,3},{3,2},{4,5},{5,4},{6,7},{7,6},{8,9},{9,8},{10,11... | collective-permute-start | bytes 786440 | tf_op jit(solution)/shard_map/ppermute | solution.py:336
  46.6 5.5 %collective-permute-start.12 = (bf16[128,1024]{1,0:T(8,128)(2,1)S(1)}, bf16[128,1024]{1,0:T(8,128)(2,1)S(1)}, u32[]{:S(2)}, u32[]{:S(2)}) collective-permute-start(bf16[128,1024]{1,0:T(8,128)(2,1)S(1)} %collective-permute-done.8.refs_7_.refs_3_), channel_id=1, source_target_pairs={{0,1},{1,0},{2,3},{3,2},{4,5},{5,4},{6,7},{7,6},{8,9},{9,8},{10,11... | collective-permute-start | bytes 786440 | tf_op jit(solution)/shard_map/ppermute | solution.py:336
  50.7 1.5 %collective-permute-start.11 = (bf16[128,1024]{1,0:T(8,128)(2,1)S(1)}, bf16[128,1024]{1,0:T(8,128)(2,1)S(1)}, u32[]{:S(2)}, u32[]{:S(2)}) collective-permute-start(bf16[128,1024]{1,0:T(8,128)(2,1)S(1)} %collective-permute-done.3.refs_6_.refs_2_), channel_id=1, source_target_pairs={{0,1},{1,0},{2,3},{3,2},{4,5},{5,4},{6,7},{7,6},{8,9},{9,8},{10,11... | collective-permute-start | bytes 786440 | tf_op jit(solution)/shard_map/ppermute | solution.py:336
  55.2 4.6 %collective-permute-start.15 = (f32[4,4,128]{2,1,0:T(4,128)S(1)}, f32[4,4,128]{2,1,0:T(4,128)S(1)}, u32[]{:S(2)}, u32[]{:S(2)}) collective-permute-start(f32[4,4,128]{2,1,0:T(4,128)S(1)} %get-tuple-element.50.refs_0_), channel_id=1, source_target_pairs={{0,6},{1,7},{2,4},{3,5},{4,2},{5,3},{6,0},{7,1},{8,14},{9,15},{10,... | collective-permute-start | bytes 24584 | tf_op jit(solution)/shard_map/ppermute | solution.py:336
  56.6 3.7 %collective-permute-start.14 = (f32[4,4,128]{2,1,0:T(4,128)S(1)}, f32[4,4,128]{2,1,0:T(4,128)S(1)}, u32[]{:S(2)}, u32[]{:S(2)}) collective-permute-start(f32[4,4,128]{2,1,0:T(4,128)S(1)} %get-tuple-element.50.refs_0_), channel_id=1, source_target_pairs={{0,4},{1,5},{2,6},{3,7},{4,0},{5,1},{6,2},{7,3},{8,12},{9,13},{10,... | collective-permute-start | bytes 24584 | tf_op jit(solution)/shard_map/ppermute | solution.py:336
  58.2 3.7 %collective-permute-start.13 = (f32[4,4,128]{2,1,0:T(4,128)S(1)}, f32[4,4,128]{2,1,0:T(4,128)S(1)}, u32[]{:S(2)}, u32[]{:S(2)}) collective-permute-start(f32[4,4,128]{2,1,0:T(4,128)S(1)} %get-tuple-element.50.refs_0_), channel_id=1, source_target_pairs={{0,2},{1,3},{2,0},{3,1},{4,6},{5,7},{6,4},{7,5},{8,10},{9,11},{10,... | collective-permute-start | bytes 24584 | tf_op jit(solution)/shard_map/ppermute | solution.py:336
  63.4 2.7 %collective-permute-start.16 = (bf16[512,1024]{1,0:T(8,128)(2,1)S(1)}, bf16[512,1024]{1,0:T(8,128)(2,1)S(1)}, u32[]{:S(2)}, u32[]{:S(2)}) collective-permute-start(bf16[512,1024]{1,0:T(8,128)(2,1)S(1)} %get-tuple-element.54), channel_id=1, source_target_pairs={{0,1},{1,0},{2,3},{3,2},{4,5},{5,4},{6,7},{7,6},{8,9},{9,8},{10,11... | collective-permute-start | bytes 3145736 | tf_op jit(solution)/shard_map/ppermute | solution.py:336
  66.2 8.6 %collective-permute-start.20 = (bf16[128,1024]{1,0:T(8,128)(2,1)S(1)}, bf16[128,1024]{1,0:T(8,128)(2,1)S(1)}, u32[]{:S(2)}, u32[]{:S(2)}) collective-permute-start(bf16[128,1024]{1,0:T(8,128)(2,1)S(1)} %get-tuple-element.61), channel_id=1, source_target_pairs={{0,8},{1,9},{2,10},{3,11},{4,12},{5,13},{6,14},{7,15},{8,0},{9,1},... | collective-permute-start | bytes 786440 | tf_op jit(solution)/shard_map/ppermute | solution.py:336
  69.2 9.3 %collective-permute-start.17 = (bf16[128,1024]{1,0:T(8,128)(2,1)S(1)}, bf16[128,1024]{1,0:T(8,128)(2,1)S(1)}, u32[]{:S(2)}, u32[]{:S(2)}) collective-permute-start(bf16[128,1024]{1,0:T(8,128)(2,1)S(1)} %get-tuple-element.57), channel_id=1, source_target_pairs={{0,2},{1,3},{2,0},{3,1},{4,6},{5,7},{6,4},{7,5},{8,10},{9,11},{10,... | collective-permute-start | bytes 786440 | tf_op jit(solution)/shard_map/ppermute | solution.py:336
  69.8 13.4 %collective-permute-start.18 = (bf16[128,1024]{1,0:T(8,128)(2,1)S(1)}, bf16[128,1024]{1,0:T(8,128)(2,1)S(1)}, u32[]{:S(2)}, u32[]{:S(2)}) collective-permute-start(bf16[128,1024]{1,0:T(8,128)(2,1)S(1)} %get-tuple-element.58), channel_id=1, source_target_pairs={{0,4},{1,5},{2,6},{3,7},{4,0},{5,1},{6,2},{7,3},{8,12},{9,13},{10,... | collective-permute-start | bytes 786440 | tf_op jit(solution)/shard_map/ppermute | solution.py:336
  70.1 13.1 %collective-permute-start.19 = (bf16[128,1024]{1,0:T(8,128)(2,1)S(1)}, bf16[128,1024]{1,0:T(8,128)(2,1)S(1)}, u32[]{:S(2)}, u32[]{:S(2)}) collective-permute-start(bf16[128,1024]{1,0:T(8,128)(2,1)S(1)} %get-tuple-element.59), channel_id=1, source_target_pairs={{0,6},{1,7},{2,4},{3,5},{4,2},{5,3},{6,0},{7,1},{8,14},{9,15},{10,... | collective-permute-start | bytes 786440 | tf_op jit(solution)/shard_map/ppermute | solution.py:336
  72.8 11.4 %collective-permute-start.22 = (bf16[128,1024]{1,0:T(8,128)(2,1)S(1)}, bf16[128,1024]{1,0:T(8,128)(2,1)S(1)}, u32[]{:S(2)}, u32[]{:S(2)}) collective-permute-start(bf16[128,1024]{1,0:T(8,128)(2,1)S(1)} %get-tuple-element.62), channel_id=1, source_target_pairs={{0,8},{1,9},{2,10},{3,11},{4,12},{5,13},{6,14},{7,15},{8,0},{9,1},... | collective-permute-start | bytes 786440 | tf_op jit(solution)/shard_map/ppermute | solution.py:336
  74.9 14.0 %collective-permute-start.21 = (bf16[128,1024]{1,0:T(8,128)(2,1)S(1)}, bf16[128,1024]{1,0:T(8,128)(2,1)S(1)}, u32[]{:S(2)}, u32[]{:S(2)}) collective-permute-start(bf16[128,1024]{1,0:T(8,128)(2,1)S(1)} %add_convert_fusion), channel_id=1, source_target_pairs={{0,16},{1,17},{2,18},{3,19},{4,20},{5,21},{6,22},{7,23},{8,24},{9,... | collective-permute-start | bytes 786440 | tf_op jit(solution)/shard_map/ppermute | solution.py:336

commit v8 on v6

--- a/solution.py
+++ b/solution.py
@@ -33,68 +33,65 @@
     return pltpu.with_memory_space_constraint(array, pltpu.HBM)
 
 
-def tower_body(chunks, held, feats, w_in, w_out, *refs):
-    out, held_in, held_out, total, sem_in, sem_out, *own = refs[-6 if held else -8 :]
-    if not held:
-        load = pltpu.make_async_copy(feats, *own)
-        load.start()
-        load.wait()
-        feats = own[0]
+def tower_body(chunks, ready, feats, w_in, w_out, *refs):
+    out, held_out, total, sem_out, *own = refs[-4 if ready else -6 :]
     step = w_in.shape[1] // chunks
 
+    def part(i):
+        return pl.ds(pl.multiple_of(i * step, step), step)
+
     def copies(i):
-        part = pl.ds(pl.multiple_of(i * step, step), step)
-        return (
-            pltpu.make_async_copy(w_in.at[:, part], held_in.at[:, part], sem_in.at[i]),
-            pltpu.make_async_copy(w_out.at[part], held_out.at[part], sem_out.at[i]),
-        )
+        both = [pltpu.make_async_copy(w_out.at[part(i)], held_out.at[part(i)], sem_out.at[i])]
+        if not ready:
+            both.insert(0, pltpu.make_async_copy(w_in.at[:, part(i)], own[0].at[:, part(i)], own[1].at[i]))
+        return both
 
     for i in range(chunks):
         for copy in copies(i):
             copy.start()
     total[...] = jnp.zeros_like(total)
+    held_in = w_in if ready else own[0]
 
     def one(i, carry):
-        first, second = copies(i)
-        part = pl.ds(pl.multiple_of(i * step, step), step)
-        first.wait()
-        hidden = jnp.dot(feats[...], held_in[:, part], preferred_element_type=jnp.float32)
+        waits = copies(i)
+        if not ready:
+            waits[0].wait()
+        hidden = jnp.dot(feats[...], held_in[:, part(i)], preferred_element_type=jnp.float32)
         hidden = jnp.maximum(hidden, 0.0).astype(jnp.bfloat16)
-        second.wait()
-        total[...] += jnp.dot(hidden, held_out[part], preferred_element_type=jnp.float32)
+        waits[-1].wait()
+        total[...] += jnp.dot(hidden, held_out[part(i)], preferred_element_type=jnp.float32)
         return carry
 
-    lax.fori_loop(0, chunks, one, 0)
+    lax.fori_loop(0, chunks, one, 0, unroll=True)
     out[...] = total[...].astype(out.dtype)
 
 
-def tower(feats, w_in, w_out, dtype, after, held):
+def tower(feats, w_in, w_out, dtype, after, ready):
     rows, width = feats.shape
     hidden = w_in.shape[1]
     chunks = max(1, hidden // 512)
-    return pl.pallas_call(
-        functools.partial(tower_body, chunks, held),
-        in_specs=[VMEM if held else ANY, ANY, ANY] + [ANY] * len(after),
+    own = [] if ready else [pltpu.VMEM(w_in.shape, w_in.dtype), pltpu.SemaphoreType.DMA((chunks,))]
+    return pl.pallas_call(
+        functools.partial(tower_body, chunks, ready),
+        in_specs=[VMEM, VMEM if ready else ANY, ANY] + [ANY] * len(after),
         out_specs=VMEM,
         out_shape=struct((rows, width), dtype),
         scratch_shapes=[
-            pltpu.VMEM(w_in.shape, w_in.dtype),
             pltpu.VMEM(w_out.shape, w_out.dtype),
             pltpu.VMEM((rows, width), jnp.float32),
             pltpu.SemaphoreType.DMA((chunks,)),
-            pltpu.SemaphoreType.DMA((chunks,)),
         ]
-        + ([] if held else [pltpu.VMEM(feats.shape, feats.dtype), pltpu.SemaphoreType.DMA]),
-        compiler_params=params(52),
+        + own,
+        compiler_params=params(20 if ready else 52),
         cost_estimate=cost(1, 1),
-    )(feats if held else in_hbm(feats), w_in, w_out, *after)
-
-
-def embed(feats, w_in, w_out, after, held):
+    )(feats, w_in if ready else in_hbm(w_in), in_hbm(w_out), *after)
+
+
+def embed(feats, w_in, w_out, after, ready):
     if lax.axis_size("tensor") == 1:
-        return tower(feats, w_in, w_out, jnp.bfloat16, after, held)
+        return tower(feats, w_in, w_out, jnp.bfloat16, after, ready)
     feats = lax.all_gather(feats, "tensor", axis=0, tiled=True)
-    partial = tower(feats, w_in, w_out, jnp.float32, after, held)
+    partial = tower(feats, w_in, w_out, jnp.float32, after, ready)
     return lax.psum_scatter(partial, "tensor", scatter_dimension=0, tiled=True).astype(jnp.bfloat16)
 
 
@@ -153,7 +150,7 @@
             pltpu.SemaphoreType.DMA((3,)),
         ],
         compiler_params=params(24),
-        cost_estimate=cost(teacher.size, 8 * teacher.size),
+        cost_estimate=cost(10**10, 8 * teacher.size),
     )(me, in_hbm(cands), count, in_hbm(owner), in_hbm(teacher))
 
 
@@ -339,11 +336,11 @@
     first, *rest = probs
     probs = [first] + [swap(part, (c + 1) * CORES) for c, part in enumerate(rest)]
 
-    item_emb = embed(item_feats, item_w_in, item_w_out, [first], False)
+    item_emb = embed(item_feats, item_w_in, item_w_out, [first], True)
     wide = planes // 2
     crossed = [swap(item_emb, z * cols * CORES) for z in range(wide, planes if planes > 1 else 0, max(wide, 1))]
     nearby = [swap(item_emb, z * cols * CORES) for z in range(1, wide)]
-    user_emb = embed(user_feats, user_w_in, user_w_out, [item_emb], True)
+    user_emb = embed(user_feats, user_w_in, user_w_out, [item_emb], False)
     user_emb, item_emb, probs, crossed, nearby = lax.optimization_barrier((user_emb, item_emb, probs, crossed, nearby))
     users = [user_emb] + over_columns(user_emb)
     derived = [swap(block, z * cols * CORES) for block in crossed for z in range(1, wide)]

time: 90.8 us -> 86.5 us (0.953)
  Pallas kernels: 34 us -> 29.9 us
  waiting for transfers between devices: 29 us -> 27.5 us
  starting transfers between devices: 24.6 us -> 25.6 us
    pallas_call x2, Pallas kernels: 24.3 us -> 19.8 us  [tower(): pl.pallas_call(functools.partial(tower_body, chunks, ready), in_specs=[VM...]
    ppermute x23, waiting for transfers between devices: 29 us -> 27.5 us  [swap(): return lax.ppermute(array, 'dp', [(i, i ^ apart) for i in range(count)])]
    ppermute x23, starting transfers between devices: 24.6 us -> 25.6 us  [swap(): return lax.ppermute(array, 'dp', [(i, i ^ apart) for i in range(count)])]
  transfers between devices with their start and end apart: 23 -> 23, of which waited for: 12 -> 13; matrix products, arithmetic and copies ran while one was open for 1% -> 1% of each run, Pallas kernels for 29% -> 25%
where the time goes in v8:
time: 86.5 us; the launch traced here: 86.3 us
  Pallas kernels  29.9 us (35%)
  waiting for transfers between devices  27.5 us (32%)
  starting transfers between devices  25.6 us (30%)
  other arithmetic  1.89 us (2%)
  between operations  1.42 us (2%)
    ppermute x23, waiting for transfers between devices, swap(): return lax.ppermute(array, 'dp', [(i, i ^ apart) for i in range(count)])  27.5 us
    ppermute x23, starting transfers between devices, swap(): return lax.ppermute(array, 'dp', [(i, i ^ apart) for i in range(count)])  25.6 us
    pallas_call x2, Pallas kernels, tower(): pl.pallas_call(functools.partial(tower_body, chunks, ready), in_specs=[VM...  19.8 us
    pallas_call x1, Pallas kernels, spread_teacher(): pl.pallas_call(functools.partial(teacher_body, cols, planes), in_specs=[S...  3.37 us
    pallas_call x1, Pallas kernels, scores(): pl.pallas_call(functools.partial(score_body, cols, places, scale), in_spe...  2.92 us
    add x2, other arithmetic, add(): functools.reduce(jnp.add, [part.astype(jnp.float32) for part in parts], s...  1.82 us
  transfers between devices with their start and end apart: 23, of which 13 were waited for; matrix products, arithmetic and copies ran while one was open for 1% of the time, Pallas kernels for 25%

profile of v8, /device:TPU:0, one launch (start us, length us, event | category | flops | bytes accessed | tf_op | source)
XLA Modules:
  0.0 86.3 jit_solution(18307905155541831973)
XLA Ops:
  1.3 0.0 copy-start
  1.3 0.0 copy-start.1
  1.3 3.4 %shard_map.121 = (f32[8,128,128]{2,1,0:T(8,128)S(1)}, f32[8,128,128]{2,1,0:T(8,128)S(1)}, f32[8,128,128]{2,1,0:T(8,128)S(1)}, f32[8,128,128]{2,1,0:T(8,128)S(1)}, f32[1,128]{1,0:T(1,128)S(1)}) custom-call(s32[1]{0:T(128)} %bitcast.me, s32[1,16]{1,0:T(1,128)} %cands_hbm.1, s32[1]{0:T(128)S(6)} %copy.13.count, s32[32]{0:T(128)} %owner_hbm.1, ...), custom_call_target="tpu_custom_call" | custom-call | flops 10000000000 | bytes 2097152 | tf_op jit(solution)/shard_map/pallas_call | solution.py:139
  4.7 3.4 %collective-permute-start = (f32[8,128,128]{2,1,0:T(8,128)S(1)}, f32[8,128,128]{2,1,0:T(8,128)S(1)}, u32[]{:S(2)}, u32[]{:S(2)}) collective-permute-start(f32[8,128,128]{2,1,0:T(8,128)S(1)} %get-tuple-element.35), channel_id=1, source_target_pairs={{0,2},{1,3},{2,0},{3,1},{4,6},{5,7},{6,4},{7,5},{8,10},{9,11},{10,... | collective-permute-start | bytes 1572872 | tf_op jit(solution)/shard_map/ppermute | solution.py:330
  8.1 1.3 %collective-permute-start.1 = (f32[8,128,128]{2,1,0:T(8,128)S(1)}, f32[8,128,128]{2,1,0:T(8,128)S(1)}, u32[]{:S(2)}, u32[]{:S(2)}) collective-permute-start(f32[8,128,128]{2,1,0:T(8,128)S(1)} %get-tuple-element.36), channel_id=1, source_target_pairs={{0,4},{1,5},{2,6},{3,7},{4,0},{5,1},{6,2},{7,3},{8,12},{9,13},{10,... | collective-permute-start | bytes 1572872 | tf_op jit(solution)/shard_map/ppermute | solution.py:330
  9.4 0.2 collective-permute-start.2
  9.6 0.0 copy-done
  9.6 0.0 copy-done.1
  9.6 0.0 copy-start.2
  9.6 8.5 %shard_map.122.refs_0_.refs_4_ = bf16[128,1024]{1,0:T(8,128)(2,1)S(1)} custom-call(bf16[128,1024]{1,0:T(8,128)(2,1)S(1)} %copy-done.1, bf16[1024,8192]{1,0:T(8,128)(2,1)S(1)} %copy-done, bf16[8192,1024]{1,0:T(8,128)(2,1)} %w_out.2, f32[8,128,128]{2,1,0:T(8,128)S(1)} %get-tuple-element.46.refs_0_.refs_12_.refs_8_), custom_call_target="tpu_custom_call" | custom-call | flops 1 | bytes 1 | tf_op jit(solution)/shard_map/pallas_call | solution.py:74
  18.1 1.9 %collective-permute-start.4 = (bf16[128,1024]{1,0:T(8,128)(2,1)S(1)}, bf16[128,1024]{1,0:T(8,128)(2,1)S(1)}, u32[]{:S(2)}, u32[]{:S(2)}) collective-permute-start(bf16[128,1024]{1,0:T(8,128)(2,1)S(1)} %shard_map.122.refs_0_.refs_4_), channel_id=1, source_target_pairs={{0,8},{1,9},{2,10},{3,11},{4,12},{5,13},{6,14},{7,15},{8,0},{9,1},... | collective-permute-start | bytes 786440 | tf_op jit(solution)/shard_map/ppermute | solution.py:330
  20.0 2.7 %collective-permute-start.3 = (bf16[128,1024]{1,0:T(8,128)(2,1)S(1)}, bf16[128,1024]{1,0:T(8,128)(2,1)S(1)}, u32[]{:S(2)}, u32[]{:S(2)}) collective-permute-start(bf16[128,1024]{1,0:T(8,128)(2,1)S(1)} %shard_map.122.refs_0_.refs_4_), channel_id=1, source_target_pairs={{0,16},{1,17},{2,18},{3,19},{4,20},{5,21},{6,22},{7,23},{8,24},{9,... | collective-permute-start | bytes 786440 | tf_op jit(solution)/shard_map/ppermute | solution.py:330
  22.7 0.0 copy-done.2
  22.7 11.3 %shard_map.123.refs_0_.refs_4_ = bf16[128,1024]{1,0:T(8,128)(2,1)S(1)} custom-call(bf16[128,1024]{1,0:T(8,128)(2,1)S(1)} %copy-done.2, bf16[1024,8192]{1,0:T(8,128)(2,1)} %w_in.3, bf16[8192,1024]{1,0:T(8,128)(2,1)} %w_out.3, bf16[128,1024]{1,0:T(8,128)(2,1)S(1)} %shard_map.122.refs_0_.refs_4_), custom_call_target="tpu_custom_call" | custom-call | flops 1 | bytes 1 | tf_op jit(solution)/shard_map/pallas_call | solution.py:74
  34.0 0.0 collective-permute-done.4.refs_5_.refs_1_
  34.0 0.0 collective-permute-done.3.refs_6_.refs_2_
  34.0 0.0 collective-permute-done.refs_13_.refs_9_
  34.0 0.0 collective-permute-done.1.refs_14_.refs_10_
  34.0 0.0 collective-permute-done.2.refs_15_.refs_11_
  34.0 1.6 %collective-permute-start.5 = (bf16[128,1024]{1,0:T(8,128)(2,1)S(1)}, bf16[128,1024]{1,0:T(8,128)(2,1)S(1)}, u32[]{:S(2)}, u32[]{:S(2)}) collective-permute-start(bf16[128,1024]{1,0:T(8,128)(2,1)S(1)} %shard_map.123.refs_0_.refs_4_), channel_id=1, source_target_pairs={{0,2},{1,3},{2,0},{3,1},{4,6},{5,7},{6,4},{7,5},{8,10},{9,11},{10,... | collective-permute-start | bytes 786440 | tf_op jit(solution)/shard_map/ppermute | solution.py:330
  35.6 0.2 collective-permute-start.8
  35.8 1.5 %collective-permute-start.7 = (bf16[128,1024]{1,0:T(8,128)(2,1)S(1)}, bf16[128,1024]{1,0:T(8,128)(2,1)S(1)}, u32[]{:S(2)}, u32[]{:S(2)}) collective-permute-start(bf16[128,1024]{1,0:T(8,128)(2,1)S(1)} %shard_map.123.refs_0_.refs_4_), channel_id=1, source_target_pairs={{0,6},{1,7},{2,4},{3,5},{4,2},{5,3},{6,0},{7,1},{8,14},{9,15},{10,... | collective-permute-start | bytes 786440 | tf_op jit(solution)/shard_map/ppermute | solution.py:330
  37.3 0.7 collective-permute-start.6
  38.0 5.4 %collective-permute-done.5.refs_1_.refs_5_ = bf16[128,1024]{1,0:T(8,128)(2,1)S(1)} collective-permute-done((bf16[128,1024]{1,0:T(8,128)(2,1)S(1)}, bf16[128,1024]{1,0:T(8,128)(2,1)S(1)}, u32[]{:S(2)}, u32[]{:S(2)}) %collective-permute-start.5) | collective-permute-done | bytes 262176 | tf_op jit(solution)/shard_map/ppermute | solution.py:330
  43.4 0.0 collective-permute-start.9
  43.4 0.5 collective-permute-start.10
  43.9 0.0 collective-permute-done.8.refs_7_.refs_3_
  43.9 0.0 collective-permute-start.12
  43.9 3.2 %collective-permute-done.7.refs_3_.refs_7_ = bf16[128,1024]{1,0:T(8,128)(2,1)S(1)} collective-permute-done((bf16[128,1024]{1,0:T(8,128)(2,1)S(1)}, bf16[128,1024]{1,0:T(8,128)(2,1)S(1)}, u32[]{:S(2)}, u32[]{:S(2)}) %collective-permute-start.7) | collective-permute-done | bytes 262176 | tf_op jit(solution)/shard_map/ppermute | solution.py:330
  47.1 0.0 collective-permute-start.11
  47.1 1.9 %collective-permute-done.6.refs_2_.refs_6_ = bf16[128,1024]{1,0:T(8,128)(2,1)S(1)} collective-permute-done((bf16[128,1024]{1,0:T(8,128)(2,1)S(1)}, bf16[128,1024]{1,0:T(8,128)(2,1)S(1)}, u32[]{:S(2)}, u32[]{:S(2)}) %collective-permute-start.6) | collective-permute-done | bytes 262176 | tf_op jit(solution)/shard_map/ppermute | solution.py:330
  49.0 0.0 collective-permute-done.12.refs_11_.refs_7_
  49.0 0.0 collective-permute-done.9.refs_8_.refs_4_
  49.0 0.0 collective-permute-done.10.refs_9_.refs_5_
  49.0 0.0 collective-permute-done.11.refs_10_.refs_6_
  49.0 2.9 %shard_map.124 = (f32[1024,512]{1,0:T(8,128)S(1)}, f32[4,4,128]{2,1,0:T(4,128)S(1)}) custom-call(bf16[128,1024]{1,0:T(8,128)(2,1)S(1)} %shard_map.123.refs_0_.refs_4_, bf16[128,1024]{1,0:T(8,128)(2,1)S(1)} %collective-permute-done.5.refs_1_.refs_5_, bf16[128,1024]{1,0:T(8,128)(2,1)S(1)} %collective-permute-done.6.refs_2_.refs_6_, ...), custom_call_target="tpu_custom_call" | custom-call | flops 1073741824 | bytes 4194304 | tf_op jit(solution)/shard_map/pallas_call | solution.py:193
  51.9 1.7 %collective-permute-start.15 = (f32[4,4,128]{2,1,0:T(4,128)S(1)}, f32[4,4,128]{2,1,0:T(4,128)S(1)}, u32[]{:S(2)}, u32[]{:S(2)}) collective-permute-start(f32[4,4,128]{2,1,0:T(4,128)S(1)} %get-tuple-element.50.refs_0_), channel_id=1, source_target_pairs={{0,6},{1,7},{2,4},{3,5},{4,2},{5,3},{6,0},{7,1},{8,14},{9,15},{10,... | collective-permute-start | bytes 24584 | tf_op jit(solution)/shard_map/ppermute | solution.py:330
  53.6 1.1 %collective-permute-start.14 = (f32[4,4,128]{2,1,0:T(4,128)S(1)}, f32[4,4,128]{2,1,0:T(4,128)S(1)}, u32[]{:S(2)}, u32[]{:S(2)}) collective-permute-start(f32[4,4,128]{2,1,0:T(4,128)S(1)} %get-tuple-element.50.refs_0_), channel_id=1, source_target_pairs={{0,4},{1,5},{2,6},{3,7},{4,0},{5,1},{6,2},{7,3},{8,12},{9,13},{10,... | collective-permute-start | bytes 24584 | tf_op jit(solution)/shard_map/ppermute | solution.py:330
  54.7 0.7 collective-permute-start.13
  55.5 1.1 %collective-permute-done.15.refs_3_ = f32[4,4,128]{2,1,0:T(4,128)S(1)} collective-permute-done((f32[4,4,128]{2,1,0:T(4,128)S(1)}, f32[4,4,128]{2,1,0:T(4,128)S(1)}, u32[]{:S(2)}, u32[]{:S(2)}) %collective-permute-start.15) | collective-permute-done | bytes 8224 | tf_op jit(solution)/shard_map/ppermute | solution.py:330
  56.5 0.7 collective-permute-done.14.refs_2_
  57.2 1.1 %collective-permute-done.13.refs_1_ = f32[4,4,128]{2,1,0:T(4,128)S(1)} collective-permute-done((f32[4,4,128]{2,1,0:T(4,128)S(1)}, f32[4,4,128]{2,1,0:T(4,128)S(1)}, u32[]{:S(2)}, u32[]{:S(2)}) %collective-permute-start.13) | collective-permute-done | bytes 8224 | tf_op jit(solution)/shard_map/ppermute | solution.py:330
  58.4 1.6 %shard_map.125 = (bf16[1024,512]{1,0:T(8,128)(2,1)S(1)}, f32[1,128]{1,0:T(1,128)}, bf16[512,1024]{1,0:T(8,128)(2,1)S(1)}) custom-call(f32[1,128]{1,0:T(1,128)S(1)} %get-tuple-element.33.entropy, f32[4,4,128]{2,1,0:T(4,128)S(1)} %get-tuple-element.50.refs_0_, f32[4,4,128]{2,1,0:T(4,128)S(1)} %collective-permute-done.13.refs_1_, ...), custom_call_target="tpu_custom_call" | custom-call | flops 536870912 | bytes 4194304 | tf_op jit(solution)/shard_map/pallas_call | solution.py:233
  60.0 0.0 collective-permute-start.16
  60.0 0.7 shard_map.126.near
  60.7 1.9 %collective-permute-done.16.far = bf16[512,1024]{1,0:T(8,128)(2,1)S(1)} collective-permute-done((bf16[512,1024]{1,0:T(8,128)(2,1)S(1)}, bf16[512,1024]{1,0:T(8,128)(2,1)S(1)}, u32[]{:S(2)}, u32[]{:S(2)}) %collective-permute-start.16) | collective-permute-done | bytes 1048608 | tf_op jit(solution)/shard_map/ppermute | solution.py:330
  62.6 0.2 shard_map.127
  62.8 1.7 %collective-permute-start.20 = (bf16[128,1024]{1,0:T(8,128)(2,1)S(1)}, bf16[128,1024]{1,0:T(8,128)(2,1)S(1)}, u32[]{:S(2)}, u32[]{:S(2)}) collective-permute-start(bf16[128,1024]{1,0:T(8,128)(2,1)S(1)} %get-tuple-element.61), channel_id=1, source_target_pairs={{0,8},{1,9},{2,10},{3,11},{4,12},{5,13},{6,14},{7,15},{8,0},{9,1},... | collective-permute-start | bytes 786440 | tf_op jit(solution)/shard_map/ppermute | solution.py:330
  64.4 1.3 %shard_map.128 = (f32[128,1024]{1,0:T(8,128)S(1)}, bf16[128,1024]{1,0:T(8,128)(2,1)S(1)}, bf16[128,1024]{1,0:T(8,128)(2,1)S(1)}, bf16[128,1024]{1,0:T(8,128)(2,1)S(1)}) custom-call(bf16[1024,512]{1,0:T(8,128)(2,1)S(1)} %get-tuple-element.53.grads, bf16[128,1024]{1,0:T(8,128)(2,1)S(1)} %shard_map.122.refs_0_.refs_4_, ...), custom_call_target="tpu_custom_call" | custom-call | flops 1073741824 | bytes 2097152 | tf_op jit(solution)/shard_map/pallas_call | solution.py:286
  65.8 0.5 collective-permute-start.17
  66.3 0.7 collective-permute-start.18
  67.0 2.3 %collective-permute-start.19 = (bf16[128,1024]{1,0:T(8,128)(2,1)S(1)}, bf16[128,1024]{1,0:T(8,128)(2,1)S(1)}, u32[]{:S(2)}, u32[]{:S(2)}) collective-permute-start(bf16[128,1024]{1,0:T(8,128)(2,1)S(1)} %get-tuple-element.59), channel_id=1, source_target_pairs={{0,6},{1,7},{2,4},{3,5},{4,2},{5,3},{6,0},{7,1},{8,14},{9,15},{10,... | collective-permute-start | bytes 786440 | tf_op jit(solution)/shard_map/ppermute | solution.py:330
  69.4 0.4 collective-permute-start.22
  69.8 1.6 %collective-permute-done.20 = bf16[128,1024]{1,0:T(8,128)(2,1)S(1)} collective-permute-done((bf16[128,1024]{1,0:T(8,128)(2,1)S(1)}, bf16[128,1024]{1,0:T(8,128)(2,1)S(1)}, u32[]{:S(2)}, u32[]{:S(2)}) %collective-permute-start.20) | collective-permute-done | bytes 262176 | tf_op jit(solution)/shard_map/ppermute | solution.py:330
  71.4 0.1 add_convert_fusion
  71.5 2.4 %collective-permute-start.21 = (bf16[128,1024]{1,0:T(8,128)(2,1)S(1)}, bf16[128,1024]{1,0:T(8,128)(2,1)S(1)}, u32[]{:S(2)}, u32[]{:S(2)}) collective-permute-start(bf16[128,1024]{1,0:T(8,128)(2,1)S(1)} %add_convert_fusion), channel_id=1, source_target_pairs={{0,16},{1,17},{2,18},{3,19},{4,20},{5,21},{6,22},{7,23},{8,24},{9,... | collective-permute-start | bytes 786440 | tf_op jit(solution)/shard_map/ppermute | solution.py:330
  73.9 1.2 %collective-permute-done.17 = bf16[128,1024]{1,0:T(8,128)(2,1)S(1)} collective-permute-done((bf16[128,1024]{1,0:T(8,128)(2,1)S(1)}, bf16[128,1024]{1,0:T(8,128)(2,1)S(1)}, u32[]{:S(2)}, u32[]{:S(2)}) %collective-permute-start.17) | collective-permute-done | bytes 262176 | tf_op jit(solution)/shard_map/ppermute | solution.py:330
  75.1 0.1 collective-permute-done.18
  75.1 4.7 %collective-permute-done.19 = bf16[128,1024]{1,0:T(8,128)(2,1)S(1)} collective-permute-done((bf16[128,1024]{1,0:T(8,128)(2,1)S(1)}, bf16[128,1024]{1,0:T(8,128)(2,1)S(1)}, u32[]{:S(2)}, u32[]{:S(2)}) %collective-permute-start.19) | collective-permute-done | bytes 262176 | tf_op jit(solution)/shard_map/ppermute | solution.py:330
  79.8 0.9 %convert_add_fusion.1 = f32[128,1024]{1,0:T(8,128)} fusion(bf16[128,1024]{1,0:T(8,128)(2,1)S(1)} %collective-permute-done.19, bf16[128,1024]{1,0:T(8,128)(2,1)S(1)} %collective-permute-done.18, f32[128,1024]{1,0:T(8,128)S(1)} %get-tuple-element.56, bf16[128,1024]{1,0:T(8,128)(2,1)S(1)} %collective-permute-done.17), kind=kLoop, calls=%fused_computation.2 | loop fusion | flops 786432 | bytes 1835008 | tf_op jit(solution)/shard_map/add | solution.py:366
  80.7 0.1 collective-permute-done.22
  80.8 4.6 %collective-permute-done.21 = bf16[128,1024]{1,0:T(8,128)(2,1)S(1)} collective-permute-done((bf16[128,1024]{1,0:T(8,128)(2,1)S(1)}, bf16[128,1024]{1,0:T(8,128)(2,1)S(1)}, u32[]{:S(2)}, u32[]{:S(2)}) %collective-permute-start.21) | collective-permute-done | bytes 262176 | tf_op jit(solution)/shard_map/ppermute | solution.py:330
  85.4 0.9 %convert_add_fusion = f32[128,1024]{1,0:T(8,128)} fusion(bf16[128,1024]{1,0:T(8,128)(2,1)S(1)} %collective-permute-done.22, f32[128,1024]{1,0:T(8,128)S(1)} %get-tuple-element.55.refs_8_, bf16[128,1024]{1,0:T(8,128)(2,1)S(1)} %collective-permute-done.21), kind=kLoop, calls=%fused_computation | loop fusion | flops 524288 | bytes 1572864 | tf_op jit(solution)/shard_map/add | solution.py:366
Async XLA Ops:
  1.3 8.3 %copy-start = (bf16[1024,8192]{1,0:T(8,128)(2,1)S(1)}, bf16[1024,8192]{1,0:T(8,128)(2,1)}, u32[]{:S(2)}) copy-start(bf16[1024,8192]{1,0:T(8,128)(2,1)} %w_in.2) | copy-start | bytes 50331652
  1.3 8.3 %copy-start.1 = (bf16[128,1024]{1,0:T(8,128)(2,1)S(1)}, bf16[128,1024]{1,0:T(8,128)(2,1)}, u32[]{:S(2)}) copy-start(bf16[128,1024]{1,0:T(8,128)(2,1)} %feats.2) | copy-start | bytes 786436
  4.7 29.3 %collective-permute-start = (f32[8,128,128]{2,1,0:T(8,128)S(1)}, f32[8,128,128]{2,1,0:T(8,128)S(1)}, u32[]{:S(2)}, u32[]{:S(2)}) collective-permute-start(f32[8,128,128]{2,1,0:T(8,128)S(1)} %get-tuple-element.35), channel_id=1, source_target_pairs={{0,2},{1,3},{2,0},{3,1},{4,6},{5,7},{6,4},{7,5},{8,10},{9,11},{10,... | collective-permute-start | bytes 1572872 | tf_op jit(solution)/shard_map/ppermute | solution.py:330
  8.1 26.0 %collective-permute-start.1 = (f32[8,128,128]{2,1,0:T(8,128)S(1)}, f32[8,128,128]{2,1,0:T(8,128)S(1)}, u32[]{:S(2)}, u32[]{:S(2)}) collective-permute-start(f32[8,128,128]{2,1,0:T(8,128)S(1)} %get-tuple-element.36), channel_id=1, source_target_pairs={{0,4},{1,5},{2,6},{3,7},{4,0},{5,1},{6,2},{7,3},{8,12},{9,13},{10,... | collective-permute-start | bytes 1572872 | tf_op jit(solution)/shard_map/ppermute | solution.py:330
  9.4 24.6 %collective-permute-start.2 = (f32[8,128,128]{2,1,0:T(8,128)S(1)}, f32[8,128,128]{2,1,0:T(8,128)S(1)}, u32[]{:S(2)}, u32[]{:S(2)}) collective-permute-start(f32[8,128,128]{2,1,0:T(8,128)S(1)} %get-tuple-element.37), channel_id=1, source_target_pairs={{0,6},{1,7},{2,4},{3,5},{4,2},{5,3},{6,0},{7,1},{8,14},{9,15},{10,... | collective-permute-start | bytes 1572872 | tf_op jit(solution)/shard_map/ppermute | solution.py:330
  9.6 13.1 %copy-start.2 = (bf16[128,1024]{1,0:T(8,128)(2,1)S(1)}, bf16[128,1024]{1,0:T(8,128)(2,1)}, u32[]{:S(2)}) copy-start(bf16[128,1024]{1,0:T(8,128)(2,1)} %feats.3) | copy-start | bytes 786436
  18.1 15.9 %collective-permute-start.4 = (bf16[128,1024]{1,0:T(8,128)(2,1)S(1)}, bf16[128,1024]{1,0:T(8,128)(2,1)S(1)}, u32[]{:S(2)}, u32[]{:S(2)}) collective-permute-start(bf16[128,1024]{1,0:T(8,128)(2,1)S(1)} %shard_map.122.refs_0_.refs_4_), channel_id=1, source_target_pairs={{0,8},{1,9},{2,10},{3,11},{4,12},{5,13},{6,14},{7,15},{8,0},{9,1},... | collective-permute-start | bytes 786440 | tf_op jit(solution)/shard_map/ppermute | solution.py:330
  20.0 14.0 %collective-permute-start.3 = (bf16[128,1024]{1,0:T(8,128)(2,1)S(1)}, bf16[128,1024]{1,0:T(8,128)(2,1)S(1)}, u32[]{:S(2)}, u32[]{:S(2)}) collective-permute-start(bf16[128,1024]{1,0:T(8,128)(2,1)S(1)} %shard_map.122.refs_0_.refs_4_), channel_id=1, source_target_pairs={{0,16},{1,17},{2,18},{3,19},{4,20},{5,21},{6,22},{7,23},{8,24},{9,... | collective-permute-start | bytes 786440 | tf_op jit(solution)/shard_map/ppermute | solution.py:330
  34.0 9.3 %collective-permute-start.5 = (bf16[128,1024]{1,0:T(8,128)(2,1)S(1)}, bf16[128,1024]{1,0:T(8,128)(2,1)S(1)}, u32[]{:S(2)}, u32[]{:S(2)}) collective-permute-start(bf16[128,1024]{1,0:T(8,128)(2,1)S(1)} %shard_map.123.refs_0_.refs_4_), channel_id=1, source_target_pairs={{0,2},{1,3},{2,0},{3,1},{4,6},{5,7},{6,4},{7,5},{8,10},{9,11},{10,... | collective-permute-start | bytes 786440 | tf_op jit(solution)/shard_map/ppermute | solution.py:330
  35.6 8.3 %collective-permute-start.8 = (bf16[128,1024]{1,0:T(8,128)(2,1)S(1)}, bf16[128,1024]{1,0:T(8,128)(2,1)S(1)}, u32[]{:S(2)}, u32[]{:S(2)}) collective-permute-start(bf16[128,1024]{1,0:T(8,128)(2,1)S(1)} %collective-permute-done.3.refs_6_.refs_2_), channel_id=1, source_target_pairs={{0,8},{1,9},{2,10},{3,11},{4,12},{5,13},{6,14},{7,15},{8,0},{9,1},... | collective-permute-start | bytes 786440 | tf_op jit(solution)/shard_map/ppermute | solution.py:330
  35.8 11.3 %collective-permute-start.7 = (bf16[128,1024]{1,0:T(8,128)(2,1)S(1)}, bf16[128,1024]{1,0:T(8,128)(2,1)S(1)}, u32[]{:S(2)}, u32[]{:S(2)}) collective-permute-start(bf16[128,1024]{1,0:T(8,128)(2,1)S(1)} %shard_map.123.refs_0_.refs_4_), channel_id=1, source_target_pairs={{0,6},{1,7},{2,4},{3,5},{4,2},{5,3},{6,0},{7,1},{8,14},{9,15},{10,... | collective-permute-start | bytes 786440 | tf_op jit(solution)/shard_map/ppermute | solution.py:330
  37.3 11.7 %collective-permute-start.6 = (bf16[128,1024]{1,0:T(8,128)(2,1)S(1)}, bf16[128,1024]{1,0:T(8,128)(2,1)S(1)}, u32[]{:S(2)}, u32[]{:S(2)}) collective-permute-start(bf16[128,1024]{1,0:T(8,128)(2,1)S(1)} %shard_map.123.refs_0_.refs_4_), channel_id=1, source_target_pairs={{0,4},{1,5},{2,6},{3,7},{4,0},{5,1},{6,2},{7,3},{8,12},{9,13},{10,... | collective-permute-start | bytes 786440 | tf_op jit(solution)/shard_map/ppermute | solution.py:330
  43.4 5.6 %collective-permute-start.9 = (bf16[128,1024]{1,0:T(8,128)(2,1)S(1)}, bf16[128,1024]{1,0:T(8,128)(2,1)S(1)}, u32[]{:S(2)}, u32[]{:S(2)}) collective-permute-start(bf16[128,1024]{1,0:T(8,128)(2,1)S(1)} %shard_map.122.refs_0_.refs_4_), channel_id=1, source_target_pairs={{0,1},{1,0},{2,3},{3,2},{4,5},{5,4},{6,7},{7,6},{8,9},{9,8},{10,11... | collective-permute-start | bytes 786440 | tf_op jit(solution)/shard_map/ppermute | solution.py:330
  43.4 5.6 %collective-permute-start.10 = (bf16[128,1024]{1,0:T(8,128)(2,1)S(1)}, bf16[128,1024]{1,0:T(8,128)(2,1)S(1)}, u32[]{:S(2)}, u32[]{:S(2)}) collective-permute-start(bf16[128,1024]{1,0:T(8,128)(2,1)S(1)} %collective-permute-done.4.refs_5_.refs_1_), channel_id=1, source_target_pairs={{0,1},{1,0},{2,3},{3,2},{4,5},{5,4},{6,7},{7,6},{8,9},{9,8},{10,11... | collective-permute-start | bytes 786440 | tf_op jit(solution)/shard_map/ppermute | solution.py:330
  43.9 5.1 %collective-permute-start.12 = (bf16[128,1024]{1,0:T(8,128)(2,1)S(1)}, bf16[128,1024]{1,0:T(8,128)(2,1)S(1)}, u32[]{:S(2)}, u32[]{:S(2)}) collective-permute-start(bf16[128,1024]{1,0:T(8,128)(2,1)S(1)} %collective-permute-done.8.refs_7_.refs_3_), channel_id=1, source_target_pairs={{0,1},{1,0},{2,3},{3,2},{4,5},{5,4},{6,7},{7,6},{8,9},{9,8},{10,11... | collective-permute-start | bytes 786440 | tf_op jit(solution)/shard_map/ppermute | solution.py:330
  47.1 1.9 %collective-permute-start.11 = (bf16[128,1024]{1,0:T(8,128)(2,1)S(1)}, bf16[128,1024]{1,0:T(8,128)(2,1)S(1)}, u32[]{:S(2)}, u32[]{:S(2)}) collective-permute-start(bf16[128,1024]{1,0:T(8,128)(2,1)S(1)} %collective-permute-done.3.refs_6_.refs_2_), channel_id=1, source_target_pairs={{0,1},{1,0},{2,3},{3,2},{4,5},{5,4},{6,7},{7,6},{8,9},{9,8},{10,11... | collective-permute-start | bytes 786440 | tf_op jit(solution)/shard_map/ppermute | solution.py:330
  51.9 4.6 %collective-permute-start.15 = (f32[4,4,128]{2,1,0:T(4,128)S(1)}, f32[4,4,128]{2,1,0:T(4,128)S(1)}, u32[]{:S(2)}, u32[]{:S(2)}) collective-permute-start(f32[4,4,128]{2,1,0:T(4,128)S(1)} %get-tuple-element.50.refs_0_), channel_id=1, source_target_pairs={{0,6},{1,7},{2,4},{3,5},{4,2},{5,3},{6,0},{7,1},{8,14},{9,15},{10,... | collective-permute-start | bytes 24584 | tf_op jit(solution)/shard_map/ppermute | solution.py:330
  53.6 3.7 %collective-permute-start.14 = (f32[4,4,128]{2,1,0:T(4,128)S(1)}, f32[4,4,128]{2,1,0:T(4,128)S(1)}, u32[]{:S(2)}, u32[]{:S(2)}) collective-permute-start(f32[4,4,128]{2,1,0:T(4,128)S(1)} %get-tuple-element.50.refs_0_), channel_id=1, source_target_pairs={{0,4},{1,5},{2,6},{3,7},{4,0},{5,1},{6,2},{7,3},{8,12},{9,13},{10,... | collective-permute-start | bytes 24584 | tf_op jit(solution)/shard_map/ppermute | solution.py:330
  54.7 3.7 %collective-permute-start.13 = (f32[4,4,128]{2,1,0:T(4,128)S(1)}, f32[4,4,128]{2,1,0:T(4,128)S(1)}, u32[]{:S(2)}, u32[]{:S(2)}) collective-permute-start(f32[4,4,128]{2,1,0:T(4,128)S(1)} %get-tuple-element.50.refs_0_), channel_id=1, source_target_pairs={{0,2},{1,3},{2,0},{3,1},{4,6},{5,7},{6,4},{7,5},{8,10},{9,11},{10,... | collective-permute-start | bytes 24584 | tf_op jit(solution)/shard_map/ppermute | solution.py:330
  60.0 2.7 %collective-permute-start.16 = (bf16[512,1024]{1,0:T(8,128)(2,1)S(1)}, bf16[512,1024]{1,0:T(8,128)(2,1)S(1)}, u32[]{:S(2)}, u32[]{:S(2)}) collective-permute-start(bf16[512,1024]{1,0:T(8,128)(2,1)S(1)} %get-tuple-element.54), channel_id=1, source_target_pairs={{0,1},{1,0},{2,3},{3,2},{4,5},{5,4},{6,7},{7,6},{8,9},{9,8},{10,11... | collective-permute-start | bytes 3145736 | tf_op jit(solution)/shard_map/ppermute | solution.py:330
  62.8 8.6 %collective-permute-start.20 = (bf16[128,1024]{1,0:T(8,128)(2,1)S(1)}, bf16[128,1024]{1,0:T(8,128)(2,1)S(1)}, u32[]{:S(2)}, u32[]{:S(2)}) collective-permute-start(bf16[128,1024]{1,0:T(8,128)(2,1)S(1)} %get-tuple-element.61), channel_id=1, source_target_pairs={{0,8},{1,9},{2,10},{3,11},{4,12},{5,13},{6,14},{7,15},{8,0},{9,1},... | collective-permute-start | bytes 786440 | tf_op jit(solution)/shard_map/ppermute | solution.py:330
  65.8 9.3 %collective-permute-start.17 = (bf16[128,1024]{1,0:T(8,128)(2,1)S(1)}, bf16[128,1024]{1,0:T(8,128)(2,1)S(1)}, u32[]{:S(2)}, u32[]{:S(2)}) collective-permute-start(bf16[128,1024]{1,0:T(8,128)(2,1)S(1)} %get-tuple-element.57), channel_id=1, source_target_pairs={{0,2},{1,3},{2,0},{3,1},{4,6},{5,7},{6,4},{7,5},{8,10},{9,11},{10,... | collective-permute-start | bytes 786440 | tf_op jit(solution)/shard_map/ppermute | solution.py:330
  66.3 8.8 %collective-permute-start.18 = (bf16[128,1024]{1,0:T(8,128)(2,1)S(1)}, bf16[128,1024]{1,0:T(8,128)(2,1)S(1)}, u32[]{:S(2)}, u32[]{:S(2)}) collective-permute-start(bf16[128,1024]{1,0:T(8,128)(2,1)S(1)} %get-tuple-element.58), channel_id=1, source_target_pairs={{0,4},{1,5},{2,6},{3,7},{4,0},{5,1},{6,2},{7,3},{8,12},{9,13},{10,... | collective-permute-start | bytes 786440 | tf_op jit(solution)/shard_map/ppermute | solution.py:330
  67.0 12.8 %collective-permute-start.19 = (bf16[128,1024]{1,0:T(8,128)(2,1)S(1)}, bf16[128,1024]{1,0:T(8,128)(2,1)S(1)}, u32[]{:S(2)}, u32[]{:S(2)}) collective-permute-start(bf16[128,1024]{1,0:T(8,128)(2,1)S(1)} %get-tuple-element.59), channel_id=1, source_target_pairs={{0,6},{1,7},{2,4},{3,5},{4,2},{5,3},{6,0},{7,1},{8,14},{9,15},{10,... | collective-permute-start | bytes 786440 | tf_op jit(solution)/shard_map/ppermute | solution.py:330
  69.4 11.5 %collective-permute-start.22 = (bf16[128,1024]{1,0:T(8,128)(2,1)S(1)}, bf16[128,1024]{1,0:T(8,128)(2,1)S(1)}, u32[]{:S(2)}, u32[]{:S(2)}) collective-permute-start(bf16[128,1024]{1,0:T(8,128)(2,1)S(1)} %get-tuple-element.62), channel_id=1, source_target_pairs={{0,8},{1,9},{2,10},{3,11},{4,12},{5,13},{6,14},{7,15},{8,0},{9,1},... | collective-permute-start | bytes 786440 | tf_op jit(solution)/shard_map/ppermute | solution.py:330
  71.5 14.0 %collective-permute-start.21 = (bf16[128,1024]{1,0:T(8,128)(2,1)S(1)}, bf16[128,1024]{1,0:T(8,128)(2,1)S(1)}, u32[]{:S(2)}, u32[]{:S(2)}) collective-permute-start(bf16[128,1024]{1,0:T(8,128)(2,1)S(1)} %add_convert_fusion), channel_id=1, source_target_pairs={{0,16},{1,17},{2,18},{3,19},{4,20},{5,21},{6,22},{7,23},{8,24},{9,... | collective-permute-start | bytes 786440 | tf_op jit(solution)/shard_map/ppermute | solution.py:330

commit v9 on v8

--- a/solution.py
+++ b/solution.py
@@ -69,7 +69,7 @@
 def tower(feats, w_in, w_out, dtype, after, ready):
     rows, width = feats.shape
     hidden = w_in.shape[1]
-    chunks = max(1, hidden // 512)
+    chunks = max(1, hidden // (2048 if ready else 1024))
     own = [] if ready else [pltpu.VMEM(w_in.shape, w_in.dtype), pltpu.SemaphoreType.DMA((chunks,))]
     return pl.pallas_call(
         functools.partial(tower_body, chunks, ready),
@@ -124,7 +124,7 @@
             apart = owner[cands[0, k]] ^ me[0]
             inside = apart % (CORES * cols)
             place = (inside % CORES) * planes + apart // (CORES * cols)
-            dense[inside // CORES, place] = prob[:, k * rows : (k + 1) * rows].T
+            dense[inside // CORES, place] = prob[:, k * rows : (k + 1) * rows]
 
     copies = [pltpu.make_async_copy(dense.at[i], outs[i], sems.at[i]) for i in range(cols)]
     for copy in copies:
@@ -152,6 +152,23 @@
         compiler_params=params(24),
         cost_estimate=cost(10**10, 8 * teacher.size),
     )(me, in_hbm(cands), count, in_hbm(owner), in_hbm(teacher))
+
+
+def turn_body(cols, *refs):
+    for source, out in zip(refs[:cols], refs[cols:]):
+        for i in range(source.shape[0]):
+            out[i] = source[i].T
+
+
+def turned(probs):
+    return pl.pallas_call(
+        functools.partial(turn_body, len(probs)),
+        in_specs=[VMEM] * len(probs),
+        out_specs=[VMEM] * len(probs),
+        out_shape=[struct(part.shape, part.dtype) for part in probs],
+        compiler_params=params(24),
+        cost_estimate=cost(1, 1),
+    )(*probs)
 
 
 def lay(sources, target):
@@ -343,9 +360,9 @@
     user_emb = embed(user_feats, user_w_in, user_w_out, [item_emb], False)
     user_emb, item_emb, probs, crossed, nearby = lax.optimization_barrier((user_emb, item_emb, probs, crossed, nearby))
     users = [user_emb] + over_columns(user_emb)
+    probs = turned(probs)
+    item_emb, nearby, crossed, probs = lax.optimization_barrier((item_emb, nearby, crossed, probs))
     derived = [swap(block, z * cols * CORES) for block in crossed for z in range(1, wide)]
-    if cols > 1:
-        users[1], item_emb, nearby, crossed = lax.optimization_barrier((users[1], item_emb, nearby, crossed))
     items = [item_emb] + nearby + crossed + derived
     items = items + [swap(block, 1) for block in items]
 

time: 86.5 us -> 84.9 us (0.982)
  Pallas kernels: 29.9 us -> 27.9 us
  waiting for transfers between devices: 27.5 us -> 28.6 us
    pallas_call x2, Pallas kernels: 19.8 us -> 18.1 us  [tower(): pl.pallas_call(functools.partial(tower_body, chunks, ready), in_specs=[VM...]
    ppermute x23, waiting for transfers between devices: 27.5 us -> 28.6 us  [swap(): return lax.ppermute(array, 'dp', [(i, i ^ apart) for i in range(count)])]
  transfers between devices with their start and end apart: 23 -> 23, of which waited for: 13 -> 15; matrix products, arithmetic and copies ran while one was open for 1% -> 1% of each run, Pallas kernels for 25% -> 24%
where the time goes in v9:
time: 84.9 us; the launch traced here: 84.7 us
  waiting for transfers between devices  28.6 us (34%)
  Pallas kernels  27.9 us (33%)
  starting transfers between devices  24.9 us (29%)
  other arithmetic  1.89 us (2%)
  between operations  1.39 us (2%)
    ppermute x23, waiting for transfers between devices, swap(): return lax.ppermute(array, 'dp', [(i, i ^ apart) for i in range(count)])  28.6 us
    ppermute x23, starting transfers between devices, swap(): return lax.ppermute(array, 'dp', [(i, i ^ apart) for i in range(count)])  24.9 us
    pallas_call x2, Pallas kernels, tower(): pl.pallas_call(functools.partial(tower_body, chunks, ready), in_specs=[VM...  18.1 us
    pallas_call x1, Pallas kernels, scores(): pl.pallas_call(functools.partial(score_body, cols, places, scale), in_spe...  2.99 us
    pallas_call x1, Pallas kernels, spread_teacher(): pl.pallas_call(functools.partial(teacher_body, cols, planes), in_specs=[S...  2.54 us
    add x2, other arithmetic, add(): functools.reduce(jnp.add, [part.astype(jnp.float32) for part in parts], s...  1.82 us
  transfers between devices with their start and end apart: 23, of which 15 were waited for; matrix products, arithmetic and copies ran while one was open for 1% of the time, Pallas kernels for 24%

profile of v9, /device:TPU:0, one launch (start us, length us, event | category | flops | bytes accessed | tf_op | source)
XLA Modules:
  0.0 84.7 jit_solution(13705364613618997674)
XLA Ops:
  1.3 0.0 copy-start
  1.3 0.0 copy-start.1
  1.3 2.5 %shard_map.121 = (f32[8,128,128]{2,1,0:T(8,128)S(1)}, f32[8,128,128]{2,1,0:T(8,128)S(1)}, f32[8,128,128]{2,1,0:T(8,128)S(1)}, f32[8,128,128]{2,1,0:T(8,128)S(1)}, f32[1,128]{1,0:T(1,128)S(1)}) custom-call(s32[1]{0:T(128)} %bitcast.me, s32[1,16]{1,0:T(1,128)} %cands_hbm.1, s32[1]{0:T(128)S(6)} %copy.13.count, s32[32]{0:T(128)} %owner_hbm.1, ...), custom_call_target="tpu_custom_call" | custom-call | flops 10000000000 | bytes 2097152 | tf_op jit(solution)/shard_map/pallas_call | solution.py:139
  3.8 3.0 %collective-permute-start = (f32[8,128,128]{2,1,0:T(8,128)S(1)}, f32[8,128,128]{2,1,0:T(8,128)S(1)}, u32[]{:S(2)}, u32[]{:S(2)}) collective-permute-start(f32[8,128,128]{2,1,0:T(8,128)S(1)} %get-tuple-element.42), channel_id=1, source_target_pairs={{0,2},{1,3},{2,0},{3,1},{4,6},{5,7},{6,4},{7,5},{8,10},{9,11},{10,... | collective-permute-start | bytes 1572872 | tf_op jit(solution)/shard_map/ppermute | solution.py:347
  6.9 1.5 %collective-permute-start.1 = (f32[8,128,128]{2,1,0:T(8,128)S(1)}, f32[8,128,128]{2,1,0:T(8,128)S(1)}, u32[]{:S(2)}, u32[]{:S(2)}) collective-permute-start(f32[8,128,128]{2,1,0:T(8,128)S(1)} %get-tuple-element.43), channel_id=1, source_target_pairs={{0,4},{1,5},{2,6},{3,7},{4,0},{5,1},{6,2},{7,3},{8,12},{9,13},{10,... | collective-permute-start | bytes 1572872 | tf_op jit(solution)/shard_map/ppermute | solution.py:347
  8.4 0.0 collective-permute-start.2
  8.4 0.0 copy-done
  8.4 0.0 copy-done.1
  8.4 0.0 copy-start.2
  8.4 6.8 %shard_map.122.refs_0_.refs_4_ = bf16[128,1024]{1,0:T(8,128)(2,1)S(1)} custom-call(bf16[128,1024]{1,0:T(8,128)(2,1)S(1)} %copy-done.1, bf16[1024,8192]{1,0:T(8,128)(2,1)S(1)} %copy-done, bf16[8192,1024]{1,0:T(8,128)(2,1)} %w_out.2, f32[8,128,128]{2,1,0:T(8,128)S(1)} %get-tuple-element.49.refs_0_), custom_call_target="tpu_custom_call" | custom-call | flops 1 | bytes 1 | tf_op jit(solution)/shard_map/pallas_call | solution.py:74
  15.2 2.1 %collective-permute-start.4 = (bf16[128,1024]{1,0:T(8,128)(2,1)S(1)}, bf16[128,1024]{1,0:T(8,128)(2,1)S(1)}, u32[]{:S(2)}, u32[]{:S(2)}) collective-permute-start(bf16[128,1024]{1,0:T(8,128)(2,1)S(1)} %shard_map.122.refs_0_.refs_4_), channel_id=1, source_target_pairs={{0,8},{1,9},{2,10},{3,11},{4,12},{5,13},{6,14},{7,15},{8,0},{9,1},... | collective-permute-start | bytes 786440 | tf_op jit(solution)/shard_map/ppermute | solution.py:347
  17.3 2.6 %collective-permute-start.3 = (bf16[128,1024]{1,0:T(8,128)(2,1)S(1)}, bf16[128,1024]{1,0:T(8,128)(2,1)S(1)}, u32[]{:S(2)}, u32[]{:S(2)}) collective-permute-start(bf16[128,1024]{1,0:T(8,128)(2,1)S(1)} %shard_map.122.refs_0_.refs_4_), channel_id=1, source_target_pairs={{0,16},{1,17},{2,18},{3,19},{4,20},{5,21},{6,22},{7,23},{8,24},{9,... | collective-permute-start | bytes 786440 | tf_op jit(solution)/shard_map/ppermute | solution.py:347
  19.9 0.0 copy-done.2
  19.9 11.3 %shard_map.123.refs_0_.refs_4_ = bf16[128,1024]{1,0:T(8,128)(2,1)S(1)} custom-call(bf16[128,1024]{1,0:T(8,128)(2,1)S(1)} %copy-done.2, bf16[1024,8192]{1,0:T(8,128)(2,1)} %w_in.3, bf16[8192,1024]{1,0:T(8,128)(2,1)} %w_out.3, bf16[128,1024]{1,0:T(8,128)(2,1)S(1)} %shard_map.122.refs_0_.refs_4_), custom_call_target="tpu_custom_call" | custom-call | flops 1 | bytes 1 | tf_op jit(solution)/shard_map/pallas_call | solution.py:74
  31.2 0.0 collective-permute-done.4.refs_5_.refs_1_
  31.2 0.4 collective-permute-done.3.refs_6_.refs_2_
  31.6 0.0 collective-permute-done.refs_1_
  31.6 0.0 collective-permute-done.1.refs_2_
  31.6 0.0 collective-permute-done.2.refs_3_
  31.6 2.5 %collective-permute-start.7 = (bf16[128,1024]{1,0:T(8,128)(2,1)S(1)}, bf16[128,1024]{1,0:T(8,128)(2,1)S(1)}, u32[]{:S(2)}, u32[]{:S(2)}) collective-permute-start(bf16[128,1024]{1,0:T(8,128)(2,1)S(1)} %shard_map.123.refs_0_.refs_4_), channel_id=1, source_target_pairs={{0,6},{1,7},{2,4},{3,5},{4,2},{5,3},{6,0},{7,1},{8,14},{9,15},{10,... | collective-permute-start | bytes 786440 | tf_op jit(solution)/shard_map/ppermute | solution.py:347
  34.1 0.5 collective-permute-start.6
  34.6 0.6 shard_map.124
  35.2 1.2 %collective-permute-start.8 = (bf16[128,1024]{1,0:T(8,128)(2,1)S(1)}, bf16[128,1024]{1,0:T(8,128)(2,1)S(1)}, u32[]{:S(2)}, u32[]{:S(2)}) collective-permute-start(bf16[128,1024]{1,0:T(8,128)(2,1)S(1)} %collective-permute-done.3.refs_6_.refs_2_), channel_id=1, source_target_pairs={{0,8},{1,9},{2,10},{3,11},{4,12},{5,13},{6,14},{7,15},{8,0},{9,1},... | collective-permute-start | bytes 786440 | tf_op jit(solution)/shard_map/ppermute | solution.py:347
  36.4 0.8 collective-permute-start.5
  37.2 0.0 collective-permute-start.11
  37.2 4.7 %collective-permute-done.7.refs_3_.refs_7_ = bf16[128,1024]{1,0:T(8,128)(2,1)S(1)} collective-permute-done((bf16[128,1024]{1,0:T(8,128)(2,1)S(1)}, bf16[128,1024]{1,0:T(8,128)(2,1)S(1)}, u32[]{:S(2)}, u32[]{:S(2)}) %collective-permute-start.7) | collective-permute-done | bytes 262176 | tf_op jit(solution)/shard_map/ppermute | solution.py:347
  41.8 0.0 collective-permute-start.9
  41.9 3.4 %collective-permute-done.6.refs_2_.refs_6_ = bf16[128,1024]{1,0:T(8,128)(2,1)S(1)} collective-permute-done((bf16[128,1024]{1,0:T(8,128)(2,1)S(1)}, bf16[128,1024]{1,0:T(8,128)(2,1)S(1)}, u32[]{:S(2)}, u32[]{:S(2)}) %collective-permute-start.6) | collective-permute-done | bytes 262176 | tf_op jit(solution)/shard_map/ppermute | solution.py:347
  45.2 0.0 collective-permute-start.10
  45.3 0.0 collective-permute-done.8.refs_7_.refs_3_
  45.3 0.5 collective-permute-start.12
  45.8 0.0 collective-permute-done.5.refs_1_.refs_5_
  45.8 0.0 collective-permute-done.9.refs_8_.refs_4_
  45.8 1.0 %collective-permute-done.10.refs_9_.refs_5_ = bf16[128,1024]{1,0:T(8,128)(2,1)S(1)} collective-permute-done((bf16[128,1024]{1,0:T(8,128)(2,1)S(1)}, bf16[128,1024]{1,0:T(8,128)(2,1)S(1)}, u32[]{:S(2)}, u32[]{:S(2)}) %collective-permute-start.10) | collective-permute-done | bytes 262176 | tf_op jit(solution)/shard_map/ppermute | solution.py:347
  46.8 0.0 collective-permute-done.11.refs_10_.refs_6_
  46.8 0.4 collective-permute-done.12.refs_11_.refs_7_
  47.2 3.0 %shard_map.125 = (f32[1024,512]{1,0:T(8,128)S(1)}, f32[4,4,128]{2,1,0:T(4,128)S(1)}) custom-call(bf16[128,1024]{1,0:T(8,128)(2,1)S(1)} %shard_map.123.refs_0_.refs_4_, bf16[128,1024]{1,0:T(8,128)(2,1)S(1)} %collective-permute-done.5.refs_1_.refs_5_, bf16[128,1024]{1,0:T(8,128)(2,1)S(1)} %collective-permute-done.6.refs_2_.refs_6_, ...), custom_call_target="tpu_custom_call" | custom-call | flops 1073741824 | bytes 4194304 | tf_op jit(solution)/shard_map/pallas_call | solution.py:210
  50.2 1.8 %collective-permute-start.15 = (f32[4,4,128]{2,1,0:T(4,128)S(1)}, f32[4,4,128]{2,1,0:T(4,128)S(1)}, u32[]{:S(2)}, u32[]{:S(2)}) collective-permute-start(f32[4,4,128]{2,1,0:T(4,128)S(1)} %get-tuple-element.64.refs_0_), channel_id=1, source_target_pairs={{0,6},{1,7},{2,4},{3,5},{4,2},{5,3},{6,0},{7,1},{8,14},{9,15},{10,... | collective-permute-start | bytes 24584 | tf_op jit(solution)/shard_map/ppermute | solution.py:347
  52.0 1.2 %collective-permute-start.14 = (f32[4,4,128]{2,1,0:T(4,128)S(1)}, f32[4,4,128]{2,1,0:T(4,128)S(1)}, u32[]{:S(2)}, u32[]{:S(2)}) collective-permute-start(f32[4,4,128]{2,1,0:T(4,128)S(1)} %get-tuple-element.64.refs_0_), channel_id=1, source_target_pairs={{0,4},{1,5},{2,6},{3,7},{4,0},{5,1},{6,2},{7,3},{8,12},{9,13},{10,... | collective-permute-start | bytes 24584 | tf_op jit(solution)/shard_map/ppermute | solution.py:347
  53.2 0.5 collective-permute-start.13
  53.7 1.1 %collective-permute-done.15.refs_3_ = f32[4,4,128]{2,1,0:T(4,128)S(1)} collective-permute-done((f32[4,4,128]{2,1,0:T(4,128)S(1)}, f32[4,4,128]{2,1,0:T(4,128)S(1)}, u32[]{:S(2)}, u32[]{:S(2)}) %collective-permute-start.15) | collective-permute-done | bytes 8224 | tf_op jit(solution)/shard_map/ppermute | solution.py:347
  54.8 0.8 collective-permute-done.14.refs_2_
  55.6 1.2 %collective-permute-done.13.refs_1_ = f32[4,4,128]{2,1,0:T(4,128)S(1)} collective-permute-done((f32[4,4,128]{2,1,0:T(4,128)S(1)}, f32[4,4,128]{2,1,0:T(4,128)S(1)}, u32[]{:S(2)}, u32[]{:S(2)}) %collective-permute-start.13) | collective-permute-done | bytes 8224 | tf_op jit(solution)/shard_map/ppermute | solution.py:347
  56.8 1.5 %shard_map.126 = (bf16[1024,512]{1,0:T(8,128)(2,1)S(1)}, f32[1,128]{1,0:T(1,128)}, bf16[512,1024]{1,0:T(8,128)(2,1)S(1)}) custom-call(f32[1,128]{1,0:T(1,128)S(1)} %get-tuple-element.40.entropy, f32[4,4,128]{2,1,0:T(4,128)S(1)} %get-tuple-element.64.refs_0_, f32[4,4,128]{2,1,0:T(4,128)S(1)} %collective-permute-done.13.refs_1_, ...), custom_call_target="tpu_custom_call" | custom-call | flops 536870912 | bytes 4194304 | tf_op jit(solution)/shard_map/pallas_call | solution.py:250
  58.4 0.0 collective-permute-start.16
  58.4 0.7 shard_map.127.near
  59.1 1.9 %collective-permute-done.16.far = bf16[512,1024]{1,0:T(8,128)(2,1)S(1)} collective-permute-done((bf16[512,1024]{1,0:T(8,128)(2,1)S(1)}, bf16[512,1024]{1,0:T(8,128)(2,1)S(1)}, u32[]{:S(2)}, u32[]{:S(2)}) %collective-permute-start.16) | collective-permute-done | bytes 1048608 | tf_op jit(solution)/shard_map/ppermute | solution.py:347
  61.0 0.2 shard_map.128
  61.2 0.8 collective-permute-start.20
  62.0 1.3 %shard_map.129 = (f32[128,1024]{1,0:T(8,128)S(1)}, bf16[128,1024]{1,0:T(8,128)(2,1)S(1)}, bf16[128,1024]{1,0:T(8,128)(2,1)S(1)}, bf16[128,1024]{1,0:T(8,128)(2,1)S(1)}) custom-call(bf16[1024,512]{1,0:T(8,128)(2,1)S(1)} %get-tuple-element.67.grads, bf16[128,1024]{1,0:T(8,128)(2,1)S(1)} %shard_map.122.refs_0_.refs_4_, ...), custom_call_target="tpu_custom_call" | custom-call | flops 1073741824 | bytes 2097152 | tf_op jit(solution)/shard_map/pallas_call | solution.py:303
  63.4 1.0 %collective-permute-start.17 = (bf16[128,1024]{1,0:T(8,128)(2,1)S(1)}, bf16[128,1024]{1,0:T(8,128)(2,1)S(1)}, u32[]{:S(2)}, u32[]{:S(2)}) collective-permute-start(bf16[128,1024]{1,0:T(8,128)(2,1)S(1)} %get-tuple-element.71), channel_id=1, source_target_pairs={{0,2},{1,3},{2,0},{3,1},{4,6},{5,7},{6,4},{7,5},{8,10},{9,11},{10,... | collective-permute-start | bytes 786440 | tf_op jit(solution)/shard_map/ppermute | solution.py:347
  64.4 0.8 collective-permute-start.18
  65.2 1.8 %collective-permute-start.19 = (bf16[128,1024]{1,0:T(8,128)(2,1)S(1)}, bf16[128,1024]{1,0:T(8,128)(2,1)S(1)}, u32[]{:S(2)}, u32[]{:S(2)}) collective-permute-start(bf16[128,1024]{1,0:T(8,128)(2,1)S(1)} %get-tuple-element.73), channel_id=1, source_target_pairs={{0,6},{1,7},{2,4},{3,5},{4,2},{5,3},{6,0},{7,1},{8,14},{9,15},{10,... | collective-permute-start | bytes 786440 | tf_op jit(solution)/shard_map/ppermute | solution.py:347
  66.9 1.3 %collective-permute-start.22 = (bf16[128,1024]{1,0:T(8,128)(2,1)S(1)}, bf16[128,1024]{1,0:T(8,128)(2,1)S(1)}, u32[]{:S(2)}, u32[]{:S(2)}) collective-permute-start(bf16[128,1024]{1,0:T(8,128)(2,1)S(1)} %get-tuple-element.76), channel_id=1, source_target_pairs={{0,8},{1,9},{2,10},{3,11},{4,12},{5,13},{6,14},{7,15},{8,0},{9,1},... | collective-permute-start | bytes 786440 | tf_op jit(solution)/shard_map/ppermute | solution.py:347
  68.2 2.2 %collective-permute-done.20 = bf16[128,1024]{1,0:T(8,128)(2,1)S(1)} collective-permute-done((bf16[128,1024]{1,0:T(8,128)(2,1)S(1)}, bf16[128,1024]{1,0:T(8,128)(2,1)S(1)}, u32[]{:S(2)}, u32[]{:S(2)}) %collective-permute-start.20) | collective-permute-done | bytes 262176 | tf_op jit(solution)/shard_map/ppermute | solution.py:347
  70.4 0.1 add_convert_fusion
  70.5 0.9 %collective-permute-start.21 = (bf16[128,1024]{1,0:T(8,128)(2,1)S(1)}, bf16[128,1024]{1,0:T(8,128)(2,1)S(1)}, u32[]{:S(2)}, u32[]{:S(2)}) collective-permute-start(bf16[128,1024]{1,0:T(8,128)(2,1)S(1)} %add_convert_fusion), channel_id=1, source_target_pairs={{0,16},{1,17},{2,18},{3,19},{4,20},{5,21},{6,22},{7,23},{8,24},{9,... | collective-permute-start | bytes 786440 | tf_op jit(solution)/shard_map/ppermute | solution.py:347
  71.4 1.2 %collective-permute-done.17 = bf16[128,1024]{1,0:T(8,128)(2,1)S(1)} collective-permute-done((bf16[128,1024]{1,0:T(8,128)(2,1)S(1)}, bf16[128,1024]{1,0:T(8,128)(2,1)S(1)}, u32[]{:S(2)}, u32[]{:S(2)}) %collective-permute-start.17) | collective-permute-done | bytes 262176 | tf_op jit(solution)/shard_map/ppermute | solution.py:347
  72.6 0.7 collective-permute-done.18
  73.3 4.5 %collective-permute-done.19 = bf16[128,1024]{1,0:T(8,128)(2,1)S(1)} collective-permute-done((bf16[128,1024]{1,0:T(8,128)(2,1)S(1)}, bf16[128,1024]{1,0:T(8,128)(2,1)S(1)}, u32[]{:S(2)}, u32[]{:S(2)}) %collective-permute-start.19) | collective-permute-done | bytes 262176 | tf_op jit(solution)/shard_map/ppermute | solution.py:347
  77.8 0.9 %convert_add_fusion.1 = f32[128,1024]{1,0:T(8,128)} fusion(bf16[128,1024]{1,0:T(8,128)(2,1)S(1)} %collective-permute-done.19, bf16[128,1024]{1,0:T(8,128)(2,1)S(1)} %collective-permute-done.18, f32[128,1024]{1,0:T(8,128)S(1)} %get-tuple-element.70, bf16[128,1024]{1,0:T(8,128)(2,1)S(1)} %collective-permute-done.17), kind=kLoop, calls=%fused_computation.2 | loop fusion | flops 786432 | bytes 1835008 | tf_op jit(solution)/shard_map/add | solution.py:383
  78.7 0.1 collective-permute-done.22
  78.9 5.0 %collective-permute-done.21 = bf16[128,1024]{1,0:T(8,128)(2,1)S(1)} collective-permute-done((bf16[128,1024]{1,0:T(8,128)(2,1)S(1)}, bf16[128,1024]{1,0:T(8,128)(2,1)S(1)}, u32[]{:S(2)}, u32[]{:S(2)}) %collective-permute-start.21) | collective-permute-done | bytes 262176 | tf_op jit(solution)/shard_map/ppermute | solution.py:347
  83.8 0.9 %convert_add_fusion = f32[128,1024]{1,0:T(8,128)} fusion(bf16[128,1024]{1,0:T(8,128)(2,1)S(1)} %collective-permute-done.22, f32[128,1024]{1,0:T(8,128)S(1)} %get-tuple-element.69.refs_8_, bf16[128,1024]{1,0:T(8,128)(2,1)S(1)} %collective-permute-done.21), kind=kLoop, calls=%fused_computation | loop fusion | flops 524288 | bytes 1572864 | tf_op jit(solution)/shard_map/add | solution.py:383
Async XLA Ops:
  1.3 7.1 %copy-start = (bf16[1024,8192]{1,0:T(8,128)(2,1)S(1)}, bf16[1024,8192]{1,0:T(8,128)(2,1)}, u32[]{:S(2)}) copy-start(bf16[1024,8192]{1,0:T(8,128)(2,1)} %w_in.2) | copy-start | bytes 50331652
  1.3 7.1 %copy-start.1 = (bf16[128,1024]{1,0:T(8,128)(2,1)S(1)}, bf16[128,1024]{1,0:T(8,128)(2,1)}, u32[]{:S(2)}) copy-start(bf16[128,1024]{1,0:T(8,128)(2,1)} %feats.2) | copy-start | bytes 786436
  3.8 27.7 %collective-permute-start = (f32[8,128,128]{2,1,0:T(8,128)S(1)}, f32[8,128,128]{2,1,0:T(8,128)S(1)}, u32[]{:S(2)}, u32[]{:S(2)}) collective-permute-start(f32[8,128,128]{2,1,0:T(8,128)S(1)} %get-tuple-element.42), channel_id=1, source_target_pairs={{0,2},{1,3},{2,0},{3,1},{4,6},{5,7},{6,4},{7,5},{8,10},{9,11},{10,... | collective-permute-start | bytes 1572872 | tf_op jit(solution)/shard_map/ppermute | solution.py:347
  6.9 24.7 %collective-permute-start.1 = (f32[8,128,128]{2,1,0:T(8,128)S(1)}, f32[8,128,128]{2,1,0:T(8,128)S(1)}, u32[]{:S(2)}, u32[]{:S(2)}) collective-permute-start(f32[8,128,128]{2,1,0:T(8,128)S(1)} %get-tuple-element.43), channel_id=1, source_target_pairs={{0,4},{1,5},{2,6},{3,7},{4,0},{5,1},{6,2},{7,3},{8,12},{9,13},{10,... | collective-permute-start | bytes 1572872 | tf_op jit(solution)/shard_map/ppermute | solution.py:347
  8.4 23.2 %collective-permute-start.2 = (f32[8,128,128]{2,1,0:T(8,128)S(1)}, f32[8,128,128]{2,1,0:T(8,128)S(1)}, u32[]{:S(2)}, u32[]{:S(2)}) collective-permute-start(f32[8,128,128]{2,1,0:T(8,128)S(1)} %get-tuple-element.44), channel_id=1, source_target_pairs={{0,6},{1,7},{2,4},{3,5},{4,2},{5,3},{6,0},{7,1},{8,14},{9,15},{10,... | collective-permute-start | bytes 1572872 | tf_op jit(solution)/shard_map/ppermute | solution.py:347
  8.4 11.5 %copy-start.2 = (bf16[128,1024]{1,0:T(8,128)(2,1)S(1)}, bf16[128,1024]{1,0:T(8,128)(2,1)}, u32[]{:S(2)}) copy-start(bf16[128,1024]{1,0:T(8,128)(2,1)} %feats.3) | copy-start | bytes 786436
  15.2 16.0 %collective-permute-start.4 = (bf16[128,1024]{1,0:T(8,128)(2,1)S(1)}, bf16[128,1024]{1,0:T(8,128)(2,1)S(1)}, u32[]{:S(2)}, u32[]{:S(2)}) collective-permute-start(bf16[128,1024]{1,0:T(8,128)(2,1)S(1)} %shard_map.122.refs_0_.refs_4_), channel_id=1, source_target_pairs={{0,8},{1,9},{2,10},{3,11},{4,12},{5,13},{6,14},{7,15},{8,0},{9,1},... | collective-permute-start | bytes 786440 | tf_op jit(solution)/shard_map/ppermute | solution.py:347
  17.3 14.3 %collective-permute-start.3 = (bf16[128,1024]{1,0:T(8,128)(2,1)S(1)}, bf16[128,1024]{1,0:T(8,128)(2,1)S(1)}, u32[]{:S(2)}, u32[]{:S(2)}) collective-permute-start(bf16[128,1024]{1,0:T(8,128)(2,1)S(1)} %shard_map.122.refs_0_.refs_4_), channel_id=1, source_target_pairs={{0,16},{1,17},{2,18},{3,19},{4,20},{5,21},{6,22},{7,23},{8,24},{9,... | collective-permute-start | bytes 786440 | tf_op jit(solution)/shard_map/ppermute | solution.py:347
  31.6 10.3 %collective-permute-start.7 = (bf16[128,1024]{1,0:T(8,128)(2,1)S(1)}, bf16[128,1024]{1,0:T(8,128)(2,1)S(1)}, u32[]{:S(2)}, u32[]{:S(2)}) collective-permute-start(bf16[128,1024]{1,0:T(8,128)(2,1)S(1)} %shard_map.123.refs_0_.refs_4_), channel_id=1, source_target_pairs={{0,6},{1,7},{2,4},{3,5},{4,2},{5,3},{6,0},{7,1},{8,14},{9,15},{10,... | collective-permute-start | bytes 786440 | tf_op jit(solution)/shard_map/ppermute | solution.py:347
  34.1 11.1 %collective-permute-start.6 = (bf16[128,1024]{1,0:T(8,128)(2,1)S(1)}, bf16[128,1024]{1,0:T(8,128)(2,1)S(1)}, u32[]{:S(2)}, u32[]{:S(2)}) collective-permute-start(bf16[128,1024]{1,0:T(8,128)(2,1)S(1)} %shard_map.123.refs_0_.refs_4_), channel_id=1, source_target_pairs={{0,4},{1,5},{2,6},{3,7},{4,0},{5,1},{6,2},{7,3},{8,12},{9,13},{10,... | collective-permute-start | bytes 786440 | tf_op jit(solution)/shard_map/ppermute | solution.py:347
  35.2 10.0 %collective-permute-start.8 = (bf16[128,1024]{1,0:T(8,128)(2,1)S(1)}, bf16[128,1024]{1,0:T(8,128)(2,1)S(1)}, u32[]{:S(2)}, u32[]{:S(2)}) collective-permute-start(bf16[128,1024]{1,0:T(8,128)(2,1)S(1)} %collective-permute-done.3.refs_6_.refs_2_), channel_id=1, source_target_pairs={{0,8},{1,9},{2,10},{3,11},{4,12},{5,13},{6,14},{7,15},{8,0},{9,1},... | collective-permute-start | bytes 786440 | tf_op jit(solution)/shard_map/ppermute | solution.py:347
  36.4 9.4 %collective-permute-start.5 = (bf16[128,1024]{1,0:T(8,128)(2,1)S(1)}, bf16[128,1024]{1,0:T(8,128)(2,1)S(1)}, u32[]{:S(2)}, u32[]{:S(2)}) collective-permute-start(bf16[128,1024]{1,0:T(8,128)(2,1)S(1)} %shard_map.123.refs_0_.refs_4_), channel_id=1, source_target_pairs={{0,2},{1,3},{2,0},{3,1},{4,6},{5,7},{6,4},{7,5},{8,10},{9,11},{10,... | collective-permute-start | bytes 786440 | tf_op jit(solution)/shard_map/ppermute | solution.py:347
  37.2 9.6 %collective-permute-start.11 = (bf16[128,1024]{1,0:T(8,128)(2,1)S(1)}, bf16[128,1024]{1,0:T(8,128)(2,1)S(1)}, u32[]{:S(2)}, u32[]{:S(2)}) collective-permute-start(bf16[128,1024]{1,0:T(8,128)(2,1)S(1)} %collective-permute-done.3.refs_6_.refs_2_), channel_id=1, source_target_pairs={{0,1},{1,0},{2,3},{3,2},{4,5},{5,4},{6,7},{7,6},{8,9},{9,8},{10,11... | collective-permute-start | bytes 786440 | tf_op jit(solution)/shard_map/ppermute | solution.py:347
  41.8 3.9 %collective-permute-start.9 = (bf16[128,1024]{1,0:T(8,128)(2,1)S(1)}, bf16[128,1024]{1,0:T(8,128)(2,1)S(1)}, u32[]{:S(2)}, u32[]{:S(2)}) collective-permute-start(bf16[128,1024]{1,0:T(8,128)(2,1)S(1)} %shard_map.122.refs_0_.refs_4_), channel_id=1, source_target_pairs={{0,1},{1,0},{2,3},{3,2},{4,5},{5,4},{6,7},{7,6},{8,9},{9,8},{10,11... | collective-permute-start | bytes 786440 | tf_op jit(solution)/shard_map/ppermute | solution.py:347
  45.2 1.5 %collective-permute-start.10 = (bf16[128,1024]{1,0:T(8,128)(2,1)S(1)}, bf16[128,1024]{1,0:T(8,128)(2,1)S(1)}, u32[]{:S(2)}, u32[]{:S(2)}) collective-permute-start(bf16[128,1024]{1,0:T(8,128)(2,1)S(1)} %collective-permute-done.4.refs_5_.refs_1_), channel_id=1, source_target_pairs={{0,1},{1,0},{2,3},{3,2},{4,5},{5,4},{6,7},{7,6},{8,9},{9,8},{10,11... | collective-permute-start | bytes 786440 | tf_op jit(solution)/shard_map/ppermute | solution.py:347
  45.3 1.9 %collective-permute-start.12 = (bf16[128,1024]{1,0:T(8,128)(2,1)S(1)}, bf16[128,1024]{1,0:T(8,128)(2,1)S(1)}, u32[]{:S(2)}, u32[]{:S(2)}) collective-permute-start(bf16[128,1024]{1,0:T(8,128)(2,1)S(1)} %collective-permute-done.8.refs_7_.refs_3_), channel_id=1, source_target_pairs={{0,1},{1,0},{2,3},{3,2},{4,5},{5,4},{6,7},{7,6},{8,9},{9,8},{10,11... | collective-permute-start | bytes 786440 | tf_op jit(solution)/shard_map/ppermute | solution.py:347
  50.2 4.6 %collective-permute-start.15 = (f32[4,4,128]{2,1,0:T(4,128)S(1)}, f32[4,4,128]{2,1,0:T(4,128)S(1)}, u32[]{:S(2)}, u32[]{:S(2)}) collective-permute-start(f32[4,4,128]{2,1,0:T(4,128)S(1)} %get-tuple-element.64.refs_0_), channel_id=1, source_target_pairs={{0,6},{1,7},{2,4},{3,5},{4,2},{5,3},{6,0},{7,1},{8,14},{9,15},{10,... | collective-permute-start | bytes 24584 | tf_op jit(solution)/shard_map/ppermute | solution.py:347
  52.0 3.7 %collective-permute-start.14 = (f32[4,4,128]{2,1,0:T(4,128)S(1)}, f32[4,4,128]{2,1,0:T(4,128)S(1)}, u32[]{:S(2)}, u32[]{:S(2)}) collective-permute-start(f32[4,4,128]{2,1,0:T(4,128)S(1)} %get-tuple-element.64.refs_0_), channel_id=1, source_target_pairs={{0,4},{1,5},{2,6},{3,7},{4,0},{5,1},{6,2},{7,3},{8,12},{9,13},{10,... | collective-permute-start | bytes 24584 | tf_op jit(solution)/shard_map/ppermute | solution.py:347
  53.2 3.7 %collective-permute-start.13 = (f32[4,4,128]{2,1,0:T(4,128)S(1)}, f32[4,4,128]{2,1,0:T(4,128)S(1)}, u32[]{:S(2)}, u32[]{:S(2)}) collective-permute-start(f32[4,4,128]{2,1,0:T(4,128)S(1)} %get-tuple-element.64.refs_0_), channel_id=1, source_target_pairs={{0,2},{1,3},{2,0},{3,1},{4,6},{5,7},{6,4},{7,5},{8,10},{9,11},{10,... | collective-permute-start | bytes 24584 | tf_op jit(solution)/shard_map/ppermute | solution.py:347
  58.4 2.7 %collective-permute-start.16 = (bf16[512,1024]{1,0:T(8,128)(2,1)S(1)}, bf16[512,1024]{1,0:T(8,128)(2,1)S(1)}, u32[]{:S(2)}, u32[]{:S(2)}) collective-permute-start(bf16[512,1024]{1,0:T(8,128)(2,1)S(1)} %get-tuple-element.68), channel_id=1, source_target_pairs={{0,1},{1,0},{2,3},{3,2},{4,5},{5,4},{6,7},{7,6},{8,9},{9,8},{10,11... | collective-permute-start | bytes 3145736 | tf_op jit(solution)/shard_map/ppermute | solution.py:347
  61.2 9.2 %collective-permute-start.20 = (bf16[128,1024]{1,0:T(8,128)(2,1)S(1)}, bf16[128,1024]{1,0:T(8,128)(2,1)S(1)}, u32[]{:S(2)}, u32[]{:S(2)}) collective-permute-start(bf16[128,1024]{1,0:T(8,128)(2,1)S(1)} %get-tuple-element.75), channel_id=1, source_target_pairs={{0,8},{1,9},{2,10},{3,11},{4,12},{5,13},{6,14},{7,15},{8,0},{9,1},... | collective-permute-start | bytes 786440 | tf_op jit(solution)/shard_map/ppermute | solution.py:347
  63.4 9.3 %collective-permute-start.17 = (bf16[128,1024]{1,0:T(8,128)(2,1)S(1)}, bf16[128,1024]{1,0:T(8,128)(2,1)S(1)}, u32[]{:S(2)}, u32[]{:S(2)}) collective-permute-start(bf16[128,1024]{1,0:T(8,128)(2,1)S(1)} %get-tuple-element.71), channel_id=1, source_target_pairs={{0,2},{1,3},{2,0},{3,1},{4,6},{5,7},{6,4},{7,5},{8,10},{9,11},{10,... | collective-permute-start | bytes 786440 | tf_op jit(solution)/shard_map/ppermute | solution.py:347
  64.4 8.9 %collective-permute-start.18 = (bf16[128,1024]{1,0:T(8,128)(2,1)S(1)}, bf16[128,1024]{1,0:T(8,128)(2,1)S(1)}, u32[]{:S(2)}, u32[]{:S(2)}) collective-permute-start(bf16[128,1024]{1,0:T(8,128)(2,1)S(1)} %get-tuple-element.72), channel_id=1, source_target_pairs={{0,4},{1,5},{2,6},{3,7},{4,0},{5,1},{6,2},{7,3},{8,12},{9,13},{10,... | collective-permute-start | bytes 786440 | tf_op jit(solution)/shard_map/ppermute | solution.py:347
  65.2 12.6 %collective-permute-start.19 = (bf16[128,1024]{1,0:T(8,128)(2,1)S(1)}, bf16[128,1024]{1,0:T(8,128)(2,1)S(1)}, u32[]{:S(2)}, u32[]{:S(2)}) collective-permute-start(bf16[128,1024]{1,0:T(8,128)(2,1)S(1)} %get-tuple-element.73), channel_id=1, source_target_pairs={{0,6},{1,7},{2,4},{3,5},{4,2},{5,3},{6,0},{7,1},{8,14},{9,15},{10,... | collective-permute-start | bytes 786440 | tf_op jit(solution)/shard_map/ppermute | solution.py:347
  66.9 11.9 %collective-permute-start.22 = (bf16[128,1024]{1,0:T(8,128)(2,1)S(1)}, bf16[128,1024]{1,0:T(8,128)(2,1)S(1)}, u32[]{:S(2)}, u32[]{:S(2)}) collective-permute-start(bf16[128,1024]{1,0:T(8,128)(2,1)S(1)} %get-tuple-element.76), channel_id=1, source_target_pairs={{0,8},{1,9},{2,10},{3,11},{4,12},{5,13},{6,14},{7,15},{8,0},{9,1},... | collective-permute-start | bytes 786440 | tf_op jit(solution)/shard_map/ppermute | solution.py:347
  70.5 13.3 %collective-permute-start.21 = (bf16[128,1024]{1,0:T(8,128)(2,1)S(1)}, bf16[128,1024]{1,0:T(8,128)(2,1)S(1)}, u32[]{:S(2)}, u32[]{:S(2)}) collective-permute-start(bf16[128,1024]{1,0:T(8,128)(2,1)S(1)} %add_convert_fusion), channel_id=1, source_target_pairs={{0,16},{1,17},{2,18},{3,19},{4,20},{5,21},{6,22},{7,23},{8,24},{9,... | collective-permute-start | bytes 786440 | tf_op jit(solution)/shard_map/ppermute | solution.py:347

commit v10 on v9

--- a/solution.py
+++ b/solution.py
@@ -223,8 +223,8 @@
 
 def far_body(cols, places, factor, entropy, *refs):
     stats, users, probs = refs[:cols], refs[cols : 2 * cols], refs[2 * cols : 3 * cols]
-    weights, grads, divergence, far = refs[3 * cols : 3 * cols + 4]
-    all_users = refs[3 * cols + 4]
+    weights, grads, divergence, ratios, far, all_users = refs[3 * cols :]
+    half = places * users[0].shape[0] // CORES
     rows = users[0].shape[0]
     lay(users, all_users)
     for i in range(cols):
@@ -237,11 +237,11 @@
             lse = top + jnp.log(norm)
             terms = [stats[j][3, j : j + 1, :] * (lse - tops[j]) - stats[j][2, j : j + 1, :] for j in range(cols)]
             divergence[...] = functools.reduce(jnp.add, terms, entropy[...])
-        prob = jnp.maximum(probs[i][...].reshape(places * rows, rows), 0.0)
+        ratios[i : i + 1, :] = ratio
+        prob = jnp.maximum(probs[i][places // CORES :].reshape(half, rows), 0.0)
         lanes = slice(i * rows, (i + 1) * rows)
-        grads[:, lanes] = (factor * (weights[:, lanes] * ratio - prob)).astype(jnp.bfloat16)
-    half = places * rows // CORES
-    far[...] = jnp.dot(grads[half:], all_users[...], preferred_element_type=jnp.float32).astype(far.dtype)
+        grads[:, lanes] = (factor * (weights[half:, lanes] * ratio - prob)).astype(jnp.bfloat16)
+    far[...] = jnp.dot(grads[...], all_users[...], preferred_element_type=jnp.float32).astype(far.dtype)
 
 
 def far_parts(factor, entropy, stats, users, probs, weights):
@@ -250,10 +250,11 @@
     return pl.pallas_call(
         functools.partial(far_body, cols, places, factor),
         in_specs=[VMEM] * (2 + 3 * cols),
-        out_specs=[VMEM] * 3,
+        out_specs=[VMEM] * 4,
         out_shape=[
-            struct(weights.shape, jnp.bfloat16),
+            struct((places * rows // CORES, cols * rows), jnp.bfloat16),
             struct((1, rows), jnp.float32),
+            struct((cols, rows), jnp.float32),
             struct((places * rows // CORES, width), jnp.bfloat16),
         ],
         scratch_shapes=[pltpu.VMEM((cols * rows, width), jnp.bfloat16)],
@@ -262,53 +263,66 @@
     )(entropy, *stats, *users, *probs, weights)
 
 
-def near_body(cols, grads, *refs):
-    users, (near, all_users) = refs[:cols], refs[cols:]
+def near_body(cols, places, factor, ratios, weights, *refs):
+    users, probs, (near, grads, all_users) = refs[:cols], refs[cols : 2 * cols], refs[2 * cols :]
+    rows = users[0].shape[0]
+    half = near.shape[0]
     lay(users, all_users)
-    near[...] = jnp.dot(grads[: near.shape[0]], all_users[...], preferred_element_type=jnp.float32)
-
-
-def near_part(grads, users):
-    cols, places = len(users), grads.shape[0]
+    for i in range(cols):
+        prob = jnp.maximum(probs[i][: places // CORES].reshape(half, rows), 0.0)
+        lanes = slice(i * rows, (i + 1) * rows)
+        grads[:, lanes] = (factor * (weights[:half, lanes] * ratios[i : i + 1, :] - prob)).astype(jnp.bfloat16)
+    near[...] = jnp.dot(grads[...], all_users[...], preferred_element_type=jnp.float32)
+
+
+def near_part(factor, ratios, weights, users, probs):
+    cols, places = len(users), probs[0].shape[0]
     rows, width = users[0].shape
-    return pl.pallas_call(
-        functools.partial(near_body, cols),
-        in_specs=[VMEM] * (1 + cols),
-        out_specs=VMEM,
-        out_shape=struct((places // CORES, width), jnp.float32),
+    half = places * rows // CORES
+    return pl.pallas_call(
+        functools.partial(near_body, cols, places, factor),
+        in_specs=[VMEM] * (2 + 2 * cols),
+        out_specs=[VMEM] * 2,
+        out_shape=[struct((half, width), jnp.float32), struct((half, cols * rows), jnp.bfloat16)],
         scratch_shapes=[pltpu.VMEM((cols * rows, width), jnp.bfloat16)],
         compiler_params=params(32),
-        cost_estimate=cost(grads.size * width, 4 * grads.size),
-    )(grads, *users)
-
-
-def user_body(cols, places, grads, *refs):
+        cost_estimate=cost(weights.size * width, 4 * weights.size),
+    )(ratios, weights, *users, *probs)
+
+
+def user_body(cols, places, near, far, *refs):
     items, refs = refs[:places], refs[-cols - 1 :]
     parts, all_items = refs[:cols], refs[cols]
     rows = items[0].shape[0]
     lay(items, all_items)
     for i in range(cols - 1, -1, -1):
-        part = lax.dot_general(
-            grads[:, i * rows : (i + 1) * rows],
-            all_items[...],
-            (((0,), (0,)), ((), ())),
-            preferred_element_type=jnp.float32,
+        part = functools.reduce(
+            jnp.add,
+            [
+                lax.dot_general(
+                    grads[:, i * rows : (i + 1) * rows],
+                    all_items[h * grads.shape[0] : (h + 1) * grads.shape[0]],
+                    (((0,), (0,)), ((), ())),
+                    preferred_element_type=jnp.float32,
+                )
+                for h, grads in enumerate((near, far))
+            ],
         )
         parts[i][...] = part.astype(parts[i].dtype)
 
 
-def user_parts(cols, grads, items, after):
+def user_parts(cols, near, far, items, after):
     places = len(items)
     rows, width = items[0].shape
     return pl.pallas_call(
         functools.partial(user_body, cols, places),
-        in_specs=[VMEM] * (1 + places) + [ANY] * len(after),
+        in_specs=[VMEM] * (2 + places) + [ANY] * len(after),
         out_specs=[VMEM] * cols,
         out_shape=[struct((rows, width), jnp.bfloat16 if i else jnp.float32) for i in range(cols)],
         scratch_shapes=[pltpu.VMEM((places * rows, width), jnp.bfloat16)],
         compiler_params=params(32),
-        cost_estimate=cost(2 * grads.size * width, 4 * grads.size),
-    )(grads, *items, *after)
+        cost_estimate=cost(4 * near.size * width, 8 * near.size),
+    )(near, far, *items, *after)
 
 
 def join_body(planes, near, far, *outs):
@@ -367,16 +381,17 @@
     items = items + [swap(block, 1) for block in items]
 
     weights, stats = scores(scale, users, items, probs)
-    grads, divergence, far = far_parts(factor, entropy, [stats] + over_columns(stats), users, probs, weights)
+    grads_far, divergence, ratios, far = far_parts(factor, entropy, [stats] + over_columns(stats), users, probs, weights)
     far = swap(far, 1)
-    parts = join(planes, near_part(grads, users), far)
+    near, grads_near = near_part(factor, ratios, weights, users, probs)
+    parts = join(planes, near, far)
     hop = cols * CORES
     if planes == 4:
         merged = (parts[2] + swap(parts[3], hop).astype(jnp.float32)).astype(jnp.bfloat16)
         sent = [swap(merged, 2 * hop), swap(parts[1], hop)]
     else:
         sent = [swap(parts[z].astype(jnp.bfloat16), z * hop) for z in range(planes - 1, 0, -1)]
-    own, *others = user_parts(cols, grads, items, [parts[0]])
+    own, *others = user_parts(cols, grads_near, grads_far, items, [parts[0]])
     arrived = [swap(part, (c + 1) * CORES) for c, part in enumerate(others)]
 
     def add(start, parts):

time: 84.9 us -> 84.6 us (level)
  transfers between devices with their start and end apart: 23 -> 23, of which waited for: 15 -> 14; matrix products, arithmetic and copies ran while one was open for 1% -> 1% of each run, Pallas kernels for 24% -> 25%
where the time goes in v10:
time: 84.6 us; the launch traced here: 84.4 us
  waiting for transfers between devices  28.3 us (33%)
  Pallas kernels  27.7 us (33%)
  starting transfers between devices  25.2 us (30%)
  other arithmetic  1.87 us (2%)
  between operations  1.39 us (2%)
    ppermute x23, waiting for transfers between devices, swap(): return lax.ppermute(array, 'dp', [(i, i ^ apart) for i in range(count)])  28.3 us
    ppermute x23, starting transfers between devices, swap(): return lax.ppermute(array, 'dp', [(i, i ^ apart) for i in range(count)])  25.2 us
    pallas_call x2, Pallas kernels, tower(): pl.pallas_call(functools.partial(tower_body, chunks, ready), in_specs=[VM...  18.1 us
    pallas_call x1, Pallas kernels, scores(): pl.pallas_call(functools.partial(score_body, cols, places, scale), in_spe...  2.98 us
    pallas_call x1, Pallas kernels, spread_teacher(): pl.pallas_call(functools.partial(teacher_body, cols, planes), in_specs=[S...  2.54 us
    add x2, other arithmetic, add(): functools.reduce(jnp.add, [part.astype(jnp.float32) for part in parts], s...  1.81 us
  transfers between devices with their start and end apart: 23, of which 14 were waited for; matrix products, arithmetic and copies ran while one was open for 1% of the time, Pallas kernels for 25%

profile of v10, /device:TPU:0, one launch (start us, length us, event | category | flops | bytes accessed | tf_op | source)
XLA Modules:
  0.0 84.4 jit_solution(10950570941762975538)
XLA Ops:
  1.3 0.0 copy-start
  1.3 0.0 copy-start.1
  1.3 2.5 %shard_map.121 = (f32[8,128,128]{2,1,0:T(8,128)S(1)}, f32[8,128,128]{2,1,0:T(8,128)S(1)}, f32[8,128,128]{2,1,0:T(8,128)S(1)}, f32[8,128,128]{2,1,0:T(8,128)S(1)}, f32[1,128]{1,0:T(1,128)S(1)}) custom-call(s32[1]{0:T(128)} %bitcast.me, s32[1,16]{1,0:T(1,128)} %cands_hbm.1, s32[1]{0:T(128)S(6)} %copy.13.count, s32[32]{0:T(128)} %owner_hbm.1, ...), custom_call_target="tpu_custom_call" | custom-call | flops 10000000000 | bytes 2097152 | tf_op jit(solution)/shard_map/pallas_call | solution.py:139
  3.8 3.0 %collective-permute-start = (f32[8,128,128]{2,1,0:T(8,128)S(1)}, f32[8,128,128]{2,1,0:T(8,128)S(1)}, u32[]{:S(2)}, u32[]{:S(2)}) collective-permute-start(f32[8,128,128]{2,1,0:T(8,128)S(1)} %get-tuple-element.45), channel_id=1, source_target_pairs={{0,2},{1,3},{2,0},{3,1},{4,6},{5,7},{6,4},{7,5},{8,10},{9,11},{10,... | collective-permute-start | bytes 1572872 | tf_op jit(solution)/shard_map/ppermute | solution.py:361
  6.9 1.5 %collective-permute-start.1 = (f32[8,128,128]{2,1,0:T(8,128)S(1)}, f32[8,128,128]{2,1,0:T(8,128)S(1)}, u32[]{:S(2)}, u32[]{:S(2)}) collective-permute-start(f32[8,128,128]{2,1,0:T(8,128)S(1)} %get-tuple-element.46), channel_id=1, source_target_pairs={{0,4},{1,5},{2,6},{3,7},{4,0},{5,1},{6,2},{7,3},{8,12},{9,13},{10,... | collective-permute-start | bytes 1572872 | tf_op jit(solution)/shard_map/ppermute | solution.py:361
  8.4 0.0 collective-permute-start.2
  8.4 0.0 copy-done
  8.4 0.0 copy-done.1
  8.4 0.0 copy-start.2
  8.4 6.8 %shard_map.122.refs_0_.refs_4_ = bf16[128,1024]{1,0:T(8,128)(2,1)S(1)} custom-call(bf16[128,1024]{1,0:T(8,128)(2,1)S(1)} %copy-done.1, bf16[1024,8192]{1,0:T(8,128)(2,1)S(1)} %copy-done, bf16[8192,1024]{1,0:T(8,128)(2,1)} %w_out.2, f32[8,128,128]{2,1,0:T(8,128)S(1)} %get-tuple-element.52.refs_0_), custom_call_target="tpu_custom_call" | custom-call | flops 1 | bytes 1 | tf_op jit(solution)/shard_map/pallas_call | solution.py:74
  15.2 2.1 %collective-permute-start.4 = (bf16[128,1024]{1,0:T(8,128)(2,1)S(1)}, bf16[128,1024]{1,0:T(8,128)(2,1)S(1)}, u32[]{:S(2)}, u32[]{:S(2)}) collective-permute-start(bf16[128,1024]{1,0:T(8,128)(2,1)S(1)} %shard_map.122.refs_0_.refs_4_), channel_id=1, source_target_pairs={{0,8},{1,9},{2,10},{3,11},{4,12},{5,13},{6,14},{7,15},{8,0},{9,1},... | collective-permute-start | bytes 786440 | tf_op jit(solution)/shard_map/ppermute | solution.py:361
  17.3 2.6 %collective-permute-start.3 = (bf16[128,1024]{1,0:T(8,128)(2,1)S(1)}, bf16[128,1024]{1,0:T(8,128)(2,1)S(1)}, u32[]{:S(2)}, u32[]{:S(2)}) collective-permute-start(bf16[128,1024]{1,0:T(8,128)(2,1)S(1)} %shard_map.122.refs_0_.refs_4_), channel_id=1, source_target_pairs={{0,16},{1,17},{2,18},{3,19},{4,20},{5,21},{6,22},{7,23},{8,24},{9,... | collective-permute-start | bytes 786440 | tf_op jit(solution)/shard_map/ppermute | solution.py:361
  19.9 0.0 copy-done.2
  19.9 11.3 %shard_map.123.refs_0_.refs_4_ = bf16[128,1024]{1,0:T(8,128)(2,1)S(1)} custom-call(bf16[128,1024]{1,0:T(8,128)(2,1)S(1)} %copy-done.2, bf16[1024,8192]{1,0:T(8,128)(2,1)} %w_in.3, bf16[8192,1024]{1,0:T(8,128)(2,1)} %w_out.3, bf16[128,1024]{1,0:T(8,128)(2,1)S(1)} %shard_map.122.refs_0_.refs_4_), custom_call_target="tpu_custom_call" | custom-call | flops 1 | bytes 1 | tf_op jit(solution)/shard_map/pallas_call | solution.py:74
  31.2 0.0 collective-permute-done.4.refs_5_.refs_1_
  31.2 0.4 collective-permute-done.3.refs_6_.refs_2_
  31.6 0.0 collective-permute-done.refs_1_
  31.6 0.0 collective-permute-done.1.refs_2_
  31.6 0.0 collective-permute-done.2.refs_3_
  31.6 2.5 %collective-permute-start.7 = (bf16[128,1024]{1,0:T(8,128)(2,1)S(1)}, bf16[128,1024]{1,0:T(8,128)(2,1)S(1)}, u32[]{:S(2)}, u32[]{:S(2)}) collective-permute-start(bf16[128,1024]{1,0:T(8,128)(2,1)S(1)} %shard_map.123.refs_0_.refs_4_), channel_id=1, source_target_pairs={{0,6},{1,7},{2,4},{3,5},{4,2},{5,3},{6,0},{7,1},{8,14},{9,15},{10,... | collective-permute-start | bytes 786440 | tf_op jit(solution)/shard_map/ppermute | solution.py:361
  34.1 0.5 collective-permute-start.6
  34.6 0.6 shard_map.124
  35.2 1.1 %collective-permute-start.8 = (bf16[128,1024]{1,0:T(8,128)(2,1)S(1)}, bf16[128,1024]{1,0:T(8,128)(2,1)S(1)}, u32[]{:S(2)}, u32[]{:S(2)}) collective-permute-start(bf16[128,1024]{1,0:T(8,128)(2,1)S(1)} %collective-permute-done.3.refs_6_.refs_2_), channel_id=1, source_target_pairs={{0,8},{1,9},{2,10},{3,11},{4,12},{5,13},{6,14},{7,15},{8,0},{9,1},... | collective-permute-start | bytes 786440 | tf_op jit(solution)/shard_map/ppermute | solution.py:361
  36.4 0.9 %collective-permute-start.5 = (bf16[128,1024]{1,0:T(8,128)(2,1)S(1)}, bf16[128,1024]{1,0:T(8,128)(2,1)S(1)}, u32[]{:S(2)}, u32[]{:S(2)}) collective-permute-start(bf16[128,1024]{1,0:T(8,128)(2,1)S(1)} %shard_map.123.refs_0_.refs_4_), channel_id=1, source_target_pairs={{0,2},{1,3},{2,0},{3,1},{4,6},{5,7},{6,4},{7,5},{8,10},{9,11},{10,... | collective-permute-start | bytes 786440 | tf_op jit(solution)/shard_map/ppermute | solution.py:361
  37.2 0.0 collective-permute-start.11
  37.2 4.6 %collective-permute-done.7.refs_3_.refs_7_ = bf16[128,1024]{1,0:T(8,128)(2,1)S(1)} collective-permute-done((bf16[128,1024]{1,0:T(8,128)(2,1)S(1)}, bf16[128,1024]{1,0:T(8,128)(2,1)S(1)}, u32[]{:S(2)}, u32[]{:S(2)}) %collective-permute-start.7) | collective-permute-done | bytes 262176 | tf_op jit(solution)/shard_map/ppermute | solution.py:361
  41.8 0.0 collective-permute-start.9
  41.9 3.4 %collective-permute-done.6.refs_2_.refs_6_ = bf16[128,1024]{1,0:T(8,128)(2,1)S(1)} collective-permute-done((bf16[128,1024]{1,0:T(8,128)(2,1)S(1)}, bf16[128,1024]{1,0:T(8,128)(2,1)S(1)}, u32[]{:S(2)}, u32[]{:S(2)}) %collective-permute-start.6) | collective-permute-done | bytes 262176 | tf_op jit(solution)/shard_map/ppermute | solution.py:361
  45.2 0.0 collective-permute-start.10
  45.3 0.0 collective-permute-done.8.refs_7_.refs_3_
  45.3 0.5 collective-permute-start.12
  45.8 0.0 collective-permute-done.5.refs_1_.refs_5_
  45.8 0.0 collective-permute-done.9.refs_8_.refs_4_
  45.8 1.0 %collective-permute-done.10.refs_9_.refs_5_ = bf16[128,1024]{1,0:T(8,128)(2,1)S(1)} collective-permute-done((bf16[128,1024]{1,0:T(8,128)(2,1)S(1)}, bf16[128,1024]{1,0:T(8,128)(2,1)S(1)}, u32[]{:S(2)}, u32[]{:S(2)}) %collective-permute-start.10) | collective-permute-done | bytes 262176 | tf_op jit(solution)/shard_map/ppermute | solution.py:361
  46.8 0.0 collective-permute-done.11.refs_10_.refs_6_
  46.8 0.4 collective-permute-done.12.refs_11_.refs_7_
  47.2 3.0 %shard_map.125 = (f32[1024,512]{1,0:T(8,128)S(1)}, f32[4,4,128]{2,1,0:T(4,128)S(1)}) custom-call(bf16[128,1024]{1,0:T(8,128)(2,1)S(1)} %shard_map.123.refs_0_.refs_4_, bf16[128,1024]{1,0:T(8,128)(2,1)S(1)} %collective-permute-done.5.refs_1_.refs_5_, bf16[128,1024]{1,0:T(8,128)(2,1)S(1)} %collective-permute-done.6.refs_2_.refs_6_, ...), custom_call_target="tpu_custom_call" | custom-call | flops 1073741824 | bytes 4194304 | tf_op jit(solution)/shard_map/pallas_call | solution.py:210
  50.1 1.8 %collective-permute-start.15 = (f32[4,4,128]{2,1,0:T(4,128)S(1)}, f32[4,4,128]{2,1,0:T(4,128)S(1)}, u32[]{:S(2)}, u32[]{:S(2)}) collective-permute-start(f32[4,4,128]{2,1,0:T(4,128)S(1)} %get-tuple-element.67.refs_0_), channel_id=1, source_target_pairs={{0,6},{1,7},{2,4},{3,5},{4,2},{5,3},{6,0},{7,1},{8,14},{9,15},{10,... | collective-permute-start | bytes 24584 | tf_op jit(solution)/shard_map/ppermute | solution.py:361
  51.9 1.2 %collective-permute-start.14 = (f32[4,4,128]{2,1,0:T(4,128)S(1)}, f32[4,4,128]{2,1,0:T(4,128)S(1)}, u32[]{:S(2)}, u32[]{:S(2)}) collective-permute-start(f32[4,4,128]{2,1,0:T(4,128)S(1)} %get-tuple-element.67.refs_0_), channel_id=1, source_target_pairs={{0,4},{1,5},{2,6},{3,7},{4,0},{5,1},{6,2},{7,3},{8,12},{9,13},{10,... | collective-permute-start | bytes 24584 | tf_op jit(solution)/shard_map/ppermute | solution.py:361
  53.2 0.5 collective-permute-start.13
  53.7 1.1 %collective-permute-done.15.refs_3_ = f32[4,4,128]{2,1,0:T(4,128)S(1)} collective-permute-done((f32[4,4,128]{2,1,0:T(4,128)S(1)}, f32[4,4,128]{2,1,0:T(4,128)S(1)}, u32[]{:S(2)}, u32[]{:S(2)}) %collective-permute-start.15) | collective-permute-done | bytes 8224 | tf_op jit(solution)/shard_map/ppermute | solution.py:361
  54.8 0.8 %collective-permute-done.14.refs_2_ = f32[4,4,128]{2,1,0:T(4,128)S(1)} collective-permute-done((f32[4,4,128]{2,1,0:T(4,128)S(1)}, f32[4,4,128]{2,1,0:T(4,128)S(1)}, u32[]{:S(2)}, u32[]{:S(2)}) %collective-permute-start.14) | collective-permute-done | bytes 8224 | tf_op jit(solution)/shard_map/ppermute | solution.py:361
  55.6 1.2 %collective-permute-done.13.refs_1_ = f32[4,4,128]{2,1,0:T(4,128)S(1)} collective-permute-done((f32[4,4,128]{2,1,0:T(4,128)S(1)}, f32[4,4,128]{2,1,0:T(4,128)S(1)}, u32[]{:S(2)}, u32[]{:S(2)}) %collective-permute-start.13) | collective-permute-done | bytes 8224 | tf_op jit(solution)/shard_map/ppermute | solution.py:361
  56.8 1.2 %shard_map.126 = (bf16[512,512]{1,0:T(8,128)(2,1)S(1)}, f32[1,128]{1,0:T(1,128)}, f32[4,128]{1,0:T(4,128)S(1)}, bf16[512,1024]{1,0:T(8,128)(2,1)S(1)}) custom-call(f32[1,128]{1,0:T(1,128)S(1)} %get-tuple-element.43.entropy, f32[4,4,128]{2,1,0:T(4,128)S(1)} %get-tuple-element.67.refs_0_, f32[4,4,128]{2,1,0:T(4,128)S(1)} %collective-permute-done.13.refs_1_, ...), custom_call_target="tpu_custom_call" | custom-call | flops 536870912 | bytes 4194304 | tf_op jit(solution)/shard_map/pallas_call | solution.py:250
  58.0 0.0 collective-permute-start.16
  58.0 0.8 shard_map.127
  58.8 1.9 %collective-permute-done.16.far = bf16[512,1024]{1,0:T(8,128)(2,1)S(1)} collective-permute-done((bf16[512,1024]{1,0:T(8,128)(2,1)S(1)}, bf16[512,1024]{1,0:T(8,128)(2,1)S(1)}, u32[]{:S(2)}, u32[]{:S(2)}) %collective-permute-start.16) | collective-permute-done | bytes 1048608 | tf_op jit(solution)/shard_map/ppermute | solution.py:361
  60.7 0.2 shard_map.128
  60.9 0.8 collective-permute-start.20
  61.8 1.3 %shard_map.129 = (f32[128,1024]{1,0:T(8,128)S(1)}, bf16[128,1024]{1,0:T(8,128)(2,1)S(1)}, bf16[128,1024]{1,0:T(8,128)(2,1)S(1)}, bf16[128,1024]{1,0:T(8,128)(2,1)S(1)}) custom-call(bf16[512,512]{1,0:T(8,128)(2,1)S(1)} %get-tuple-element.71.near, bf16[512,512]{1,0:T(8,128)(2,1)S(1)} %get-tuple-element.72.far, ...), custom_call_target="tpu_custom_call" | custom-call | flops 1073741824 | bytes 2097152 | tf_op jit(solution)/shard_map/pallas_call | solution.py:317
  63.1 1.2 %collective-permute-start.17 = (bf16[128,1024]{1,0:T(8,128)(2,1)S(1)}, bf16[128,1024]{1,0:T(8,128)(2,1)S(1)}, u32[]{:S(2)}, u32[]{:S(2)}) collective-permute-start(bf16[128,1024]{1,0:T(8,128)(2,1)S(1)} %get-tuple-element.77), channel_id=1, source_target_pairs={{0,2},{1,3},{2,0},{3,1},{4,6},{5,7},{6,4},{7,5},{8,10},{9,11},{10,... | collective-permute-start | bytes 786440 | tf_op jit(solution)/shard_map/ppermute | solution.py:361
  64.3 0.6 collective-permute-start.18
  64.9 1.7 %collective-permute-start.19 = (bf16[128,1024]{1,0:T(8,128)(2,1)S(1)}, bf16[128,1024]{1,0:T(8,128)(2,1)S(1)}, u32[]{:S(2)}, u32[]{:S(2)}) collective-permute-start(bf16[128,1024]{1,0:T(8,128)(2,1)S(1)} %get-tuple-element.79), channel_id=1, source_target_pairs={{0,6},{1,7},{2,4},{3,5},{4,2},{5,3},{6,0},{7,1},{8,14},{9,15},{10,... | collective-permute-start | bytes 786440 | tf_op jit(solution)/shard_map/ppermute | solution.py:361
  66.6 1.3 %collective-permute-start.22 = (bf16[128,1024]{1,0:T(8,128)(2,1)S(1)}, bf16[128,1024]{1,0:T(8,128)(2,1)S(1)}, u32[]{:S(2)}, u32[]{:S(2)}) collective-permute-start(bf16[128,1024]{1,0:T(8,128)(2,1)S(1)} %get-tuple-element.82), channel_id=1, source_target_pairs={{0,8},{1,9},{2,10},{3,11},{4,12},{5,13},{6,14},{7,15},{8,0},{9,1},... | collective-permute-start | bytes 786440 | tf_op jit(solution)/shard_map/ppermute | solution.py:361
  67.9 2.2 %collective-permute-done.20 = bf16[128,1024]{1,0:T(8,128)(2,1)S(1)} collective-permute-done((bf16[128,1024]{1,0:T(8,128)(2,1)S(1)}, bf16[128,1024]{1,0:T(8,128)(2,1)S(1)}, u32[]{:S(2)}, u32[]{:S(2)}) %collective-permute-start.20) | collective-permute-done | bytes 262176 | tf_op jit(solution)/shard_map/ppermute | solution.py:361
  70.1 0.1 add_convert_fusion
  70.2 1.2 %collective-permute-start.21 = (bf16[128,1024]{1,0:T(8,128)(2,1)S(1)}, bf16[128,1024]{1,0:T(8,128)(2,1)S(1)}, u32[]{:S(2)}, u32[]{:S(2)}) collective-permute-start(bf16[128,1024]{1,0:T(8,128)(2,1)S(1)} %add_convert_fusion), channel_id=1, source_target_pairs={{0,16},{1,17},{2,18},{3,19},{4,20},{5,21},{6,22},{7,23},{8,24},{9,... | collective-permute-start | bytes 786440 | tf_op jit(solution)/shard_map/ppermute | solution.py:361
  71.4 1.0 %collective-permute-done.17 = bf16[128,1024]{1,0:T(8,128)(2,1)S(1)} collective-permute-done((bf16[128,1024]{1,0:T(8,128)(2,1)S(1)}, bf16[128,1024]{1,0:T(8,128)(2,1)S(1)}, u32[]{:S(2)}, u32[]{:S(2)}) %collective-permute-start.17) | collective-permute-done | bytes 262176 | tf_op jit(solution)/shard_map/ppermute | solution.py:361
  72.3 5.3 %collective-permute-done.18 = bf16[128,1024]{1,0:T(8,128)(2,1)S(1)} collective-permute-done((bf16[128,1024]{1,0:T(8,128)(2,1)S(1)}, bf16[128,1024]{1,0:T(8,128)(2,1)S(1)}, u32[]{:S(2)}, u32[]{:S(2)}) %collective-permute-start.18) | collective-permute-done | bytes 262176 | tf_op jit(solution)/shard_map/ppermute | solution.py:361
  77.7 0.0 collective-permute-done.19
  77.7 0.9 %convert_add_fusion.1 = f32[128,1024]{1,0:T(8,128)} fusion(bf16[128,1024]{1,0:T(8,128)(2,1)S(1)} %collective-permute-done.19, bf16[128,1024]{1,0:T(8,128)(2,1)S(1)} %collective-permute-done.18, f32[128,1024]{1,0:T(8,128)S(1)} %get-tuple-element.76, bf16[128,1024]{1,0:T(8,128)(2,1)S(1)} %collective-permute-done.17), kind=kLoop, calls=%fused_computation.2 | loop fusion | flops 786432 | bytes 1835008 | tf_op jit(solution)/shard_map/add | solution.py:398
  78.6 0.1 collective-permute-done.22
  78.7 4.9 %collective-permute-done.21 = bf16[128,1024]{1,0:T(8,128)(2,1)S(1)} collective-permute-done((bf16[128,1024]{1,0:T(8,128)(2,1)S(1)}, bf16[128,1024]{1,0:T(8,128)(2,1)S(1)}, u32[]{:S(2)}, u32[]{:S(2)}) %collective-permute-start.21) | collective-permute-done | bytes 262176 | tf_op jit(solution)/shard_map/ppermute | solution.py:361
  83.6 0.9 %convert_add_fusion = f32[128,1024]{1,0:T(8,128)} fusion(bf16[128,1024]{1,0:T(8,128)(2,1)S(1)} %collective-permute-done.22, f32[128,1024]{1,0:T(8,128)S(1)} %get-tuple-element.75.refs_8_, bf16[128,1024]{1,0:T(8,128)(2,1)S(1)} %collective-permute-done.21), kind=kLoop, calls=%fused_computation | loop fusion | flops 524288 | bytes 1572864 | tf_op jit(solution)/shard_map/add | solution.py:398
Async XLA Ops:
  1.3 7.1 %copy-start = (bf16[1024,8192]{1,0:T(8,128)(2,1)S(1)}, bf16[1024,8192]{1,0:T(8,128)(2,1)}, u32[]{:S(2)}) copy-start(bf16[1024,8192]{1,0:T(8,128)(2,1)} %w_in.2) | copy-start | bytes 50331652
  1.3 7.1 %copy-start.1 = (bf16[128,1024]{1,0:T(8,128)(2,1)S(1)}, bf16[128,1024]{1,0:T(8,128)(2,1)}, u32[]{:S(2)}) copy-start(bf16[128,1024]{1,0:T(8,128)(2,1)} %feats.2) | copy-start | bytes 786436
  3.8 27.7 %collective-permute-start = (f32[8,128,128]{2,1,0:T(8,128)S(1)}, f32[8,128,128]{2,1,0:T(8,128)S(1)}, u32[]{:S(2)}, u32[]{:S(2)}) collective-permute-start(f32[8,128,128]{2,1,0:T(8,128)S(1)} %get-tuple-element.45), channel_id=1, source_target_pairs={{0,2},{1,3},{2,0},{3,1},{4,6},{5,7},{6,4},{7,5},{8,10},{9,11},{10,... | collective-permute-start | bytes 1572872 | tf_op jit(solution)/shard_map/ppermute | solution.py:361
  6.9 24.7 %collective-permute-start.1 = (f32[8,128,128]{2,1,0:T(8,128)S(1)}, f32[8,128,128]{2,1,0:T(8,128)S(1)}, u32[]{:S(2)}, u32[]{:S(2)}) collective-permute-start(f32[8,128,128]{2,1,0:T(8,128)S(1)} %get-tuple-element.46), channel_id=1, source_target_pairs={{0,4},{1,5},{2,6},{3,7},{4,0},{5,1},{6,2},{7,3},{8,12},{9,13},{10,... | collective-permute-start | bytes 1572872 | tf_op jit(solution)/shard_map/ppermute | solution.py:361
  8.4 23.2 %collective-permute-start.2 = (f32[8,128,128]{2,1,0:T(8,128)S(1)}, f32[8,128,128]{2,1,0:T(8,128)S(1)}, u32[]{:S(2)}, u32[]{:S(2)}) collective-permute-start(f32[8,128,128]{2,1,0:T(8,128)S(1)} %get-tuple-element.47), channel_id=1, source_target_pairs={{0,6},{1,7},{2,4},{3,5},{4,2},{5,3},{6,0},{7,1},{8,14},{9,15},{10,... | collective-permute-start | bytes 1572872 | tf_op jit(solution)/shard_map/ppermute | solution.py:361
  8.4 11.5 %copy-start.2 = (bf16[128,1024]{1,0:T(8,128)(2,1)S(1)}, bf16[128,1024]{1,0:T(8,128)(2,1)}, u32[]{:S(2)}) copy-start(bf16[128,1024]{1,0:T(8,128)(2,1)} %feats.3) | copy-start | bytes 786436
  15.2 16.0 %collective-permute-start.4 = (bf16[128,1024]{1,0:T(8,128)(2,1)S(1)}, bf16[128,1024]{1,0:T(8,128)(2,1)S(1)}, u32[]{:S(2)}, u32[]{:S(2)}) collective-permute-start(bf16[128,1024]{1,0:T(8,128)(2,1)S(1)} %shard_map.122.refs_0_.refs_4_), channel_id=1, source_target_pairs={{0,8},{1,9},{2,10},{3,11},{4,12},{5,13},{6,14},{7,15},{8,0},{9,1},... | collective-permute-start | bytes 786440 | tf_op jit(solution)/shard_map/ppermute | solution.py:361
  17.3 14.3 %collective-permute-start.3 = (bf16[128,1024]{1,0:T(8,128)(2,1)S(1)}, bf16[128,1024]{1,0:T(8,128)(2,1)S(1)}, u32[]{:S(2)}, u32[]{:S(2)}) collective-permute-start(bf16[128,1024]{1,0:T(8,128)(2,1)S(1)} %shard_map.122.refs_0_.refs_4_), channel_id=1, source_target_pairs={{0,16},{1,17},{2,18},{3,19},{4,20},{5,21},{6,22},{7,23},{8,24},{9,... | collective-permute-start | bytes 786440 | tf_op jit(solution)/shard_map/ppermute | solution.py:361
  31.6 10.3 %collective-permute-start.7 = (bf16[128,1024]{1,0:T(8,128)(2,1)S(1)}, bf16[128,1024]{1,0:T(8,128)(2,1)S(1)}, u32[]{:S(2)}, u32[]{:S(2)}) collective-permute-start(bf16[128,1024]{1,0:T(8,128)(2,1)S(1)} %shard_map.123.refs_0_.refs_4_), channel_id=1, source_target_pairs={{0,6},{1,7},{2,4},{3,5},{4,2},{5,3},{6,0},{7,1},{8,14},{9,15},{10,... | collective-permute-start | bytes 786440 | tf_op jit(solution)/shard_map/ppermute | solution.py:361
  34.1 11.1 %collective-permute-start.6 = (bf16[128,1024]{1,0:T(8,128)(2,1)S(1)}, bf16[128,1024]{1,0:T(8,128)(2,1)S(1)}, u32[]{:S(2)}, u32[]{:S(2)}) collective-permute-start(bf16[128,1024]{1,0:T(8,128)(2,1)S(1)} %shard_map.123.refs_0_.refs_4_), channel_id=1, source_target_pairs={{0,4},{1,5},{2,6},{3,7},{4,0},{5,1},{6,2},{7,3},{8,12},{9,13},{10,... | collective-permute-start | bytes 786440 | tf_op jit(solution)/shard_map/ppermute | solution.py:361
  35.2 10.0 %collective-permute-start.8 = (bf16[128,1024]{1,0:T(8,128)(2,1)S(1)}, bf16[128,1024]{1,0:T(8,128)(2,1)S(1)}, u32[]{:S(2)}, u32[]{:S(2)}) collective-permute-start(bf16[128,1024]{1,0:T(8,128)(2,1)S(1)} %collective-permute-done.3.refs_6_.refs_2_), channel_id=1, source_target_pairs={{0,8},{1,9},{2,10},{3,11},{4,12},{5,13},{6,14},{7,15},{8,0},{9,1},... | collective-permute-start | bytes 786440 | tf_op jit(solution)/shard_map/ppermute | solution.py:361
  36.4 9.4 %collective-permute-start.5 = (bf16[128,1024]{1,0:T(8,128)(2,1)S(1)}, bf16[128,1024]{1,0:T(8,128)(2,1)S(1)}, u32[]{:S(2)}, u32[]{:S(2)}) collective-permute-start(bf16[128,1024]{1,0:T(8,128)(2,1)S(1)} %shard_map.123.refs_0_.refs_4_), channel_id=1, source_target_pairs={{0,2},{1,3},{2,0},{3,1},{4,6},{5,7},{6,4},{7,5},{8,10},{9,11},{10,... | collective-permute-start | bytes 786440 | tf_op jit(solution)/shard_map/ppermute | solution.py:361
  37.2 9.6 %collective-permute-start.11 = (bf16[128,1024]{1,0:T(8,128)(2,1)S(1)}, bf16[128,1024]{1,0:T(8,128)(2,1)S(1)}, u32[]{:S(2)}, u32[]{:S(2)}) collective-permute-start(bf16[128,1024]{1,0:T(8,128)(2,1)S(1)} %collective-permute-done.3.refs_6_.refs_2_), channel_id=1, source_target_pairs={{0,1},{1,0},{2,3},{3,2},{4,5},{5,4},{6,7},{7,6},{8,9},{9,8},{10,11... | collective-permute-start | bytes 786440 | tf_op jit(solution)/shard_map/ppermute | solution.py:361
  41.8 3.9 %collective-permute-start.9 = (bf16[128,1024]{1,0:T(8,128)(2,1)S(1)}, bf16[128,1024]{1,0:T(8,128)(2,1)S(1)}, u32[]{:S(2)}, u32[]{:S(2)}) collective-permute-start(bf16[128,1024]{1,0:T(8,128)(2,1)S(1)} %shard_map.122.refs_0_.refs_4_), channel_id=1, source_target_pairs={{0,1},{1,0},{2,3},{3,2},{4,5},{5,4},{6,7},{7,6},{8,9},{9,8},{10,11... | collective-permute-start | bytes 786440 | tf_op jit(solution)/shard_map/ppermute | solution.py:361
  45.2 1.5 %collective-permute-start.10 = (bf16[128,1024]{1,0:T(8,128)(2,1)S(1)}, bf16[128,1024]{1,0:T(8,128)(2,1)S(1)}, u32[]{:S(2)}, u32[]{:S(2)}) collective-permute-start(bf16[128,1024]{1,0:T(8,128)(2,1)S(1)} %collective-permute-done.4.refs_5_.refs_1_), channel_id=1, source_target_pairs={{0,1},{1,0},{2,3},{3,2},{4,5},{5,4},{6,7},{7,6},{8,9},{9,8},{10,11... | collective-permute-start | bytes 786440 | tf_op jit(solution)/shard_map/ppermute | solution.py:361
  45.3 1.9 %collective-permute-start.12 = (bf16[128,1024]{1,0:T(8,128)(2,1)S(1)}, bf16[128,1024]{1,0:T(8,128)(2,1)S(1)}, u32[]{:S(2)}, u32[]{:S(2)}) collective-permute-start(bf16[128,1024]{1,0:T(8,128)(2,1)S(1)} %collective-permute-done.8.refs_7_.refs_3_), channel_id=1, source_target_pairs={{0,1},{1,0},{2,3},{3,2},{4,5},{5,4},{6,7},{7,6},{8,9},{9,8},{10,11... | collective-permute-start | bytes 786440 | tf_op jit(solution)/shard_map/ppermute | solution.py:361
  50.1 4.6 %collective-permute-start.15 = (f32[4,4,128]{2,1,0:T(4,128)S(1)}, f32[4,4,128]{2,1,0:T(4,128)S(1)}, u32[]{:S(2)}, u32[]{:S(2)}) collective-permute-start(f32[4,4,128]{2,1,0:T(4,128)S(1)} %get-tuple-element.67.refs_0_), channel_id=1, source_target_pairs={{0,6},{1,7},{2,4},{3,5},{4,2},{5,3},{6,0},{7,1},{8,14},{9,15},{10,... | collective-permute-start | bytes 24584 | tf_op jit(solution)/shard_map/ppermute | solution.py:361
  51.9 3.7 %collective-permute-start.14 = (f32[4,4,128]{2,1,0:T(4,128)S(1)}, f32[4,4,128]{2,1,0:T(4,128)S(1)}, u32[]{:S(2)}, u32[]{:S(2)}) collective-permute-start(f32[4,4,128]{2,1,0:T(4,128)S(1)} %get-tuple-element.67.refs_0_), channel_id=1, source_target_pairs={{0,4},{1,5},{2,6},{3,7},{4,0},{5,1},{6,2},{7,3},{8,12},{9,13},{10,... | collective-permute-start | bytes 24584 | tf_op jit(solution)/shard_map/ppermute | solution.py:361
  53.2 3.7 %collective-permute-start.13 = (f32[4,4,128]{2,1,0:T(4,128)S(1)}, f32[4,4,128]{2,1,0:T(4,128)S(1)}, u32[]{:S(2)}, u32[]{:S(2)}) collective-permute-start(f32[4,4,128]{2,1,0:T(4,128)S(1)} %get-tuple-element.67.refs_0_), channel_id=1, source_target_pairs={{0,2},{1,3},{2,0},{3,1},{4,6},{5,7},{6,4},{7,5},{8,10},{9,11},{10,... | collective-permute-start | bytes 24584 | tf_op jit(solution)/shard_map/ppermute | solution.py:361
  58.0 2.7 %collective-permute-start.16 = (bf16[512,1024]{1,0:T(8,128)(2,1)S(1)}, bf16[512,1024]{1,0:T(8,128)(2,1)S(1)}, u32[]{:S(2)}, u32[]{:S(2)}) collective-permute-start(bf16[512,1024]{1,0:T(8,128)(2,1)S(1)} %get-tuple-element.74), channel_id=1, source_target_pairs={{0,1},{1,0},{2,3},{3,2},{4,5},{5,4},{6,7},{7,6},{8,9},{9,8},{10,11... | collective-permute-start | bytes 3145736 | tf_op jit(solution)/shard_map/ppermute | solution.py:361
  60.9 9.2 %collective-permute-start.20 = (bf16[128,1024]{1,0:T(8,128)(2,1)S(1)}, bf16[128,1024]{1,0:T(8,128)(2,1)S(1)}, u32[]{:S(2)}, u32[]{:S(2)}) collective-permute-start(bf16[128,1024]{1,0:T(8,128)(2,1)S(1)} %get-tuple-element.81), channel_id=1, source_target_pairs={{0,8},{1,9},{2,10},{3,11},{4,12},{5,13},{6,14},{7,15},{8,0},{9,1},... | collective-permute-start | bytes 786440 | tf_op jit(solution)/shard_map/ppermute | solution.py:361
  63.1 9.3 %collective-permute-start.17 = (bf16[128,1024]{1,0:T(8,128)(2,1)S(1)}, bf16[128,1024]{1,0:T(8,128)(2,1)S(1)}, u32[]{:S(2)}, u32[]{:S(2)}) collective-permute-start(bf16[128,1024]{1,0:T(8,128)(2,1)S(1)} %get-tuple-element.77), channel_id=1, source_target_pairs={{0,2},{1,3},{2,0},{3,1},{4,6},{5,7},{6,4},{7,5},{8,10},{9,11},{10,... | collective-permute-start | bytes 786440 | tf_op jit(solution)/shard_map/ppermute | solution.py:361
  64.3 13.4 %collective-permute-start.18 = (bf16[128,1024]{1,0:T(8,128)(2,1)S(1)}, bf16[128,1024]{1,0:T(8,128)(2,1)S(1)}, u32[]{:S(2)}, u32[]{:S(2)}) collective-permute-start(bf16[128,1024]{1,0:T(8,128)(2,1)S(1)} %get-tuple-element.78), channel_id=1, source_target_pairs={{0,4},{1,5},{2,6},{3,7},{4,0},{5,1},{6,2},{7,3},{8,12},{9,13},{10,... | collective-permute-start | bytes 786440 | tf_op jit(solution)/shard_map/ppermute | solution.py:361
  64.9 12.8 %collective-permute-start.19 = (bf16[128,1024]{1,0:T(8,128)(2,1)S(1)}, bf16[128,1024]{1,0:T(8,128)(2,1)S(1)}, u32[]{:S(2)}, u32[]{:S(2)}) collective-permute-start(bf16[128,1024]{1,0:T(8,128)(2,1)S(1)} %get-tuple-element.79), channel_id=1, source_target_pairs={{0,6},{1,7},{2,4},{3,5},{4,2},{5,3},{6,0},{7,1},{8,14},{9,15},{10,... | collective-permute-start | bytes 786440 | tf_op jit(solution)/shard_map/ppermute | solution.py:361
  66.6 12.0 %collective-permute-start.22 = (bf16[128,1024]{1,0:T(8,128)(2,1)S(1)}, bf16[128,1024]{1,0:T(8,128)(2,1)S(1)}, u32[]{:S(2)}, u32[]{:S(2)}) collective-permute-start(bf16[128,1024]{1,0:T(8,128)(2,1)S(1)} %get-tuple-element.82), channel_id=1, source_target_pairs={{0,8},{1,9},{2,10},{3,11},{4,12},{5,13},{6,14},{7,15},{8,0},{9,1},... | collective-permute-start | bytes 786440 | tf_op jit(solution)/shard_map/ppermute | solution.py:361
  70.2 13.3 %collective-permute-start.21 = (bf16[128,1024]{1,0:T(8,128)(2,1)S(1)}, bf16[128,1024]{1,0:T(8,128)(2,1)S(1)}, u32[]{:S(2)}, u32[]{:S(2)}) collective-permute-start(bf16[128,1024]{1,0:T(8,128)(2,1)S(1)} %add_convert_fusion), channel_id=1, source_target_pairs={{0,16},{1,17},{2,18},{3,19},{4,20},{5,21},{6,22},{7,23},{8,24},{9,... | collective-permute-start | bytes 786440 | tf_op jit(solution)/shard_map/ppermute | solution.py:361
